TPU v7x, 32 devices: a whole 2x2x4 slice. The times are simulated.
32 devices in a mesh: groups: 2 (over y), wide: 4 (over x, core), narrow: 4 (over z).
Axes of the slice: x: 2, y: 2, z: 4, core: 2. Of those that a mesh axis runs over, the one named last changes fastest.
Arguments:
- order_init: float32 [16, 12, 32, 512], P('groups', None, 'wide', 'narrow'), parts along dimension 0, may hold values from 0 to 1
- cotangent: float32 [16, 12, 32, 512], P('groups', None, 'wide', 'narrow'), parts along dimension 0, may hold values from -6 to 6
- grain_map: int32 [24, 32, 512], P('groups', 'wide', 'narrow'), parts along dimension 0, may hold values from 0 to 63
- brick_grains: int32 [32, 64], P('groups'), parts along dimension 0, may hold values from 0 to 6271, as said below
- grain_slot: int32 [12544], P('groups'), parts along dimension 0, may hold values from 0 to 6271, each once
- mobility: float32 [12544], P(('groups', 'wide', 'narrow')), parts along dimension 0, may hold values from 0.25 to 1
Outputs:
- order_final: float32 [16, 12, 32, 512], P('groups', None, 'wide', 'narrow'), parts along dimension 0
- order_adjoint: float32 [16, 12, 32, 512], P('groups', None, 'wide', 'narrow'), parts along dimension 0
- mobility_grad: float32 [12544], P(('groups', 'wide', 'narrow')), parts along dimension 0
There are 2 independent parts, one for each index of `groups`. A program takes and returns all parts, laid end to end along the dimension named above; each array names one. Nothing has to cross between parts.
Inputs may be any that keep to these rules, and one draw needn't show every extreme that they name: `brick_grains`: each row lists 64 different grain ids.
All inputs are finite; a program needn't handle non-finite values.
Results may differ from a plain program's by a relative error of at most 0.00011.
Values sent between devices are 32-bit elements; how exact they have to be, the bound alone decides.
No kernel may reach another device: no remote copies, remote signals or barrier semaphores. Data moves between devices by JAX's collectives and lax.ppermute only.
A program may use at most 64 MiB of HBM per device.

v0:
```python
import jax
import jax.numpy as jnp
from jax import lax
from jax.sharding import PartitionSpec as P

ITERS = 4


linear_coef = 1.0
cubic_coef = 1.0
cross_coef = 0.75
gradient_coef = 1.0
time_step = 0.05


def extended(value, sides, width):
    for axis, dim in sides:
        count, length = (lax.axis_size(axis), value.shape[dim])
        up = [(i, (i + 1) % count) for i in range(count)]
        down = [(j, i) for i, j in up]
        last = lax.slice_in_dim(value, length - width, length, axis=dim)
        leading = lax.slice_in_dim(value, 0, width, axis=dim)
        before = lax.ppermute(last, axis, up)
        after = lax.ppermute(leading, axis, down)
        value = jnp.concatenate([before, value, after], axis=dim)
    return value


def reaction(order):
    squares = order * order
    total = jnp.sum(squares, axis=0, keepdims=True)
    return (
        -linear_coef * order
        + cubic_coef * order * squares
        + 2.0 * cross_coef * order * (total - squares)
    )


def second_variation(order, weighted):
    squares = order * order
    total = jnp.sum(squares, axis=0, keepdims=True)
    inner = jnp.sum(order * weighted, axis=0, keepdims=True)
    diagonal = -linear_coef + 3.0 * cubic_coef * squares + 2.0 * cross_coef * (total - squares)
    return diagonal * weighted + 4.0 * cross_coef * order * (inner - order * weighted)


def laplace_padded(padded):
    core = padded[:, :, 1:-1, 1:-1]
    side = (
        padded[:, :, 2:, 1:-1]
        + padded[:, :, :-2, 1:-1]
        + padded[:, :, 1:-1, 2:]
        + padded[:, :, 1:-1, :-2]
    )
    below = jnp.concatenate([core[:, :1], core[:, :-1]], axis=1)
    above = jnp.concatenate([core[:, 1:], core[:, -1:]], axis=1)
    return side + below + above - 6.0 * core


def spread_values(grain_map, values):
    labels = jnp.arange(values.shape[0], dtype=jnp.int32)

    def spread_one_layer(layer):
        return jnp.sum(
            jnp.where(layer[None] == labels[:, None, None], values[:, None, None], 0.0), axis=0
        )

    return lax.map(spread_one_layer, grain_map)


def collect_values(grain_map, cell_values, count):
    labels = jnp.arange(count, dtype=jnp.int32)

    def collect_one_layer(pair):
        layer, values = pair
        return jnp.sum(
            jnp.where(layer[None] == labels[:, None, None], values[None], 0.0), axis=(1, 2)
        )

    return jnp.sum(lax.map(collect_one_layer, (grain_map, cell_values)), axis=0)


def per_device(order_init, cotangent, grain_map, brick_grains, grain_slot, mobility):
    listed_count = brick_grains.shape[1]
    owned = mobility.shape[0]
    narrow_count = lax.axis_size("narrow")
    brick = lax.axis_index("wide") * narrow_count + lax.axis_index("narrow")
    listed = lax.dynamic_index_in_dim(brick_grains, brick, 0, keepdims=False)
    slots = grain_slot[listed]
    every_mobility = lax.all_gather(mobility, ("wide", "narrow"), axis=0, tiled=True)
    brick_mobility = every_mobility[slots]
    cell_mobility = spread_values(grain_map, brick_mobility)[None]
    order = order_init
    states = []
    rates = []
    for step in range(ITERS):
        padded = extended(order, (("wide", 2), ("narrow", 3)), 1)
        rate = reaction(order) - gradient_coef * laplace_padded(padded)
        states.append(order)
        rates.append(rate)
        order = order - time_step * cell_mobility * rate
    adjoint = cotangent
    cell_sum = jnp.zeros(grain_map.shape, jnp.float32)
    for step in reversed(range(ITERS)):
        old = states[step]
        weighted = cell_mobility * adjoint
        rate = rates[step]
        padded_weighted = extended(weighted, (("wide", 2), ("narrow", 3)), 1)
        lap_weighted = laplace_padded(padded_weighted)
        cell_sum = cell_sum - time_step * jnp.sum(adjoint * rate, axis=0)
        adjoint = (
            adjoint
            - time_step * second_variation(old, weighted)
            + time_step * gradient_coef * lap_weighted
        )
    local_sums = collect_values(grain_map, cell_sum, listed_count)
    whole = (
        jnp.zeros((owned * lax.axis_size("wide") * narrow_count,), jnp.float32)
        .at[slots]
        .add(local_sums)
    )
    grads = lax.psum_scatter(whole, ("wide", "narrow"), scatter_dimension=0, tiled=True)
    return (order, adjoint, grads)


def solution(mesh):
    placed = (
        P("groups", None, "wide", "narrow"),
        P("groups", None, "wide", "narrow"),
        P("groups", "wide", "narrow"),
        P("groups", None),
        P("groups"),
        P(("groups", "wide", "narrow")),
    )
    return jax.shard_map(
        per_device,
        mesh=mesh,
        in_specs=placed,
        out_specs=(
            P("groups", None, "wide", "narrow"),
            P("groups", None, "wide", "narrow"),
            P(("groups", "wide", "narrow")),
        ),
        check_vma=False,
    )
```

profile of v0, /device:TPU:0, one launch (start us, length us, event | category | flops | bytes accessed | tf_op | source)
XLA Modules:
  0.0 285.9 jit_solution(2610137993895382042)
XLA Ops:
  0.7 4.2 %copy.143 = f32[8,12,8,128]{1,0,3,2:T(8,128)} copy(f32[8,12,8,128]{3,2,1,0:T(8,128)} %param.10) | data formatting | bytes 786432 | tf_op args[0]
  4.9 2.1 fusion.115
  7.0 2.4 collective-permute-start
  12.5 62.6 %all-reduce = f32[6272]{0:T(1024)S(1)} all-reduce(f32[6272]{0:T(1024)S(1)} %dynamic-update-slice), channel_id=1, replica_groups=mesh['groups'=2,'wide'=4,'narrow'=4] {'wide','narrow'}, use_global_device_ids=true, to_apply=%add | all-reduce | flops 6272 | bytes 50176
  75.8 10.3 %while.22 = (s32[]{:T(128)}, f32[12,8,128]{2,1,0:T(8,128)S(1)}, s32[12,8,128]{2,1,0:T(8,128)}, f32[64]{0:T(128)S(1)}, s32[]{:T(128)}) while((s32[]{:T(128)}, f32[12,8,128]{2,1,0:T(8,128)S(1)}, s32[12,8,128]{2,1,0:T(8,128)}, f32[64]{0:T(128)S(1)}, s32[]{:T(128)}) %tuple.93), condition=%wide.region_2.3_spmd.clone, body=%wide.region_0.2_spmd.clone.sunk | while | flops 195586 | bytes 24901 | solution.py:68
  90.6 2.6 pad_maximum_fusion
  93.2 2.3 copy-done.1
  95.6 2.0 collective-permute-start.3
  97.8 4.0 %copy.150 = f32[8,12,10,128]{3,0,2,1:T(8,128)} copy(f32[8,12,10,128]{1,0,3,2:T(8,128)} %copy-done.1) | data formatting | bytes 983040 | tf_op jit(solution)/shard_map/concatenate | solution.py:25
  106.9 3.7 %multiply_subtract_fusion.4 = (f32[8,12,8,128]{3,0,2,1:T(8,128)S(1)}, f32[8,12,8,128]{3,0,2,1:T(8,128)}, f32[8,12,8,128]{3,0,2,1:T(8,128)}) fusion(f32[12,8,128]{2,1,0:T(8,128)S(1)} %broadcast_multiply_fusion.3, f32[8,12,8,128]{3,2,1,0:T(8,128)S(1)} %copy-done.2, f32[8,12,8,128]{3,0,2,1:T(8,128)} %copy.157, f32[8,12,8,128]{3,2,1,0:T(8,128)} %get-tuple-element.205, ...), kind=kOutput, calls=%fused_computation.187 | output fusion | flops 2174983 | bytes 3399168 | tf_op jit(solution)/shard_map/sub | solution.py:35
  115.5 3.6 %collective-permute-start.6 = (f32[8,12,10,1]{1,0,3,2:T(8,128)S(1)}, f32[8,12,10,1]{1,0,3,2:T(8,128)S(1)}, u32[]{:S(2)}, u32[]{:S(2)}) collective-permute-start(f32[8,12,10,1]{1,0,3,2:T(8,128)S(1)} %copy.202), channel_id=1, source_target_pairs={{1,0},{2,1},{3,2},{0,3},{5,4},{6,5},{7,6},{4,7},{9,8},{10,9},{11,1... | collective-permute-start | bytes 11528 | tf_op jit(solution)/shard_map/ppermute | solution.py:24
  126.1 2.3 multiply_subtract_fusion.3
  130.3 2.0 collective-permute-done.9
  133.1 2.2 collective-permute-start.10
  137.8 3.9 %collective-permute-done.11 = f32[8,12,10,1]{1,0,3,2:T(8,128)S(1)} collective-permute-done((f32[8,12,10,1]{1,0,3,2:T(8,128)S(1)}, f32[8,12,10,1]{1,0,3,2:T(8,128)S(1)}, u32[]{:S(2)}, u32[]{:S(2)}) %collective-permute-start.11) | collective-permute-done | bytes 3872 | tf_op jit(solution)/shard_map/ppermute | solution.py:23
  142.3 2.5 multiply_subtract_fusion.2
  146.6 1.9 collective-permute-done.13
  150.0 2.0 collective-permute-start.15
  158.4 2.1 fusion.27
  174.2 1.9 fusion.31
  184.5 2.1 collective-permute-start.27
  192.0 2.1 fusion.35
  199.1 15.6 %while.23 = (s32[]{:T(128)}, f32[12,64]{1,0:T(8,128)S(1)}, s32[12,8,128]{2,1,0:T(8,128)}, f32[12,8,128]{2,1,0:T(8,128)S(1)}, s32[]{:T(128)}, /*index=5*/s32[]{:T(128)}) while((s32[]{:T(128)}, f32[12,64]{1,0:T(8,128)S(1)}, s32[12,8,128]{2,1,0:T(8,128)}, f32[12,8,128]{2,1,0:T(8,128)S(1)}, s32[]{:T(128)}, ...), condition=%wide.region_17.18_spmd.clone, body=%wide.region_15.17_spmd.clone.sunk | while | flops 196546 | bytes 25425 | solution.py:80
  221.8 59.7 %all-reduce.1 = f32[6272]{0:T(1024)S(1)} all-reduce(f32[6272]{0:T(1024)S(1)} %scatter_custom_fusion), channel_id=2, replica_groups=mesh['groups'=2,'wide'=4,'narrow'=4] {'wide','narrow'}, use_global_device_ids=true, to_apply=%region_20.21.clone | all-reduce | flops 6272 | bytes 50176
  (266 shorter events, 108.6 us)
Async XLA Ops:
  7.0 83.6 %collective-permute-start = (f32[8,12,1,128]{1,0,3,2:T(8,128)}, f32[8,12,1,128]{1,0,3,2:T(8,128)S(1)}, u32[]{:S(2)}, u32[]{:S(2)}) collective-permute-start(f32[8,12,1,128]{1,0,3,2:T(8,128)} %get-tuple-element.131), channel_id=1, source_target_pairs={{4,0},{8,4},{12,8},{0,12},{5,1},{9,5},{13,9},{1,13},{6,2},{10,6},{... | collective-permute-start | bytes 147464 | tf_op jit(solution)/shard_map/ppermute | solution.py:24
  9.4 81.2 %collective-permute-start.1 = (f32[8,12,1,128]{1,0,3,2:T(8,128)S(1)}, f32[8,12,1,128]{1,0,3,2:T(8,128)S(1)}, u32[]{:S(2)}, u32[]{:S(2)}) collective-permute-start(f32[8,12,1,128]{1,0,3,2:T(8,128)S(1)} %get-tuple-element.130), channel_id=1, source_target_pairs={{0,4},{4,8},{8,12},{12,0},{1,5},{5,9},{9,13},{13,1},{2,6},{6,10},{... | collective-permute-start | bytes 147464 | tf_op jit(solution)/shard_map/ppermute | solution.py:23
  86.5 11.1 %collective-permute-start.16 = (f32[8,12,1,128]{3,0,2,1:T(8,128)S(1)}, f32[8,12,1,128]{3,0,2,1:T(8,128)S(1)}, u32[]{:S(2)}, u32[]{:S(2)}) collective-permute-start(f32[8,12,1,128]{3,0,2,1:T(8,128)S(1)} %get-tuple-element.175), channel_id=1, source_target_pairs={{4,0},{8,4},{12,8},{0,12},{5,1},{9,5},{13,9},{1,13},{6,2},{10,6},{... | collective-permute-start | bytes 147464 | tf_op jit(solution)/shard_map/ppermute | solution.py:24
  86.5 11.1 %collective-permute-start.17 = (f32[8,12,1,128]{3,0,2,1:T(8,128)S(1)}, f32[8,12,1,128]{3,0,2,1:T(8,128)S(1)}, u32[]{:S(2)}, u32[]{:S(2)}) collective-permute-start(f32[8,12,1,128]{3,0,2,1:T(8,128)S(1)} %get-tuple-element.174), channel_id=1, source_target_pairs={{0,4},{4,8},{8,12},{12,0},{1,5},{5,9},{9,13},{13,1},{2,6},{6,10},{... | collective-permute-start | bytes 147464 | tf_op jit(solution)/shard_map/ppermute | solution.py:23
  95.6 10.0 %collective-permute-start.2 = (f32[8,12,10,1]{1,0,3,2:T(8,128)S(1)}, f32[8,12,10,1]{1,0,3,2:T(8,128)S(1)}, u32[]{:S(2)}, u32[]{:S(2)}) collective-permute-start(f32[8,12,10,1]{1,0,3,2:T(8,128)S(1)} %get-tuple-element.128), channel_id=1, source_target_pairs={{1,0},{2,1},{3,2},{0,3},{5,4},{6,5},{7,6},{4,7},{9,8},{10,9},{11,1... | collective-permute-start | bytes 11528 | tf_op jit(solution)/shard_map/ppermute | solution.py:24
  95.6 10.6 %collective-permute-start.3 = (f32[8,12,10,1]{1,0,3,2:T(8,128)S(1)}, f32[8,12,10,1]{1,0,3,2:T(8,128)S(1)}, u32[]{:S(2)}, u32[]{:S(2)}) collective-permute-start(f32[8,12,10,1]{1,0,3,2:T(8,128)S(1)} %get-tuple-element.129), channel_id=1, source_target_pairs={{0,1},{1,2},{2,3},{3,0},{4,5},{5,6},{6,7},{7,4},{8,9},{9,10},{10,1... | collective-permute-start | bytes 11528 | tf_op jit(solution)/shard_map/ppermute | solution.py:23
  102.4 17.9 %collective-permute-start.18 = (f32[8,12,10,1]{1,0,3,2:T(8,128)S(1)}, f32[8,12,10,1]{1,0,3,2:T(8,128)S(1)}, u32[]{:S(2)}, u32[]{:S(2)}) collective-permute-start(f32[8,12,10,1]{1,0,3,2:T(8,128)S(1)} %copy.208), channel_id=1, source_target_pairs={{1,0},{2,1},{3,2},{0,3},{5,4},{6,5},{7,6},{4,7},{9,8},{10,9},{11,1... | collective-permute-start | bytes 11528 | tf_op jit(solution)/shard_map/ppermute | solution.py:24
  104.9 16.9 %collective-permute-start.19 = (f32[8,12,10,1]{1,0,3,2:T(8,128)S(1)}, f32[8,12,10,1]{1,0,3,2:T(8,128)S(1)}, u32[]{:S(2)}, u32[]{:S(2)}) collective-permute-start(f32[8,12,10,1]{1,0,3,2:T(8,128)S(1)} %copy.209), channel_id=1, source_target_pairs={{0,1},{1,2},{2,3},{3,0},{4,5},{5,6},{6,7},{7,4},{8,9},{9,10},{10,1... | collective-permute-start | bytes 11528 | tf_op jit(solution)/shard_map/ppermute | solution.py:23
  115.5 7.7 %collective-permute-start.6 = (f32[8,12,10,1]{1,0,3,2:T(8,128)S(1)}, f32[8,12,10,1]{1,0,3,2:T(8,128)S(1)}, u32[]{:S(2)}, u32[]{:S(2)}) collective-permute-start(f32[8,12,10,1]{1,0,3,2:T(8,128)S(1)} %copy.202), channel_id=1, source_target_pairs={{1,0},{2,1},{3,2},{0,3},{5,4},{6,5},{7,6},{4,7},{9,8},{10,9},{11,1... | collective-permute-start | bytes 11528 | tf_op jit(solution)/shard_map/ppermute | solution.py:24
  119.7 5.8 %collective-permute-start.7 = (f32[8,12,10,1]{1,0,3,2:T(8,128)S(1)}, f32[8,12,10,1]{1,0,3,2:T(8,128)S(1)}, u32[]{:S(2)}, u32[]{:S(2)}) collective-permute-start(f32[8,12,10,1]{1,0,3,2:T(8,128)S(1)} %copy.203), channel_id=1, source_target_pairs={{0,1},{1,2},{2,3},{3,0},{4,5},{5,6},{6,7},{7,4},{8,9},{9,10},{10,1... | collective-permute-start | bytes 11528 | tf_op jit(solution)/shard_map/ppermute | solution.py:23
  128.6 3.7 %collective-permute-start.9 = (f32[8,12,1,128]{3,0,2,1:T(8,128)S(1)}, f32[8,12,1,128]{3,0,2,1:T(8,128)S(1)}, u32[]{:S(2)}, u32[]{:S(2)}) collective-permute-start(f32[8,12,1,128]{3,0,2,1:T(8,128)S(1)} %get-tuple-element.182), channel_id=1, source_target_pairs={{0,4},{4,8},{8,12},{12,0},{1,5},{5,9},{9,13},{13,1},{2,6},{6,10},{... | collective-permute-start | bytes 147464 | tf_op jit(solution)/shard_map/ppermute | solution.py:23
  133.1 4.0 %collective-permute-start.10 = (f32[8,12,10,1]{1,0,3,2:T(8,128)S(1)}, f32[8,12,10,1]{1,0,3,2:T(8,128)S(1)}, u32[]{:S(2)}, u32[]{:S(2)}) collective-permute-start(f32[8,12,10,1]{1,0,3,2:T(8,128)S(1)} %copy.204), channel_id=1, source_target_pairs={{1,0},{2,1},{3,2},{0,3},{5,4},{6,5},{7,6},{4,7},{9,8},{10,9},{11,1... | collective-permute-start | bytes 11528 | tf_op jit(solution)/shard_map/ppermute | solution.py:24
  135.9 5.8 %collective-permute-start.11 = (f32[8,12,10,1]{1,0,3,2:T(8,128)S(1)}, f32[8,12,10,1]{1,0,3,2:T(8,128)S(1)}, u32[]{:S(2)}, u32[]{:S(2)}) collective-permute-start(f32[8,12,10,1]{1,0,3,2:T(8,128)S(1)} %copy.205), channel_id=1, source_target_pairs={{0,1},{1,2},{2,3},{3,0},{4,5},{5,6},{6,7},{7,4},{8,9},{9,10},{10,1... | collective-permute-start | bytes 11528 | tf_op jit(solution)/shard_map/ppermute | solution.py:23
  144.9 3.7 %collective-permute-start.13 = (f32[8,12,1,128]{3,0,2,1:T(8,128)S(1)}, f32[8,12,1,128]{3,0,2,1:T(8,128)S(1)}, u32[]{:S(2)}, u32[]{:S(2)}) collective-permute-start(f32[8,12,1,128]{3,0,2,1:T(8,128)S(1)} %get-tuple-element.176), channel_id=1, source_target_pairs={{0,4},{4,8},{8,12},{12,0},{1,5},{5,9},{9,13},{13,1},{2,6},{6,10},{... | collective-permute-start | bytes 147464 | tf_op jit(solution)/shard_map/ppermute | solution.py:23
  149.4 4.0 %collective-permute-start.14 = (f32[8,12,10,1]{1,0,3,2:T(8,128)S(1)}, f32[8,12,10,1]{1,0,3,2:T(8,128)S(1)}, u32[]{:S(2)}, u32[]{:S(2)}) collective-permute-start(f32[8,12,10,1]{1,0,3,2:T(8,128)S(1)} %copy.206), channel_id=1, source_target_pairs={{1,0},{2,1},{3,2},{0,3},{5,4},{6,5},{7,6},{4,7},{9,8},{10,9},{11,1... | collective-permute-start | bytes 11528 | tf_op jit(solution)/shard_map/ppermute | solution.py:24
  150.0 5.8 %collective-permute-start.15 = (f32[8,12,10,1]{1,0,3,2:T(8,128)S(1)}, f32[8,12,10,1]{1,0,3,2:T(8,128)S(1)}, u32[]{:S(2)}, u32[]{:S(2)}) collective-permute-start(f32[8,12,10,1]{1,0,3,2:T(8,128)S(1)} %copy.207), channel_id=1, source_target_pairs={{0,1},{1,2},{2,3},{3,0},{4,5},{5,6},{6,7},{7,4},{8,9},{9,10},{10,1... | collective-permute-start | bytes 11528 | tf_op jit(solution)/shard_map/ppermute | solution.py:23
  166.3 4.0 %collective-permute-start.22 = (f32[8,12,10,1]{1,0,3,2:T(8,128)S(1)}, f32[8,12,10,1]{1,0,3,2:T(8,128)S(1)}, u32[]{:S(2)}, u32[]{:S(2)}) collective-permute-start(f32[8,12,10,1]{1,0,3,2:T(8,128)S(1)} %copy.210), channel_id=1, source_target_pairs={{1,0},{2,1},{3,2},{0,3},{5,4},{6,5},{7,6},{4,7},{9,8},{10,9},{11,1... | collective-permute-start | bytes 11528 | tf_op jit(solution)/shard_map/ppermute | solution.py:24
  167.0 5.8 %collective-permute-start.23 = (f32[8,12,10,1]{1,0,3,2:T(8,128)S(1)}, f32[8,12,10,1]{1,0,3,2:T(8,128)S(1)}, u32[]{:S(2)}, u32[]{:S(2)}) collective-permute-start(f32[8,12,10,1]{1,0,3,2:T(8,128)S(1)} %copy.211), channel_id=1, source_target_pairs={{0,1},{1,2},{2,3},{3,0},{4,5},{5,6},{6,7},{7,4},{8,9},{9,10},{10,1... | collective-permute-start | bytes 11528 | tf_op jit(solution)/shard_map/ppermute | solution.py:23
  177.6 3.6 %collective-permute-start.25 = (f32[8,12,1,128]{3,0,2,1:T(8,128)S(1)}, f32[8,12,1,128]{3,0,2,1:T(8,128)S(1)}, u32[]{:S(2)}, u32[]{:S(2)}) collective-permute-start(f32[8,12,1,128]{3,0,2,1:T(8,128)S(1)} %get-tuple-element.162), channel_id=1, source_target_pairs={{0,4},{4,8},{8,12},{12,0},{1,5},{5,9},{9,13},{13,1},{2,6},{6,10},{... | collective-permute-start | bytes 147464 | tf_op jit(solution)/shard_map/ppermute | solution.py:23
  183.8 4.0 %collective-permute-start.26 = (f32[8,12,10,1]{1,0,3,2:T(8,128)S(1)}, f32[8,12,10,1]{1,0,3,2:T(8,128)S(1)}, u32[]{:S(2)}, u32[]{:S(2)}) collective-permute-start(f32[8,12,10,1]{1,0,3,2:T(8,128)S(1)} %copy.212), channel_id=1, source_target_pairs={{1,0},{2,1},{3,2},{0,3},{5,4},{6,5},{7,6},{4,7},{9,8},{10,9},{11,1... | collective-permute-start | bytes 11528 | tf_op jit(solution)/shard_map/ppermute | solution.py:24
  184.5 6.0 %collective-permute-start.27 = (f32[8,12,10,1]{1,0,3,2:T(8,128)S(1)}, f32[8,12,10,1]{1,0,3,2:T(8,128)S(1)}, u32[]{:S(2)}, u32[]{:S(2)}) collective-permute-start(f32[8,12,10,1]{1,0,3,2:T(8,128)S(1)} %copy.213), channel_id=1, source_target_pairs={{0,1},{1,2},{2,3},{3,0},{4,5},{5,6},{6,7},{7,4},{8,9},{9,10},{10,1... | collective-permute-start | bytes 11528 | tf_op jit(solution)/shard_map/ppermute | solution.py:23
  214.7 3.6 %collective-permute-start.29 = (f32[8,12,1,128]{3,0,2,1:T(8,128)S(1)}, f32[8,12,1,128]{3,0,2,1:T(8,128)S(1)}, u32[]{:S(2)}, u32[]{:S(2)}) collective-permute-start(f32[8,12,1,128]{3,0,2,1:T(8,128)S(1)} %get-tuple-element.156), channel_id=1, source_target_pairs={{0,4},{4,8},{8,12},{12,0},{1,5},{5,9},{9,13},{13,1},{2,6},{6,10},{... | collective-permute-start | bytes 147464 | tf_op jit(solution)/shard_map/ppermute | solution.py:23
  219.1 63.1 %collective-permute-start.30 = (f32[8,12,10,1]{1,0,3,2:T(8,128)S(1)}, f32[8,12,10,1]{1,0,3,2:T(8,128)S(1)}, u32[]{:S(2)}, u32[]{:S(2)}) collective-permute-start(f32[8,12,10,1]{1,0,3,2:T(8,128)S(1)} %copy.214), channel_id=1, source_target_pairs={{1,0},{2,1},{3,2},{0,3},{5,4},{6,5},{7,6},{4,7},{9,8},{10,9},{11,1... | collective-permute-start | bytes 11528 | tf_op jit(solution)/shard_map/ppermute | solution.py:24
  220.5 62.3 %collective-permute-start.31 = (f32[8,12,10,1]{1,0,3,2:T(8,128)S(1)}, f32[8,12,10,1]{1,0,3,2:T(8,128)S(1)}, u32[]{:S(2)}, u32[]{:S(2)}) collective-permute-start(f32[8,12,10,1]{1,0,3,2:T(8,128)S(1)} %copy.215), channel_id=1, source_target_pairs={{0,1},{1,2},{2,3},{3,0},{4,5},{5,6},{6,7},{7,4},{8,9},{9,10},{10,1... | collective-permute-start | bytes 11528 | tf_op jit(solution)/shard_map/ppermute | solution.py:23
  (21 other events, 430.2 us)
where the time goes:
time: 287 us; the launch traced here: 286 us
  blocking collectives  122 us (43%)
  local copies, waits for them, and re-layouts  73.3 us (26%)
  other arithmetic  36.6 us (13%)
  waiting for transfers between devices  26 us (9%)
  starting transfers between devices  24.8 us (9%)
    unnamed x2, blocking collectives  122 us
    unnamed x53, local copies, waits for them, and re-layouts  23 us
    ppermute x16, waiting for transfers between devices, extended(): before = lax.ppermute(last, axis, up)  21.8 us
    ppermute x16, starting transfers between devices, extended(): before = lax.ppermute(last, axis, up)  12.5 us
    ppermute x16, starting transfers between devices, extended(): after = lax.ppermute(leading, axis, down)  12.2 us
    sub x4, other arithmetic, reaction(): total - squares  10.4 us
    eq x12, local copies, waits for them, and re-layouts, collect_one_layer(): layer[None] == labels[:, None, None]  8.32 us
    eq x12, local copies, waits for them, and re-layouts, spread_one_layer(): layer[None] == labels[:, None, None]  8.3 us
  transfers between devices with their start and end apart: 32, of which 21 were waited for; matrix products, arithmetic and copies ran while one was open for 18% of the time, Pallas kernels for 0%

commit v1 on v0

v1 whole, which is shorter than its diff:
```python
import functools

import jax
import jax.numpy as jnp
from jax import lax
from jax.experimental import pallas as pl
from jax.experimental.pallas import tpu as pltpu
from jax.sharding import PartitionSpec as P

ITERS = 4
TIME_STEP = 0.05

EDGE = 6
ADJ_EDGE = 4
ROWS = 24
COLS = 10
CORNER = (5, 3, 4)

VMEM_LIMIT = 50 * 1024 * 1024


def lanes(shape):
    return lax.broadcasted_iota(jnp.int32, shape, len(shape) - 1)


def roll(value, shift):
    return pltpu.roll(value, shift, 1)


def pack_rows(order_ref, map_ref, down_ref, up_ref):
    params, layers = order_ref.shape[:2]
    for p in range(params):
        for z in range(layers):
            k = (p * layers + z) * EDGE
            down_ref[k : k + EDGE, :] = order_ref[p, z, 8 - EDGE : 8, :]
            up_ref[k : k + EDGE, :] = order_ref[p, z, 0:EDGE, :]
    for z in range(layers):
        k = (params * layers + z) * EDGE
        cells = map_ref[z].astype(jnp.float32)
        down_ref[k : k + EDGE, :] = cells[8 - EDGE : 8]
        up_ref[k : k + EDGE, :] = cells[0:EDGE]


def pack_strips(
    order_ref, cot_ref, map_ref,
    cot_down_ref, cot_up_ref, right_ref, left_ref,
    right_down_ref, left_down_ref, right_up_ref, left_up_ref,
):
    params, layers = order_ref.shape[:2]
    lane = lanes((8, 128))
    to_right = []
    to_left = []
    for z in range(layers):
        first = 10 * z - 1
        inside = (lane >= first) & (lane < first + 6)
        if z == 0:
            inside = inside | (lane == 127)
        to_right.append(inside)
        to_left.append((lane >= 10 * z + 5) & (lane < 10 * z + 11))

    def strip_of(read):
        right = jnp.zeros((8, 128), jnp.float32)
        left = jnp.zeros((8, 128), jnp.float32)
        for z in range(layers):
            moved = roll(read(z), 10 * z + 5)
            right = jnp.where(to_right[z], moved, right)
            left = jnp.where(to_left[z], moved, left)
        return right, left

    at = 0
    for field in range(2 * params + 1):
        if field < params:
            kind, read = 0, lambda z, p=field: order_ref[p, z]
        elif field < 2 * params:
            kind, read = 1, lambda z, p=field - params: cot_ref[p, z]
        else:
            kind, read = 2, lambda z: map_ref[z].astype(jnp.float32)
        right, left = strip_of(read)
        right_ref[8 * field : 8 * field + 8, :] = right
        left_ref[8 * field : 8 * field + 8, :] = left
        n = CORNER[kind]
        right_down_ref[at : at + n, :] = right[8 - n : 8]
        left_down_ref[at : at + n, :] = left[8 - n : 8]
        right_up_ref[at : at + n, :] = right[0:n]
        left_up_ref[at : at + n, :] = left[0:n]
        at += n
    for p in range(params):
        for z in range(layers):
            k = (p * layers + z) * ADJ_EDGE
            cot_down_ref[k : k + ADJ_EDGE, :] = cot_ref[p, z, 8 - ADJ_EDGE : 8, :]
            cot_up_ref[k : k + ADJ_EDGE, :] = cot_ref[p, z, 0:ADJ_EDGE, :]


def find_slots(bricks_ref, slot_ref, out_ref):
    count, listed = bricks_ref.shape
    rows = slot_ref.shape[0]
    pad = jnp.zeros((8, 128 - listed), jnp.int32)
    for k in range(0, count, 8):
        grain = jnp.concatenate([bricks_ref[k : k + 8, :], pad], axis=1)
        row, col = grain >> 7, grain & 127

        def body(r, found, row=row, col=col):
            table = jnp.broadcast_to(slot_ref[pl.ds(r, 1), :], (8, 128))
            taken = jnp.take_along_axis(table, col, axis=1, mode="promise_in_bounds")
            return jnp.where(row == r, taken, found)

        found = lax.fori_loop(0, rows, body, jnp.zeros((8, 128), jnp.int32), unroll=7)
        out_ref[k : k + 8, :] = jnp.where(lanes((8, 128)) < listed, found, -1)


def evolve(
    counts, owned,
    order_ref, cot_ref, map_ref, above_ref, below_ref, cot_above_ref, cot_below_ref,
    left_ref, right_ref, left_above_ref, right_above_ref, left_below_ref, right_below_ref,
    slots_ref, mob_ref,
    final_ref, adjoint_ref, sums_ref,
    e_ref, se_ref, rate_ref, inject_ref, outer_ref, lam_ref, slam_ref, u_ref, su_ref,
    m_ref, ms_ref, g_ref, gs_ref, near_ref, table_ref, cell_ref, binned_ref,
):
    wide_count, narrow_count = counts
    params, layers = order_ref.shape[:2]
    tile = (8, 128)
    lane = lanes(tile)
    col = lane % COLS
    wide, narrow = lax.axis_index("wide"), lax.axis_index("narrow")

    for i in range(3):
        for j in range(3):
            w = lax.rem(wide + i - 1 + wide_count, wide_count)
            n = lax.rem(narrow + j - 1 + narrow_count, narrow_count)
            near_ref[3 * i + j : 3 * i + j + 1, :] = slots_ref[pl.ds(w * narrow_count + n, 1), :]
    near_ref[9:16, :] = jnp.zeros((7, 128), jnp.int32)
    per_owner = mob_ref.shape[0] // (wide_count * narrow_count)
    for k in (0, 8):
        slot = jnp.maximum(near_ref[k : k + 8, :], 0)
        owner = jnp.floor((slot.astype(jnp.float32) + 0.5) * (1.0 / owned)).astype(jnp.int32)
        inner = slot - owner * owned
        by_wide = jnp.floor((owner.astype(jnp.float32) + 0.5) * (1.0 / narrow_count)).astype(jnp.int32)
        by_narrow = owner - by_wide * narrow_count
        back_w = wide - by_wide
        back_w = jnp.where(back_w < 0, back_w + wide_count, back_w)
        back_n = narrow - by_narrow
        back_n = jnp.where(back_n < 0, back_n + narrow_count, back_n)
        row = (back_n * wide_count + back_w) * per_owner + (inner >> 7)
        place = inner & 127

        def body(r, found, row=row, place=place):
            values = jnp.broadcast_to(mob_ref[pl.ds(r, 1), :], tile)
            taken = jnp.take_along_axis(values, place, axis=1, mode="promise_in_bounds")
            return jnp.where(row == r, taken, found)

        found = lax.fori_loop(0, mob_ref.shape[0], body, jnp.zeros(tile, jnp.float32), unroll=8)
        table_ref[k : k + 8, :] = TIME_STEP * found

    for z in range(layers):
        g_ref[z, 0:8, :] = jnp.zeros(tile, jnp.float32)
        g_ref[z, 16:24, :] = jnp.zeros(tile, jnp.float32)
        k = (params * layers + z) * EDGE
        g_ref[z, 8 - EDGE : 8, :] = above_ref[k : k + EDGE, :]
        g_ref[z, 16 : 16 + EDGE, :] = below_ref[k : k + EDGE, :]
    for p in range(params):
        for z in range(layers):
            k = (p * layers + z) * EDGE
            e_ref[0, p, z, 8 - EDGE : 8, :] = above_ref[k : k + EDGE, :]
            e_ref[0, p, z, 8:16, :] = order_ref[p, z]
            e_ref[0, p, z, 16 : 16 + EDGE, :] = below_ref[k : k + EDGE, :]
            k = (p * layers + z) * ADJ_EDGE
            lam_ref[p, z, 8 - ADJ_EDGE : 8, :] = cot_above_ref[k : k + ADJ_EDGE, :]
            lam_ref[p, z, 8:16, :] = cot_ref[p, z]
            lam_ref[p, z, 16 : 16 + ADJ_EDGE, :] = cot_below_ref[k : k + ADJ_EDGE, :]

    def merged(from_left, from_right):
        c = lanes(from_left.shape) % COLS
        return jnp.where(c < 5, from_left, from_right)

    def outermost(from_left, from_right):
        return jnp.where(lanes(from_left.shape) % COLS == 0, roll(from_left, 1), roll(from_right, 127))

    at = 0
    for field in range(2 * params + 1):
        kind = 0 if field < params else 1 if field < 2 * params else 2
        n = CORNER[kind]
        blocks = (
            (left_above_ref[at : at + n, :], right_above_ref[at : at + n, :], 8 - n, n),
            (left_ref[8 * field : 8 * field + 8, :], right_ref[8 * field : 8 * field + 8, :], 8, 8),
            (left_below_ref[at : at + n, :], right_below_ref[at : at + n, :], 16, n),
        )
        at += n
        if kind == 2:
            gs_ref[...] = jnp.zeros_like(gs_ref)
        for a, b, first, n in blocks:
            if kind == 0:
                se_ref[0, field, first : first + n, :] = merged(a, b)
                outer_ref[field, first : first + n, :] = outermost(a, b)
            elif kind == 1:
                slam_ref[field - params, first : first + n, :] = merged(a, b)
            else:
                gs_ref[first : first + n, :] = merged(a, b)

    def lookup(index, which):
        values = jnp.broadcast_to(table_ref[which : which + 1, :], tile)
        return jnp.take_along_axis(values, index, axis=1, mode="promise_in_bounds")

    for i in range(3):
        r = 8 * i
        for z in range(layers):
            index = map_ref[z] if i == 1 else g_ref[z, r : r + 8, :].astype(jnp.int32)
            m_ref[z, r : r + 8, :] = lookup(index, 3 * i + 1)
        index = gs_ref[r : r + 8, :].astype(jnp.int32)
        ms_ref[r : r + 8, :] = jnp.where(col < 5, lookup(index, 3 * i), lookup(index, 3 * i + 2))

    def sides(value, strip, z):
        ends = roll(strip, 123 - 10 * z)
        left = roll(jnp.where(lane == 127, ends, value), 1)
        right = roll(jnp.where(lane == 0, ends, value), 127)
        return left + right

    def note_ends(value, p, r, z):
        moved = roll(value, 10 * z + 5)
        here = (lane == 10 * z + 4) | (lane == 10 * z + 5)
        inject_ref[p, r : r + 8, :] = jnp.where(here, moved, inject_ref[p, r : r + 8, :])

    def strip_sides(value, ends, outer=None):
        left = roll(jnp.where(col == 4, ends, value), 1)
        right = roll(jnp.where(col == 5, ends, value), 127)
        if outer is not None:
            left = jnp.where(col == 0, outer, left)
            right = jnp.where(col == 9, outer, right)
        below = jnp.where(lane < COLS, value, roll(value, COLS))
        above = jnp.where(lane >= COLS * (layers - 1), value, roll(value, 128 - COLS))
        return (left + right) + (below + above)

    def total_of(values):
        while len(values) > 1:
            values = [a + b for a, b in zip(values[::2], values[1::2])]
        return values[0]

    def forward(t, windows, last):
        old, old_strip = e_ref.at[t], se_ref.at[t]

        def layer(z, carry):
            below, above = jnp.maximum(z - 1, 0), jnp.minimum(z + 1, layers - 1)
            for r in windows:
                rows = slice(r, r + 8)
                e = [old[p, z, rows, :] for p in range(params)]
                squares = [x * x for x in e]
                base = 1.5 * total_of(squares) + 5.0
                m = m_ref[z, rows, :]
                for p in range(params):
                    near = sides(e[p], old_strip[p, rows, :], z)
                    near = near + (old[p, z, r - 1 : r + 7, :] + old[p, z, r + 1 : r + 9, :])
                    near = near + (old[p, below, rows, :] + old[p, above, rows, :])
                    rate = e[p] * (base - 0.5 * squares[p]) - near
                    rate_ref[t, p, z, rows, :] = rate
                    new = e[p] - m * rate
                    if last:
                        final_ref[p, z] = new
                    else:
                        e_ref[t + 1, p, z, rows, :] = new
                        note_ends(e[p], p, r, z)
            return carry

        lax.fori_loop(0, layers, layer, 0)
        if last:
            return
        for r in windows:
            rows = slice(r, r + 8)
            e = [old_strip[p, rows, :] for p in range(params)]
            squares = [x * x for x in e]
            base = 1.5 * total_of(squares) + 5.0
            m = ms_ref[rows, :]
            for p in range(params):
                near = strip_sides(e[p], inject_ref[p, rows, :], outer_ref[p, rows, :] if t == 0 else None)
                near = near + (old_strip[p, r - 1 : r + 7, :] + old_strip[p, r + 1 : r + 9, :])
                rate = e[p] * (base - 0.5 * squares[p]) - near
                se_ref[t + 1, p, rows, :] = e[p] - m * rate

    inject_ref[...] = jnp.zeros_like(inject_ref)
    forward(0, (3, 11, 13), False)
    forward(1, (4, 12), False)
    forward(2, (4, 12), False)
    forward(3, (8,), True)

    def weigh(z, carry):
        for r in (4, 12):
            rows = slice(r, r + 8)
            m = m_ref[z, rows, :]
            for p in range(params):
                u_ref[0, p, z, rows, :] = m * lam_ref[p, z, rows, :]
            cell_ref[z, rows, :] = jnp.zeros(tile, jnp.float32)
        return carry

    lax.fori_loop(0, layers, weigh, 0)
    for r in (4, 12):
        rows = slice(r, r + 8)
        for p in range(params):
            su_ref[0, p, rows, :] = ms_ref[rows, :] * slam_ref[p, rows, :]

    def backward(t, slot, windows, last):
        old, old_strip = u_ref.at[slot], su_ref.at[slot]

        def layer(z, carry):
            below, above = jnp.maximum(z - 1, 0), jnp.minimum(z + 1, layers - 1)
            for r in windows:
                rows = slice(r, r + 8)
                e = [e_ref[t, p, z, rows, :] for p in range(params)]
                u = [old[p, z, rows, :] for p in range(params)]
                lam = [lam_ref[p, z, rows, :] for p in range(params)]
                squares = [x * x for x in e]
                base = 1.5 * total_of(squares) + 5.0
                inner = 3.0 * total_of([x * y for x, y in zip(e, u)])
                m = m_ref[z, rows, :]
                worked = total_of([lam[p] * rate_ref[t, p, z, rows, :] for p in range(params)])
                cell_ref[z, rows, :] = cell_ref[z, rows, :] + worked
                for p in range(params):
                    near = sides(u[p], old_strip[p, rows, :], z)
                    near = near + (old[p, z, r - 1 : r + 7, :] + old[p, z, r + 1 : r + 9, :])
                    near = near + (old[p, below, rows, :] + old[p, above, rows, :])
                    change = u[p] * (base - 1.5 * squares[p]) + e[p] * inner - near
                    new = lam[p] - change
                    if last:
                        adjoint_ref[p, z] = new
                    else:
                        lam_ref[p, z, rows, :] = new
                        u_ref[1 - slot, p, z, rows, :] = m * new
                        note_ends(u[p], p, r, z)
            return carry

        lax.fori_loop(0, layers, layer, 0)
        if last:
            return
        for r in windows:
            rows = slice(r, r + 8)
            e = [se_ref[t, p, rows, :] for p in range(params)]
            u = [old_strip[p, rows, :] for p in range(params)]
            squares = [x * x for x in e]
            base = 1.5 * total_of(squares) + 5.0
            inner = 3.0 * total_of([x * y for x, y in zip(e, u)])
            m = ms_ref[rows, :]
            for p in range(params):
                near = strip_sides(u[p], inject_ref[p, rows, :])
                near = near + (old_strip[p, r - 1 : r + 7, :] + old_strip[p, r + 1 : r + 9, :])
                change = u[p] * (base - 1.5 * squares[p]) + e[p] * inner - near
                new = slam_ref[p, rows, :] - change
                slam_ref[p, rows, :] = new
                su_ref[1 - slot, p, rows, :] = m * new

    backward(3, 0, (4, 12), False)
    backward(2, 1, (4, 12), False)
    backward(1, 0, (4, 12), False)
    backward(0, 1, (8,), True)

    grains = [map_ref[z] for z in range(layers)]
    cells = [cell_ref[z, 8:16, :] for z in range(layers)]

    def bin_one(g, carry):
        total = total_of([
            a + b for a, b in (
                (jnp.where(grains[z] == g, cells[z], 0.0), jnp.where(grains[z + 1] == g, cells[z + 1], 0.0))
                for z in range(0, layers, 2)
            )
        ][:4]) + total_of([
            a + b for a, b in (
                (jnp.where(grains[z] == g, cells[z], 0.0), jnp.where(grains[z + 1] == g, cells[z + 1], 0.0))
                for z in range(8, layers, 2)
            )
        ])
        binned_ref[pl.ds(g, 1), :] = jnp.sum(total, axis=0, keepdims=True)
        return carry

    lax.fori_loop(0, binned_ref.shape[0], bin_one, 0, unroll=4)
    ones = jnp.full((8, 128), -TIME_STEP, jnp.float32)
    sums = lax.dot_general(
        ones, binned_ref[...], (((1,), (1,)), ((), ())),
        precision=lax.Precision.HIGHEST, preferred_element_type=jnp.float32,
    )
    sums_ref[...] = sums[0:1, :]


def pick_owned(counts, owned, slots_ref, sums_ref, out_ref, slot_rows, value_rows, total_ref):
    wide_count, narrow_count = counts
    count = wide_count * narrow_count
    wide, narrow = lax.axis_index("wide"), lax.axis_index("narrow")
    base = (wide * narrow_count + narrow) * owned
    listed = sums_ref.shape[1]
    tile = (8, 128)
    for k in range(count):
        n = lax.rem(narrow + narrow_count - k // wide_count, narrow_count)
        w = lax.rem(wide + wide_count - k % wide_count, wide_count)
        slot = slots_ref[pl.ds(w * narrow_count + n, 1), :] - base
        slot_rows[k] = jnp.broadcast_to(slot, tile)
        value = jnp.concatenate([sums_ref[k : k + 1, :], jnp.zeros((1, 128 - listed), jnp.float32)], axis=1)
        value_rows[k] = jnp.broadcast_to(value, tile)
    sub = lax.broadcasted_iota(jnp.int32, tile, 0)
    blocks = total_ref.shape[0] // 8
    step = 16
    for first in range(0, blocks, step):
        some = range(first, min(first + step, blocks))

        def body(k, acc, some=some):
            slot, value = slot_rows[k], value_rows[k]
            shifted = slot - sub
            return tuple(a + jnp.where(shifted == 8 * j, value, 0.0) for a, j in zip(acc, some))

        acc = lax.fori_loop(0, count, body, tuple(jnp.zeros(tile, jnp.float32) for _ in some), unroll=4)
        for a, j in zip(acc, some):
            total_ref[8 * j : 8 * j + 8, :] = a
    whole = lax.dot_general(
        jnp.ones(tile, jnp.float32), total_ref[...], (((1,), (1,)), ((), ())),
        precision=lax.Precision.HIGHEST, preferred_element_type=jnp.float32,
    )
    out_ref[...] = whole[0:1, 0:owned]


def f32(*shape):
    return jax.ShapeDtypeStruct(shape, jnp.float32)


def kernel(body, out_shape, scratch=(), name=None):
    return pl.pallas_call(
        body, out_shape=out_shape, scratch_shapes=list(scratch), name=name,
        compiler_params=pltpu.CompilerParams(vmem_limit_bytes=VMEM_LIMIT),
    )


def shifted(value, axis, count, by):
    return lax.ppermute(value, axis, [(i, (i + by) % count) for i in range(count)])


def gathered(value, counts):
    wide_count, narrow_count = counts
    parts = [value] + [shifted(value, "wide", wide_count, d) for d in range(1, wide_count)]
    column = jnp.concatenate(parts, axis=0)
    parts = [column] + [shifted(column, "narrow", narrow_count, d) for d in range(1, narrow_count)]
    return jnp.concatenate(parts, axis=0)


def diagonal(value, counts, by_wide, by_narrow):
    wide_count, narrow_count = counts
    pairs = [
        (w * narrow_count + n, (w + by_wide) % wide_count * narrow_count + (n + by_narrow) % narrow_count)
        for w in range(wide_count) for n in range(narrow_count)
    ]
    return lax.ppermute(value, ("wide", "narrow"), pairs)


def per_device(counts, order_init, cotangent, grain_map, brick_grains, grain_slot, mobility):
    wide_count, narrow_count = counts
    params, layers = order_init.shape[:2]
    assert order_init.shape[2:] == (8, 128) and layers * COLS < 128
    owned = mobility.shape[0]
    listed = brick_grains.shape[1]
    bricks = brick_grains.shape[0]

    edge_rows = (params + 1) * layers * EDGE
    down, up = kernel(pack_rows, (f32(edge_rows, 128), f32(edge_rows, 128)), name="pack_rows")(order_init, grain_map)
    above = shifted(down, "wide", wide_count, 1)
    below = shifted(up, "wide", wide_count, -1)

    padded = -owned % 128
    own = jnp.pad(mobility, (0, padded)).reshape(-1, 128)
    every = gathered(own, counts)

    cot_rows = params * layers * ADJ_EDGE
    strip_rows = (2 * params + 1) * 8
    corner_rows = params * CORNER[0] + params * CORNER[1] + CORNER[2]
    corner_rows += -corner_rows % 8
    packed = kernel(
        pack_strips,
        (f32(cot_rows, 128),) * 2 + (f32(strip_rows, 128),) * 2 + (f32(corner_rows, 128),) * 4,
        name="pack_strips",
    )(order_init, cotangent, grain_map)
    cot_down, cot_up, to_right, to_left, right_down, left_down, right_up, left_up = packed
    from_left = shifted(to_right, "narrow", narrow_count, 1)
    from_right = shifted(to_left, "narrow", narrow_count, -1)
    left_above = diagonal(right_down, counts, 1, 1)
    right_above = diagonal(left_down, counts, 1, -1)
    left_below = diagonal(right_up, counts, -1, 1)
    right_below = diagonal(left_up, counts, -1, -1)
    cot_above = shifted(cot_down, "wide", wide_count, 1)
    cot_below = shifted(cot_up, "wide", wide_count, -1)

    slots = kernel(
        find_slots, jax.ShapeDtypeStruct((bricks, 128), jnp.int32), name="find_slots"
    )(brick_grains, grain_slot.reshape(-1, 128))

    vmem = lambda *shape: pltpu.VMEM(shape, jnp.float32)
    block = (params, layers, ROWS, 128)
    strip = (params, ROWS, 128)
    final, adjoint, sums = kernel(
        functools.partial(evolve, counts, owned),
        (f32(*order_init.shape), f32(*order_init.shape), f32(1, listed)),
        (
            vmem(ITERS, *block), vmem(ITERS, *strip), vmem(ITERS, *block), vmem(*strip), vmem(*strip),
            vmem(*block), vmem(*strip), vmem(2, *block), vmem(2, *strip),
            vmem(layers, ROWS, 128), vmem(ROWS, 128), vmem(layers, ROWS, 128), vmem(ROWS, 128),
            pltpu.VMEM((16, 128), jnp.int32), vmem(16, 128), vmem(layers, ROWS, 128), vmem(listed, 128),
        ),
        name="evolve",
    )(
        order_init, cotangent, grain_map, above, below, cot_above, cot_below,
        from_left, from_right, left_above, right_above, left_below, right_below,
        slots, every,
    )

    every_sum = gathered(sums, counts)
    count = wide_count * narrow_count
    grads = kernel(
        functools.partial(pick_owned, counts, owned),
        f32(1, owned),
        (pltpu.VMEM((count, 8, 128), jnp.int32), vmem(count, 8, 128), vmem(owned + -owned % 8, 128)),
        name="pick_owned",
    )(slots, every_sum)
    return final, adjoint, grads.reshape(owned)


def solution(mesh):
    counts = (mesh.shape["wide"], mesh.shape["narrow"])
    field = P("groups", None, "wide", "narrow")
    spread = P(("groups", "wide", "narrow"))
    return jax.shard_map(
        functools.partial(per_device, counts),
        mesh=mesh,
        in_specs=(field, field, P("groups", "wide", "narrow"), P("groups", None), P("groups"), spread),
        out_specs=(field, field, spread),
        check_vma=False,
    )
```

time: 287 us -> 95.2 us (0.33)
  blocking collectives: 122 us -> 0 us
  local copies, waits for them, and re-layouts: 73.3 us -> 2.59 us
  Pallas kernels: 0 us -> 39.8 us
  other arithmetic: 36.6 us -> 0.02 us
  waiting for transfers between devices: 26 us -> 33.7 us
  starting transfers between devices: 24.8 us -> 18.2 us
    unnamed x2 -> x0, blocking collectives: 122 us -> none
    pallas_call x0 -> x5, Pallas kernels: none -> 39.8 us  [the longest x1 36.9 us: per_device(): kernel(functools.partial(evolve, counts, owned), (f32(*order_init.shape),...]
    unnamed x53 -> x14, local copies, waits for them, and re-layouts: 23 us -> 1.82 us
    sub x10 -> x0, other arithmetic: 19.2 us -> none  [the longest x4 10.4 us: reaction(): total - squares]
    eq x24 -> x0, local copies, waits for them, and re-layouts: 16.6 us -> none  [the longest x12 8.32 us: collect_one_layer(): layer[None] == labels[:, None, None]]
    ppermute x18 -> x0, local copies, waits for them, and re-layouts: 14.4 us -> none  [the longest x9 7.59 us: extended(): before = lax.ppermute(last, axis, up)]
    slice x32 -> x0, local copies, waits for them, and re-layouts: 13.2 us -> none  [the longest x8 4.62 us: laplace_padded(): below = jnp.concatenate([core[:, :1], core[:, :-1]], axis=1)]
    reduce_sum x28 -> x0, other arithmetic: 11.7 us -> none  [the longest x12 6.69 us: collect_one_layer(): jnp.sum(jnp.where(layer[None] == labels[:, None, None], values[None], 0.0...]
  transfers between devices with their start and end apart: 32 -> 22, of which waited for: 21 -> 12; matrix products, arithmetic and copies ran while one was open for 18% -> 0% of each run, Pallas kernels for 0% -> 2%
where the time goes in v1:
time: 95.2 us; the launch traced here: 94.9 us
  Pallas kernels  39.8 us (42%)
  waiting for transfers between devices  33.7 us (35%)
  starting transfers between devices  18.2 us (19%)
  local copies, waits for them, and re-layouts  2.59 us (3%)
    pallas_call x1, Pallas kernels, per_device(): kernel(functools.partial(evolve, counts, owned), (f32(*order_init.shape),...  36.9 us
    ppermute x18, waiting for transfers between devices, shifted(): lax.ppermute(value, axis, [(i, (i + by) % count) for i in range(count)])  26.8 us
    ppermute x18, starting transfers between devices, shifted(): lax.ppermute(value, axis, [(i, (i + by) % count) for i in range(count)])  13.8 us
    ppermute x4, waiting for transfers between devices, diagonal(): return lax.ppermute(value, ('wide', 'narrow'), pairs)  6.81 us
    ppermute x4, starting transfers between devices, diagonal(): return lax.ppermute(value, ('wide', 'narrow'), pairs)  4.33 us
  transfers between devices with their start and end apart: 22, of which 12 were waited for; matrix products, arithmetic and copies ran while one was open for 0% of the time, Pallas kernels for 2%

profile of v1, /device:TPU:0, one launch (start us, length us, event | category | flops | bytes accessed | tf_op | source)
XLA Modules:
  0.0 94.9 jit_solution(14778067631097894413)
XLA Ops:
  0.6 0.7 pad_bitcast_fusion
  1.3 2.4 %collective-permute-start.12 = (f32[4,128]{1,0:T(4,128)S(1)}, f32[4,128]{1,0:T(4,128)S(1)}, u32[]{:S(2)}, u32[]{:S(2)}) collective-permute-start(f32[4,128]{1,0:T(4,128)S(1)} %pad_bitcast_fusion), channel_id=1, source_target_pairs={{0,12},{4,0},{8,4},{12,8},{1,13},{5,1},{9,5},{13,9},{2,14},{6,2},{... | collective-permute-start | bytes 6152 | tf_op jit(solution)/shard_map/ppermute | solution.py:427
  4.5 1.0 %copy-done = f32[8,12,8,128]{3,2,1,0:T(8,128)S(1)} copy-done((f32[8,12,8,128]{3,2,1,0:T(8,128)S(1)}, f32[8,12,8,128]{3,2,1,0:T(8,128)}, u32[]{:S(2)}) %copy-start) | copy-done | bytes 393240
  5.5 0.8 copy-done.3
  6.4 1.4 %collective-permute-start = (f32[648,128]{1,0:T(8,128)S(1)}, f32[648,128]{1,0:T(8,128)S(1)}, u32[]{:S(2)}, u32[]{:S(2)}) collective-permute-start(f32[648,128]{1,0:T(8,128)S(1)} %get-tuple-element.16), channel_id=1, source_target_pairs={{0,4},{4,8},{8,12},{12,0},{1,5},{5,9},{9,13},{13,1},{2,6},{6,10},{... | collective-permute-start | bytes 995336 | tf_op jit(solution)/shard_map/ppermute | solution.py:427
  8.2 3.7 %collective-permute-start.15 = (f32[16,128]{1,0:T(8,128)S(1)}, f32[16,128]{1,0:T(8,128)S(1)}, u32[]{:S(2)}, u32[]{:S(2)}) collective-permute-start(f32[16,128]{1,0:T(8,128)S(1)} %pad_maximum_fusion), channel_id=1, source_target_pairs={{0,3},{1,0},{2,1},{3,2},{4,7},{5,4},{6,5},{7,6},{8,11},{9,8},{10,9... | collective-permute-start | bytes 24584 | tf_op jit(solution)/shard_map/ppermute | solution.py:427
  12.2 4.3 %collective-permute-start.7 = (f32[72,128]{1,0:T(8,128)S(1)}, f32[72,128]{1,0:T(8,128)S(1)}, u32[]{:S(2)}, u32[]{:S(2)}) collective-permute-start(f32[72,128]{1,0:T(8,128)S(1)} %get-tuple-element.23), channel_id=1, source_target_pairs={{0,7},{1,4},{2,5},{3,6},{4,11},{5,8},{6,9},{7,10},{8,15},{9,12},{1... | collective-permute-start | bytes 110600 | tf_op jit(solution)/shard_map/ppermute | solution.py:444
  16.5 4.5 %collective-permute-done.14 = f32[16,128]{1,0:T(8,128)S(1)} collective-permute-done((f32[16,128]{1,0:T(8,128)S(1)}, f32[16,128]{1,0:T(8,128)S(1)}, u32[]{:S(2)}, u32[]{:S(2)}) %collective-permute-start.14) | collective-permute-done | bytes 8224 | tf_op jit(solution)/shard_map/ppermute | solution.py:427
  21.1 5.4 %collective-permute-done.13 = f32[16,128]{1,0:T(8,128)S(1)} collective-permute-done((f32[16,128]{1,0:T(8,128)S(1)}, f32[16,128]{1,0:T(8,128)S(1)}, u32[]{:S(2)}, u32[]{:S(2)}) %collective-permute-start.13) | collective-permute-done | bytes 8224 | tf_op jit(solution)/shard_map/ppermute | solution.py:427
  26.5 1.7 %collective-permute-start.3 = (f32[384,128]{1,0:T(8,128)S(1)}, f32[384,128]{1,0:T(8,128)S(1)}, u32[]{:S(2)}, u32[]{:S(2)}) collective-permute-start(f32[384,128]{1,0:T(8,128)S(1)} %get-tuple-element.19), channel_id=1, source_target_pairs={{0,12},{4,0},{8,4},{12,8},{1,13},{5,1},{9,5},{13,9},{2,14},{6,2},{... | collective-permute-start | bytes 589832 | tf_op jit(solution)/shard_map/ppermute | solution.py:427
  28.3 3.4 %collective-permute-done.8.left_below_ref = f32[72,128]{1,0:T(8,128)S(1)} collective-permute-done((f32[72,128]{1,0:T(8,128)S(1)}, f32[72,128]{1,0:T(8,128)S(1)}, u32[]{:S(2)}, u32[]{:S(2)}) %collective-permute-start.8) | collective-permute-done | bytes 36896 | tf_op jit(solution)/shard_map/ppermute | solution.py:444
  31.7 3.4 %collective-permute-done.9.right_below_ref = f32[72,128]{1,0:T(8,128)S(1)} collective-permute-done((f32[72,128]{1,0:T(8,128)S(1)}, f32[72,128]{1,0:T(8,128)S(1)}, u32[]{:S(2)}, u32[]{:S(2)}) %collective-permute-start.9) | collective-permute-done | bytes 36896 | tf_op jit(solution)/shard_map/ppermute | solution.py:444
  35.1 6.2 %collective-permute-done.4.left_ref = f32[136,128]{1,0:T(8,128)S(1)} collective-permute-done((f32[136,128]{1,0:T(8,128)S(1)}, f32[136,128]{1,0:T(8,128)S(1)}, u32[]{:S(2)}, u32[]{:S(2)}) %collective-permute-start.4) | collective-permute-done | bytes 69664 | tf_op jit(solution)/shard_map/ppermute | solution.py:427
  41.3 1.1 %find_slots.1.slots_ref = s32[16,128]{1,0:T(8,128)S(1)} custom-call(s32[16,64]{1,0:T(8,128)S(1)} %copy-done.6, s32[49,128]{1,0:T(8,128)S(1)} %bitcast.4), custom_call_target="tpu_custom_call" | custom-call | tf_op jit(solution)/shard_map/find_slots/pallas_call | solution.py:483
  42.5 3.1 %collective-permute-done.5.right_ref = f32[136,128]{1,0:T(8,128)S(1)} collective-permute-done((f32[136,128]{1,0:T(8,128)S(1)}, f32[136,128]{1,0:T(8,128)S(1)}, u32[]{:S(2)}, u32[]{:S(2)}) %collective-permute-start.5) | collective-permute-done | bytes 69664 | tf_op jit(solution)/shard_map/ppermute | solution.py:427
  45.6 36.9 %evolve.1 = (f32[8,12,8,128]{3,2,1,0:T(8,128)}, f32[8,12,8,128]{3,2,1,0:T(8,128)}, f32[1,64]{1,0:T(1,128)S(1)}) custom-call(f32[8,12,8,128]{3,2,1,0:T(8,128)S(1)} %copy-done.1, f32[8,12,8,128]{3,2,1,0:T(8,128)S(1)} %copy-done.2, s32[12,8,128]{2,1,0:T(8,128)S(1)} %copy-done.4, f32[648,128]{1,0:T(8,128)S(1)} %collective-permute-done.above_ref, ...), custom_call_target="tpu_custom_call" | custom-call | tf_op jit(solution)/shard_map/evolve/pallas_call | solution.py:490
  82.6 0.6 collective-permute-start.17
  83.9 2.2 %collective-permute-done.17 = f32[1,64]{1,0:T(1,128)S(1)} collective-permute-done((f32[1,64]{1,0:T(1,128)S(1)}, f32[1,64]{1,0:T(1,128)S(1)}, u32[]{:S(2)}, u32[]{:S(2)}) %collective-permute-start.17) | collective-permute-done | bytes 288 | tf_op jit(solution)/shard_map/ppermute | solution.py:427
  86.2 2.0 %collective-permute-start.21 = (f32[4,64]{1,0:T(4,128)S(1)}, f32[4,64]{1,0:T(4,128)S(1)}, u32[]{:S(2)}, u32[]{:S(2)}) collective-permute-start(f32[4,64]{1,0:T(4,128)S(1)} %pad_maximum_fusion.1), channel_id=1, source_target_pairs={{0,3},{1,0},{2,1},{3,2},{4,7},{5,4},{6,5},{7,6},{8,11},{9,8},{10,9... | collective-permute-start | bytes 3080 | tf_op jit(solution)/shard_map/ppermute | solution.py:427
  88.2 0.6 collective-permute-start.19
  88.8 1.0 %collective-permute-done.21 = f32[4,64]{1,0:T(4,128)S(1)} collective-permute-done((f32[4,64]{1,0:T(4,128)S(1)}, f32[4,64]{1,0:T(4,128)S(1)}, u32[]{:S(2)}, u32[]{:S(2)}) %collective-permute-start.21) | collective-permute-done | bytes 1056 | tf_op jit(solution)/shard_map/ppermute | solution.py:427
  89.8 2.8 %collective-permute-done.20 = f32[4,64]{1,0:T(4,128)S(1)} collective-permute-done((f32[4,64]{1,0:T(4,128)S(1)}, f32[4,64]{1,0:T(4,128)S(1)}, u32[]{:S(2)}, u32[]{:S(2)}) %collective-permute-start.20) | collective-permute-done | bytes 1056 | tf_op jit(solution)/shard_map/ppermute | solution.py:427
  92.6 0.9 collective-permute-done.19
  93.6 1.4 %pick_owned.1 = f32[1,392]{1,0:T(1,128)} custom-call(s32[16,128]{1,0:T(8,128)S(1)} %find_slots.1.slots_ref, f32[16,64]{1,0:T(8,128)S(1)} %concatenate.17.sums_ref), custom_call_target="tpu_custom_call" | custom-call | tf_op jit(solution)/shard_map/pick_owned/pallas_call | solution.py:508
  (44 shorter events, 2.5 us)
Async XLA Ops:
  1.3 6.8 %collective-permute-start.12 = (f32[4,128]{1,0:T(4,128)S(1)}, f32[4,128]{1,0:T(4,128)S(1)}, u32[]{:S(2)}, u32[]{:S(2)}) collective-permute-start(f32[4,128]{1,0:T(4,128)S(1)} %pad_bitcast_fusion), channel_id=1, source_target_pairs={{0,12},{4,0},{8,4},{12,8},{1,13},{5,1},{9,5},{13,9},{2,14},{6,2},{... | collective-permute-start | bytes 6152 | tf_op jit(solution)/shard_map/ppermute | solution.py:427
  3.7 4.5 %collective-permute-start.11 = (f32[4,128]{1,0:T(4,128)S(1)}, f32[4,128]{1,0:T(4,128)S(1)}, u32[]{:S(2)}, u32[]{:S(2)}) collective-permute-start(f32[4,128]{1,0:T(4,128)S(1)} %pad_bitcast_fusion), channel_id=1, source_target_pairs={{0,8},{4,12},{8,0},{12,4},{1,9},{5,13},{9,1},{13,5},{2,10},{6,14},... | collective-permute-start | bytes 6152 | tf_op jit(solution)/shard_map/ppermute | solution.py:427
  4.3 3.9 %collective-permute-start.10 = (f32[4,128]{1,0:T(4,128)S(1)}, f32[4,128]{1,0:T(4,128)S(1)}, u32[]{:S(2)}, u32[]{:S(2)}) collective-permute-start(f32[4,128]{1,0:T(4,128)S(1)} %pad_bitcast_fusion), channel_id=1, source_target_pairs={{0,4},{4,8},{8,12},{12,0},{1,5},{5,9},{9,13},{13,1},{2,6},{6,10},{... | collective-permute-start | bytes 6152 | tf_op jit(solution)/shard_map/ppermute | solution.py:427
  6.4 39.3 %collective-permute-start = (f32[648,128]{1,0:T(8,128)S(1)}, f32[648,128]{1,0:T(8,128)S(1)}, u32[]{:S(2)}, u32[]{:S(2)}) collective-permute-start(f32[648,128]{1,0:T(8,128)S(1)} %get-tuple-element.16), channel_id=1, source_target_pairs={{0,4},{4,8},{8,12},{12,0},{1,5},{5,9},{9,13},{13,1},{2,6},{6,10},{... | collective-permute-start | bytes 995336 | tf_op jit(solution)/shard_map/ppermute | solution.py:427
  7.8 37.9 %collective-permute-start.1 = (f32[648,128]{1,0:T(8,128)S(1)}, f32[648,128]{1,0:T(8,128)S(1)}, u32[]{:S(2)}, u32[]{:S(2)}) collective-permute-start(f32[648,128]{1,0:T(8,128)S(1)} %get-tuple-element.17), channel_id=1, source_target_pairs={{0,12},{4,0},{8,4},{12,8},{1,13},{5,1},{9,5},{13,9},{2,14},{6,2},{... | collective-permute-start | bytes 995336 | tf_op jit(solution)/shard_map/ppermute | solution.py:427
  8.2 37.4 %copy-start.1 = (f32[8,12,8,128]{3,2,1,0:T(8,128)S(1)}, f32[8,12,8,128]{3,2,1,0:T(8,128)}, u32[]{:S(2)}) copy-start(f32[8,12,8,128]{3,2,1,0:T(8,128)} %order_ref.5) | copy-start | bytes 1179652
  8.2 8.3 %collective-permute-start.15 = (f32[16,128]{1,0:T(8,128)S(1)}, f32[16,128]{1,0:T(8,128)S(1)}, u32[]{:S(2)}, u32[]{:S(2)}) collective-permute-start(f32[16,128]{1,0:T(8,128)S(1)} %pad_maximum_fusion), channel_id=1, source_target_pairs={{0,3},{1,0},{2,1},{3,2},{4,7},{5,4},{6,5},{7,6},{8,11},{9,8},{10,9... | collective-permute-start | bytes 24584 | tf_op jit(solution)/shard_map/ppermute | solution.py:427
  11.9 29.4 %copy-start.5 = (s32[6272]{0:T(1024)S(1)}, s32[6272]{0:T(1024)}, u32[]{:S(2)}) copy-start(s32[6272]{0:T(1024)} %param.10) | copy-start | bytes 75268
  12.2 14.3 %collective-permute-start.6 = (f32[72,128]{1,0:T(8,128)S(1)}, f32[72,128]{1,0:T(8,128)S(1)}, u32[]{:S(2)}, u32[]{:S(2)}) collective-permute-start(f32[72,128]{1,0:T(8,128)S(1)} %get-tuple-element.22), channel_id=1, source_target_pairs={{0,5},{1,6},{2,7},{3,4},{4,9},{5,10},{6,11},{7,8},{8,13},{9,14},{1... | collective-permute-start | bytes 110600 | tf_op jit(solution)/shard_map/ppermute | solution.py:444
  12.2 14.3 %collective-permute-start.7 = (f32[72,128]{1,0:T(8,128)S(1)}, f32[72,128]{1,0:T(8,128)S(1)}, u32[]{:S(2)}, u32[]{:S(2)}) collective-permute-start(f32[72,128]{1,0:T(8,128)S(1)} %get-tuple-element.23), channel_id=1, source_target_pairs={{0,7},{1,4},{2,5},{3,6},{4,11},{5,8},{6,9},{7,10},{8,15},{9,12},{1... | collective-permute-start | bytes 110600 | tf_op jit(solution)/shard_map/ppermute | solution.py:444
  16.5 4.6 %collective-permute-start.14 = (f32[16,128]{1,0:T(8,128)S(1)}, f32[16,128]{1,0:T(8,128)S(1)}, u32[]{:S(2)}, u32[]{:S(2)}) collective-permute-start(f32[16,128]{1,0:T(8,128)S(1)} %pad_maximum_fusion), channel_id=1, source_target_pairs={{0,2},{1,3},{2,0},{3,1},{4,6},{5,7},{6,4},{7,5},{8,10},{9,11},{10,... | collective-permute-start | bytes 24584 | tf_op jit(solution)/shard_map/ppermute | solution.py:427
  21.1 5.4 %collective-permute-start.13 = (f32[16,128]{1,0:T(8,128)S(1)}, f32[16,128]{1,0:T(8,128)S(1)}, u32[]{:S(2)}, u32[]{:S(2)}) collective-permute-start(f32[16,128]{1,0:T(8,128)S(1)} %pad_maximum_fusion), channel_id=1, source_target_pairs={{0,1},{1,2},{2,3},{3,0},{4,5},{5,6},{6,7},{7,4},{8,9},{9,10},{10,1... | collective-permute-start | bytes 24584 | tf_op jit(solution)/shard_map/ppermute | solution.py:427
  26.5 5.2 %collective-permute-start.8 = (f32[72,128]{1,0:T(8,128)S(1)}, f32[72,128]{1,0:T(8,128)S(1)}, u32[]{:S(2)}, u32[]{:S(2)}) collective-permute-start(f32[72,128]{1,0:T(8,128)S(1)} %get-tuple-element.24), channel_id=1, source_target_pairs={{0,13},{1,14},{2,15},{3,12},{4,1},{5,2},{6,3},{7,0},{8,5},{9,6},{1... | collective-permute-start | bytes 110600 | tf_op jit(solution)/shard_map/ppermute | solution.py:444
  26.5 19.1 %collective-permute-start.2 = (f32[384,128]{1,0:T(8,128)S(1)}, f32[384,128]{1,0:T(8,128)S(1)}, u32[]{:S(2)}, u32[]{:S(2)}) collective-permute-start(f32[384,128]{1,0:T(8,128)S(1)} %get-tuple-element.18), channel_id=1, source_target_pairs={{0,4},{4,8},{8,12},{12,0},{1,5},{5,9},{9,13},{13,1},{2,6},{6,10},{... | collective-permute-start | bytes 589832 | tf_op jit(solution)/shard_map/ppermute | solution.py:427
  26.5 19.1 %collective-permute-start.3 = (f32[384,128]{1,0:T(8,128)S(1)}, f32[384,128]{1,0:T(8,128)S(1)}, u32[]{:S(2)}, u32[]{:S(2)}) collective-permute-start(f32[384,128]{1,0:T(8,128)S(1)} %get-tuple-element.19), channel_id=1, source_target_pairs={{0,12},{4,0},{8,4},{12,8},{1,13},{5,1},{9,5},{13,9},{2,14},{6,2},{... | collective-permute-start | bytes 589832 | tf_op jit(solution)/shard_map/ppermute | solution.py:427
  31.7 3.4 %collective-permute-start.9 = (f32[72,128]{1,0:T(8,128)S(1)}, f32[72,128]{1,0:T(8,128)S(1)}, u32[]{:S(2)}, u32[]{:S(2)}) collective-permute-start(f32[72,128]{1,0:T(8,128)S(1)} %get-tuple-element.25), channel_id=1, source_target_pairs={{0,15},{1,12},{2,13},{3,14},{4,3},{5,0},{6,1},{7,2},{8,7},{9,4},{1... | collective-permute-start | bytes 110600 | tf_op jit(solution)/shard_map/ppermute | solution.py:444
  35.1 6.2 %collective-permute-start.4 = (f32[136,128]{1,0:T(8,128)S(1)}, f32[136,128]{1,0:T(8,128)S(1)}, u32[]{:S(2)}, u32[]{:S(2)}) collective-permute-start(f32[136,128]{1,0:T(8,128)S(1)} %get-tuple-element.20), channel_id=1, source_target_pairs={{0,1},{1,2},{2,3},{3,0},{4,5},{5,6},{6,7},{7,4},{8,9},{9,10},{10,1... | collective-permute-start | bytes 208904 | tf_op jit(solution)/shard_map/ppermute | solution.py:427
  41.3 4.3 %collective-permute-start.5 = (f32[136,128]{1,0:T(8,128)S(1)}, f32[136,128]{1,0:T(8,128)S(1)}, u32[]{:S(2)}, u32[]{:S(2)}) collective-permute-start(f32[136,128]{1,0:T(8,128)S(1)} %get-tuple-element.21), channel_id=1, source_target_pairs={{0,3},{1,0},{2,1},{3,2},{4,7},{5,4},{6,5},{7,6},{8,11},{9,8},{10,9... | collective-permute-start | bytes 208904 | tf_op jit(solution)/shard_map/ppermute | solution.py:427
  82.6 1.3 %collective-permute-start.18 = (f32[1,64]{1,0:T(1,128)S(1)}, f32[1,64]{1,0:T(1,128)S(1)}, u32[]{:S(2)}, u32[]{:S(2)}) collective-permute-start(f32[1,64]{1,0:T(1,128)S(1)} %get-tuple-element.28), channel_id=1, source_target_pairs={{0,12},{4,0},{8,4},{12,8},{1,13},{5,1},{9,5},{13,9},{2,14},{6,2},{... | collective-permute-start | bytes 776 | tf_op jit(solution)/shard_map/ppermute | solution.py:427
  82.6 3.5 %collective-permute-start.17 = (f32[1,64]{1,0:T(1,128)S(1)}, f32[1,64]{1,0:T(1,128)S(1)}, u32[]{:S(2)}, u32[]{:S(2)}) collective-permute-start(f32[1,64]{1,0:T(1,128)S(1)} %get-tuple-element.28), channel_id=1, source_target_pairs={{0,8},{4,12},{8,0},{12,4},{1,9},{5,13},{9,1},{13,5},{2,10},{6,14},... | collective-permute-start | bytes 776 | tf_op jit(solution)/shard_map/ppermute | solution.py:427
  83.2 3.0 %collective-permute-start.16 = (f32[1,64]{1,0:T(1,128)S(1)}, f32[1,64]{1,0:T(1,128)S(1)}, u32[]{:S(2)}, u32[]{:S(2)}) collective-permute-start(f32[1,64]{1,0:T(1,128)S(1)} %get-tuple-element.28), channel_id=1, source_target_pairs={{0,4},{4,8},{8,12},{12,0},{1,5},{5,9},{9,13},{13,1},{2,6},{6,10},{... | collective-permute-start | bytes 776 | tf_op jit(solution)/shard_map/ppermute | solution.py:427
  86.2 3.6 %collective-permute-start.21 = (f32[4,64]{1,0:T(4,128)S(1)}, f32[4,64]{1,0:T(4,128)S(1)}, u32[]{:S(2)}, u32[]{:S(2)}) collective-permute-start(f32[4,64]{1,0:T(4,128)S(1)} %pad_maximum_fusion.1), channel_id=1, source_target_pairs={{0,3},{1,0},{2,1},{3,2},{4,7},{5,4},{6,5},{7,6},{8,11},{9,8},{10,9... | collective-permute-start | bytes 3080 | tf_op jit(solution)/shard_map/ppermute | solution.py:427
  88.2 4.5 %collective-permute-start.20 = (f32[4,64]{1,0:T(4,128)S(1)}, f32[4,64]{1,0:T(4,128)S(1)}, u32[]{:S(2)}, u32[]{:S(2)}) collective-permute-start(f32[4,64]{1,0:T(4,128)S(1)} %pad_maximum_fusion.1), channel_id=1, source_target_pairs={{0,2},{1,3},{2,0},{3,1},{4,6},{5,7},{6,4},{7,5},{8,10},{9,11},{10,... | collective-permute-start | bytes 3080 | tf_op jit(solution)/shard_map/ppermute | solution.py:427
  88.2 5.4 %collective-permute-start.19 = (f32[4,64]{1,0:T(4,128)S(1)}, f32[4,64]{1,0:T(4,128)S(1)}, u32[]{:S(2)}, u32[]{:S(2)}) collective-permute-start(f32[4,64]{1,0:T(4,128)S(1)} %pad_maximum_fusion.1), channel_id=1, source_target_pairs={{0,1},{1,2},{2,3},{3,0},{4,5},{5,6},{6,7},{7,4},{8,9},{9,10},{10,1... | collective-permute-start | bytes 3080 | tf_op jit(solution)/shard_map/ppermute | solution.py:427
  (5 other events, 40.8 us)

commit v2 on v1

v2 whole, which is shorter than its diff:
```python
import functools

import jax
import jax.numpy as jnp
from jax import lax
from jax.experimental import pallas as pl
from jax.experimental.pallas import tpu as pltpu
from jax.sharding import PartitionSpec as P

ITERS = 4
TIME_STEP = 0.05

EDGE = 6
ADJ_EDGE = 4
ROWS = 24
COLS = 10
LEAD = 8
CORNER = (5, 3, 4)

VMEM_LIMIT = 50 * 1024 * 1024


def lanes(shape):
    return lax.broadcasted_iota(jnp.int32, shape, len(shape) - 1)


def roll(value, shift):
    return pltpu.roll(value, shift, 1)


def pack_rows(order_ref, map_ref, down_ref, up_ref):
    params, layers = order_ref.shape[:2]
    for p in range(params):
        for z in range(layers):
            k = LEAD + (p * layers + z) * EDGE
            down_ref[k : k + EDGE, :] = order_ref[p, z, 8 - EDGE : 8, :]
            up_ref[k : k + EDGE, :] = order_ref[p, z, 0:EDGE, :]
    for ref in (down_ref, up_ref):
        ref[0:LEAD, :] = jnp.zeros((LEAD, 128), jnp.float32)
        ref[ref.shape[0] - LEAD :, :] = jnp.zeros((LEAD, 128), jnp.float32)
    for z in range(layers):
        k = LEAD + (params * layers + z) * EDGE
        cells = map_ref[z].astype(jnp.float32)
        down_ref[k : k + EDGE, :] = cells[8 - EDGE : 8]
        up_ref[k : k + EDGE, :] = cells[0:EDGE]


def pack_strips(order_ref, cot_ref, map_ref, after_ref, right_ref, left_ref):
    params, layers = order_ref.shape[:2]
    lane = lanes((8, 128))
    to_right = []
    to_left = []
    for z in range(layers):
        first = 10 * z - 1
        inside = (lane >= first) & (lane < first + 6)
        if z == 0:
            inside = inside | (lane == 127)
        to_right.append(inside)
        to_left.append((lane >= 10 * z + 5) & (lane < 10 * z + 11))

    def strip_of(read):
        right = jnp.zeros((8, 128), jnp.float32)
        left = jnp.zeros((8, 128), jnp.float32)
        for z in range(layers):
            moved = roll(read(z), 10 * z + 5)
            right = jnp.where(to_right[z], moved, right)
            left = jnp.where(to_left[z], moved, left)
        return right, left

    for field in range(2 * params + 1):
        if field < params:
            read = lambda z, p=field: order_ref[p, z]
        elif field < 2 * params:
            read = lambda z, p=field - params: cot_ref[p, z]
        else:
            read = lambda z: map_ref[z].astype(jnp.float32)
        right, left = strip_of(read)
        right_ref[8 * field : 8 * field + 8, :] = right
        left_ref[8 * field : 8 * field + 8, :] = left


def corner_rows(params):
    return -(-(params * (CORNER[0] + CORNER[1]) + CORNER[2]) // 8) * 8


def pack_corners(cot_ref, left_ref, right_ref, down_ref, up_ref):
    params, layers = cot_ref.shape[:2]
    at = 0
    for field in range(2 * params + 1):
        n = CORNER[0 if field < params else 1 if field < 2 * params else 2]
        rows = slice(8 * field, 8 * field + 8)
        both = jnp.where(lanes((8, 128)) % COLS < 5, left_ref[rows, :], right_ref[rows, :])
        down_ref[at : at + n, :] = both[8 - n : 8]
        up_ref[at : at + n, :] = both[0:n]
        at += n
    for ref in (down_ref, up_ref):
        ref[at:, :] = jnp.zeros((ref.shape[0] - at, 128), jnp.float32)
    at = corner_rows(params) + LEAD
    for p in range(params):
        for z in range(layers):
            k = at + (p * layers + z) * ADJ_EDGE
            down_ref[k : k + ADJ_EDGE, :] = cot_ref[p, z, 8 - ADJ_EDGE : 8, :]
            up_ref[k : k + ADJ_EDGE, :] = cot_ref[p, z, 0:ADJ_EDGE, :]


def find_slots(bricks_ref, slot_ref, out_ref):
    count, listed = bricks_ref.shape
    rows = slot_ref.shape[0]
    pad = jnp.zeros((8, 128 - listed), jnp.int32)
    for k in range(0, count, 8):
        grain = jnp.concatenate([bricks_ref[k : k + 8, :], pad], axis=1)
        row, col = grain >> 7, grain & 127

        def body(r, found, row=row, col=col):
            table = jnp.broadcast_to(slot_ref[pl.ds(r, 1), :], (8, 128))
            taken = jnp.take_along_axis(table, col, axis=1, mode="promise_in_bounds")
            return jnp.where(row == r, taken, found)

        found = lax.fori_loop(0, rows, body, jnp.zeros((8, 128), jnp.int32), unroll=7)
        out_ref[k : k + 8, :] = jnp.where(lanes((8, 128)) < listed, found, -1)


def find_mobility(counts, owned, slots_ref, mob_ref, table_ref, near_ref):
    wide_count, narrow_count = counts
    tile = (8, 128)
    wide, narrow = lax.axis_index("wide"), lax.axis_index("narrow")
    for i in range(3):
        for j in range(3):
            w = lax.rem(wide + i - 1 + wide_count, wide_count)
            n = lax.rem(narrow + j - 1 + narrow_count, narrow_count)
            near_ref[3 * i + j : 3 * i + j + 1, :] = slots_ref[pl.ds(w * narrow_count + n, 1), :]
    near_ref[9:16, :] = jnp.zeros((7, 128), jnp.int32)
    per_owner = mob_ref.shape[0] // (wide_count * narrow_count)
    slot = [jnp.maximum(near_ref[k : k + 8, :], 0) for k in (0, 8)]
    owner = [jnp.floor((x.astype(jnp.float32) + 0.5) * (1.0 / owned)).astype(jnp.int32) for x in slot]
    inner = [x - y * owned for x, y in zip(slot, owner)]
    row = [y * per_owner + (x >> 7) for x, y in zip(inner, owner)]
    place = [x & 127 for x in inner]

    def body(r, found):
        values = jnp.broadcast_to(mob_ref[pl.ds(r, 1), :], tile)
        return tuple(
            jnp.where(row[k] == r, jnp.take_along_axis(values, place[k], axis=1, mode="promise_in_bounds"), found[k])
            for k in range(2)
        )

    zero = jnp.zeros(tile, jnp.float32)
    found = lax.fori_loop(0, mob_ref.shape[0], body, (zero, zero), unroll=16)
    for k in range(2):
        table_ref[8 * k : 8 * k + 8, :] = TIME_STEP * found[k]


def evolve(
    order_ref, cot_ref, map_ref, above_ref, below_ref, far_above_ref, far_below_ref,
    left_ref, right_ref, table_ref,
    final_ref, adjoint_ref, sums_ref,
    e_ref, se_ref, rate_ref, inject_ref, outer_ref, lam_ref, slam_ref, u_ref, su_ref,
    m_ref, ms_ref, g_ref, gs_ref, cell_ref, binned_ref,
):
    params, layers = order_ref.shape[:2]
    tile = (8, 128)
    lane = lanes(tile)
    col = lane % COLS

    def place_map(z, carry):
        k = LEAD + (params * layers + z) * EDGE
        g_ref[z, 0:8, :] = above_ref[pl.ds(k + EDGE - 8, 8), :]
        g_ref[z, 16:24, :] = below_ref[pl.ds(k, 8), :]
        return carry

    lax.fori_loop(0, layers, place_map, 0)

    def place(z, carry):
        for p in range(params):
            k = LEAD + (p * layers + z) * EDGE
            e_ref[0, p, z, 0:8, :] = above_ref[pl.ds(k + EDGE - 8, 8), :]
            e_ref[0, p, z, 8:16, :] = order_ref[p, z]
            e_ref[0, p, z, 16:24, :] = below_ref[pl.ds(k, 8), :]
            k = corner_rows(params) + LEAD + (p * layers + z) * ADJ_EDGE
            lam_ref[p, z, 0:8, :] = far_above_ref[pl.ds(k + ADJ_EDGE - 8, 8), :]
            lam_ref[p, z, 8:16, :] = cot_ref[p, z]
            lam_ref[p, z, 16:24, :] = far_below_ref[pl.ds(k, 8), :]
        return carry

    lax.fori_loop(0, layers, place, 0)

    at = 0
    gs_ref[...] = jnp.zeros_like(gs_ref)
    for field in range(2 * params + 1):
        kind = 0 if field < params else 1 if field < 2 * params else 2
        n = CORNER[kind]
        a, b = left_ref[8 * field : 8 * field + 8, :], right_ref[8 * field : 8 * field + 8, :]
        blocks = (
            (far_above_ref[at : at + n, :], 8 - n, n),
            (jnp.where(col < 5, a, b), 8, 8),
            (far_below_ref[at : at + n, :], 16, n),
        )
        at += n
        for value, first, n in blocks:
            if kind == 0:
                se_ref[0, field, first : first + n, :] = value
            elif kind == 1:
                slam_ref[field - params, first : first + n, :] = value
            else:
                gs_ref[first : first + n, :] = value
        if kind == 0:
            outer_ref[field, 8:16, :] = jnp.where(col == 0, roll(a, 1), roll(b, 127))

    def lookup(index, which):
        values = jnp.broadcast_to(table_ref[which : which + 1, :], tile)
        return jnp.take_along_axis(values, index, axis=1, mode="promise_in_bounds")

    for i in range(3):
        r = 8 * i
        for z in range(layers):
            index = map_ref[z] if i == 1 else g_ref[z, r : r + 8, :].astype(jnp.int32) & 127
            m_ref[z, r : r + 8, :] = lookup(index, 3 * i + 1)
        index = gs_ref[r : r + 8, :].astype(jnp.int32) & 127
        ms_ref[r : r + 8, :] = jnp.where(col < 5, lookup(index, 3 * i), lookup(index, 3 * i + 2))

    def sides(value, strip, z):
        ends = roll(strip, 123 - 10 * z)
        left = roll(jnp.where(lane == 127, ends, value), 1)
        right = roll(jnp.where(lane == 0, ends, value), 127)
        return left + right

    def note_ends(value, p, rows, z):
        moved = roll(value, 10 * z + 5)
        here = (lane == 10 * z + 4) | (lane == 10 * z + 5)
        inject_ref[p, rows, :] = jnp.where(here, moved, inject_ref[p, rows, :])

    def strip_sides(value, ends, outer=None):
        left = roll(jnp.where(col == 4, ends, value), 1)
        right = roll(jnp.where(col == 5, ends, value), 127)
        if outer is not None:
            left = jnp.where(col == 0, outer, left)
            right = jnp.where(col == 9, outer, right)
        below = jnp.where(lane < COLS, value, roll(value, COLS))
        above = jnp.where(lane >= COLS * (layers - 1), value, roll(value, 128 - COLS))
        return (left + right) + (below + above)

    def total_of(values):
        while len(values) > 1:
            values = [a + b for a, b in zip(values[::2], values[1::2])]
        return values[0]

    def row_slices(r):
        return pl.ds(r, 8), pl.ds(r - 1, 8), pl.ds(r + 1, 8)

    def each_window(windows, z, body):
        start, count, most = windows
        for i in range(count):
            body(jnp.minimum(start + 8 * i + ((z + 16) >> 5), most))

    def forward(t, windows, last):
        old, old_strip = e_ref.at[t], se_ref.at[t]

        def layer(z, carry):
            below, above = jnp.maximum(z - 1, 0), jnp.minimum(z + 1, layers - 1)

            def window(r):
                rows, before, after = row_slices(r)
                e = [old[p, z, rows, :] for p in range(params)]
                squares = [x * x for x in e]
                base = 1.5 * total_of(squares) + 5.0
                m = m_ref[z, rows, :]
                for p in range(params):
                    near = sides(e[p], old_strip[p, rows, :], z)
                    near = near + (old[p, z, before, :] + old[p, z, after, :])
                    near = near + (old[p, below, rows, :] + old[p, above, rows, :])
                    rate = e[p] * (base - 0.5 * squares[p]) - near
                    rate_ref[t, p, z, rows, :] = rate
                    new = e[p] - m * rate
                    if last:
                        final_ref[p, z] = new
                    else:
                        e_ref[t + 1, p, z, rows, :] = new
                        note_ends(e[p], p, rows, z)

            each_window(windows, z, window)
            return carry

        lax.fori_loop(0, layers, layer, 0)
        if last:
            return

        def strip_window(i, carry):
            rows, before, after = row_slices(jnp.minimum(windows[0] + 8 * i, windows[2]))
            e = [old_strip[p, rows, :] for p in range(params)]
            squares = [x * x for x in e]
            base = 1.5 * total_of(squares) + 5.0
            m = ms_ref[rows, :]
            for p in range(params):
                near = strip_sides(e[p], inject_ref[p, rows, :], outer_ref[p, rows, :] if t == 0 else None)
                near = near + (old_strip[p, before, :] + old_strip[p, after, :])
                rate = e[p] * (base - 0.5 * squares[p]) - near
                se_ref[t + 1, p, rows, :] = e[p] - m * rate
            return carry

        lax.fori_loop(0, windows[1], strip_window, 0)

    inject_ref[...] = jnp.zeros_like(inject_ref)
    forward(0, (3, 3, 13), False)
    forward(1, (4, 2, 12), False)
    forward(2, (4, 2, 12), False)
    forward(3, (8, 1, 8), True)

    def weigh(z, carry):
        for r in (0, 8, 16):
            rows = slice(r, r + 8)
            m = m_ref[z, rows, :]
            for p in range(params):
                u_ref[0, p, z, rows, :] = m * lam_ref[p, z, rows, :]
            cell_ref[z, rows, :] = jnp.zeros(tile, jnp.float32)
        return carry

    lax.fori_loop(0, layers, weigh, 0)
    for r in (0, 8, 16):
        rows = slice(r, r + 8)
        for p in range(params):
            su_ref[0, p, rows, :] = ms_ref[rows, :] * slam_ref[p, rows, :]

    def backward(t, slot, windows, last):
        old, old_strip = u_ref.at[slot], su_ref.at[slot]

        def layer(z, carry):
            below, above = jnp.maximum(z - 1, 0), jnp.minimum(z + 1, layers - 1)

            def window(r):
                rows, before, after = row_slices(r)
                e = [e_ref[t, p, z, rows, :] for p in range(params)]
                u = [old[p, z, rows, :] for p in range(params)]
                lam = [lam_ref[p, z, rows, :] for p in range(params)]
                squares = [x * x for x in e]
                base = 1.5 * total_of(squares) + 5.0
                inner = 3.0 * total_of([x * y for x, y in zip(e, u)])
                m = m_ref[z, rows, :]
                worked = total_of([lam[p] * rate_ref[t, p, z, rows, :] for p in range(params)])
                cell_ref[z, rows, :] = cell_ref[z, rows, :] + worked
                for p in range(params):
                    near = sides(u[p], old_strip[p, rows, :], z)
                    near = near + (old[p, z, before, :] + old[p, z, after, :])
                    near = near + (old[p, below, rows, :] + old[p, above, rows, :])
                    change = u[p] * (base - 1.5 * squares[p]) + e[p] * inner - near
                    new = lam[p] - change
                    if last:
                        adjoint_ref[p, z] = new
                    else:
                        lam_ref[p, z, rows, :] = new
                        u_ref[1 - slot, p, z, rows, :] = m * new
                        note_ends(u[p], p, rows, z)

            each_window(windows, z, window)
            return carry

        lax.fori_loop(0, layers, layer, 0)
        if last:
            return

        def strip_window(i, carry):
            rows, before, after = row_slices(jnp.minimum(windows[0] + 8 * i, windows[2]))
            e = [se_ref[t, p, rows, :] for p in range(params)]
            u = [old_strip[p, rows, :] for p in range(params)]
            squares = [x * x for x in e]
            base = 1.5 * total_of(squares) + 5.0
            inner = 3.0 * total_of([x * y for x, y in zip(e, u)])
            m = ms_ref[rows, :]
            for p in range(params):
                near = strip_sides(u[p], inject_ref[p, rows, :])
                near = near + (old_strip[p, before, :] + old_strip[p, after, :])
                change = u[p] * (base - 1.5 * squares[p]) + e[p] * inner - near
                new = slam_ref[p, rows, :] - change
                slam_ref[p, rows, :] = new
                su_ref[1 - slot, p, rows, :] = m * new
            return carry

        lax.fori_loop(0, windows[1], strip_window, 0)

    backward(3, 0, (4, 2, 12), False)
    backward(2, 1, (4, 2, 12), False)
    backward(1, 0, (4, 2, 12), False)
    backward(0, 1, (8, 1, 8), True)

    grains = [map_ref[z] for z in range(layers)]
    cells = [cell_ref[z, 8:16, :] for z in range(layers)]

    def bin_one(g, carry):
        kept = [jnp.where(grains[z] == g, cells[z], 0.0) for z in range(layers)]
        total = sum(kept[1:4], kept[0]) + sum(kept[5:8], kept[4]) + sum(kept[9:], kept[8])
        binned_ref[pl.ds(g, 1), :] = jnp.sum(total, axis=0, keepdims=True)
        return carry

    lax.fori_loop(0, binned_ref.shape[0], bin_one, 0, unroll=4)
    ones = jnp.full((8, 128), -TIME_STEP, jnp.float32)
    sums = lax.dot_general(
        ones, binned_ref[...], (((1,), (1,)), ((), ())),
        precision=lax.Precision.HIGHEST, preferred_element_type=jnp.float32,
    )
    for k in range(0, sums_ref.shape[0], 8):
        sums_ref[k : k + 8, :] = sums


def pick_owned(counts, owned, slots_ref, sums_ref, out_ref, slot_rows, value_rows, total_ref):
    wide_count, narrow_count = counts
    count = wide_count * narrow_count
    wide, narrow = lax.axis_index("wide"), lax.axis_index("narrow")
    base = (wide * narrow_count + narrow) * owned
    listed = sums_ref.shape[1]
    tile = (8, 128)
    for k in range(count):
        slot = slots_ref[k : k + 1, :] - base
        slot_rows[k] = jnp.broadcast_to(slot, tile)
        value = jnp.concatenate([sums_ref[k : k + 1, :], jnp.zeros((1, 128 - listed), jnp.float32)], axis=1)
        value_rows[k] = jnp.broadcast_to(value, tile)
    sub = lax.broadcasted_iota(jnp.int32, tile, 0)
    blocks = total_ref.shape[0] // 8
    step = 16
    for first in range(0, blocks, step):
        some = range(first, min(first + step, blocks))

        def body(k, acc, some=some):
            slot, value = slot_rows[k], value_rows[k]
            shifted = slot - sub
            return tuple(a + jnp.where(shifted == 8 * j, value, 0.0) for a, j in zip(acc, some))

        acc = lax.fori_loop(0, count, body, tuple(jnp.zeros(tile, jnp.float32) for _ in some), unroll=4)
        for a, j in zip(acc, some):
            total_ref[8 * j : 8 * j + 8, :] = a
    whole = lax.dot_general(
        jnp.ones(tile, jnp.float32), total_ref[...], (((1,), (1,)), ((), ())),
        precision=lax.Precision.HIGHEST, preferred_element_type=jnp.float32,
    )
    out_ref[...] = whole[0:1, 0:owned]


def f32(*shape):
    return jax.ShapeDtypeStruct(shape, jnp.float32)


def kernel(body, out_shape, scratch=(), name=None, **specs):
    return pl.pallas_call(
        body, out_shape=out_shape, scratch_shapes=list(scratch), name=name, **specs,
        compiler_params=pltpu.CompilerParams(vmem_limit_bytes=VMEM_LIMIT),
    )


def shifted(value, axis, count, by):
    return lax.ppermute(value, axis, [(i, (i + by) % count) for i in range(count)])


def per_device(counts, order_init, cotangent, grain_map, brick_grains, grain_slot, mobility):
    wide_count, narrow_count = counts
    params, layers = order_init.shape[:2]
    assert order_init.shape[2:] == (8, 128) and layers * COLS < 128
    owned = mobility.shape[0]
    listed = brick_grains.shape[1]
    bricks = brick_grains.shape[0]

    both = ("wide", "narrow")
    count = wide_count * narrow_count

    padded = -owned % 128
    own = jnp.pad(mobility, (0, padded)).reshape(-1, 128)
    every = lax.all_gather(own, both, axis=0, tiled=True)

    edge_rows = (params + 1) * layers * EDGE + 2 * LEAD
    down, up = kernel(pack_rows, (f32(edge_rows, 128),) * 2, name="pack_rows")(order_init, grain_map)
    above = shifted(down, "wide", wide_count, 1)
    below = shifted(up, "wide", wide_count, -1)

    strip_rows = (2 * params + 1) * 8
    here = pl.BlockSpec(memory_space=pltpu.VMEM)
    to_right, to_left = kernel(
        pack_strips, (f32(strip_rows, 128),) * 2, name="pack_strips",
        in_specs=[here, here, here, pl.BlockSpec(memory_space=pl.ANY)],
    )(order_init, cotangent, grain_map, down)
    from_left = shifted(to_right, "narrow", narrow_count, 1)
    from_right = shifted(to_left, "narrow", narrow_count, -1)

    slots = kernel(
        find_slots, jax.ShapeDtypeStruct((bricks, 128), jnp.int32), name="find_slots"
    )(brick_grains, grain_slot.reshape(-1, 128))

    far_rows = corner_rows(params) + params * layers * ADJ_EDGE + 2 * LEAD
    far_down, far_up = kernel(pack_corners, (f32(far_rows, 128),) * 2, name="pack_corners")(
        cotangent, from_left, from_right
    )
    far_above = shifted(far_down, "wide", wide_count, 1)
    far_below = shifted(far_up, "wide", wide_count, -1)

    table = kernel(
        functools.partial(find_mobility, counts, owned), f32(16, 128),
        (pltpu.VMEM((16, 128), jnp.int32),), name="find_mobility",
    )(slots, every)

    vmem = lambda *shape: pltpu.VMEM(shape, jnp.float32)
    block = (params, layers, ROWS, 128)
    strip = (params, ROWS, 128)
    final, adjoint, sums = kernel(
        evolve,
        (f32(*order_init.shape), f32(*order_init.shape), f32(count, listed)),
        (
            vmem(ITERS, *block), vmem(ITERS, *strip), vmem(ITERS, *block), vmem(*strip), vmem(*strip),
            vmem(*block), vmem(*strip), vmem(2, *block), vmem(2, *strip),
            vmem(layers, ROWS, 128), vmem(ROWS, 128), vmem(layers, ROWS, 128), vmem(ROWS, 128),
            vmem(layers, ROWS, 128), vmem(listed, 128),
        ),
        name="evolve",
    )(
        order_init, cotangent, grain_map, above, below, far_above, far_below,
        from_left, from_right, table,
    )

    every_sum = lax.all_to_all(sums, both, 0, 0, tiled=True)
    grads = kernel(
        functools.partial(pick_owned, counts, owned),
        f32(1, owned),
        (pltpu.VMEM((count, 8, 128), jnp.int32), vmem(count, 8, 128), vmem(owned + -owned % 8, 128)),
        name="pick_owned",
    )(slots, every_sum)
    return final, adjoint, grads.reshape(owned)


def solution(mesh):
    counts = (mesh.shape["wide"], mesh.shape["narrow"])
    field = P("groups", None, "wide", "narrow")
    spread = P(("groups", "wide", "narrow"))
    return jax.shard_map(
        functools.partial(per_device, counts),
        mesh=mesh,
        in_specs=(field, field, P("groups", "wide", "narrow"), P("groups", None), P("groups"), spread),
        out_specs=(field, field, spread),
        check_vma=False,
    )
```

time: 95.2 us -> 96.8 us (1.017)
  blocking collectives: 0 us -> 39.7 us
  waiting for transfers between devices: 33.7 us -> 3.8 us
  starting transfers between devices: 18.2 us -> 8.1 us
  Pallas kernels: 39.8 us -> 42.3 us
    all_gather x0 -> x1, blocking collectives: none -> 30.8 us  [per_device(): every = lax.all_gather(own, both, axis=0, tiled=True)]
    ppermute x18 -> x6, waiting for transfers between devices: 26.8 us -> 3.8 us  [shifted(): lax.ppermute(value, axis, [(i, (i + by) % count) for i in range(count)])]
    all_to_all x0 -> x1, blocking collectives: none -> 8.95 us  [per_device(): every_sum = lax.all_to_all(sums, both, 0, 0, tiled=True)]
    ppermute x4 -> x0, waiting for transfers between devices: 6.81 us -> none  [diagonal(): return lax.ppermute(value, ('wide', 'narrow'), pairs)]
    ppermute x18 -> x6, starting transfers between devices: 13.8 us -> 8.1 us  [shifted(): lax.ppermute(value, axis, [(i, (i + by) % count) for i in range(count)])]
    ppermute x4 -> x0, starting transfers between devices: 4.33 us -> none  [diagonal(): return lax.ppermute(value, ('wide', 'narrow'), pairs)]
    pallas_call x3 -> x5, Pallas kernels: 37.3 us -> 39.9 us  [the longest x1 39 us: per_device(): kernel(evolve, (f32(*order_init.shape), f32(*order_init.shape), f32(count...]
  transfers between devices with their start and end apart: 22 -> 6, of which waited for: 12 -> 2; matrix products, arithmetic and copies ran while one was open for 0% -> 0% of each run, Pallas kernels for 2% -> 2%
where the time goes in v2:
time: 96.8 us; the launch traced here: 96.5 us
  Pallas kernels  42.3 us (44%)
  blocking collectives  39.7 us (41%)
  starting transfers between devices  8.1 us (8%)
  waiting for transfers between devices  3.8 us (4%)
  local copies, waits for them, and re-layouts  1.82 us (2%)
    pallas_call x1, Pallas kernels, per_device(): kernel(evolve, (f32(*order_init.shape), f32(*order_init.shape), f32(count...  39 us
    all_gather x1, blocking collectives, per_device(): every = lax.all_gather(own, both, axis=0, tiled=True)  30.8 us
    all_to_all x1, blocking collectives, per_device(): every_sum = lax.all_to_all(sums, both, 0, 0, tiled=True)  8.95 us
    ppermute x6, starting transfers between devices, shifted(): lax.ppermute(value, axis, [(i, (i + by) % count) for i in range(count)])  8.1 us
    ppermute x6, waiting for transfers between devices, shifted(): lax.ppermute(value, axis, [(i, (i + by) % count) for i in range(count)])  3.8 us
  transfers between devices with their start and end apart: 6, of which 2 were waited for; matrix products, arithmetic and copies ran while one was open for 0% of the time, Pallas kernels for 2%

profile of v2, /device:TPU:0, one launch (start us, length us, event | category | flops | bytes accessed | tf_op | source)
XLA Modules:
  0.0 96.5 jit_solution(17695398140484482226)
XLA Ops:
  0.6 0.0 copy-start
  0.6 1.0 %copy-done = f32[8,12,8,128]{3,2,1,0:T(8,128)S(1)} copy-done((f32[8,12,8,128]{3,2,1,0:T(8,128)S(1)}, f32[8,12,8,128]{3,2,1,0:T(8,128)}, u32[]{:S(2)}) %copy-start) | copy-done | bytes 393240
  1.6 0.8 copy-done.3
  2.4 0.1 pack_rows.1
  2.5 2.4 %collective-permute-start.1 = (f32[664,128]{1,0:T(8,128)S(1)}, f32[664,128]{1,0:T(8,128)S(1)}, u32[]{:S(2)}, u32[]{:S(2)}) collective-permute-start(f32[664,128]{1,0:T(8,128)S(1)} %get-tuple-element.13), channel_id=1, source_target_pairs={{0,12},{4,0},{8,4},{12,8},{1,13},{5,1},{9,5},{13,9},{2,14},{6,2},{... | collective-permute-start | bytes 1019912 | tf_op jit(solution)/shard_map/ppermute | solution.py:448
  4.9 0.0 collective-permute-start
  4.9 0.3 pack_strips.1
  5.2 0.0 copy-start.1
  5.2 1.6 %collective-permute-start.2 = (f32[136,128]{1,0:T(8,128)S(1)}, f32[136,128]{1,0:T(8,128)S(1)}, u32[]{:S(2)}, u32[]{:S(2)}) collective-permute-start(f32[136,128]{1,0:T(8,128)S(1)} %get-tuple-element.14), channel_id=1, source_target_pairs={{0,1},{1,2},{2,3},{3,0},{4,5},{5,6},{6,7},{7,4},{8,9},{9,10},{10,1... | collective-permute-start | bytes 208904 | tf_op jit(solution)/shard_map/ppermute | solution.py:448
  6.9 2.2 %collective-permute-start.3 = (f32[136,128]{1,0:T(8,128)S(1)}, f32[136,128]{1,0:T(8,128)S(1)}, u32[]{:S(2)}, u32[]{:S(2)}) collective-permute-start(f32[136,128]{1,0:T(8,128)S(1)} %get-tuple-element.15), channel_id=1, source_target_pairs={{0,3},{1,0},{2,1},{3,2},{4,7},{5,4},{6,5},{7,6},{8,11},{9,8},{10,9... | collective-permute-start | bytes 208904 | tf_op jit(solution)/shard_map/ppermute | solution.py:448
  9.1 3.0 %collective-permute-done.2.left_ref = f32[136,128]{1,0:T(8,128)S(1)} collective-permute-done((f32[136,128]{1,0:T(8,128)S(1)}, f32[136,128]{1,0:T(8,128)S(1)}, u32[]{:S(2)}, u32[]{:S(2)}) %collective-permute-start.2) | collective-permute-done | bytes 69664 | tf_op jit(solution)/shard_map/ppermute | solution.py:448
  12.1 0.8 collective-permute-done.3.right_ref
  12.9 0.1 pack_corners.1
  13.0 0.1 collective-permute-start.4
  13.1 1.7 %collective-permute-start.5 = (f32[472,128]{1,0:T(8,128)S(1)}, f32[472,128]{1,0:T(8,128)S(1)}, u32[]{:S(2)}, u32[]{:S(2)}) collective-permute-start(f32[472,128]{1,0:T(8,128)S(1)} %get-tuple-element.17), channel_id=1, source_target_pairs={{0,12},{4,0},{8,4},{12,8},{1,13},{5,1},{9,5},{13,9},{2,14},{6,2},{... | collective-permute-start | bytes 725000 | tf_op jit(solution)/shard_map/ppermute | solution.py:448
  14.8 1.1 %find_slots.1.slots_ref = s32[16,128]{1,0:T(8,128)S(1)} custom-call(s32[16,64]{1,0:T(8,128)S(1)} %copy-done.6, s32[49,128]{1,0:T(8,128)S(1)} %bitcast.11), custom_call_target="tpu_custom_call" | custom-call | tf_op jit(solution)/shard_map/find_slots/pallas_call | solution.py:480
  15.9 0.0 copy-start.4
  15.9 30.8 %all-gather = f32[16,4,128]{2,1,0:T(4,128)S(1)} all-gather(f32[1,4,128]{2,1,0:T(4,128)S(1)} %pad_bitcast_fusion), channel_id=1, replica_groups=mesh['groups'=2,'wide'=4,'narrow'=4] {'wide','narrow'}, dimensions={0}, use_global_device_ids=true | all-gather | bytes 34816 | tf_op jit(solution)/shard_map/all_gather | solution.py:464
  46.7 0.4 find_mobility.1.table_ref
  47.2 0.0 collective-permute-done.5.far_below_ref
  47.2 0.0 collective-permute-done.1.below_ref
  47.2 39.0 %evolve.1 = (f32[8,12,8,128]{3,2,1,0:T(8,128)}, f32[8,12,8,128]{3,2,1,0:T(8,128)}, f32[16,64]{1,0:T(8,128)S(1)}) custom-call(f32[8,12,8,128]{3,2,1,0:T(8,128)S(1)} %copy-done.1, f32[8,12,8,128]{3,2,1,0:T(8,128)S(1)} %copy-done.2, s32[12,8,128]{2,1,0:T(8,128)S(1)} %copy-done.4, f32[664,128]{1,0:T(8,128)S(1)} %collective-permute-done.above_ref, ...), custom_call_target="tpu_custom_call" | custom-call | tf_op jit(solution)/shard_map/evolve/pallas_call | solution.py:499
  86.2 9.0 %all_to_all.11 = f32[16,1,64]{2,1,0:T(1,128)S(1)} all-to-all(f32[16,1,64]{2,1,0:T(1,128)S(1)} %bitcast.12), channel_id=1, replica_groups=mesh['groups'=2,'wide'=4,'narrow'=4] {'wide','narrow'}, dimensions={0} | all-to-all | bytes 8192 | tf_op jit(solution)/shard_map/all_to_all | solution.py:514
  95.2 1.3 %pick_owned.1 = f32[1,392]{1,0:T(1,128)} custom-call(s32[16,128]{1,0:T(8,128)S(1)} %find_slots.1.slots_ref, f32[16,64]{1,0:T(8,128)S(1)} %bitcast.10), custom_call_target="tpu_custom_call" | custom-call | tf_op jit(solution)/shard_map/pick_owned/pallas_call | solution.py:515
  (14 shorter events, 0.0 us)
Async XLA Ops:
  0.6 1.0 %copy-start = (f32[8,12,8,128]{3,2,1,0:T(8,128)S(1)}, f32[8,12,8,128]{3,2,1,0:T(8,128)}, u32[]{:S(2)}) copy-start(f32[8,12,8,128]{3,2,1,0:T(8,128)} %order_ref.5) | copy-start | bytes 1179652
  1.6 0.8 copy-start.3
  2.4 2.5 %copy-start.2 = (f32[8,12,8,128]{3,2,1,0:T(8,128)S(1)}, f32[8,12,8,128]{3,2,1,0:T(8,128)}, u32[]{:S(2)}) copy-start(f32[8,12,8,128]{3,2,1,0:T(8,128)} %cot_ref.5) | copy-start | bytes 1179652
  2.5 44.7 %collective-permute-start.1 = (f32[664,128]{1,0:T(8,128)S(1)}, f32[664,128]{1,0:T(8,128)S(1)}, u32[]{:S(2)}, u32[]{:S(2)}) collective-permute-start(f32[664,128]{1,0:T(8,128)S(1)} %get-tuple-element.13), channel_id=1, source_target_pairs={{0,12},{4,0},{8,4},{12,8},{1,13},{5,1},{9,5},{13,9},{2,14},{6,2},{... | collective-permute-start | bytes 1019912 | tf_op jit(solution)/shard_map/ppermute | solution.py:448
  4.9 42.3 %collective-permute-start = (f32[664,128]{1,0:T(8,128)S(1)}, f32[664,128]{1,0:T(8,128)S(1)}, u32[]{:S(2)}, u32[]{:S(2)}) collective-permute-start(f32[664,128]{1,0:T(8,128)S(1)} %get-tuple-element.12.after_ref), channel_id=1, source_target_pairs={{0,4},{4,8},{8,12},{12,0},{1,5},{5,9},{9,13},{13,1},{2,6},{6,10},{... | collective-permute-start | bytes 1019912 | tf_op jit(solution)/shard_map/ppermute | solution.py:448
  5.2 42.0 %copy-start.1 = (f32[8,12,8,128]{3,2,1,0:T(8,128)S(1)}, f32[8,12,8,128]{3,2,1,0:T(8,128)}, u32[]{:S(2)}) copy-start(f32[8,12,8,128]{3,2,1,0:T(8,128)} %order_ref.5) | copy-start | bytes 1179652
  5.2 6.9 %collective-permute-start.2 = (f32[136,128]{1,0:T(8,128)S(1)}, f32[136,128]{1,0:T(8,128)S(1)}, u32[]{:S(2)}, u32[]{:S(2)}) collective-permute-start(f32[136,128]{1,0:T(8,128)S(1)} %get-tuple-element.14), channel_id=1, source_target_pairs={{0,1},{1,2},{2,3},{3,0},{4,5},{5,6},{6,7},{7,4},{8,9},{9,10},{10,1... | collective-permute-start | bytes 208904 | tf_op jit(solution)/shard_map/ppermute | solution.py:448
  6.9 7.9 %copy-start.5 = (s32[6272]{0:T(1024)S(1)}, s32[6272]{0:T(1024)}, u32[]{:S(2)}) copy-start(s32[6272]{0:T(1024)} %param.10) | copy-start | bytes 75268
  6.9 6.0 %collective-permute-start.3 = (f32[136,128]{1,0:T(8,128)S(1)}, f32[136,128]{1,0:T(8,128)S(1)}, u32[]{:S(2)}, u32[]{:S(2)}) collective-permute-start(f32[136,128]{1,0:T(8,128)S(1)} %get-tuple-element.15), channel_id=1, source_target_pairs={{0,3},{1,0},{2,1},{3,2},{4,7},{5,4},{6,5},{7,6},{8,11},{9,8},{10,9... | collective-permute-start | bytes 208904 | tf_op jit(solution)/shard_map/ppermute | solution.py:448
  12.9 1.9 %copy-start.6 = (s32[16,64]{1,0:T(8,128)S(1)}, s32[16,64]{1,0:T(8,128)}, u32[]{:S(2)}) copy-start(s32[16,64]{1,0:T(8,128)} %bricks_ref.1) | copy-start | bytes 12292
  13.0 34.2 %collective-permute-start.4 = (f32[472,128]{1,0:T(8,128)S(1)}, f32[472,128]{1,0:T(8,128)S(1)}, u32[]{:S(2)}, u32[]{:S(2)}) collective-permute-start(f32[472,128]{1,0:T(8,128)S(1)} %get-tuple-element.16), channel_id=1, source_target_pairs={{0,4},{4,8},{8,12},{12,0},{1,5},{5,9},{9,13},{13,1},{2,6},{6,10},{... | collective-permute-start | bytes 725000 | tf_op jit(solution)/shard_map/ppermute | solution.py:448
  13.1 34.1 %collective-permute-start.5 = (f32[472,128]{1,0:T(8,128)S(1)}, f32[472,128]{1,0:T(8,128)S(1)}, u32[]{:S(2)}, u32[]{:S(2)}) collective-permute-start(f32[472,128]{1,0:T(8,128)S(1)} %get-tuple-element.17), channel_id=1, source_target_pairs={{0,12},{4,0},{8,4},{12,8},{1,13},{5,1},{9,5},{13,9},{2,14},{6,2},{... | collective-permute-start | bytes 725000 | tf_op jit(solution)/shard_map/ppermute | solution.py:448
  14.8 1.1 %copy-start.7 = (f32[392]{0:T(512)S(1)}, f32[392]{0:T(512)}, u32[]{:S(2)}) copy-start(f32[392]{0:T(512)} %param.11) | copy-start | bytes 4708
  15.9 31.3 %copy-start.4 = (s32[12,8,128]{2,1,0:T(8,128)S(1)}, s32[12,8,128]{2,1,0:T(8,128)}, u32[]{:S(2)}) copy-start(s32[12,8,128]{2,1,0:T(8,128)} %map_ref.5) | copy-start | bytes 147460

commit v3 on v2

v3 whole, which is shorter than its diff:
```python
import functools

import jax
import jax.numpy as jnp
from jax import lax
from jax.experimental import pallas as pl
from jax.experimental.pallas import tpu as pltpu
from jax.sharding import PartitionSpec as P

ITERS = 4
TIME_STEP = 0.05

EDGE = 6
MAP_EDGE = 5
ADJ_EDGE = 4
ROWS = 24
COLS = 10
LEAD = 8
CORNER = (5, 3, 4)

VMEM_LIMIT = 50 * 1024 * 1024


def lanes(shape):
    return lax.broadcasted_iota(jnp.int32, shape, len(shape) - 1)


def roll(value, shift):
    return pltpu.roll(value, shift, 1)


def pack_rows(order_ref, down_ref, up_ref):
    params, layers = order_ref.shape[:2]
    for p in range(params):
        for z in range(layers):
            k = LEAD + (p * layers + z) * EDGE
            down_ref[k : k + EDGE, :] = order_ref[p, z, 8 - EDGE : 8, :]
            up_ref[k : k + EDGE, :] = order_ref[p, z, 0:EDGE, :]
    for ref in (down_ref, up_ref):
        ref[0:LEAD, :] = jnp.zeros((LEAD, 128), jnp.float32)
        ref[ref.shape[0] - LEAD :, :] = jnp.zeros((LEAD, 128), jnp.float32)


def pack_strips(order_ref, cot_ref, map_ref, mob_ref, after_ref, right_ref, left_ref, own_ref):
    params, layers = order_ref.shape[:2]
    owned = mob_ref.shape[1]
    lane = lanes((8, 128))
    zero = jnp.zeros((8, 128), jnp.float32)

    def span(first, size):
        return ((lane - first) & 127) < size

    for field in range(params + 1):
        right, left = zero, zero
        for z in range(layers):
            value = order_ref[field, z] if field < params else map_ref[z].astype(jnp.float32)
            moved = roll(value, 10 * z + 5)
            right = jnp.where(span(10 * z - 1, 6), moved, right)
            left = jnp.where(span(10 * z + 5, 6), moved, left)
            if field < params:
                right = jnp.where(span(10 * z + 5, 4), roll(cot_ref[field, z], 10 * z + 9), right)
                left = jnp.where(span(10 * z + 1, 4), roll(cot_ref[field, z], 10 * z + 1), left)
        right_ref[8 * field : 8 * field + 8, :] = right
        left_ref[8 * field : 8 * field + 8, :] = left
    rows = own_ref.shape[0]
    at = 8 * (params + 1)
    for i in range(rows):
        size = min(128, owned - 128 * i)
        row = mob_ref[0:1, 128 * i : 128 * i + size]
        if size < 128:
            row = jnp.concatenate([row, jnp.zeros((1, 128 - size), jnp.float32)], axis=1)
        for ref, k in ((own_ref, i), (right_ref, at + i), (left_ref, at + i)):
            ref[k : k + 1, :] = row


def corner_rows(params):
    return -(-(params * (CORNER[0] + CORNER[1]) + CORNER[2]) // 8) * 8


def far_places(params, layers, block):
    mobs = corner_rows(params)
    cots = mobs + block + LEAD
    maps = cots + params * layers * ADJ_EDGE + LEAD
    length = maps + layers * MAP_EDGE + LEAD
    return mobs, cots, maps, length + -length % 8


def merged_strips(params, left_ref, right_ref):
    first = lanes((8, 128)) % COLS < 5
    fields = []
    for field in range(params + 1):
        rows = slice(8 * field, 8 * field + 8)
        fields.append((left_ref[rows, :], right_ref[rows, :]))
    order = [jnp.where(first, a, b) for a, b in fields[:params]]
    cot = [jnp.where(first, roll(a, 124), roll(b, 4)) for a, b in fields[:params]]
    return order + cot + [jnp.where(first, *fields[params])]


def pack_far(cot_ref, map_ref, left_ref, right_ref, own_ref, *refs):
    *other_refs, down_ref, up_ref, block_ref = refs
    params, layers = cot_ref.shape[:2]
    rows = own_ref.shape[0]
    at = 8 * (params + 1)
    pieces = [own_ref[...], left_ref[at : at + rows, :]]
    pieces += [ref[...] for ref in other_refs]
    pieces.append(right_ref[at : at + rows, :])
    mobs, cots, maps, length = far_places(params, layers, block_ref.shape[0])
    for i, piece in enumerate(pieces):
        for ref, k in ((block_ref, 0), (down_ref, mobs), (up_ref, mobs)):
            ref[k + i * rows : k + (i + 1) * rows, :] = piece
    at = 0
    for field, both in enumerate(merged_strips(params, left_ref, right_ref)):
        n = CORNER[0 if field < params else 1 if field < 2 * params else 2]
        down_ref[at : at + n, :] = both[8 - n : 8]
        up_ref[at : at + n, :] = both[0:n]
        at += n
    for ref in (down_ref, up_ref):
        for first, last in (
            (at, mobs), (cots - LEAD, cots), (maps - LEAD, maps), (maps + layers * MAP_EDGE, length)
        ):
            ref[first:last, :] = jnp.zeros((last - first, 128), jnp.float32)
    for p in range(params):
        for z in range(layers):
            k = cots + (p * layers + z) * ADJ_EDGE
            down_ref[k : k + ADJ_EDGE, :] = cot_ref[p, z, 8 - ADJ_EDGE : 8, :]
            up_ref[k : k + ADJ_EDGE, :] = cot_ref[p, z, 0:ADJ_EDGE, :]
    for z in range(layers):
        k = maps + z * MAP_EDGE
        cells = map_ref[z].astype(jnp.float32)
        down_ref[k : k + MAP_EDGE, :] = cells[8 - MAP_EDGE : 8]
        up_ref[k : k + MAP_EDGE, :] = cells[0:MAP_EDGE]


def find_slots(bricks_ref, slot_ref, out_ref):
    count, listed = bricks_ref.shape
    rows = slot_ref.shape[0]
    pad = jnp.zeros((8, 128 - listed), jnp.int32)
    for k in range(0, count, 8):
        grain = jnp.concatenate([bricks_ref[k : k + 8, :], pad], axis=1)
        row, col = grain >> 7, grain & 127

        def body(r, found, row=row, col=col):
            table = jnp.broadcast_to(slot_ref[pl.ds(r, 1), :], (8, 128))
            taken = jnp.take_along_axis(table, col, axis=1, mode="promise_in_bounds")
            return jnp.where(row == r, taken, found)

        found = lax.fori_loop(0, rows, body, jnp.zeros((8, 128), jnp.int32), unroll=7)
        out_ref[k : k + 8, :] = jnp.where(lanes((8, 128)) < listed, found, -1)


def find_mobility(counts, owned, at, slots_ref, block_ref, above_ref, below_ref, *refs):
    *other_refs, table_ref, near_ref, mob_ref = refs
    wide_count, narrow_count = counts
    tile = (8, 128)
    wide, narrow = lax.axis_index("wide"), lax.axis_index("narrow")
    size = block_ref.shape[0]
    per_owner = size // narrow_count
    pieces = [block_ref[...], above_ref[at : at + size, :]]
    pieces += [ref[...] for ref in other_refs]
    pieces.append(below_ref[at : at + size, :])
    for i, piece in enumerate(pieces):
        mob_ref[i * size : (i + 1) * size, :] = piece
    for i in range(3):
        for j in range(3):
            w = lax.rem(wide + i - 1 + wide_count, wide_count)
            n = lax.rem(narrow + j - 1 + narrow_count, narrow_count)
            near_ref[3 * i + j : 3 * i + j + 1, :] = slots_ref[pl.ds(w * narrow_count + n, 1), :]
    near_ref[9:16, :] = jnp.zeros((7, 128), jnp.int32)
    slot = [jnp.maximum(near_ref[k : k + 8, :], 0) for k in (0, 8)]
    owner = [jnp.floor((x.astype(jnp.float32) + 0.5) * (1.0 / owned)).astype(jnp.int32) for x in slot]
    inner = [x - y * owned for x, y in zip(slot, owner)]
    by_wide = [jnp.floor((y.astype(jnp.float32) + 0.5) * (1.0 / narrow_count)).astype(jnp.int32) for y in owner]
    back_w = [wide - y for y in by_wide]
    back_n = [narrow - (x - y * narrow_count) for x, y in zip(owner, by_wide)]
    back_w = [jnp.where(x < 0, x + wide_count, x) for x in back_w]
    back_n = [jnp.where(x < 0, x + narrow_count, x) for x in back_n]
    row = [(a * narrow_count + b) * per_owner + (x >> 7) for a, b, x in zip(back_w, back_n, inner)]
    place = [x & 127 for x in inner]

    def body(r, found):
        values = jnp.broadcast_to(mob_ref[pl.ds(r, 1), :], tile)
        return tuple(
            jnp.where(row[k] == r, jnp.take_along_axis(values, place[k], axis=1, mode="promise_in_bounds"), found[k])
            for k in range(2)
        )

    zero = jnp.zeros(tile, jnp.float32)
    found = lax.fori_loop(0, mob_ref.shape[0], body, (zero, zero), unroll=16)
    for k in range(2):
        table_ref[8 * k : 8 * k + 8, :] = TIME_STEP * found[k]


def evolve(
    block,
    order_ref, cot_ref, map_ref, above_ref, below_ref, far_above_ref, far_below_ref,
    left_ref, right_ref, table_ref,
    final_ref, adjoint_ref, sums_ref,
    e_refs, se_refs, rate_refs, lam_refs, slam_refs, u_refs, su_refs,
    inject_ref, outer_ref, m_ref, ms_ref, g_ref, gs_ref, work_ref, binned_ref,
):
    params, layers = order_ref.shape[:2]
    tile = (8, 128)
    lane = lanes(tile)
    col = lane % COLS
    _, cots, maps, _ = far_places(params, layers, block)

    def place(z, carry):
        k = maps + z * MAP_EDGE
        g_ref[z, 0:8, :] = far_above_ref[pl.ds(k + MAP_EDGE - 8, 8), :]
        g_ref[z, 16:24, :] = far_below_ref[pl.ds(k, 8), :]
        for p in range(params):
            k = LEAD + (p * layers + z) * EDGE
            e_refs[0][p, z, 0:8, :] = above_ref[pl.ds(k + EDGE - 8, 8), :]
            e_refs[0][p, z, 8:16, :] = order_ref[p, z]
            e_refs[0][p, z, 16:24, :] = below_ref[pl.ds(k, 8), :]
            k = cots + (p * layers + z) * ADJ_EDGE
            lam_refs[0][p, z, 0:8, :] = far_above_ref[pl.ds(k + ADJ_EDGE - 8, 8), :]
            lam_refs[0][p, z, 8:16, :] = cot_ref[p, z]
            lam_refs[0][p, z, 16:24, :] = far_below_ref[pl.ds(k, 8), :]
        return carry

    lax.fori_loop(0, layers, place, 0)

    at = 0
    gs_ref[...] = jnp.zeros_like(gs_ref)
    for field, both in enumerate(merged_strips(params, left_ref, right_ref)):
        kind = 0 if field < params else 1 if field < 2 * params else 2
        n = CORNER[kind]
        ref = se_refs[0].at[field] if kind == 0 else slam_refs[0].at[field - params] if kind == 1 else gs_ref
        ref[8 - n : 8, :] = far_above_ref[at : at + n, :]
        ref[8:16, :] = both
        ref[16 : 16 + n, :] = far_below_ref[at : at + n, :]
        at += n
    for p in range(params):
        a, b = left_ref[8 * p : 8 * p + 8, :], right_ref[8 * p : 8 * p + 8, :]
        outer_ref[p, 8:16, :] = jnp.where(col == 0, roll(a, 1), roll(b, 127))

    def lookup(index, which):
        values = jnp.broadcast_to(table_ref[which : which + 1, :], tile)
        return jnp.take_along_axis(values, index, axis=1, mode="promise_in_bounds")

    for i in range(3):
        r = 8 * i
        for z in range(layers):
            index = map_ref[z] if i == 1 else g_ref[z, r : r + 8, :].astype(jnp.int32) & 127
            m_ref[z, r : r + 8, :] = lookup(index, 3 * i + 1)
        index = gs_ref[r : r + 8, :].astype(jnp.int32) & 127
        ms_ref[r : r + 8, :] = jnp.where(col < 5, lookup(index, 3 * i), lookup(index, 3 * i + 2))

    def sides(value, strip, z):
        ends = roll(strip, 123 - 10 * z)
        left = roll(jnp.where(lane == 127, ends, value), 1)
        right = roll(jnp.where(lane == 0, ends, value), 127)
        return left + right

    def note_ends(values, i, z):
        here = (lane == 10 * z + 4) | (lane == 10 * z + 5)
        kept = [inject_ref[p, i] for p in range(params)]
        moved = [roll(x, 10 * z + 5) for x in values]
        for p in range(params):
            inject_ref[p, i] = jnp.where(here, moved[p], kept[p])

    def strip_sides(value, ends, outer=None):
        left = roll(jnp.where(col == 4, ends, value), 1)
        right = roll(jnp.where(col == 5, ends, value), 127)
        if outer is not None:
            left = jnp.where(col == 0, outer, left)
            right = jnp.where(col == 9, outer, right)
        below = jnp.where(lane < COLS, value, roll(value, COLS))
        above = jnp.where(lane >= COLS * (layers - 1), value, roll(value, 128 - COLS))
        return (left + right) + (below + above)

    def total_of(values):
        while len(values) > 1:
            values = [a + b for a, b in zip(values[::2], values[1::2])]
        return values[0]

    def row_slices(r):
        return pl.ds(r, 8), pl.ds(r - 1, 8), pl.ds(r + 1, 8)

    def each_window(windows, z, body):
        start, count, most = windows
        for i in range(count):
            body(i, jnp.minimum(start + 8 * i + ((z + 16) >> 5), most))

    def neighbours(ref, strip_ref, values, z, r):
        rows, before, after = row_slices(r)
        below, above = jnp.maximum(z - 1, 0), jnp.minimum(z + 1, layers - 1)
        near = []
        for p in range(params):
            total = sides(values[p], strip_ref[p, rows, :], z)
            total = total + (ref[p, z, before, :] + ref[p, z, after, :])
            near.append(total + (ref[p, below, rows, :] + ref[p, above, rows, :]))
        return near

    def strip_neighbours(ref, values, i, r, outer=False):
        rows, before, after = row_slices(r)
        near = []
        for p in range(params):
            total = strip_sides(values[p], inject_ref[p, i], outer_ref[p, rows, :] if outer else None)
            near.append(total + (ref[p, before, :] + ref[p, after, :]))
        return near

    def rates(e, near):
        squares = [x * x for x in e]
        base = 1.5 * total_of(squares) + 5.0
        return [x * (base - 0.5 * y) - n for x, y, n in zip(e, squares, near)]

    def changes(e, u, near):
        squares = [x * x for x in e]
        base = 1.5 * total_of(squares) + 5.0
        inner = 3.0 * total_of([x * y for x, y in zip(e, u)])
        return [y * (base - 1.5 * s) + x * inner - n for x, y, s, n in zip(e, u, squares, near)]

    def forward(t, windows, last):
        old, old_strip = e_refs[t], se_refs[t]

        def layer(z, carry):
            def window(i, r):
                rows = pl.ds(r, 8)
                e = [old[p, z, rows, :] for p in range(params)]
                m = m_ref[z, rows, :]
                rate = rates(e, neighbours(old, old_strip, e, z, r))
                new = [x - m * y for x, y in zip(e, rate)]
                for p in range(params):
                    rate_refs[t][p, z, rows, :] = rate[p]
                    if last:
                        final_ref[p, z] = new[p]
                    else:
                        e_refs[t + 1][p, z, rows, :] = new[p]
                if not last:
                    note_ends(e, i, z)

            each_window(windows, z, window)
            return carry

        lax.fori_loop(0, layers, layer, 0)
        if last:
            return

        def strip_window(i, carry):
            r = jnp.minimum(windows[0] + 8 * i, windows[2])
            rows = pl.ds(r, 8)
            e = [old_strip[p, rows, :] for p in range(params)]
            m = ms_ref[rows, :]
            rate = rates(e, strip_neighbours(old_strip, e, i, r, t == 0))
            for p in range(params):
                se_refs[t + 1][p, rows, :] = e[p] - m * rate[p]
            return carry

        lax.fori_loop(0, windows[1], strip_window, 0)

    inject_ref[...] = jnp.zeros_like(inject_ref)
    forward(0, (3, 3, 13), False)
    forward(1, (4, 2, 12), False)
    forward(2, (4, 2, 12), False)
    forward(3, (8, 1, 8), True)

    def weigh(z, carry):
        for r in (0, 8, 16):
            rows = slice(r, r + 8)
            m = m_ref[z, rows, :]
            for p in range(params):
                u_refs[0][p, z, rows, :] = m * lam_refs[0][p, z, rows, :]
        return carry

    lax.fori_loop(0, layers, weigh, 0)
    for r in (0, 8, 16):
        rows = slice(r, r + 8)
        for p in range(params):
            su_refs[0][p, rows, :] = ms_ref[rows, :] * slam_refs[0][p, rows, :]

    def backward(t, slot, windows, last):
        old, old_strip = u_refs[slot], su_refs[slot]

        def layer(z, carry):
            def window(i, r):
                rows = pl.ds(r, 8)
                e = [e_refs[t][p, z, rows, :] for p in range(params)]
                u = [old[p, z, rows, :] for p in range(params)]
                m = m_ref[z, rows, :]
                change = changes(e, u, neighbours(old, old_strip, u, z, r))
                lam = [lam_refs[slot][p, z, rows, :] for p in range(params)]
                work_ref[t, z, i] = total_of([lam[p] * rate_refs[t][p, z, rows, :] for p in range(params)])
                new = [x - y for x, y in zip(lam, change)]
                for p in range(params):
                    if last:
                        adjoint_ref[p, z] = new[p]
                    else:
                        lam_refs[1 - slot][p, z, rows, :] = new[p]
                        u_refs[1 - slot][p, z, rows, :] = m * new[p]
                if not last:
                    note_ends(u, i, z)

            each_window(windows, z, window)
            return carry

        lax.fori_loop(0, layers, layer, 0)
        if last:
            return

        def strip_window(i, carry):
            r = windows[0] + 8 * i
            rows = pl.ds(r, 8)
            e = [se_refs[t][p, rows, :] for p in range(params)]
            u = [old_strip[p, rows, :] for p in range(params)]
            m = ms_ref[rows, :]
            change = changes(e, u, strip_neighbours(old_strip, u, i, r))
            for p in range(params):
                new = slam_refs[slot][p, rows, :] - change[p]
                slam_refs[1 - slot][p, rows, :] = new
                su_refs[1 - slot][p, rows, :] = m * new
            return carry

        lax.fori_loop(0, windows[1], strip_window, 0)

    backward(3, 0, (4, 2, 12), False)
    backward(2, 1, (4, 2, 12), False)
    backward(1, 0, (4, 2, 12), False)
    backward(0, 1, (8, 1, 8), True)

    grains = [map_ref[z] for z in range(layers)]
    cells = []
    for z in range(layers):
        upper = work_ref[1, z, 0] + work_ref[2, z, 0] + work_ref[3, z, 0]
        lower = work_ref[1, z, 1] + work_ref[2, z, 1] + work_ref[3, z, 1]
        cells.append(jnp.concatenate([upper[4:8], lower[0:4]], axis=0) + work_ref[0, z, 0])

    def bin_one(g, carry):
        kept = [jnp.where(grains[z] == g, cells[z], 0.0) for z in range(layers)]
        total = sum(kept[1:4], kept[0]) + sum(kept[5:8], kept[4]) + sum(kept[9:], kept[8])
        binned_ref[pl.ds(g, 1), :] = jnp.sum(total, axis=0, keepdims=True)
        return carry

    lax.fori_loop(0, binned_ref.shape[0], bin_one, 0, unroll=4)
    ones = jnp.full((8, 128), -TIME_STEP, jnp.float32)
    sums = lax.dot_general(
        ones, binned_ref[...], (((1,), (1,)), ((), ())),
        precision=lax.Precision.HIGHEST, preferred_element_type=jnp.float32,
    )
    for k in range(0, sums_ref.shape[0], 8):
        sums_ref[k : k + 8, :] = sums


def pick_owned(counts, owned, slots_ref, sums_ref, out_ref, slot_rows, value_rows, total_ref):
    wide_count, narrow_count = counts
    count = wide_count * narrow_count
    wide, narrow = lax.axis_index("wide"), lax.axis_index("narrow")
    base = (wide * narrow_count + narrow) * owned
    listed = sums_ref.shape[1]
    tile = (8, 128)
    for k in range(count):
        slot = slots_ref[k : k + 1, :] - base
        slot_rows[k] = jnp.broadcast_to(slot, tile)
        value = jnp.concatenate([sums_ref[k : k + 1, :], jnp.zeros((1, 128 - listed), jnp.float32)], axis=1)
        value_rows[k] = jnp.broadcast_to(value, tile)
    sub = lax.broadcasted_iota(jnp.int32, tile, 0)
    blocks = total_ref.shape[0] // 8
    step = 16
    for first in range(0, blocks, step):
        some = range(first, min(first + step, blocks))

        def body(k, acc, some=some):
            slot, value = slot_rows[k], value_rows[k]
            shifted = slot - sub
            return tuple(a + jnp.where(shifted == 8 * j, value, 0.0) for a, j in zip(acc, some))

        acc = lax.fori_loop(0, count, body, tuple(jnp.zeros(tile, jnp.float32) for _ in some), unroll=4)
        for a, j in zip(acc, some):
            total_ref[8 * j : 8 * j + 8, :] = a
    whole = lax.dot_general(
        jnp.ones(tile, jnp.float32), total_ref[...], (((1,), (1,)), ((), ())),
        precision=lax.Precision.HIGHEST, preferred_element_type=jnp.float32,
    )
    out_ref[...] = whole[0:1, 0:owned]


def f32(*shape):
    return jax.ShapeDtypeStruct(shape, jnp.float32)


def kernel(body, out_shape, scratch=(), name=None, **specs):
    return pl.pallas_call(
        body, out_shape=out_shape, scratch_shapes=list(scratch), name=name, **specs,
        compiler_params=pltpu.CompilerParams(vmem_limit_bytes=VMEM_LIMIT),
    )


def shifted(value, axis, count, by):
    return lax.ppermute(value, axis, [(i, (i + by) % count) for i in range(count)])


def per_device(counts, order_init, cotangent, grain_map, brick_grains, grain_slot, mobility):
    wide_count, narrow_count = counts
    params, layers = order_init.shape[:2]
    assert order_init.shape[2:] == (8, 128) and layers * COLS < 128
    owned = mobility.shape[0]
    listed = brick_grains.shape[1]
    bricks = brick_grains.shape[0]

    both = ("wide", "narrow")
    count = wide_count * narrow_count

    edge_rows = params * layers * EDGE + 2 * LEAD
    down, up = kernel(pack_rows, (f32(edge_rows, 128),) * 2, name="pack_rows")(order_init)
    above = shifted(down, "wide", wide_count, 1)
    below = shifted(up, "wide", wide_count, -1)

    owned_rows = -(-owned // 128)
    strip_rows = (params + 1) * 8 + owned_rows
    here = pl.BlockSpec(memory_space=pltpu.VMEM)
    to_right, to_left, own = kernel(
        pack_strips, (f32(strip_rows, 128),) * 2 + (f32(owned_rows, 128),), name="pack_strips",
        in_specs=[here] * 4 + [pl.BlockSpec(memory_space=pl.ANY)],
    )(order_init, cotangent, grain_map, mobility.reshape(1, owned), down)
    from_left = shifted(to_right, "narrow", narrow_count, 1)
    from_right = shifted(to_left, "narrow", narrow_count, -1)
    others = [shifted(own, "narrow", narrow_count, d) for d in range(2, narrow_count - 1)]

    block_rows = narrow_count * owned_rows
    far_rows = far_places(params, layers, block_rows)[3]
    far_down, far_up, block = kernel(
        pack_far, (f32(far_rows, 128),) * 2 + (f32(block_rows, 128),), name="pack_far"
    )(cotangent, grain_map, from_left, from_right, own, *others)
    far_above = shifted(far_down, "wide", wide_count, 1)
    far_below = shifted(far_up, "wide", wide_count, -1)
    others = [shifted(block, "wide", wide_count, d) for d in range(2, wide_count - 1)]

    slots = kernel(
        find_slots, jax.ShapeDtypeStruct((bricks, 128), jnp.int32), name="find_slots"
    )(brick_grains, grain_slot.reshape(-1, 128))
    table = kernel(
        functools.partial(find_mobility, counts, owned, far_places(params, layers, block_rows)[0]),
        f32(16, 128),
        (pltpu.VMEM((16, 128), jnp.int32), pltpu.VMEM((wide_count * block_rows, 128), jnp.float32)),
        name="find_mobility",
    )(slots, block, far_above, far_below, *others)

    vmem = lambda *shape: pltpu.VMEM(shape, jnp.float32)
    padded = (params, layers, ROWS, 128)
    strip = (params, ROWS, 128)
    final, adjoint, sums = kernel(
        functools.partial(evolve, block_rows),
        (f32(*order_init.shape), f32(*order_init.shape), f32(count, listed)),
        (
            [vmem(*padded)] * ITERS, [vmem(*strip)] * ITERS, [vmem(*padded)] * ITERS,
            [vmem(*padded)] * 2, [vmem(*strip)] * 2, [vmem(*padded)] * 2, [vmem(*strip)] * 2,
            vmem(params, 3, 8, 128), vmem(*strip),
            vmem(layers, ROWS, 128), vmem(ROWS, 128), vmem(layers, ROWS, 128), vmem(ROWS, 128),
            vmem(ITERS, layers, 2, 8, 128), vmem(listed, 128),
        ),
        name="evolve",
    )(
        order_init, cotangent, grain_map, above, below, far_above, far_below,
        from_left, from_right, table,
    )

    every_sum = lax.all_to_all(sums, both, 0, 0, tiled=True)
    grads = kernel(
        functools.partial(pick_owned, counts, owned),
        f32(1, owned),
        (pltpu.VMEM((count, 8, 128), jnp.int32), vmem(count, 8, 128), vmem(owned + -owned % 8, 128)),
        name="pick_owned",
    )(slots, every_sum)
    return final, adjoint, grads.reshape(owned)


def solution(mesh):
    counts = (mesh.shape["wide"], mesh.shape["narrow"])
    field = P("groups", None, "wide", "narrow")
    spread = P(("groups", "wide", "narrow"))
    return jax.shard_map(
        functools.partial(per_device, counts),
        mesh=mesh,
        in_specs=(field, field, P("groups", "wide", "narrow"), P("groups", None), P("groups"), spread),
        out_specs=(field, field, spread),
        check_vma=False,
    )
```

time: 96.8 us -> 57.1 us (0.59)
  blocking collectives: 39.7 us -> 9.68 us
  Pallas kernels: 42.3 us -> 23.8 us
  waiting for transfers between devices: 3.8 us -> 9.96 us
  starting transfers between devices: 8.1 us -> 9.93 us
    all_gather x1 -> x0, blocking collectives: 30.8 us -> none  [per_device(): every = lax.all_gather(own, both, axis=0, tiled=True)]
    pallas_call x5, Pallas kernels: 39.9 us -> 21.4 us  [the longest x1 20.3 us: per_device(): kernel(functools.partial(evolve, block_rows), (f32(*order_init.shape), f3...]
    ppermute x6 -> x8, waiting for transfers between devices: 3.8 us -> 9.96 us  [shifted(): lax.ppermute(value, axis, [(i, (i + by) % count) for i in range(count)])]
    ppermute x6 -> x8, starting transfers between devices: 8.1 us -> 9.93 us  [shifted(): lax.ppermute(value, axis, [(i, (i + by) % count) for i in range(count)])]
    unnamed x17 -> x16, local copies, waits for them, and re-layouts: 1.82 us -> 2.73 us
  transfers between devices with their start and end apart: 6 -> 8, of which waited for: 2 -> 2; matrix products, arithmetic and copies ran while one was open for 0% -> 0% of each run, Pallas kernels for 2% -> 3%
where the time goes in v3:
time: 57.1 us; the launch traced here: 56.8 us
  Pallas kernels  23.8 us (42%)
  waiting for transfers between devices  9.96 us (17%)
  starting transfers between devices  9.93 us (17%)
  blocking collectives  9.68 us (17%)
  local copies, waits for them, and re-layouts  2.73 us (5%)
  between operations  0.73 us (1%)
    pallas_call x1, Pallas kernels, per_device(): kernel(functools.partial(evolve, block_rows), (f32(*order_init.shape), f3...  20.3 us
    ppermute x8, waiting for transfers between devices, shifted(): lax.ppermute(value, axis, [(i, (i + by) % count) for i in range(count)])  9.96 us
    ppermute x8, starting transfers between devices, shifted(): lax.ppermute(value, axis, [(i, (i + by) % count) for i in range(count)])  9.93 us
    all_to_all x1, blocking collectives, per_device(): every_sum = lax.all_to_all(sums, both, 0, 0, tiled=True)  9.68 us
    unnamed x16, local copies, waits for them, and re-layouts  2.73 us
    pallas_call x1, Pallas kernels, per_device(): kernel(functools.partial(pick_owned, counts, owned), f32(1, owned), (pltp...  1.34 us
  transfers between devices with their start and end apart: 8, of which 2 were waited for; matrix products, arithmetic and copies ran while one was open for 0% of the time, Pallas kernels for 3%

profile of v3, /device:TPU:0, one launch (start us, length us, event | category | flops | bytes accessed | tf_op | source)
XLA Modules:
  0.0 56.8 jit_solution(14327660078067886196)
XLA Ops:
  0.6 0.0 copy-start
  0.6 1.0 %copy-done = f32[8,12,8,128]{3,2,1,0:T(8,128)S(1)} copy-done((f32[8,12,8,128]{3,2,1,0:T(8,128)S(1)}, f32[8,12,8,128]{3,2,1,0:T(8,128)}, u32[]{:S(2)}) %copy-start) | copy-done | bytes 393240
  1.6 0.1 pack_rows.1
  1.7 0.0 copy-start.7
  1.7 0.9 %copy-done.2 = f32[8,12,8,128]{3,2,1,0:T(8,128)S(1)} copy-done((f32[8,12,8,128]{3,2,1,0:T(8,128)S(1)}, f32[8,12,8,128]{3,2,1,0:T(8,128)}, u32[]{:S(2)}) %copy-start.2) | copy-done | bytes 393240
  2.6 0.8 %copy-done.3 = s32[12,8,128]{2,1,0:T(8,128)S(1)} copy-done((s32[12,8,128]{2,1,0:T(8,128)S(1)}, s32[12,8,128]{2,1,0:T(8,128)}, u32[]{:S(2)}) %copy-start.3) | copy-done | bytes 49176
  3.4 0.4 pack_strips.1
  3.8 3.1 %collective-permute-start.2 = (f32[76,128]{1,0:T(8,128)S(1)}, f32[76,128]{1,0:T(8,128)S(1)}, u32[]{:S(2)}, u32[]{:S(2)}) collective-permute-start(f32[76,128]{1,0:T(8,128)S(1)} %get-tuple-element.16), channel_id=1, source_target_pairs={{0,1},{1,2},{2,3},{3,0},{4,5},{5,6},{6,7},{7,4},{8,9},{9,10},{10,1... | collective-permute-start | bytes 116744 | tf_op jit(solution)/shard_map/ppermute | solution.py:490
  6.9 2.1 %collective-permute-start.3 = (f32[76,128]{1,0:T(8,128)S(1)}, f32[76,128]{1,0:T(8,128)S(1)}, u32[]{:S(2)}, u32[]{:S(2)}) collective-permute-start(f32[76,128]{1,0:T(8,128)S(1)} %get-tuple-element.17), channel_id=1, source_target_pairs={{0,3},{1,0},{2,1},{3,2},{4,7},{5,4},{6,5},{7,6},{8,11},{9,8},{10,9... | collective-permute-start | bytes 116744 | tf_op jit(solution)/shard_map/ppermute | solution.py:490
  9.0 0.7 %collective-permute-start.1 = (f32[592,128]{1,0:T(8,128)S(1)}, f32[592,128]{1,0:T(8,128)S(1)}, u32[]{:S(2)}, u32[]{:S(2)}) collective-permute-start(f32[592,128]{1,0:T(8,128)S(1)} %get-tuple-element.15), channel_id=1, source_target_pairs={{0,12},{4,0},{8,4},{12,8},{1,13},{5,1},{9,5},{13,9},{2,14},{6,2},{... | collective-permute-start | bytes 909320 | tf_op jit(solution)/shard_map/ppermute | solution.py:490
  9.6 0.8 %collective-permute-start.4 = (f32[4,128]{1,0:T(4,128)S(1)}, f32[4,128]{1,0:T(4,128)S(1)}, u32[]{:S(2)}, u32[]{:S(2)}) collective-permute-start(f32[4,128]{1,0:T(4,128)S(1)} %get-tuple-element.18.own_ref), channel_id=1, source_target_pairs={{0,2},{1,3},{2,0},{3,1},{4,6},{5,7},{6,4},{7,5},{8,10},{9,11},{10,... | collective-permute-start | bytes 6152 | tf_op jit(solution)/shard_map/ppermute | solution.py:490
  10.4 3.7 %collective-permute-done.4.refs_0_ = f32[4,128]{1,0:T(4,128)S(1)} collective-permute-done((f32[4,128]{1,0:T(4,128)S(1)}, f32[4,128]{1,0:T(4,128)S(1)}, u32[]{:S(2)}, u32[]{:S(2)}) %collective-permute-start.4) | collective-permute-done | bytes 2080 | tf_op jit(solution)/shard_map/ppermute | solution.py:490
  14.1 0.0 copy-start.6
  14.1 0.2 pack_far.1
  14.3 0.0 copy-start.1
  14.3 0.2 collective-permute-start.5
  14.5 1.6 %collective-permute-start.6 = (f32[560,128]{1,0:T(8,128)S(1)}, f32[560,128]{1,0:T(8,128)S(1)}, u32[]{:S(2)}, u32[]{:S(2)}) collective-permute-start(f32[560,128]{1,0:T(8,128)S(1)} %get-tuple-element.20), channel_id=1, source_target_pairs={{0,12},{4,0},{8,4},{12,8},{1,13},{5,1},{9,5},{13,9},{2,14},{6,2},{... | collective-permute-start | bytes 860168 | tf_op jit(solution)/shard_map/ppermute | solution.py:490
  16.1 1.5 %collective-permute-start.7 = (f32[16,128]{1,0:T(8,128)S(1)}, f32[16,128]{1,0:T(8,128)S(1)}, u32[]{:S(2)}, u32[]{:S(2)}) collective-permute-start(f32[16,128]{1,0:T(8,128)S(1)} %get-tuple-element.21.block_ref), channel_id=1, source_target_pairs={{0,8},{4,12},{8,0},{12,4},{1,9},{5,13},{9,1},{13,5},{2,10},{6,14},... | collective-permute-start | bytes 24584 | tf_op jit(solution)/shard_map/ppermute | solution.py:490
  17.6 1.1 %find_slots.1.slots_ref = s32[16,128]{1,0:T(8,128)S(1)} custom-call(s32[16,64]{1,0:T(8,128)S(1)} %copy-done.6, s32[49,128]{1,0:T(8,128)S(1)} %bitcast.8), custom_call_target="tpu_custom_call" | custom-call | tf_op jit(solution)/shard_map/find_slots/pallas_call | solution.py:529
  18.7 6.3 %collective-permute-done.7.refs_0_ = f32[16,128]{1,0:T(8,128)S(1)} collective-permute-done((f32[16,128]{1,0:T(8,128)S(1)}, f32[16,128]{1,0:T(8,128)S(1)}, u32[]{:S(2)}, u32[]{:S(2)}) %collective-permute-start.7) | collective-permute-done | bytes 8224 | tf_op jit(solution)/shard_map/ppermute | solution.py:490
  25.0 0.5 find_mobility.1.table_ref
  25.5 20.3 %evolve.1 = (f32[8,12,8,128]{3,2,1,0:T(8,128)}, f32[8,12,8,128]{3,2,1,0:T(8,128)}, f32[16,64]{1,0:T(8,128)S(1)}) custom-call(f32[8,12,8,128]{3,2,1,0:T(8,128)S(1)} %copy-done.1, f32[8,12,8,128]{3,2,1,0:T(8,128)S(1)} %copy-done.2, s32[12,8,128]{2,1,0:T(8,128)S(1)} %copy-done.4, f32[592,128]{1,0:T(8,128)S(1)} %collective-permute-done.above_ref, ...), custom_call_target="tpu_custom_call" | custom-call | tf_op jit(solution)/shard_map/evolve/pallas_call | solution.py:542
  45.8 9.7 %all_to_all.11 = f32[16,1,64]{2,1,0:T(1,128)S(1)} all-to-all(f32[16,1,64]{2,1,0:T(1,128)S(1)} %bitcast.9), channel_id=1, replica_groups=mesh['groups'=2,'wide'=4,'narrow'=4] {'wide','narrow'}, dimensions={0} | all-to-all | bytes 8192 | tf_op jit(solution)/shard_map/all_to_all | solution.py:558
  55.5 1.3 %pick_owned.1 = f32[1,392]{1,0:T(1,128)} custom-call(s32[16,128]{1,0:T(8,128)S(1)} %find_slots.1.slots_ref, f32[16,64]{1,0:T(8,128)S(1)} %bitcast.7), custom_call_target="tpu_custom_call" | custom-call | tf_op jit(solution)/shard_map/pick_owned/pallas_call | solution.py:559
  (16 shorter events, 0.0 us)
Async XLA Ops:
  0.6 1.0 %copy-start = (f32[8,12,8,128]{3,2,1,0:T(8,128)S(1)}, f32[8,12,8,128]{3,2,1,0:T(8,128)}, u32[]{:S(2)}) copy-start(f32[8,12,8,128]{3,2,1,0:T(8,128)} %order_ref.5) | copy-start | bytes 1179652
  1.6 1.0 %copy-start.2 = (f32[8,12,8,128]{3,2,1,0:T(8,128)S(1)}, f32[8,12,8,128]{3,2,1,0:T(8,128)}, u32[]{:S(2)}) copy-start(f32[8,12,8,128]{3,2,1,0:T(8,128)} %cot_ref.5) | copy-start | bytes 1179652
  1.7 0.9 %copy-start.7 = (f32[392]{0:T(512)S(1)}, f32[392]{0:T(512)}, u32[]{:S(2)}) copy-start(f32[392]{0:T(512)} %param.11) | copy-start | bytes 4708
  2.6 0.8 %copy-start.3 = (s32[12,8,128]{2,1,0:T(8,128)S(1)}, s32[12,8,128]{2,1,0:T(8,128)}, u32[]{:S(2)}) copy-start(s32[12,8,128]{2,1,0:T(8,128)} %map_ref.5) | copy-start | bytes 147460
  3.4 10.7 %copy-start.4 = (s32[12,8,128]{2,1,0:T(8,128)S(1)}, s32[12,8,128]{2,1,0:T(8,128)}, u32[]{:S(2)}) copy-start(s32[12,8,128]{2,1,0:T(8,128)} %map_ref.5) | copy-start | bytes 147460
  3.8 10.3 %collective-permute-start.2 = (f32[76,128]{1,0:T(8,128)S(1)}, f32[76,128]{1,0:T(8,128)S(1)}, u32[]{:S(2)}, u32[]{:S(2)}) collective-permute-start(f32[76,128]{1,0:T(8,128)S(1)} %get-tuple-element.16), channel_id=1, source_target_pairs={{0,1},{1,2},{2,3},{3,0},{4,5},{5,6},{6,7},{7,4},{8,9},{9,10},{10,1... | collective-permute-start | bytes 116744 | tf_op jit(solution)/shard_map/ppermute | solution.py:490
  6.9 7.2 %collective-permute-start.3 = (f32[76,128]{1,0:T(8,128)S(1)}, f32[76,128]{1,0:T(8,128)S(1)}, u32[]{:S(2)}, u32[]{:S(2)}) collective-permute-start(f32[76,128]{1,0:T(8,128)S(1)} %get-tuple-element.17), channel_id=1, source_target_pairs={{0,3},{1,0},{2,1},{3,2},{4,7},{5,4},{6,5},{7,6},{8,11},{9,8},{10,9... | collective-permute-start | bytes 116744 | tf_op jit(solution)/shard_map/ppermute | solution.py:490
  9.0 16.5 %collective-permute-start.1 = (f32[592,128]{1,0:T(8,128)S(1)}, f32[592,128]{1,0:T(8,128)S(1)}, u32[]{:S(2)}, u32[]{:S(2)}) collective-permute-start(f32[592,128]{1,0:T(8,128)S(1)} %get-tuple-element.15), channel_id=1, source_target_pairs={{0,12},{4,0},{8,4},{12,8},{1,13},{5,1},{9,5},{13,9},{2,14},{6,2},{... | collective-permute-start | bytes 909320 | tf_op jit(solution)/shard_map/ppermute | solution.py:490
  9.6 15.8 %collective-permute-start = (f32[592,128]{1,0:T(8,128)S(1)}, f32[592,128]{1,0:T(8,128)S(1)}, u32[]{:S(2)}, u32[]{:S(2)}) collective-permute-start(f32[592,128]{1,0:T(8,128)S(1)} %get-tuple-element.14.after_ref), channel_id=1, source_target_pairs={{0,4},{4,8},{8,12},{12,0},{1,5},{5,9},{9,13},{13,1},{2,6},{6,10},{... | collective-permute-start | bytes 909320 | tf_op jit(solution)/shard_map/ppermute | solution.py:490
  9.6 8.0 %copy-start.5 = (s32[6272]{0:T(1024)S(1)}, s32[6272]{0:T(1024)}, u32[]{:S(2)}) copy-start(s32[6272]{0:T(1024)} %param.10) | copy-start | bytes 75268
  9.6 4.5 %collective-permute-start.4 = (f32[4,128]{1,0:T(4,128)S(1)}, f32[4,128]{1,0:T(4,128)S(1)}, u32[]{:S(2)}, u32[]{:S(2)}) collective-permute-start(f32[4,128]{1,0:T(4,128)S(1)} %get-tuple-element.18.own_ref), channel_id=1, source_target_pairs={{0,2},{1,3},{2,0},{3,1},{4,6},{5,7},{6,4},{7,5},{8,10},{9,11},{10,... | collective-permute-start | bytes 6152 | tf_op jit(solution)/shard_map/ppermute | solution.py:490
  14.1 3.5 %copy-start.6 = (s32[16,64]{1,0:T(8,128)S(1)}, s32[16,64]{1,0:T(8,128)}, u32[]{:S(2)}) copy-start(s32[16,64]{1,0:T(8,128)} %bricks_ref.1) | copy-start | bytes 12292
  14.3 11.2 %copy-start.1 = (f32[8,12,8,128]{3,2,1,0:T(8,128)S(1)}, f32[8,12,8,128]{3,2,1,0:T(8,128)}, u32[]{:S(2)}) copy-start(f32[8,12,8,128]{3,2,1,0:T(8,128)} %order_ref.5) | copy-start | bytes 1179652
  14.3 10.7 %collective-permute-start.5 = (f32[560,128]{1,0:T(8,128)S(1)}, f32[560,128]{1,0:T(8,128)S(1)}, u32[]{:S(2)}, u32[]{:S(2)}) collective-permute-start(f32[560,128]{1,0:T(8,128)S(1)} %get-tuple-element.19), channel_id=1, source_target_pairs={{0,4},{4,8},{8,12},{12,0},{1,5},{5,9},{9,13},{13,1},{2,6},{6,10},{... | collective-permute-start | bytes 860168 | tf_op jit(solution)/shard_map/ppermute | solution.py:490
  14.5 10.5 %collective-permute-start.6 = (f32[560,128]{1,0:T(8,128)S(1)}, f32[560,128]{1,0:T(8,128)S(1)}, u32[]{:S(2)}, u32[]{:S(2)}) collective-permute-start(f32[560,128]{1,0:T(8,128)S(1)} %get-tuple-element.20), channel_id=1, source_target_pairs={{0,12},{4,0},{8,4},{12,8},{1,13},{5,1},{9,5},{13,9},{2,14},{6,2},{... | collective-permute-start | bytes 860168 | tf_op jit(solution)/shard_map/ppermute | solution.py:490
  16.1 8.9 %collective-permute-start.7 = (f32[16,128]{1,0:T(8,128)S(1)}, f32[16,128]{1,0:T(8,128)S(1)}, u32[]{:S(2)}, u32[]{:S(2)}) collective-permute-start(f32[16,128]{1,0:T(8,128)S(1)} %get-tuple-element.21.block_ref), channel_id=1, source_target_pairs={{0,8},{4,12},{8,0},{12,4},{1,9},{5,13},{9,1},{13,5},{2,10},{6,14},... | collective-permute-start | bytes 24584 | tf_op jit(solution)/shard_map/ppermute | solution.py:490

commit v4 on v3

v4 whole, which is shorter than its diff:
```python
import functools

import jax
import jax.numpy as jnp
from jax import lax
from jax.experimental import pallas as pl
from jax.experimental.pallas import tpu as pltpu
from jax.sharding import PartitionSpec as P

ITERS = 4
TIME_STEP = 0.05

EDGE = 6
MAP_EDGE = 5
ADJ_EDGE = 4
ROWS = 24
COLS = 10
LEAD = 8
CORNER = (5, 3, 4)

VMEM_LIMIT = 24 * 1024 * 1024


def lanes(shape):
    return lax.broadcasted_iota(jnp.int32, shape, len(shape) - 1)


def roll(value, shift):
    return pltpu.roll(value, shift, 1)


def pack(
    order_hbm, cot_hbm, map_hbm, mob_ref,
    down_ref, up_ref, right_ref, left_ref, own_ref, cot_down_ref, cot_up_ref,
    order_ref, cot_ref, map_ref, sems,
):
    copies = [
        pltpu.make_async_copy(source, target, sems.at[i])
        for i, (source, target) in enumerate(
            ((order_hbm, order_ref), (cot_hbm, cot_ref), (map_hbm, map_ref))
        )
    ]
    for copy in copies:
        copy.start()
    params, layers = order_ref.shape[:2]
    maps = row_places(params, layers)[0]
    gap = jnp.zeros((LEAD, 128), jnp.float32)
    for ref in (down_ref, up_ref):
        ref[0:LEAD, :] = gap
        ref[maps - LEAD : maps, :] = gap
        ref[ref.shape[0] - LEAD :, :] = gap
    for ref in (cot_down_ref, cot_up_ref):
        ref[0:LEAD, :] = gap
        ref[ref.shape[0] - LEAD :, :] = gap
    owned = mob_ref.shape[1]
    at = 8 * (params + 1)
    for i in range(own_ref.shape[0]):
        size = min(128, owned - 128 * i)
        row = mob_ref[0:1, 128 * i : 128 * i + size]
        if size < 128:
            row = jnp.concatenate([row, jnp.zeros((1, 128 - size), jnp.float32)], axis=1)
        for ref, k in ((own_ref, i), (right_ref, at + i), (left_ref, at + i)):
            ref[k : k + 1, :] = row

    copies[0].wait()
    for p in range(params):
        for z in range(layers):
            k = LEAD + (p * layers + z) * EDGE
            down_ref[k : k + EDGE, :] = order_ref[p, z, 8 - EDGE : 8, :]
            up_ref[k : k + EDGE, :] = order_ref[p, z, 0:EDGE, :]
    copies[2].wait()
    for z in range(layers):
        k = maps + z * MAP_EDGE
        cells = map_ref[z].astype(jnp.float32)
        down_ref[k : k + MAP_EDGE, :] = cells[8 - MAP_EDGE : 8]
        up_ref[k : k + MAP_EDGE, :] = cells[0:MAP_EDGE]
    copies[1].wait()
    for p in range(params):
        for z in range(layers):
            k = LEAD + (p * layers + z) * ADJ_EDGE
            cot_down_ref[k : k + ADJ_EDGE, :] = cot_ref[p, z, 8 - ADJ_EDGE : 8, :]
            cot_up_ref[k : k + ADJ_EDGE, :] = cot_ref[p, z, 0:ADJ_EDGE, :]

    lane = lanes((8, 128))
    zero = jnp.zeros((8, 128), jnp.float32)

    def span(first, size):
        return ((lane - first) & 127) < size

    for field in range(params + 1):
        right, left = zero, zero
        for z in range(layers):
            value = order_ref[field, z] if field < params else map_ref[z].astype(jnp.float32)
            moved = roll(value, 10 * z + 5)
            right = jnp.where(span(10 * z - 1, 6), moved, right)
            left = jnp.where(span(10 * z + 5, 6), moved, left)
            if field < params:
                right = jnp.where(span(10 * z + 5, 4), roll(cot_ref[field, z], 10 * z + 9), right)
                left = jnp.where(span(10 * z + 1, 4), roll(cot_ref[field, z], 10 * z + 1), left)
        right_ref[8 * field : 8 * field + 8, :] = right
        left_ref[8 * field : 8 * field + 8, :] = left


def row_places(params, layers):
    maps = LEAD + params * layers * EDGE + LEAD
    length = maps + layers * MAP_EDGE
    return maps, length + -length % 8 + LEAD


def corner_rows(params):
    return -(-(params * (CORNER[0] + CORNER[1]) + CORNER[2]) // 8) * 8


def merged_strips(params, left_ref, right_ref):
    first = lanes((8, 128)) % COLS < 5
    fields = []
    for field in range(params + 1):
        rows = slice(8 * field, 8 * field + 8)
        fields.append((left_ref[rows, :], right_ref[rows, :]))
    order = [jnp.where(first, a, b) for a, b in fields[:params]]
    cot = [jnp.where(first, roll(a, 124), roll(b, 4)) for a, b in fields[:params]]
    return order, cot, jnp.where(first, *fields[params])


def pack_far(params, left_ref, right_ref, own_ref, *refs):
    *other_refs, down_ref, up_ref, block_ref = refs
    rows = own_ref.shape[0]
    at = 8 * (params + 1)
    pieces = [own_ref[...], left_ref[at : at + rows, :]]
    pieces += [ref[...] for ref in other_refs]
    pieces.append(right_ref[at : at + rows, :])
    mobs = corner_rows(params)
    for i, piece in enumerate(pieces):
        for ref, k in ((block_ref, 0), (down_ref, mobs), (up_ref, mobs)):
            ref[k + i * rows : k + (i + 1) * rows, :] = piece
    at = 0
    order, cot, cells = merged_strips(params, left_ref, right_ref)
    for n, fields in zip(CORNER, (order, cot, [cells])):
        for both in fields:
            down_ref[at : at + n, :] = both[8 - n : 8]
            up_ref[at : at + n, :] = both[0:n]
            at += n
    for ref in (down_ref, up_ref):
        ref[at:mobs, :] = jnp.zeros((mobs - at, 128), jnp.float32)


def find_slots(bricks_ref, slot_ref, out_ref):
    count, listed = bricks_ref.shape
    rows = slot_ref.shape[0]
    pad = jnp.zeros((8, 128 - listed), jnp.int32)
    for k in range(0, count, 8):
        grain = jnp.concatenate([bricks_ref[k : k + 8, :], pad], axis=1)
        row, col = grain >> 7, grain & 127

        def body(r, found, row=row, col=col):
            table = jnp.broadcast_to(slot_ref[pl.ds(r, 1), :], (8, 128))
            taken = jnp.take_along_axis(table, col, axis=1, mode="promise_in_bounds")
            return jnp.where(row == r, taken, found)

        found = lax.fori_loop(0, rows, body, jnp.zeros((8, 128), jnp.int32), unroll=7)
        out_ref[k : k + 8, :] = jnp.where(lanes((8, 128)) < listed, found, -1)


def find_mobility(counts, owned, at, slots_ref, block_ref, above_ref, below_ref, *refs):
    *other_refs, table_ref, near_ref, mob_ref = refs
    wide_count, narrow_count = counts
    tile = (8, 128)
    wide, narrow = lax.axis_index("wide"), lax.axis_index("narrow")
    size = block_ref.shape[0]
    per_owner = size // narrow_count
    pieces = [block_ref[...], above_ref[at : at + size, :]]
    pieces += [ref[...] for ref in other_refs]
    pieces.append(below_ref[at : at + size, :])
    for i, piece in enumerate(pieces):
        mob_ref[i * size : (i + 1) * size, :] = piece
    for i in range(3):
        for j in range(3):
            w = lax.rem(wide + i - 1 + wide_count, wide_count)
            n = lax.rem(narrow + j - 1 + narrow_count, narrow_count)
            near_ref[3 * i + j : 3 * i + j + 1, :] = slots_ref[pl.ds(w * narrow_count + n, 1), :]
    near_ref[9:16, :] = jnp.zeros((7, 128), jnp.int32)
    slot = [jnp.maximum(near_ref[k : k + 8, :], 0) for k in (0, 8)]
    owner = [jnp.floor((x.astype(jnp.float32) + 0.5) * (1.0 / owned)).astype(jnp.int32) for x in slot]
    inner = [x - y * owned for x, y in zip(slot, owner)]
    by_wide = [jnp.floor((y.astype(jnp.float32) + 0.5) * (1.0 / narrow_count)).astype(jnp.int32) for y in owner]
    back_w = [wide - y for y in by_wide]
    back_n = [narrow - (x - y * narrow_count) for x, y in zip(owner, by_wide)]
    back_w = [jnp.where(x < 0, x + wide_count, x) for x in back_w]
    back_n = [jnp.where(x < 0, x + narrow_count, x) for x in back_n]
    row = [(a * narrow_count + b) * per_owner + (x >> 7) for a, b, x in zip(back_w, back_n, inner)]
    place = [x & 127 for x in inner]

    def body(r, found):
        values = jnp.broadcast_to(mob_ref[pl.ds(r, 1), :], tile)
        return tuple(
            jnp.where(row[k] == r, jnp.take_along_axis(values, place[k], axis=1, mode="promise_in_bounds"), found[k])
            for k in range(2)
        )

    zero = jnp.zeros(tile, jnp.float32)
    found = lax.fori_loop(0, mob_ref.shape[0], body, (zero, zero), unroll=16)
    for k in range(2):
        table_ref[8 * k : 8 * k + 8, :] = TIME_STEP * found[k]


def total_of(values):
    while len(values) > 1:
        values = [a + b for a, b in zip(values[::2], values[1::2])]
    return values[0]


def each_tile(layers, windows, body):
    start, count, most = windows
    group = 2 if count == 1 else 1

    def some(step, carry):
        stores = []
        for j in range(group):
            z = step * group + j
            for i in range(count):
                stores += body(z, i, jnp.minimum(start + 8 * i + ((z + 16) >> 5), most))
        for store in stores:
            store()
        return carry

    lax.fori_loop(0, layers // group, some, 0)


def each_window(windows, body):
    def one(i, carry):
        body(windows[0] + 8 * i)
        return carry

    lax.fori_loop(0, windows[1], one, 0)


def put(ref, index, value):
    def store():
        ref[index] = value

    return store


def neighbours(ref, ends_ref, values, z, r):
    params, layers = ref.shape[:2]
    lane = lanes((8, 128))
    rows, before, after = pl.ds(r, 8), pl.ds(r - 1, 8), pl.ds(r + 1, 8)
    below, above = jnp.maximum(z - 1, 0), jnp.minimum(z + 1, layers - 1)
    near = []
    for p in range(params):
        ends = ends_ref[p, z, rows, :]
        left = roll(jnp.where(lane == 127, ends, values[p]), 1)
        right = roll(jnp.where(lane == 0, ends, values[p]), 127)
        total = (left + right) + (ref[p, z, before, :] + ref[p, z, after, :])
        near.append(total + (ref[p, below, rows, :] + ref[p, above, rows, :]))
    return near


def strip_neighbours(ref, core_ref, values, r, outer_ref=None):
    params, layers = core_ref.shape[:2]
    lane = lanes((8, 128))
    col = lane % COLS
    rows, before, after = pl.ds(r, 8), pl.ds(r - 1, 8), pl.ds(r + 1, 8)
    near = []
    for p in range(params):
        value = values[p]
        ends = jnp.zeros((8, 128), jnp.float32)
        for z in range(layers):
            here = (lane == 10 * z + 4) | (lane == 10 * z + 5)
            ends = jnp.where(here, roll(core_ref[p, z, rows, :], 10 * z + 5), ends)
        left = roll(jnp.where(col == 4, ends, value), 1)
        right = roll(jnp.where(col == 5, ends, value), 127)
        if outer_ref is not None:
            outer = outer_ref[p, rows, :]
            left = jnp.where(col == 0, outer, left)
            right = jnp.where(col == 9, outer, right)
        below = jnp.where(lane < COLS, value, roll(value, COLS))
        above = jnp.where(lane >= COLS * (layers - 1), value, roll(value, 128 - COLS))
        total = (left + right) + (below + above)
        near.append(total + (ref[p, before, :] + ref[p, after, :]))
    return near


def spread_ends(ends_ref, values, rows):
    params, layers = ends_ref.shape[:2]
    for p in range(params):
        for z in range(layers):
            ends_ref[p, z, rows, :] = roll(values[p], 123 - 10 * z)


def rates(e, near):
    squares = [x * x for x in e]
    base = 1.5 * total_of(squares) + 5.0
    return [x * (base - 0.5 * y) - n for x, y, n in zip(e, squares, near)]


def changes(e, u, near):
    squares = [x * x for x in e]
    base = 1.5 * total_of(squares) + 5.0
    inner = 3.0 * total_of([x * y for x, y in zip(e, u)])
    return [y * (base - 1.5 * s) + x * inner - n for x, y, s, n in zip(e, u, squares, near)]


def forward(
    order_ref, map_ref, above_ref, below_ref, far_above_ref, far_below_ref, left_ref, right_ref, table_ref,
    final_ref, e_refs, rate_refs, se_refs, m_ref, ms_ref,
    first_strip_ref, outer_ref, ends_ref, g_ref, gs_ref,
):
    params, layers = order_ref.shape[:2]
    tile = (8, 128)
    col = lanes(tile) % COLS
    maps = row_places(params, layers)[0]
    strip_refs = [first_strip_ref, *se_refs]
    every = range(params)

    def place(z, carry):
        k = maps + z * MAP_EDGE
        g_ref[z, 0:8, :] = above_ref[pl.ds(k + MAP_EDGE - 8, 8), :]
        g_ref[z, 16:24, :] = below_ref[pl.ds(k, 8), :]
        for p in every:
            k = LEAD + (p * layers + z) * EDGE
            e_refs[0][p, z, 0:8, :] = above_ref[pl.ds(k + EDGE - 8, 8), :]
            e_refs[0][p, z, 8:16, :] = order_ref[p, z]
            e_refs[0][p, z, 16:24, :] = below_ref[pl.ds(k, 8), :]
        return carry

    lax.fori_loop(0, layers, place, 0)

    order, _, cells = merged_strips(params, left_ref, right_ref)
    n = CORNER[0]
    for p in every:
        ref = first_strip_ref.at[p]
        ref[0:8, :] = jnp.zeros(tile, jnp.float32)
        ref[16:24, :] = jnp.zeros(tile, jnp.float32)
        ref[8 - n : 8, :] = far_above_ref[n * p : n * p + n, :]
        ref[8:16, :] = order[p]
        ref[16 : 16 + n, :] = far_below_ref[n * p : n * p + n, :]
        a, b = left_ref[8 * p : 8 * p + 8, :], right_ref[8 * p : 8 * p + 8, :]
        outer_ref[p, 8:16, :] = jnp.where(col == 0, roll(a, 1), roll(b, 127))
    at, n = params * (CORNER[0] + CORNER[1]), CORNER[2]
    gs_ref[...] = jnp.zeros_like(gs_ref)
    gs_ref[8 - n : 8, :] = far_above_ref[at : at + n, :]
    gs_ref[8:16, :] = cells
    gs_ref[16 : 16 + n, :] = far_below_ref[at : at + n, :]
    for r in (0, 8, 16):
        rows = slice(r, r + 8)
        spread_ends(ends_ref, [first_strip_ref[p, rows, :] for p in every], rows)

    def lookup(index, which):
        values = jnp.broadcast_to(table_ref[which : which + 1, :], tile)
        return jnp.take_along_axis(values, index, axis=1, mode="promise_in_bounds")

    for i in range(3):
        r = 8 * i
        for z in range(layers):
            index = map_ref[z] if i == 1 else g_ref[z, r : r + 8, :].astype(jnp.int32) & 127
            m_ref[z, r : r + 8, :] = lookup(index, 3 * i + 1)
        index = gs_ref[r : r + 8, :].astype(jnp.int32) & 127
        ms_ref[r : r + 8, :] = jnp.where(col < 5, lookup(index, 3 * i), lookup(index, 3 * i + 2))

    def step(t, windows, strip_windows, end_windows):
        old, old_strip = e_refs[t], strip_refs[t]
        last = t == ITERS - 1

        def core(z, i, r):
            rows = pl.ds(r, 8)
            e = [old[p, z, rows, :] for p in every]
            m = m_ref[z, rows, :]
            rate = rates(e, neighbours(old, ends_ref, e, z, r))
            stores = []
            for p in every:
                new = e[p] - m * rate[p]
                stores.append(put(rate_refs[t], (p, z, rows, slice(None)), rate[p]))
                if last:
                    stores.append(put(final_ref, (p, z), new))
                else:
                    stores.append(put(e_refs[t + 1], (p, z, rows, slice(None)), new))
            return stores

        each_tile(layers, windows, core)
        if last:
            return

        def strip(r):
            rows = pl.ds(r, 8)
            e = [old_strip[p, rows, :] for p in every]
            m = ms_ref[rows, :]
            rate = rates(e, strip_neighbours(old_strip, old, e, r, outer_ref if t == 0 else None))
            for p in every:
                strip_refs[t + 1][p, rows, :] = e[p] - m * rate[p]

        each_window(strip_windows, strip)

        def ends(r):
            rows = pl.ds(r, 8)
            spread_ends(ends_ref, [strip_refs[t + 1][p, rows, :] for p in every], rows)

        each_window(end_windows, ends)

    step(0, (3, 3, 13), (4, 2), (4, 2))
    step(1, (4, 2, 12), (4, 2), (4, 2))
    step(2, (4, 2, 12), (4, 2), (8, 1))
    step(3, (8, 1, 8), None, None)


def backward(
    cot_ref, map_ref, above_ref, below_ref, far_above_ref, far_below_ref, left_ref, right_ref,
    e_refs, rate_refs, se_refs, m_ref, ms_ref,
    adjoint_ref, sums_ref,
    lam_refs, slam_refs, u_refs, su_refs, ends_ref, work_ref, binned_ref,
):
    params, layers = cot_ref.shape[:2]
    tile = (8, 128)
    every = range(params)

    def place(z, carry):
        m = [m_ref[z, 8 * i : 8 * i + 8, :] for i in range(3)]
        for p in every:
            k = LEAD + (p * layers + z) * ADJ_EDGE
            blocks = (above_ref[pl.ds(k + ADJ_EDGE - 8, 8), :], cot_ref[p, z], below_ref[pl.ds(k, 8), :])
            for i in range(3):
                lam_refs[0][p, z, 8 * i : 8 * i + 8, :] = blocks[i]
                u_refs[0][p, z, 8 * i : 8 * i + 8, :] = m[i] * blocks[i]
        return carry

    lax.fori_loop(0, layers, place, 0)
    _, cot, _ = merged_strips(params, left_ref, right_ref)
    n = CORNER[1]
    for p in every:
        at = params * CORNER[0] + n * p
        ref = slam_refs[0].at[p]
        ref[0:8, :] = jnp.zeros(tile, jnp.float32)
        ref[16:24, :] = jnp.zeros(tile, jnp.float32)
        ref[8 - n : 8, :] = far_above_ref[at : at + n, :]
        ref[8:16, :] = cot[p]
        ref[16 : 16 + n, :] = far_below_ref[at : at + n, :]
        for r in (0, 8, 16):
            su_refs[0][p, r : r + 8, :] = ms_ref[r : r + 8, :] * ref[r : r + 8, :]

    def spread(slot, windows):
        def ends(r):
            rows = pl.ds(r, 8)
            spread_ends(ends_ref, [su_refs[slot][p, rows, :] for p in every], rows)

        each_window(windows, ends)

    def step(t, slot, windows, strip_windows, end_windows):
        old, old_strip = u_refs[slot], su_refs[slot]
        last = t == 0

        def core(z, i, r):
            rows = pl.ds(r, 8)
            e = [e_refs[t][p, z, rows, :] for p in every]
            u = [old[p, z, rows, :] for p in every]
            m = m_ref[z, rows, :]
            change = changes(e, u, neighbours(old, ends_ref, u, z, r))
            lam = [lam_refs[slot][p, z, rows, :] for p in every]
            work = total_of([lam[p] * rate_refs[t][p, z, rows, :] for p in every])
            stores = [put(work_ref, (t, z, i), work)]
            for p in every:
                new = lam[p] - change[p]
                if last:
                    stores.append(put(adjoint_ref, (p, z), new))
                else:
                    stores.append(put(lam_refs[1 - slot], (p, z, rows, slice(None)), new))
                    stores.append(put(u_refs[1 - slot], (p, z, rows, slice(None)), m * new))
            return stores

        each_tile(layers, windows, core)
        if last:
            return

        def strip(r):
            rows = pl.ds(r, 8)
            e = [se_refs[t - 1][p, rows, :] for p in every]
            u = [old_strip[p, rows, :] for p in every]
            m = ms_ref[rows, :]
            change = changes(e, u, strip_neighbours(old_strip, old, u, r))
            for p in every:
                new = slam_refs[slot][p, rows, :] - change[p]
                slam_refs[1 - slot][p, rows, :] = new
                su_refs[1 - slot][p, rows, :] = m * new

        each_window(strip_windows, strip)
        spread(1 - slot, end_windows)

    spread(0, (4, 2))
    step(3, 0, (4, 2, 12), (4, 2), (4, 2))
    step(2, 1, (4, 2, 12), (4, 2), (4, 2))
    step(1, 0, (4, 2, 12), (8, 1), (8, 1))
    step(0, 1, (8, 1, 8), None, None)

    grains = [map_ref[z] for z in range(layers)]
    cells = []
    for z in range(layers):
        upper = work_ref[1, z, 0] + work_ref[2, z, 0] + work_ref[3, z, 0]
        lower = work_ref[1, z, 1] + work_ref[2, z, 1] + work_ref[3, z, 1]
        cells.append(jnp.concatenate([upper[4:8], lower[0:4]], axis=0) + work_ref[0, z, 0])

    def bin_one(g, carry):
        kept = [jnp.where(grains[z] == g, cells[z], 0.0) for z in range(layers)]
        total = sum(kept[1:4], kept[0]) + sum(kept[5:8], kept[4]) + sum(kept[9:], kept[8])
        binned_ref[pl.ds(g, 1), :] = jnp.sum(total, axis=0, keepdims=True)
        return carry

    lax.fori_loop(0, binned_ref.shape[0], bin_one, 0, unroll=4)
    ones = jnp.full((8, 128), -TIME_STEP, jnp.float32)
    sums = lax.dot_general(
        ones, binned_ref[...], (((1,), (1,)), ((), ())),
        precision=lax.Precision.HIGHEST, preferred_element_type=jnp.float32,
    )
    for k in range(0, sums_ref.shape[0], 8):
        sums_ref[k : k + 8, :] = sums


def pick_owned(counts, owned, slots_ref, sums_ref, out_ref, slot_rows, value_rows, total_ref):
    wide_count, narrow_count = counts
    count = wide_count * narrow_count
    wide, narrow = lax.axis_index("wide"), lax.axis_index("narrow")
    base = (wide * narrow_count + narrow) * owned
    listed = sums_ref.shape[1]
    tile = (8, 128)
    for k in range(count):
        slot = slots_ref[k : k + 1, :] - base
        slot_rows[k] = jnp.broadcast_to(slot, tile)
        value = jnp.concatenate([sums_ref[k : k + 1, :], jnp.zeros((1, 128 - listed), jnp.float32)], axis=1)
        value_rows[k] = jnp.broadcast_to(value, tile)
    sub = lax.broadcasted_iota(jnp.int32, tile, 0)
    blocks = total_ref.shape[0] // 8
    step = 16
    for first in range(0, blocks, step):
        some = range(first, min(first + step, blocks))

        def body(k, acc, some=some):
            slot, value = slot_rows[k], value_rows[k]
            shifted = slot - sub
            return tuple(a + jnp.where(shifted == 8 * j, value, 0.0) for a, j in zip(acc, some))

        acc = lax.fori_loop(0, count, body, tuple(jnp.zeros(tile, jnp.float32) for _ in some), unroll=4)
        for a, j in zip(acc, some):
            total_ref[8 * j : 8 * j + 8, :] = a
    whole = lax.dot_general(
        jnp.ones(tile, jnp.float32), total_ref[...], (((1,), (1,)), ((), ())),
        precision=lax.Precision.HIGHEST, preferred_element_type=jnp.float32,
    )
    out_ref[...] = whole[0:1, 0:owned]


def f32(*shape):
    return jax.ShapeDtypeStruct(shape, jnp.float32)


def kernel(body, out_shape, scratch=(), name=None, **specs):
    return pl.pallas_call(
        body, out_shape=out_shape, scratch_shapes=list(scratch), name=name, **specs,
        compiler_params=pltpu.CompilerParams(vmem_limit_bytes=VMEM_LIMIT),
    )


def shifted(value, axis, count, by):
    return lax.ppermute(value, axis, [(i, (i + by) % count) for i in range(count)])


def per_device(counts, order_init, cotangent, grain_map, brick_grains, grain_slot, mobility):
    wide_count, narrow_count = counts
    params, layers = order_init.shape[:2]
    assert order_init.shape[2:] == (8, 128) and layers * COLS < 128
    owned = mobility.shape[0]
    listed = brick_grains.shape[1]
    bricks = brick_grains.shape[0]

    both = ("wide", "narrow")
    count = wide_count * narrow_count

    owned_rows = -(-owned // 128)
    strip_rows = (params + 1) * 8 + owned_rows
    edge_rows = row_places(params, layers)[1]
    cot_rows = params * layers * ADJ_EDGE + 2 * LEAD
    away, here = pl.BlockSpec(memory_space=pltpu.HBM), pl.BlockSpec(memory_space=pltpu.VMEM)
    vmem = lambda *shape: pltpu.VMEM(shape, jnp.float32)
    down, up, to_right, to_left, own, cot_down, cot_up = kernel(
        pack,
        (f32(edge_rows, 128),) * 2 + (f32(strip_rows, 128),) * 2 + (f32(owned_rows, 128),)
        + (f32(cot_rows, 128),) * 2,
        (
            vmem(*order_init.shape), vmem(*cotangent.shape), pltpu.VMEM(grain_map.shape, jnp.int32),
            pltpu.SemaphoreType.DMA((3,)),
        ),
        name="pack", in_specs=[away, away, away, here],
    )(order_init, cotangent, grain_map, mobility.reshape(1, owned))
    above = shifted(down, "wide", wide_count, 1)
    below = shifted(up, "wide", wide_count, -1)
    from_left = shifted(to_right, "narrow", narrow_count, 1)
    from_right = shifted(to_left, "narrow", narrow_count, -1)
    others = [shifted(own, "narrow", narrow_count, d) for d in range(2, narrow_count - 1)]

    block_rows = narrow_count * owned_rows
    far_rows = corner_rows(params) + block_rows
    far_down, far_up, block = kernel(
        functools.partial(pack_far, params),
        (f32(far_rows, 128),) * 2 + (f32(block_rows, 128),), name="pack_far",
    )(from_left, from_right, own, *others)
    far_above = shifted(far_down, "wide", wide_count, 1)
    far_below = shifted(far_up, "wide", wide_count, -1)
    others = [shifted(block, "wide", wide_count, d) for d in range(2, wide_count - 1)]
    cot_above = shifted(cot_down, "wide", wide_count, 1)
    cot_below = shifted(cot_up, "wide", wide_count, -1)

    slots = kernel(
        find_slots, jax.ShapeDtypeStruct((bricks, 128), jnp.int32), name="find_slots"
    )(brick_grains, grain_slot.reshape(-1, 128))
    table = kernel(
        functools.partial(find_mobility, counts, owned, corner_rows(params)),
        f32(16, 128),
        (pltpu.VMEM((16, 128), jnp.int32), vmem(wide_count * block_rows, 128)),
        name="find_mobility",
    )(slots, block, far_above, far_below, *others)

    padded, strip = (params, layers, ROWS, 128), (params, ROWS, 128)
    final, states, rate, strips, m, ms = kernel(
        forward,
        (
            f32(*order_init.shape), [f32(*padded)] * ITERS, [f32(*padded)] * ITERS,
            [f32(*strip)] * (ITERS - 1), f32(layers, ROWS, 128), f32(ROWS, 128),
        ),
        (vmem(*strip), vmem(*strip), vmem(*padded), vmem(layers, ROWS, 128), vmem(ROWS, 128)),
        name="forward",
    )(order_init, grain_map, above, below, far_above, far_below, from_left, from_right, table)
    adjoint, sums = kernel(
        backward,
        (f32(*order_init.shape), f32(count, listed)),
        (
            [vmem(*padded)] * 2, [vmem(*strip)] * 2, [vmem(*padded)] * 2, [vmem(*strip)] * 2,
            vmem(*padded), vmem(ITERS, layers, 2, 8, 128), vmem(listed, 128),
        ),
        name="backward",
    )(
        cotangent, grain_map, cot_above, cot_below, far_above, far_below, from_left, from_right,
        states, rate, strips, m, ms,
    )

    every_sum = lax.all_to_all(sums, both, 0, 0, tiled=True)
    grads = kernel(
        functools.partial(pick_owned, counts, owned),
        f32(1, owned),
        (pltpu.VMEM((count, 8, 128), jnp.int32), vmem(count, 8, 128), vmem(owned + -owned % 8, 128)),
        name="pick_owned",
    )(slots, every_sum)
    return final, adjoint, grads.reshape(owned)


def solution(mesh):
    counts = (mesh.shape["wide"], mesh.shape["narrow"])
    field = P("groups", None, "wide", "narrow")
    spread = P(("groups", "wide", "narrow"))
    return jax.shard_map(
        functools.partial(per_device, counts),
        mesh=mesh,
        in_specs=(field, field, P("groups", "wide", "narrow"), P("groups", None), P("groups"), spread),
        out_specs=(field, field, spread),
        check_vma=False,
    )
```

time: 57.1 us -> 69.2 us (1.21)
  starting transfers between devices: 9.93 us -> 13.5 us
  local copies, waits for them, and re-layouts: 2.73 us -> 5.71 us
  waiting for transfers between devices: 9.96 us -> 12.7 us
  blocking collectives: 9.68 us -> 12.4 us
    ppermute x8 -> x10, starting transfers between devices: 9.93 us -> 13.5 us  [shifted(): lax.ppermute(value, axis, [(i, (i + by) % count) for i in range(count)])]
    unnamed x16 -> x18, local copies, waits for them, and re-layouts: 2.73 us -> 5.71 us
    ppermute x8 -> x10, waiting for transfers between devices: 9.96 us -> 12.7 us  [shifted(): lax.ppermute(value, axis, [(i, (i + by) % count) for i in range(count)])]
    all_to_all x1, blocking collectives: 9.68 us -> 12.4 us  [per_device(): every_sum = lax.all_to_all(sums, both, 0, 0, tiled=True)]
  transfers between devices with their start and end apart: 8 -> 10, of which waited for: 2 -> 5; matrix products, arithmetic and copies ran while one was open for 0% -> 0% of each run, Pallas kernels for 3% -> 16%
where the time goes in v4:
time: 69.2 us; the launch traced here: 68.7 us
  Pallas kernels  23.6 us (34%)
  starting transfers between devices  13.5 us (20%)
  waiting for transfers between devices  12.7 us (18%)
  blocking collectives  12.4 us (18%)
  local copies, waits for them, and re-layouts  5.71 us (8%)
  between operations  0.72 us (1%)
    ppermute x10, starting transfers between devices, shifted(): lax.ppermute(value, axis, [(i, (i + by) % count) for i in range(count)])  13.5 us
    ppermute x10, waiting for transfers between devices, shifted(): lax.ppermute(value, axis, [(i, (i + by) % count) for i in range(count)])  12.7 us
    all_to_all x1, blocking collectives, per_device(): every_sum = lax.all_to_all(sums, both, 0, 0, tiled=True)  12.4 us
    pallas_call x1, Pallas kernels, per_device(): kernel(backward, (f32(*order_init.shape), f32(count, listed)), ([vmem(*pa...  10.2 us
    pallas_call x1, Pallas kernels, per_device(): kernel(forward, (f32(*order_init.shape), [f32(*padded)] * ITERS, [f32(*pa...  9.41 us
    unnamed x18, local copies, waits for them, and re-layouts  5.71 us
  transfers between devices with their start and end apart: 10, of which 5 were waited for; matrix products, arithmetic and copies ran while one was open for 0% of the time, Pallas kernels for 16%

profile of v4, /device:TPU:0, one launch (start us, length us, event | category | flops | bytes accessed | tf_op | source)
XLA Modules:
  0.0 68.7 jit_solution(10914670380766788578)
XLA Ops:
  0.6 1.0 %copy-done = f32[8,12,8,128]{3,2,1,0:T(8,128)S(1)} copy-done((f32[8,12,8,128]{3,2,1,0:T(8,128)S(1)}, f32[8,12,8,128]{3,2,1,0:T(8,128)}, u32[]{:S(2)}) %copy-start) | copy-done | bytes 393240
  1.6 1.0 %copy-done.2 = f32[8,12,8,128]{3,2,1,0:T(8,128)S(1)} copy-done((f32[8,12,8,128]{3,2,1,0:T(8,128)S(1)}, f32[8,12,8,128]{3,2,1,0:T(8,128)}, u32[]{:S(2)}) %copy-start.2) | copy-done | bytes 393240
  2.6 0.8 %copy-done.4 = s32[12,8,128]{2,1,0:T(8,128)S(1)} copy-done((s32[12,8,128]{2,1,0:T(8,128)S(1)}, s32[12,8,128]{2,1,0:T(8,128)}, u32[]{:S(2)}) %copy-start.4) | copy-done | bytes 49176
  3.4 0.7 copy-done.8
  4.1 1.0 %pack.1 = (f32[664,128]{1,0:T(8,128)S(1)}, f32[664,128]{1,0:T(8,128)S(1)}, f32[76,128]{1,0:T(8,128)S(1)}, f32[76,128]{1,0:T(8,128)S(1)}, f32[4,128]{1,0:T(4,128)...) custom-call(f32[8,12,8,128]{3,2,1,0:T(8,128)S(1)} %copy-done.2, f32[8,12,8,128]{3,2,1,0:T(8,128)S(1)} %copy-done, ...), custom_call_target="tpu_custom_call" | custom-call | tf_op jit(solution)/shard_map/pack/pallas_call | solution.py:581
  5.6 2.0 %collective-permute-start.1 = (f32[664,128]{1,0:T(8,128)S(1)}, f32[664,128]{1,0:T(8,128)S(1)}, u32[]{:S(2)}, u32[]{:S(2)}) collective-permute-start(f32[664,128]{1,0:T(8,128)S(1)} %get-tuple-element.30), channel_id=1, source_target_pairs={{0,12},{4,0},{8,4},{12,8},{1,13},{5,1},{9,5},{13,9},{2,14},{6,2},{... | collective-permute-start | bytes 1019912 | tf_op jit(solution)/shard_map/ppermute | solution.py:561
  8.2 1.1 %collective-permute-start.9 = (f32[400,128]{1,0:T(8,128)S(1)}, f32[400,128]{1,0:T(8,128)S(1)}, u32[]{:S(2)}, u32[]{:S(2)}) collective-permute-start(f32[400,128]{1,0:T(8,128)S(1)} %get-tuple-element.39), channel_id=1, source_target_pairs={{0,12},{4,0},{8,4},{12,8},{1,13},{5,1},{9,5},{13,9},{2,14},{6,2},{... | collective-permute-start | bytes 614408 | tf_op jit(solution)/shard_map/ppermute | solution.py:561
  9.3 3.3 %collective-permute-start.4 = (f32[4,128]{1,0:T(4,128)S(1)}, f32[4,128]{1,0:T(4,128)S(1)}, u32[]{:S(2)}, u32[]{:S(2)}) collective-permute-start(f32[4,128]{1,0:T(4,128)S(1)} %get-tuple-element.33.own_ref), channel_id=1, source_target_pairs={{0,2},{1,3},{2,0},{3,1},{4,6},{5,7},{6,4},{7,5},{8,10},{9,11},{10,... | collective-permute-start | bytes 6152 | tf_op jit(solution)/shard_map/ppermute | solution.py:561
  12.7 1.6 %collective-permute-done.4.refs_0_ = f32[4,128]{1,0:T(4,128)S(1)} collective-permute-done((f32[4,128]{1,0:T(4,128)S(1)}, f32[4,128]{1,0:T(4,128)S(1)}, u32[]{:S(2)}, u32[]{:S(2)}) %collective-permute-start.4) | collective-permute-done | bytes 2080 | tf_op jit(solution)/shard_map/ppermute | solution.py:561
  14.3 1.9 %collective-permute-start.2 = (f32[76,128]{1,0:T(8,128)S(1)}, f32[76,128]{1,0:T(8,128)S(1)}, u32[]{:S(2)}, u32[]{:S(2)}) collective-permute-start(f32[76,128]{1,0:T(8,128)S(1)} %get-tuple-element.31), channel_id=1, source_target_pairs={{0,1},{1,2},{2,3},{3,0},{4,5},{5,6},{6,7},{7,4},{8,9},{9,10},{10,1... | collective-permute-start | bytes 116744 | tf_op jit(solution)/shard_map/ppermute | solution.py:561
  16.2 4.0 %collective-permute-done.2.left_ref = f32[76,128]{1,0:T(8,128)S(1)} collective-permute-done((f32[76,128]{1,0:T(8,128)S(1)}, f32[76,128]{1,0:T(8,128)S(1)}, u32[]{:S(2)}, u32[]{:S(2)}) %collective-permute-start.2) | collective-permute-done | bytes 38944 | tf_op jit(solution)/shard_map/ppermute | solution.py:561
  20.2 2.0 %collective-permute-start.3 = (f32[76,128]{1,0:T(8,128)S(1)}, f32[76,128]{1,0:T(8,128)S(1)}, u32[]{:S(2)}, u32[]{:S(2)}) collective-permute-start(f32[76,128]{1,0:T(8,128)S(1)} %get-tuple-element.32), channel_id=1, source_target_pairs={{0,3},{1,0},{2,1},{3,2},{4,7},{5,4},{6,5},{7,6},{8,11},{9,8},{10,9... | collective-permute-start | bytes 116744 | tf_op jit(solution)/shard_map/ppermute | solution.py:561
  22.2 2.0 %collective-permute-done.3.right_ref = f32[76,128]{1,0:T(8,128)S(1)} collective-permute-done((f32[76,128]{1,0:T(8,128)S(1)}, f32[76,128]{1,0:T(8,128)S(1)}, u32[]{:S(2)}, u32[]{:S(2)}) %collective-permute-start.3) | collective-permute-done | bytes 38944 | tf_op jit(solution)/shard_map/ppermute | solution.py:561
  24.3 2.0 %collective-permute-start.7 = (f32[16,128]{1,0:T(8,128)S(1)}, f32[16,128]{1,0:T(8,128)S(1)}, u32[]{:S(2)}, u32[]{:S(2)}) collective-permute-start(f32[16,128]{1,0:T(8,128)S(1)} %get-tuple-element.36.block_ref), channel_id=1, source_target_pairs={{0,8},{4,12},{8,0},{12,4},{1,9},{5,13},{9,1},{13,5},{2,10},{6,14},... | collective-permute-start | bytes 24584 | tf_op jit(solution)/shard_map/ppermute | solution.py:561
  26.3 1.7 %collective-permute-done.7.refs_0_ = f32[16,128]{1,0:T(8,128)S(1)} collective-permute-done((f32[16,128]{1,0:T(8,128)S(1)}, f32[16,128]{1,0:T(8,128)S(1)}, u32[]{:S(2)}, u32[]{:S(2)}) %collective-permute-start.7) | collective-permute-done | bytes 8224 | tf_op jit(solution)/shard_map/ppermute | solution.py:561
  28.0 3.5 %collective-permute-done.5.above_ref.far_above_ref = f32[88,128]{1,0:T(8,128)S(1)} collective-permute-done((f32[88,128]{1,0:T(8,128)S(1)}, f32[88,128]{1,0:T(8,128)S(1)}, u32[]{:S(2)}, u32[]{:S(2)}) %collective-permute-start.5) | collective-permute-done | bytes 45088 | tf_op jit(solution)/shard_map/ppermute | solution.py:561
  31.5 0.7 %copy-done.6 = s32[6272]{0:T(1024)S(1)} copy-done((s32[6272]{0:T(1024)S(1)}, s32[6272]{0:T(1024)}, u32[]{:S(2)}) %copy-start.6) | copy-done | bytes 25112
  32.2 0.7 %copy-done.7 = s32[16,64]{1,0:T(8,128)S(1)} copy-done((s32[16,64]{1,0:T(8,128)S(1)}, s32[16,64]{1,0:T(8,128)}, u32[]{:S(2)}) %copy-start.7) | copy-done | bytes 4120
  32.9 1.1 %find_slots.1.slots_ref = s32[16,128]{1,0:T(8,128)S(1)} custom-call(s32[16,64]{1,0:T(8,128)S(1)} %copy-done.7, s32[49,128]{1,0:T(8,128)S(1)} %bitcast.8), custom_call_target="tpu_custom_call" | custom-call | tf_op jit(solution)/shard_map/find_slots/pallas_call | solution.py:609
  34.5 0.8 %copy-done.5 = s32[12,8,128]{2,1,0:T(8,128)S(1)} copy-done((s32[12,8,128]{2,1,0:T(8,128)S(1)}, s32[12,8,128]{2,1,0:T(8,128)}, u32[]{:S(2)}) %copy-start.5) | copy-done | bytes 49176
  35.3 9.4 %forward.1 = (f32[8,12,8,128]{3,2,1,0:T(8,128)}, f32[8,12,24,128]{3,2,1,0:T(8,128)S(1)}, f32[8,12,24,128]{3,2,1,0:T(8,128)S(1)}, f32[8,12,24,128]{3,2,1,0:T(8,12...) custom-call(f32[8,12,8,128]{3,2,1,0:T(8,128)S(1)} %copy-done.3, ...), custom_call_target="tpu_custom_call" | custom-call | tf_op jit(solution)/shard_map/forward/pallas_call | solution.py:620
  44.8 10.2 %backward.1 = (f32[8,12,8,128]{3,2,1,0:T(8,128)}, f32[16,64]{1,0:T(8,128)S(1)}) custom-call(f32[8,12,8,128]{3,2,1,0:T(8,128)S(1)} %copy-done.1, s32[12,8,128]{2,1,0:T(8,128)S(1)} %copy-done.5, f32[400,128]{1,0:T(8,128)S(1)} %collective-permute-done.8.above_ref, f32[400,128]{1,0:T(8,128)S(1)} %collective-permute-done.9.below_ref, ...), custom_call_target="tpu_custom_call" | custom-call | tf_op jit(solution)/shard_map/backward/pallas_call | solution.py:629
  55.0 12.4 %all_to_all.11 = f32[16,1,64]{2,1,0:T(1,128)S(1)} all-to-all(f32[16,1,64]{2,1,0:T(1,128)S(1)} %bitcast.9), channel_id=1, replica_groups=mesh['groups'=2,'wide'=4,'narrow'=4] {'wide','narrow'}, dimensions={0} | all-to-all | bytes 8192 | tf_op jit(solution)/shard_map/all_to_all | solution.py:642
  67.4 1.3 %pick_owned.1 = f32[1,392]{1,0:T(1,128)} custom-call(s32[16,128]{1,0:T(8,128)S(1)} %find_slots.1.slots_ref, f32[16,64]{1,0:T(8,128)S(1)} %bitcast.7), custom_call_target="tpu_custom_call" | custom-call | tf_op jit(solution)/shard_map/pick_owned/pallas_call | solution.py:643
  (22 shorter events, 1.7 us)
Async XLA Ops:
  0.6 1.0 %copy-start = (f32[8,12,8,128]{3,2,1,0:T(8,128)S(1)}, f32[8,12,8,128]{3,2,1,0:T(8,128)}, u32[]{:S(2)}) copy-start(f32[8,12,8,128]{3,2,1,0:T(8,128)} %cot_ref.1) | copy-start | bytes 1179652
  1.6 1.0 %copy-start.2 = (f32[8,12,8,128]{3,2,1,0:T(8,128)S(1)}, f32[8,12,8,128]{3,2,1,0:T(8,128)}, u32[]{:S(2)}) copy-start(f32[8,12,8,128]{3,2,1,0:T(8,128)} %order_ref.1) | copy-start | bytes 1179652
  2.6 0.8 %copy-start.4 = (s32[12,8,128]{2,1,0:T(8,128)S(1)}, s32[12,8,128]{2,1,0:T(8,128)}, u32[]{:S(2)}) copy-start(s32[12,8,128]{2,1,0:T(8,128)} %map_ref.3) | copy-start | bytes 147460
  3.4 0.7 copy-start.8
  4.1 30.4 %copy-start.3 = (f32[8,12,8,128]{3,2,1,0:T(8,128)S(1)}, f32[8,12,8,128]{3,2,1,0:T(8,128)}, u32[]{:S(2)}) copy-start(f32[8,12,8,128]{3,2,1,0:T(8,128)} %order_ref.1) | copy-start | bytes 1179652
  4.1 40.6 %copy-start.1 = (f32[8,12,8,128]{3,2,1,0:T(8,128)S(1)}, f32[8,12,8,128]{3,2,1,0:T(8,128)}, u32[]{:S(2)}) copy-start(f32[8,12,8,128]{3,2,1,0:T(8,128)} %cot_ref.1) | copy-start | bytes 1179652
  5.1 29.4 %collective-permute-start = (f32[664,128]{1,0:T(8,128)S(1)}, f32[664,128]{1,0:T(8,128)S(1)}, u32[]{:S(2)}, u32[]{:S(2)}) collective-permute-start(f32[664,128]{1,0:T(8,128)S(1)} %get-tuple-element.29), channel_id=1, source_target_pairs={{0,4},{4,8},{8,12},{12,0},{1,5},{5,9},{9,13},{13,1},{2,6},{6,10},{... | collective-permute-start | bytes 1019912 | tf_op jit(solution)/shard_map/ppermute | solution.py:561
  5.6 28.9 %collective-permute-start.1 = (f32[664,128]{1,0:T(8,128)S(1)}, f32[664,128]{1,0:T(8,128)S(1)}, u32[]{:S(2)}, u32[]{:S(2)}) collective-permute-start(f32[664,128]{1,0:T(8,128)S(1)} %get-tuple-element.30), channel_id=1, source_target_pairs={{0,12},{4,0},{8,4},{12,8},{1,13},{5,1},{9,5},{13,9},{2,14},{6,2},{... | collective-permute-start | bytes 1019912 | tf_op jit(solution)/shard_map/ppermute | solution.py:561
  7.6 37.1 %collective-permute-start.8 = (f32[400,128]{1,0:T(8,128)S(1)}, f32[400,128]{1,0:T(8,128)S(1)}, u32[]{:S(2)}, u32[]{:S(2)}) collective-permute-start(f32[400,128]{1,0:T(8,128)S(1)} %get-tuple-element.38), channel_id=1, source_target_pairs={{0,4},{4,8},{8,12},{12,0},{1,5},{5,9},{9,13},{13,1},{2,6},{6,10},{... | collective-permute-start | bytes 614408 | tf_op jit(solution)/shard_map/ppermute | solution.py:561
  8.2 36.5 %collective-permute-start.9 = (f32[400,128]{1,0:T(8,128)S(1)}, f32[400,128]{1,0:T(8,128)S(1)}, u32[]{:S(2)}, u32[]{:S(2)}) collective-permute-start(f32[400,128]{1,0:T(8,128)S(1)} %get-tuple-element.39), channel_id=1, source_target_pairs={{0,12},{4,0},{8,4},{12,8},{1,13},{5,1},{9,5},{13,9},{2,14},{6,2},{... | collective-permute-start | bytes 614408 | tf_op jit(solution)/shard_map/ppermute | solution.py:561
  9.3 4.9 %collective-permute-start.4 = (f32[4,128]{1,0:T(4,128)S(1)}, f32[4,128]{1,0:T(4,128)S(1)}, u32[]{:S(2)}, u32[]{:S(2)}) collective-permute-start(f32[4,128]{1,0:T(4,128)S(1)} %get-tuple-element.33.own_ref), channel_id=1, source_target_pairs={{0,2},{1,3},{2,0},{3,1},{4,6},{5,7},{6,4},{7,5},{8,10},{9,11},{10,... | collective-permute-start | bytes 6152 | tf_op jit(solution)/shard_map/ppermute | solution.py:561
  14.3 5.9 %collective-permute-start.2 = (f32[76,128]{1,0:T(8,128)S(1)}, f32[76,128]{1,0:T(8,128)S(1)}, u32[]{:S(2)}, u32[]{:S(2)}) collective-permute-start(f32[76,128]{1,0:T(8,128)S(1)} %get-tuple-element.31), channel_id=1, source_target_pairs={{0,1},{1,2},{2,3},{3,0},{4,5},{5,6},{6,7},{7,4},{8,9},{9,10},{10,1... | collective-permute-start | bytes 116744 | tf_op jit(solution)/shard_map/ppermute | solution.py:561
  20.2 4.0 %collective-permute-start.3 = (f32[76,128]{1,0:T(8,128)S(1)}, f32[76,128]{1,0:T(8,128)S(1)}, u32[]{:S(2)}, u32[]{:S(2)}) collective-permute-start(f32[76,128]{1,0:T(8,128)S(1)} %get-tuple-element.32), channel_id=1, source_target_pairs={{0,3},{1,0},{2,1},{3,2},{4,7},{5,4},{6,5},{7,6},{8,11},{9,8},{10,9... | collective-permute-start | bytes 116744 | tf_op jit(solution)/shard_map/ppermute | solution.py:561
  24.3 3.7 %collective-permute-start.7 = (f32[16,128]{1,0:T(8,128)S(1)}, f32[16,128]{1,0:T(8,128)S(1)}, u32[]{:S(2)}, u32[]{:S(2)}) collective-permute-start(f32[16,128]{1,0:T(8,128)S(1)} %get-tuple-element.36.block_ref), channel_id=1, source_target_pairs={{0,8},{4,12},{8,0},{12,4},{1,9},{5,13},{9,1},{13,5},{2,10},{6,14},... | collective-permute-start | bytes 24584 | tf_op jit(solution)/shard_map/ppermute | solution.py:561
  28.0 3.5 %collective-permute-start.5 = (f32[88,128]{1,0:T(8,128)S(1)}, f32[88,128]{1,0:T(8,128)S(1)}, u32[]{:S(2)}, u32[]{:S(2)}) collective-permute-start(f32[88,128]{1,0:T(8,128)S(1)} %get-tuple-element.34), channel_id=1, source_target_pairs={{0,4},{4,8},{8,12},{12,0},{1,5},{5,9},{9,13},{13,1},{2,6},{6,10},{... | collective-permute-start | bytes 135176 | tf_op jit(solution)/shard_map/ppermute | solution.py:561
  31.5 2.6 %collective-permute-start.6 = (f32[88,128]{1,0:T(8,128)S(1)}, f32[88,128]{1,0:T(8,128)S(1)}, u32[]{:S(2)}, u32[]{:S(2)}) collective-permute-start(f32[88,128]{1,0:T(8,128)S(1)} %get-tuple-element.35), channel_id=1, source_target_pairs={{0,12},{4,0},{8,4},{12,8},{1,13},{5,1},{9,5},{13,9},{2,14},{6,2},{... | collective-permute-start | bytes 135176 | tf_op jit(solution)/shard_map/ppermute | solution.py:561
  31.5 0.7 %copy-start.6 = (s32[6272]{0:T(1024)S(1)}, s32[6272]{0:T(1024)}, u32[]{:S(2)}) copy-start(s32[6272]{0:T(1024)} %param.10) | copy-start | bytes 75268
  32.2 0.7 %copy-start.7 = (s32[16,64]{1,0:T(8,128)S(1)}, s32[16,64]{1,0:T(8,128)}, u32[]{:S(2)}) copy-start(s32[16,64]{1,0:T(8,128)} %bricks_ref.1) | copy-start | bytes 12292
  34.5 0.8 %copy-start.5 = (s32[12,8,128]{2,1,0:T(8,128)S(1)}, s32[12,8,128]{2,1,0:T(8,128)}, u32[]{:S(2)}) copy-start(s32[12,8,128]{2,1,0:T(8,128)} %map_ref.3) | copy-start | bytes 147460

commit v5 on v4

--- a/solution.py
+++ b/solution.py
@@ -29,57 +29,57 @@
     return pltpu.roll(value, shift, 1)
 
 
-def pack(
-    order_hbm, cot_hbm, map_hbm, mob_ref,
-    down_ref, up_ref, right_ref, left_ref, own_ref, cot_down_ref, cot_up_ref,
-    order_ref, cot_ref, map_ref, sems,
-):
-    copies = [
-        pltpu.make_async_copy(source, target, sems.at[i])
-        for i, (source, target) in enumerate(
-            ((order_hbm, order_ref), (cot_hbm, cot_ref), (map_hbm, map_ref))
-        )
-    ]
+def pack_rows(*refs):
+    count = (len(refs) - 3) // 2
+    sources, targets = refs[:count], refs[count : 2 * count]
+    down_ref, up_ref, sems = refs[2 * count :]
+    copies = [pltpu.make_async_copy(a, b, sems.at[i]) for i, (a, b) in enumerate(zip(sources, targets))]
     for copy in copies:
         copy.start()
+    order_ref, map_ref = targets[:2]
     params, layers = order_ref.shape[:2]
     maps = row_places(params, layers)[0]
     gap = jnp.zeros((LEAD, 128), jnp.float32)
     for ref in (down_ref, up_ref):
         ref[0:LEAD, :] = gap
         ref[maps - LEAD : maps, :] = gap
+        ref[ref.shape[0] - 2 * LEAD : ref.shape[0] - LEAD, :] = gap
         ref[ref.shape[0] - LEAD :, :] = gap
-    for ref in (cot_down_ref, cot_up_ref):
-        ref[0:LEAD, :] = gap
-        ref[ref.shape[0] - LEAD :, :] = gap
-    owned = mob_ref.shape[1]
-    at = 8 * (params + 1)
-    for i in range(own_ref.shape[0]):
-        size = min(128, owned - 128 * i)
-        row = mob_ref[0:1, 128 * i : 128 * i + size]
-        if size < 128:
-            row = jnp.concatenate([row, jnp.zeros((1, 128 - size), jnp.float32)], axis=1)
-        for ref, k in ((own_ref, i), (right_ref, at + i), (left_ref, at + i)):
-            ref[k : k + 1, :] = row
-
     copies[0].wait()
     for p in range(params):
         for z in range(layers):
             k = LEAD + (p * layers + z) * EDGE
             down_ref[k : k + EDGE, :] = order_ref[p, z, 8 - EDGE : 8, :]
             up_ref[k : k + EDGE, :] = order_ref[p, z, 0:EDGE, :]
-    copies[2].wait()
+    copies[1].wait()
     for z in range(layers):
         k = maps + z * MAP_EDGE
         cells = map_ref[z].astype(jnp.float32)
         down_ref[k : k + MAP_EDGE, :] = cells[8 - MAP_EDGE : 8]
         up_ref[k : k + MAP_EDGE, :] = cells[0:MAP_EDGE]
-    copies[1].wait()
-    for p in range(params):
-        for z in range(layers):
-            k = LEAD + (p * layers + z) * ADJ_EDGE
-            cot_down_ref[k : k + ADJ_EDGE, :] = cot_ref[p, z, 8 - ADJ_EDGE : 8, :]
-            cot_up_ref[k : k + ADJ_EDGE, :] = cot_ref[p, z, 0:ADJ_EDGE, :]
+    for copy in copies[2:]:
+        copy.wait()
+
+
+def around(axis, count):
+    place = lax.axis_index(axis)
+    return lax.rem(place + count - 1, count), lax.rem(place + 1, count)
+
+
+def pack_strips(order_ref, cot_ref, map_ref, mob_ref, after_ref, out_ref):
+    params, layers = order_ref.shape[:2]
+    count = out_ref.shape[0]
+    before, after = around("narrow", count)
+    owned = mob_ref.shape[1]
+    at = 8 * (params + 1)
+    out_ref[...] = jnp.zeros_like(out_ref)
+    for i in range(-(-owned // 128)):
+        size = min(128, owned - 128 * i)
+        row = mob_ref[0:1, 128 * i : 128 * i + size]
+        if size < 128:
+            row = jnp.concatenate([row, jnp.zeros((1, 128 - size), jnp.float32)], axis=1)
+        for j in range(count):
+            out_ref[j, at + i : at + i + 1, :] = row
 
     lane = lanes((8, 128))
     zero = jnp.zeros((8, 128), jnp.float32)
@@ -97,8 +97,8 @@
             if field < params:
                 right = jnp.where(span(10 * z + 5, 4), roll(cot_ref[field, z], 10 * z + 9), right)
                 left = jnp.where(span(10 * z + 1, 4), roll(cot_ref[field, z], 10 * z + 1), left)
-        right_ref[8 * field : 8 * field + 8, :] = right
-        left_ref[8 * field : 8 * field + 8, :] = left
+        out_ref[after, 8 * field : 8 * field + 8, :] = right
+        out_ref[before, 8 * field : 8 * field + 8, :] = left
 
 
 def row_places(params, layers):
@@ -111,37 +111,37 @@
     return -(-(params * (CORNER[0] + CORNER[1]) + CORNER[2]) // 8) * 8
 
 
-def merged_strips(params, left_ref, right_ref):
+def side_strips(params, strips_ref):
+    before, after = around("narrow", strips_ref.shape[0])
+    rows = [slice(8 * field, 8 * field + 8) for field in range(params + 1)]
+    return [(strips_ref[before, r, :], strips_ref[after, r, :]) for r in rows]
+
+
+def merged_strips(params, strips_ref):
     first = lanes((8, 128)) % COLS < 5
-    fields = []
-    for field in range(params + 1):
-        rows = slice(8 * field, 8 * field + 8)
-        fields.append((left_ref[rows, :], right_ref[rows, :]))
+    fields = side_strips(params, strips_ref)
     order = [jnp.where(first, a, b) for a, b in fields[:params]]
     cot = [jnp.where(first, roll(a, 124), roll(b, 4)) for a, b in fields[:params]]
     return order, cot, jnp.where(first, *fields[params])
 
 
-def pack_far(params, left_ref, right_ref, own_ref, *refs):
-    *other_refs, down_ref, up_ref, block_ref = refs
-    rows = own_ref.shape[0]
+def pack_far(params, owned_rows, strips_ref, slots_ref, out_ref):
+    count = out_ref.shape[0]
+    before, after = around("wide", count)
+    mobs = corner_rows(params)
+    out_ref[...] = jnp.zeros_like(out_ref)
     at = 8 * (params + 1)
-    pieces = [own_ref[...], left_ref[at : at + rows, :]]
-    pieces += [ref[...] for ref in other_refs]
-    pieces.append(right_ref[at : at + rows, :])
-    mobs = corner_rows(params)
-    for i, piece in enumerate(pieces):
-        for ref, k in ((block_ref, 0), (down_ref, mobs), (up_ref, mobs)):
-            ref[k + i * rows : k + (i + 1) * rows, :] = piece
+    for i in range(strips_ref.shape[0]):
+        piece = strips_ref[i, at : at + owned_rows, :]
+        for j in range(count):
+            out_ref[j, mobs + i * owned_rows : mobs + (i + 1) * owned_rows, :] = piece
     at = 0
-    order, cot, cells = merged_strips(params, left_ref, right_ref)
+    order, cot, cells = merged_strips(params, strips_ref)
     for n, fields in zip(CORNER, (order, cot, [cells])):
         for both in fields:
-            down_ref[at : at + n, :] = both[8 - n : 8]
-            up_ref[at : at + n, :] = both[0:n]
+            out_ref[after, at : at + n, :] = both[8 - n : 8]
+            out_ref[before, at : at + n, :] = both[0:n]
             at += n
-    for ref in (down_ref, up_ref):
-        ref[at:mobs, :] = jnp.zeros((mobs - at, 128), jnp.float32)
 
 
 def find_slots(bricks_ref, slot_ref, out_ref):
@@ -161,18 +161,25 @@
         out_ref[k : k + 8, :] = jnp.where(lanes((8, 128)) < listed, found, -1)
 
 
-def find_mobility(counts, owned, at, slots_ref, block_ref, above_ref, below_ref, *refs):
-    *other_refs, table_ref, near_ref, mob_ref = refs
+def find_mobility(
+    counts, owned, owned_rows, slots_ref, far_ref, cot_ref, table_ref, cot_down_ref, cot_up_ref, near_ref, mob_ref
+):
+    params, layers = cot_ref.shape[:2]
+    for ref in (cot_down_ref, cot_up_ref):
+        ref[0:LEAD, :] = jnp.zeros((LEAD, 128), jnp.float32)
+        ref[ref.shape[0] - LEAD :, :] = jnp.zeros((LEAD, 128), jnp.float32)
+    for p in range(params):
+        for z in range(layers):
+            k = LEAD + (p * layers + z) * ADJ_EDGE
+            cot_down_ref[k : k + ADJ_EDGE, :] = cot_ref[p, z, 8 - ADJ_EDGE : 8, :]
+            cot_up_ref[k : k + ADJ_EDGE, :] = cot_ref[p, z, 0:ADJ_EDGE, :]
+
     wide_count, narrow_count = counts
     tile = (8, 128)
     wide, narrow = lax.axis_index("wide"), lax.axis_index("narrow")
-    size = block_ref.shape[0]
-    per_owner = size // narrow_count
-    pieces = [block_ref[...], above_ref[at : at + size, :]]
-    pieces += [ref[...] for ref in other_refs]
-    pieces.append(below_ref[at : at + size, :])
-    for i, piece in enumerate(pieces):
-        mob_ref[i * size : (i + 1) * size, :] = piece
+    size, at = narrow_count * owned_rows, corner_rows(params)
+    for i in range(wide_count):
+        mob_ref[i * size : (i + 1) * size, :] = far_ref[i, at : at + size, :]
     for i in range(3):
         for j in range(3):
             w = lax.rem(wide + i - 1 + wide_count, wide_count)
@@ -182,12 +189,7 @@
     slot = [jnp.maximum(near_ref[k : k + 8, :], 0) for k in (0, 8)]
     owner = [jnp.floor((x.astype(jnp.float32) + 0.5) * (1.0 / owned)).astype(jnp.int32) for x in slot]
     inner = [x - y * owned for x, y in zip(slot, owner)]
-    by_wide = [jnp.floor((y.astype(jnp.float32) + 0.5) * (1.0 / narrow_count)).astype(jnp.int32) for y in owner]
-    back_w = [wide - y for y in by_wide]
-    back_n = [narrow - (x - y * narrow_count) for x, y in zip(owner, by_wide)]
-    back_w = [jnp.where(x < 0, x + wide_count, x) for x in back_w]
-    back_n = [jnp.where(x < 0, x + narrow_count, x) for x in back_n]
-    row = [(a * narrow_count + b) * per_owner + (x >> 7) for a, b, x in zip(back_w, back_n, inner)]
+    row = [y * owned_rows + (x >> 7) for x, y in zip(inner, owner)]
     place = [x & 127 for x in inner]
 
     def body(r, found):
@@ -211,7 +213,7 @@
 
 def each_tile(layers, windows, body):
     start, count, most = windows
-    group = 2 if count == 1 else 1
+    group = 4 // count if count < 3 else 1
 
     def some(step, carry):
         stores = []
@@ -302,7 +304,7 @@
 
 
 def forward(
-    order_ref, map_ref, above_ref, below_ref, far_above_ref, far_below_ref, left_ref, right_ref, table_ref,
+    order_ref, map_ref, above_ref, below_ref, far_ref, strips_ref, table_ref,
     final_ref, e_refs, rate_refs, se_refs, m_ref, ms_ref,
     first_strip_ref, outer_ref, ends_ref, g_ref, gs_ref,
 ):
@@ -326,22 +328,23 @@
 
     lax.fori_loop(0, layers, place, 0)
 
-    order, _, cells = merged_strips(params, left_ref, right_ref)
+    far_above, far_below = around("wide", far_ref.shape[0])
+    sides = side_strips(params, strips_ref)
+    order, _, cells = merged_strips(params, strips_ref)
     n = CORNER[0]
     for p in every:
         ref = first_strip_ref.at[p]
         ref[0:8, :] = jnp.zeros(tile, jnp.float32)
         ref[16:24, :] = jnp.zeros(tile, jnp.float32)
-        ref[8 - n : 8, :] = far_above_ref[n * p : n * p + n, :]
+        ref[8 - n : 8, :] = far_ref[far_above, n * p : n * p + n, :]
         ref[8:16, :] = order[p]
-        ref[16 : 16 + n, :] = far_below_ref[n * p : n * p + n, :]
-        a, b = left_ref[8 * p : 8 * p + 8, :], right_ref[8 * p : 8 * p + 8, :]
-        outer_ref[p, 8:16, :] = jnp.where(col == 0, roll(a, 1), roll(b, 127))
+        ref[16 : 16 + n, :] = far_ref[far_below, n * p : n * p + n, :]
+        outer_ref[p, 8:16, :] = jnp.where(col == 0, roll(sides[p][0], 1), roll(sides[p][1], 127))
     at, n = params * (CORNER[0] + CORNER[1]), CORNER[2]
     gs_ref[...] = jnp.zeros_like(gs_ref)
-    gs_ref[8 - n : 8, :] = far_above_ref[at : at + n, :]
+    gs_ref[8 - n : 8, :] = far_ref[far_above, at : at + n, :]
     gs_ref[8:16, :] = cells
-    gs_ref[16 : 16 + n, :] = far_below_ref[at : at + n, :]
+    gs_ref[16 : 16 + n, :] = far_ref[far_below, at : at + n, :]
     for r in (0, 8, 16):
         rows = slice(r, r + 8)
         spread_ends(ends_ref, [first_strip_ref[p, rows, :] for p in every], rows)
@@ -404,7 +407,7 @@
 
 
 def backward(
-    cot_ref, map_ref, above_ref, below_ref, far_above_ref, far_below_ref, left_ref, right_ref,
+    cot_ref, map_ref, above_ref, below_ref, far_ref, strips_ref,
     e_refs, rate_refs, se_refs, m_ref, ms_ref,
     adjoint_ref, sums_ref,
     lam_refs, slam_refs, u_refs, su_refs, ends_ref, work_ref, binned_ref,
@@ -424,16 +427,17 @@
         return carry
 
     lax.fori_loop(0, layers, place, 0)
-    _, cot, _ = merged_strips(params, left_ref, right_ref)
+    far_above, far_below = around("wide", far_ref.shape[0])
+    _, cot, _ = merged_strips(params, strips_ref)
     n = CORNER[1]
     for p in every:
         at = params * CORNER[0] + n * p
         ref = slam_refs[0].at[p]
         ref[0:8, :] = jnp.zeros(tile, jnp.float32)
         ref[16:24, :] = jnp.zeros(tile, jnp.float32)
-        ref[8 - n : 8, :] = far_above_ref[at : at + n, :]
+        ref[8 - n : 8, :] = far_ref[far_above, at : at + n, :]
         ref[8:16, :] = cot[p]
-        ref[16 : 16 + n, :] = far_below_ref[at : at + n, :]
+        ref[16 : 16 + n, :] = far_ref[far_below, at : at + n, :]
         for r in (0, 8, 16):
             su_refs[0][p, r : r + 8, :] = ms_ref[r : r + 8, :] * ref[r : r + 8, :]
 
@@ -573,51 +577,53 @@
     count = wide_count * narrow_count
 
     owned_rows = -(-owned // 128)
-    strip_rows = (params + 1) * 8 + owned_rows
+    strip_rows = 8 * (params + 1) + owned_rows
+    strip_rows += -strip_rows % 8
     edge_rows = row_places(params, layers)[1]
     cot_rows = params * layers * ADJ_EDGE + 2 * LEAD
-    away, here = pl.BlockSpec(memory_space=pltpu.HBM), pl.BlockSpec(memory_space=pltpu.VMEM)
+    anywhere, here = pl.BlockSpec(memory_space=pl.ANY), pl.BlockSpec(memory_space=pltpu.VMEM)
     vmem = lambda *shape: pltpu.VMEM(shape, jnp.float32)
-    down, up, to_right, to_left, own, cot_down, cot_up = kernel(
-        pack,
-        (f32(edge_rows, 128),) * 2 + (f32(strip_rows, 128),) * 2 + (f32(owned_rows, 128),)
-        + (f32(cot_rows, 128),) * 2,
-        (
-            vmem(*order_init.shape), vmem(*cotangent.shape), pltpu.VMEM(grain_map.shape, jnp.int32),
-            pltpu.SemaphoreType.DMA((3,)),
-        ),
-        name="pack", in_specs=[away, away, away, here],
-    )(order_init, cotangent, grain_map, mobility.reshape(1, owned))
+
+    arguments = (
+        order_init, grain_map, cotangent, mobility.reshape(1, owned), brick_grains, grain_slot.reshape(-1, 128)
+    )
+    *fetched, down, up = kernel(
+        pack_rows,
+        tuple(jax.ShapeDtypeStruct(x.shape, x.dtype) for x in arguments) + (f32(edge_rows, 128),) * 2,
+        (pltpu.SemaphoreType.DMA((len(arguments),)),), name="pack_rows",
+        in_specs=[pl.BlockSpec(memory_space=pltpu.HBM)] * len(arguments),
+    )(*(pltpu.with_memory_space_constraint(x, pltpu.HBM) for x in arguments))
+    order_init, grain_map, cotangent, mobility, brick_grains, grain_slot = fetched
     above = shifted(down, "wide", wide_count, 1)
     below = shifted(up, "wide", wide_count, -1)
-    from_left = shifted(to_right, "narrow", narrow_count, 1)
-    from_right = shifted(to_left, "narrow", narrow_count, -1)
-    others = [shifted(own, "narrow", narrow_count, d) for d in range(2, narrow_count - 1)]
-
-    block_rows = narrow_count * owned_rows
-    far_rows = corner_rows(params) + block_rows
-    far_down, far_up, block = kernel(
-        functools.partial(pack_far, params),
-        (f32(far_rows, 128),) * 2 + (f32(block_rows, 128),), name="pack_far",
-    )(from_left, from_right, own, *others)
-    far_above = shifted(far_down, "wide", wide_count, 1)
-    far_below = shifted(far_up, "wide", wide_count, -1)
-    others = [shifted(block, "wide", wide_count, d) for d in range(2, wide_count - 1)]
+    slots = kernel(
+        find_slots, jax.ShapeDtypeStruct((bricks, 128), jnp.int32), name="find_slots"
+    )(brick_grains, grain_slot)
+    strips = kernel(
+        pack_strips, f32(narrow_count, strip_rows, 128),
+        name="pack_strips", in_specs=[here] * 4 + [anywhere],
+    )(order_init, cotangent, grain_map, mobility, down)
+    strips = lax.all_to_all(strips, "narrow", 0, 0, tiled=True)
+
+    far_rows = corner_rows(params) + narrow_count * owned_rows
+    far_rows += -far_rows % 8
+    far = kernel(
+        functools.partial(pack_far, params, owned_rows), f32(wide_count, far_rows, 128),
+        name="pack_far", in_specs=[here, anywhere],
+    )(strips, slots)
+    far = lax.all_to_all(far, "wide", 0, 0, tiled=True)
+
+    table, cot_down, cot_up = kernel(
+        functools.partial(find_mobility, counts, owned, owned_rows),
+        (f32(16, 128),) + (f32(cot_rows, 128),) * 2,
+        (pltpu.VMEM((16, 128), jnp.int32), vmem(count * owned_rows, 128)),
+        name="find_mobility",
+    )(slots, far, cotangent)
     cot_above = shifted(cot_down, "wide", wide_count, 1)
     cot_below = shifted(cot_up, "wide", wide_count, -1)
 
-    slots = kernel(
-        find_slots, jax.ShapeDtypeStruct((bricks, 128), jnp.int32), name="find_slots"
-    )(brick_grains, grain_slot.reshape(-1, 128))
-    table = kernel(
-        functools.partial(find_mobility, counts, owned, corner_rows(params)),
-        f32(16, 128),
-        (pltpu.VMEM((16, 128), jnp.int32), vmem(wide_count * block_rows, 128)),
-        name="find_mobility",
-    )(slots, block, far_above, far_below, *others)
-
     padded, strip = (params, layers, ROWS, 128), (params, ROWS, 128)
-    final, states, rate, strips, m, ms = kernel(
+    final, states, rate, halos, m, ms = kernel(
         forward,
         (
             f32(*order_init.shape), [f32(*padded)] * ITERS, [f32(*padded)] * ITERS,
@@ -625,7 +631,7 @@
         ),
         (vmem(*strip), vmem(*strip), vmem(*padded), vmem(layers, ROWS, 128), vmem(ROWS, 128)),
         name="forward",
-    )(order_init, grain_map, above, below, far_above, far_below, from_left, from_right, table)
+    )(order_init, grain_map, above, below, far, strips, table)
     adjoint, sums = kernel(
         backward,
         (f32(*order_init.shape), f32(count, listed)),
@@ -635,8 +641,8 @@
         ),
         name="backward",
     )(
-        cotangent, grain_map, cot_above, cot_below, far_above, far_below, from_left, from_right,
-        states, rate, strips, m, ms,
+        cotangent, grain_map, cot_above, cot_below, far, strips,
+        states, rate, halos, m, ms,
     )
 
     every_sum = lax.all_to_all(sums, both, 0, 0, tiled=True)

time: 69.2 us -> 55.9 us (0.81)
  local copies, waits for them, and re-layouts: 5.71 us -> 0 us
  blocking collectives: 12.4 us -> 9.34 us
  waiting for transfers between devices: 12.7 us -> 10.7 us
  Pallas kernels: 23.6 us -> 22.3 us
  starting transfers between devices: 13.5 us -> 12.6 us
    ppermute x10 -> x4, waiting for transfers between devices: 12.7 us -> 0.85 us  [shifted(): lax.ppermute(value, axis, [(i, (i + by) % count) for i in range(count)])]
    ppermute x10 -> x4, starting transfers between devices: 13.5 us -> 2.91 us  [shifted(): lax.ppermute(value, axis, [(i, (i + by) % count) for i in range(count)])]
    all_to_all x0 -> x2, waiting for transfers between devices: none -> 9.8 us  [the longest x1 5.13 us: per_device(): far = lax.all_to_all(far, 'wide', 0, 0, tiled=True)]
    all_to_all x0 -> x2, starting transfers between devices: none -> 9.67 us  [the longest x1 6.32 us: per_device(): strips = lax.all_to_all(strips, 'narrow', 0, 0, tiled=True)]
    unnamed x18 -> x0, local copies, waits for them, and re-layouts: 5.71 us -> none
    all_to_all x1, blocking collectives: 12.4 us -> 9.34 us  [per_device(): every_sum = lax.all_to_all(sums, both, 0, 0, tiled=True)]
    pallas_call x3 -> x4, Pallas kernels: 1.55 us -> 3.55 us  [the longest x1 1.2 us: per_device(): kernel(pack_rows, tuple((jax.ShapeDtypeStruct(x.shape, x.dtype) for x in...]
    pallas_call x1, Pallas kernels: 10.2 us -> 8.28 us  [per_device(): kernel(backward, (f32(*order_init.shape), f32(count, listed)), ([vmem(*pa...]
  transfers between devices with their start and end apart: 10 -> 6, of which waited for: 5 -> 3; matrix products, arithmetic and copies ran while one was open for 0% -> 0% of each run, Pallas kernels for 16% -> 19%
where the time goes in v5:
time: 55.9 us; the launch traced here: 55.5 us
  Pallas kernels  22.3 us (40%)
  starting transfers between devices  12.6 us (23%)
  waiting for transfers between devices  10.7 us (19%)
  blocking collectives  9.34 us (17%)
  between operations  0.67 us (1%)
    all_to_all x1, blocking collectives, per_device(): every_sum = lax.all_to_all(sums, both, 0, 0, tiled=True)  9.34 us
    pallas_call x1, Pallas kernels, per_device(): kernel(backward, (f32(*order_init.shape), f32(count, listed)), ([vmem(*pa...  8.28 us
    pallas_call x1, Pallas kernels, per_device(): kernel(forward, (f32(*order_init.shape), [f32(*padded)] * ITERS, [f32(*pa...  8.02 us
    all_to_all x1, starting transfers between devices, per_device(): strips = lax.all_to_all(strips, 'narrow', 0, 0, tiled=True)  6.32 us
    all_to_all x1, waiting for transfers between devices, per_device(): far = lax.all_to_all(far, 'wide', 0, 0, tiled=True)  5.13 us
    all_to_all x1, waiting for transfers between devices, per_device(): strips = lax.all_to_all(strips, 'narrow', 0, 0, tiled=True)  4.68 us
    all_to_all x1, starting transfers between devices, per_device(): far = lax.all_to_all(far, 'wide', 0, 0, tiled=True)  3.36 us
    ppermute x4, starting transfers between devices, shifted(): lax.ppermute(value, axis, [(i, (i + by) % count) for i in range(count)])  2.91 us
  transfers between devices with their start and end apart: 6, of which 3 were waited for; matrix products, arithmetic and copies ran while one was open for 0% of the time, Pallas kernels for 19%

profile of v5, /device:TPU:0, one launch (start us, length us, event | category | flops | bytes accessed | tf_op | source)
XLA Modules:
  0.0 55.5 jit_solution(15471622030608027289)
XLA Ops:
  0.6 1.2 %pack_rows.1 = (f32[8,12,8,128]{3,2,1,0:T(8,128)S(1)}, s32[12,8,128]{2,1,0:T(8,128)S(1)}, f32[8,12,8,128]{3,2,1,0:T(8,128)S(1)}, f32[1,392]{1,0:T(1,128)S(1)}, s...) custom-call(f32[8,12,8,128]{3,2,1,0:T(8,128)} %refs_0_.1, ...), custom_call_target="tpu_custom_call" | custom-call | tf_op jit(solution)/shard_map/pack_rows/pallas_call | solution.py:590
  1.8 1.1 %pack_strips.1 = f32[4,80,128]{2,1,0:T(8,128)} custom-call(f32[8,12,8,128]{3,2,1,0:T(8,128)S(1)} %get-tuple-element.30.order_ref, f32[8,12,8,128]{3,2,1,0:T(8,128)S(1)} %get-tuple-element.34.cot_ref, s32[12,8,128]{2,1,0:T(8,128)S(1)} %get-tuple-element.31.map_ref, f32[1,392]{1,0:T(1,128)S(1)} %get-tuple-element.35.mob_ref, ...), custom_call_target="tpu_custom_call" | custom-call | tf_op jit(solution)/shard_map/pack_strips/pallas_call | solution.py:602
  2.9 6.3 %all-to-all-start = ((f32[4,80,128]{2,1,0:T(8,128)}), f32[4,80,128]{2,1,0:T(8,128)S(1)}, u32[]{:S(2)}, u32[]{:S(2)}) async-start(f32[4,80,128]{2,1,0:T(8,128)} %pack_strips.1), calls=%async_computation | async-start | bytes 327680 | tf_op jit(solution)/shard_map/all_to_all | solution.py:606
  9.2 0.7 %collective-permute-start.1 = (f32[664,128]{1,0:T(8,128)S(1)}, f32[664,128]{1,0:T(8,128)S(1)}, u32[]{:S(2)}, u32[]{:S(2)}) collective-permute-start(f32[664,128]{1,0:T(8,128)S(1)} %get-tuple-element.33), channel_id=1, source_target_pairs={{0,12},{4,0},{8,4},{12,8},{1,13},{5,1},{9,5},{13,9},{2,14},{6,2},{... | collective-permute-start | bytes 1019912 | tf_op jit(solution)/shard_map/ppermute | solution.py:565
  9.9 1.1 %find_slots.1.slots_ref = s32[16,128]{1,0:T(8,128)S(1)} custom-call(s32[16,64]{1,0:T(8,128)S(1)} %get-tuple-element.36.bricks_ref, s32[49,128]{1,0:T(8,128)S(1)} %get-tuple-element.37.slot_ref), custom_call_target="tpu_custom_call" | custom-call | tf_op jit(solution)/shard_map/find_slots/pallas_call | solution.py:599
  11.0 4.7 %all-to-all-done.strips_ref = f32[4,80,128]{2,1,0:T(8,128)S(1)} async-done(((f32[4,80,128]{2,1,0:T(8,128)}), f32[4,80,128]{2,1,0:T(8,128)S(1)}, u32[]{:S(2)}, u32[]{:S(2)}) %all-to-all-start) | async-done | bytes 163872 | tf_op jit(solution)/shard_map/all_to_all | solution.py:606
  15.6 0.8 %pack_far.1 = f32[4,88,128]{2,1,0:T(8,128)} custom-call(f32[4,80,128]{2,1,0:T(8,128)S(1)} %all-to-all-done.strips_ref, s32[16,128]{1,0:T(8,128)S(1)} %find_slots.1.slots_ref), custom_call_target="tpu_custom_call" | custom-call | tf_op jit(solution)/shard_map/pack_far/pallas_call | solution.py:610
  16.4 3.4 %all-to-all-start.1 = ((f32[4,88,128]{2,1,0:T(8,128)}), f32[4,88,128]{2,1,0:T(8,128)S(1)}, u32[]{:S(2)}, u32[]{:S(2)}) async-start(f32[4,88,128]{2,1,0:T(8,128)} %pack_far.1), calls=%async_computation.1 | async-start | bytes 360448 | tf_op jit(solution)/shard_map/all_to_all | solution.py:614
  19.8 0.5 collective-permute-start
  20.2 5.1 %all-to-all-done.1.far_ref = f32[4,88,128]{2,1,0:T(8,128)S(1)} async-done(((f32[4,88,128]{2,1,0:T(8,128)}), f32[4,88,128]{2,1,0:T(8,128)S(1)}, u32[]{:S(2)}, u32[]{:S(2)}) %all-to-all-start.1) | async-done | bytes 180256 | tf_op jit(solution)/shard_map/all_to_all | solution.py:614
  25.4 0.5 find_mobility.1
  25.9 0.1 collective-permute-start.2
  26.0 1.7 %collective-permute-start.3 = (f32[400,128]{1,0:T(8,128)S(1)}, f32[400,128]{1,0:T(8,128)S(1)}, u32[]{:S(2)}, u32[]{:S(2)}) collective-permute-start(f32[400,128]{1,0:T(8,128)S(1)} %get-tuple-element.41), channel_id=1, source_target_pairs={{0,12},{4,0},{8,4},{12,8},{1,13},{5,1},{9,5},{13,9},{2,14},{6,2},{... | collective-permute-start | bytes 614408 | tf_op jit(solution)/shard_map/ppermute | solution.py:565
  27.7 0.0 collective-permute-done.1.below_ref
  27.7 0.8 %collective-permute-done.above_ref = f32[664,128]{1,0:T(8,128)S(1)} collective-permute-done((f32[664,128]{1,0:T(8,128)S(1)}, f32[664,128]{1,0:T(8,128)S(1)}, u32[]{:S(2)}, u32[]{:S(2)}) %collective-permute-start) | collective-permute-done | bytes 340000 | tf_op jit(solution)/shard_map/ppermute | solution.py:565
  28.5 8.0 %forward.1 = (f32[8,12,8,128]{3,2,1,0:T(8,128)}, f32[8,12,24,128]{3,2,1,0:T(8,128)S(1)}, f32[8,12,24,128]{3,2,1,0:T(8,128)S(1)}, f32[8,12,24,128]{3,2,1,0:T(8,12...) custom-call(f32[8,12,8,128]{3,2,1,0:T(8,128)S(1)} %get-tuple-element, ...), custom_call_target="tpu_custom_call" | custom-call | tf_op jit(solution)/shard_map/forward/pallas_call | solution.py:626
  36.6 0.0 collective-permute-done.2.above_ref
  36.6 0.0 collective-permute-done.3.below_ref
  36.6 8.3 %backward.1 = (f32[8,12,8,128]{3,2,1,0:T(8,128)}, f32[16,64]{1,0:T(8,128)S(1)}) custom-call(f32[8,12,8,128]{3,2,1,0:T(8,128)S(1)} %get-tuple-element.34.cot_ref, s32[12,8,128]{2,1,0:T(8,128)S(1)} %get-tuple-element.31.map_ref, f32[400,128]{1,0:T(8,128)S(1)} %collective-permute-done.2.above_ref, f32[400,128]{1,0:T(8,128)S(1)} %collective-permute-done.3.below_ref, ...), custom_call_target="tpu_custom_call" | custom-call | tf_op jit(solution)/shard_map/backward/pallas_call | solution.py:635
  44.9 9.3 %all_to_all.21 = f32[16,1,64]{2,1,0:T(1,128)S(1)} all-to-all(f32[16,1,64]{2,1,0:T(1,128)S(1)} %bitcast.8), channel_id=1, replica_groups=mesh['groups'=2,'wide'=4,'narrow'=4] {'wide','narrow'}, dimensions={0} | all-to-all | bytes 8192 | tf_op jit(solution)/shard_map/all_to_all | solution.py:648
  54.2 1.3 %pick_owned.1 = f32[1,392]{1,0:T(1,128)} custom-call(s32[16,128]{1,0:T(8,128)S(1)} %find_slots.1.slots_ref, f32[16,64]{1,0:T(8,128)S(1)} %bitcast.7), custom_call_target="tpu_custom_call" | custom-call | tf_op jit(solution)/shard_map/pick_owned/pallas_call | solution.py:649
Async XLA Ops:
  2.9 12.7 %all-to-all-start = ((f32[4,80,128]{2,1,0:T(8,128)}), f32[4,80,128]{2,1,0:T(8,128)S(1)}, u32[]{:S(2)}, u32[]{:S(2)}) async-start(f32[4,80,128]{2,1,0:T(8,128)} %pack_strips.1), calls=%async_computation | async-start | bytes 327680 | tf_op jit(solution)/shard_map/all_to_all | solution.py:606
  9.2 18.5 %collective-permute-start.1 = (f32[664,128]{1,0:T(8,128)S(1)}, f32[664,128]{1,0:T(8,128)S(1)}, u32[]{:S(2)}, u32[]{:S(2)}) collective-permute-start(f32[664,128]{1,0:T(8,128)S(1)} %get-tuple-element.33), channel_id=1, source_target_pairs={{0,12},{4,0},{8,4},{12,8},{1,13},{5,1},{9,5},{13,9},{2,14},{6,2},{... | collective-permute-start | bytes 1019912 | tf_op jit(solution)/shard_map/ppermute | solution.py:565
  16.4 9.0 %all-to-all-start.1 = ((f32[4,88,128]{2,1,0:T(8,128)}), f32[4,88,128]{2,1,0:T(8,128)S(1)}, u32[]{:S(2)}, u32[]{:S(2)}) async-start(f32[4,88,128]{2,1,0:T(8,128)} %pack_far.1), calls=%async_computation.1 | async-start | bytes 360448 | tf_op jit(solution)/shard_map/all_to_all | solution.py:614
  19.8 8.8 %collective-permute-start = (f32[664,128]{1,0:T(8,128)S(1)}, f32[664,128]{1,0:T(8,128)S(1)}, u32[]{:S(2)}, u32[]{:S(2)}) collective-permute-start(f32[664,128]{1,0:T(8,128)S(1)} %get-tuple-element.32.after_ref), channel_id=1, source_target_pairs={{0,4},{4,8},{8,12},{12,0},{1,5},{5,9},{9,13},{13,1},{2,6},{6,10},{... | collective-permute-start | bytes 1019912 | tf_op jit(solution)/shard_map/ppermute | solution.py:565
  25.9 10.7 %collective-permute-start.2 = (f32[400,128]{1,0:T(8,128)S(1)}, f32[400,128]{1,0:T(8,128)S(1)}, u32[]{:S(2)}, u32[]{:S(2)}) collective-permute-start(f32[400,128]{1,0:T(8,128)S(1)} %get-tuple-element.40), channel_id=1, source_target_pairs={{0,4},{4,8},{8,12},{12,0},{1,5},{5,9},{9,13},{13,1},{2,6},{6,10},{... | collective-permute-start | bytes 614408 | tf_op jit(solution)/shard_map/ppermute | solution.py:565
  26.0 10.6 %collective-permute-start.3 = (f32[400,128]{1,0:T(8,128)S(1)}, f32[400,128]{1,0:T(8,128)S(1)}, u32[]{:S(2)}, u32[]{:S(2)}) collective-permute-start(f32[400,128]{1,0:T(8,128)S(1)} %get-tuple-element.41), channel_id=1, source_target_pairs={{0,12},{4,0},{8,4},{12,8},{1,13},{5,1},{9,5},{13,9},{2,14},{6,2},{... | collective-permute-start | bytes 614408 | tf_op jit(solution)/shard_map/ppermute | solution.py:565

commit v6 on v5

--- a/solution.py
+++ b/solution.py
@@ -29,18 +29,25 @@
     return pltpu.roll(value, shift, 1)
 
 
-def pack_rows(*refs):
-    count = (len(refs) - 3) // 2
+def is_odd(axis):
+    return lax.rem(lax.axis_index(axis), 2) == 1
+
+
+def pack(*refs):
+    count = (len(refs) - 6) // 2
     sources, targets = refs[:count], refs[count : 2 * count]
-    down_ref, up_ref, sems = refs[2 * count :]
+    *row_refs, strip_a_ref, strip_b_ref, own_ref, sems = refs[2 * count :]
     copies = [pltpu.make_async_copy(a, b, sems.at[i]) for i, (a, b) in enumerate(zip(sources, targets))]
     for copy in copies:
         copy.start()
-    order_ref, map_ref = targets[:2]
+    order_ref, map_ref, cot_ref, mob_ref = targets[:4]
     params, layers = order_ref.shape[:2]
     maps = row_places(params, layers)[0]
     gap = jnp.zeros((LEAD, 128), jnp.float32)
-    for ref in (down_ref, up_ref):
+    odd = is_odd("wide")
+    odd_y = is_odd("narrow")
+    last = (jnp.where(odd, 0, 1), jnp.where(odd, 1, 0))
+    for ref in row_refs:
         ref[0:LEAD, :] = gap
         ref[maps - LEAD : maps, :] = gap
         ref[ref.shape[0] - 2 * LEAD : ref.shape[0] - LEAD, :] = gap
@@ -49,37 +56,15 @@
     for p in range(params):
         for z in range(layers):
             k = LEAD + (p * layers + z) * EDGE
-            down_ref[k : k + EDGE, :] = order_ref[p, z, 8 - EDGE : 8, :]
-            up_ref[k : k + EDGE, :] = order_ref[p, z, 0:EDGE, :]
+            for ref, is_last in zip(row_refs, last):
+                ref[k : k + EDGE, :] = order_ref[p, z, pl.ds((8 - EDGE) * is_last, EDGE), :]
     copies[1].wait()
     for z in range(layers):
         k = maps + z * MAP_EDGE
-        cells = map_ref[z].astype(jnp.float32)
-        down_ref[k : k + MAP_EDGE, :] = cells[8 - MAP_EDGE : 8]
-        up_ref[k : k + MAP_EDGE, :] = cells[0:MAP_EDGE]
+        for ref, is_last in zip(row_refs, last):
+            ref[k : k + MAP_EDGE, :] = map_ref[z, pl.ds((8 - MAP_EDGE) * is_last, MAP_EDGE), :].astype(jnp.float32)
     for copy in copies[2:]:
         copy.wait()
-
-
-def around(axis, count):
-    place = lax.axis_index(axis)
-    return lax.rem(place + count - 1, count), lax.rem(place + 1, count)
-
-
-def pack_strips(order_ref, cot_ref, map_ref, mob_ref, after_ref, out_ref):
-    params, layers = order_ref.shape[:2]
-    count = out_ref.shape[0]
-    before, after = around("narrow", count)
-    owned = mob_ref.shape[1]
-    at = 8 * (params + 1)
-    out_ref[...] = jnp.zeros_like(out_ref)
-    for i in range(-(-owned // 128)):
-        size = min(128, owned - 128 * i)
-        row = mob_ref[0:1, 128 * i : 128 * i + size]
-        if size < 128:
-            row = jnp.concatenate([row, jnp.zeros((1, 128 - size), jnp.float32)], axis=1)
-        for j in range(count):
-            out_ref[j, at + i : at + i + 1, :] = row
 
     lane = lanes((8, 128))
     zero = jnp.zeros((8, 128), jnp.float32)
@@ -97,8 +82,18 @@
             if field < params:
                 right = jnp.where(span(10 * z + 5, 4), roll(cot_ref[field, z], 10 * z + 9), right)
                 left = jnp.where(span(10 * z + 1, 4), roll(cot_ref[field, z], 10 * z + 1), left)
-        out_ref[after, 8 * field : 8 * field + 8, :] = right
-        out_ref[before, 8 * field : 8 * field + 8, :] = left
+        rows = slice(8 * field, 8 * field + 8)
+        strip_a_ref[rows, :] = jnp.where(odd_y, left, right)
+        strip_b_ref[rows, :] = jnp.where(odd_y, right, left)
+    owned = mob_ref.shape[1]
+    at = 8 * (params + 1)
+    for i in range(own_ref.shape[0]):
+        size = min(128, owned - 128 * i)
+        row = mob_ref[0:1, 128 * i : 128 * i + size]
+        if size < 128:
+            row = jnp.concatenate([row, jnp.zeros((1, 128 - size), jnp.float32)], axis=1)
+        for ref, k in ((own_ref, i), (strip_a_ref, at + i), (strip_b_ref, at + i)):
+            ref[k : k + 1, :] = row
 
 
 def row_places(params, layers):
@@ -111,37 +106,50 @@
     return -(-(params * (CORNER[0] + CORNER[1]) + CORNER[2]) // 8) * 8
 
 
-def side_strips(params, strips_ref):
-    before, after = around("narrow", strips_ref.shape[0])
-    rows = [slice(8 * field, 8 * field + 8) for field in range(params + 1)]
-    return [(strips_ref[before, r, :], strips_ref[after, r, :]) for r in rows]
-
-
-def merged_strips(params, strips_ref):
+def side_strips(params, strip_a_ref, strip_b_ref):
+    odd = is_odd("narrow")
+    fields = []
+    for field in range(params + 1):
+        rows = slice(8 * field, 8 * field + 8)
+        a, b = strip_a_ref[rows, :], strip_b_ref[rows, :]
+        fields.append((jnp.where(odd, a, b), jnp.where(odd, b, a)))
+    return fields
+
+
+def merged_strips(params, *strip_refs):
     first = lanes((8, 128)) % COLS < 5
-    fields = side_strips(params, strips_ref)
+    fields = side_strips(params, *strip_refs)
     order = [jnp.where(first, a, b) for a, b in fields[:params]]
     cot = [jnp.where(first, roll(a, 124), roll(b, 4)) for a, b in fields[:params]]
     return order, cot, jnp.where(first, *fields[params])
 
 
-def pack_far(params, owned_rows, strips_ref, slots_ref, out_ref):
-    count = out_ref.shape[0]
-    before, after = around("wide", count)
+def pieces_back(odd, own, a, b, others):
+    return [own, jnp.where(odd, a, b), *others, jnp.where(odd, b, a)]
+
+
+def pack_far(params, strip_a_ref, strip_b_ref, own_ref, slots_ref, *refs):
+    *other_refs, far_a_ref, far_b_ref, block_ref = refs
+    rows = own_ref.shape[0]
+    at = 8 * (params + 1)
+    pieces = pieces_back(
+        is_odd("narrow"), own_ref[...], strip_a_ref[at : at + rows, :], strip_b_ref[at : at + rows, :],
+        [ref[...] for ref in other_refs],
+    )
     mobs = corner_rows(params)
-    out_ref[...] = jnp.zeros_like(out_ref)
-    at = 8 * (params + 1)
-    for i in range(strips_ref.shape[0]):
-        piece = strips_ref[i, at : at + owned_rows, :]
-        for j in range(count):
-            out_ref[j, mobs + i * owned_rows : mobs + (i + 1) * owned_rows, :] = piece
+    for i, piece in enumerate(pieces):
+        for ref, k in ((block_ref, 0), (far_a_ref, mobs), (far_b_ref, mobs)):
+            ref[k + i * rows : k + (i + 1) * rows, :] = piece
     at = 0
-    order, cot, cells = merged_strips(params, strips_ref)
+    odd = is_odd("wide")
+    order, cot, cells = merged_strips(params, strip_a_ref, strip_b_ref)
     for n, fields in zip(CORNER, (order, cot, [cells])):
         for both in fields:
-            out_ref[after, at : at + n, :] = both[8 - n : 8]
-            out_ref[before, at : at + n, :] = both[0:n]
+            far_a_ref[at : at + n, :] = jnp.where(odd, both[0:n], both[8 - n : 8])
+            far_b_ref[at : at + n, :] = jnp.where(odd, both[8 - n : 8], both[0:n])
             at += n
+    for ref in (far_a_ref, far_b_ref):
+        ref[at:mobs, :] = jnp.zeros((mobs - at, 128), jnp.float32)
 
 
 def find_slots(bricks_ref, slot_ref, out_ref):
@@ -161,25 +169,31 @@
         out_ref[k : k + 8, :] = jnp.where(lanes((8, 128)) < listed, found, -1)
 
 
-def find_mobility(
-    counts, owned, owned_rows, slots_ref, far_ref, cot_ref, table_ref, cot_down_ref, cot_up_ref, near_ref, mob_ref
-):
+def find_mobility(counts, owned, slots_ref, block_ref, far_a_ref, far_b_ref, cot_ref, *refs):
+    *other_refs, table_ref, cot_a_ref, cot_b_ref, near_ref, mob_ref = refs
     params, layers = cot_ref.shape[:2]
-    for ref in (cot_down_ref, cot_up_ref):
+    odd = is_odd("wide")
+    last = (jnp.where(odd, 0, 1), jnp.where(odd, 1, 0))
+    for ref in (cot_a_ref, cot_b_ref):
         ref[0:LEAD, :] = jnp.zeros((LEAD, 128), jnp.float32)
         ref[ref.shape[0] - LEAD :, :] = jnp.zeros((LEAD, 128), jnp.float32)
     for p in range(params):
         for z in range(layers):
             k = LEAD + (p * layers + z) * ADJ_EDGE
-            cot_down_ref[k : k + ADJ_EDGE, :] = cot_ref[p, z, 8 - ADJ_EDGE : 8, :]
-            cot_up_ref[k : k + ADJ_EDGE, :] = cot_ref[p, z, 0:ADJ_EDGE, :]
+            for ref, is_last in zip((cot_a_ref, cot_b_ref), last):
+                ref[k : k + ADJ_EDGE, :] = cot_ref[p, z, pl.ds((8 - ADJ_EDGE) * is_last, ADJ_EDGE), :]
 
     wide_count, narrow_count = counts
     tile = (8, 128)
     wide, narrow = lax.axis_index("wide"), lax.axis_index("narrow")
-    size, at = narrow_count * owned_rows, corner_rows(params)
-    for i in range(wide_count):
-        mob_ref[i * size : (i + 1) * size, :] = far_ref[i, at : at + size, :]
+    size, at = block_ref.shape[0], corner_rows(params)
+    owned_rows = size // narrow_count
+    pieces = pieces_back(
+        odd, block_ref[...], far_a_ref[at : at + size, :], far_b_ref[at : at + size, :],
+        [ref[...] for ref in other_refs],
+    )
+    for i, piece in enumerate(pieces):
+        mob_ref[i * size : (i + 1) * size, :] = piece
     for i in range(3):
         for j in range(3):
             w = lax.rem(wide + i - 1 + wide_count, wide_count)
@@ -189,7 +203,12 @@
     slot = [jnp.maximum(near_ref[k : k + 8, :], 0) for k in (0, 8)]
     owner = [jnp.floor((x.astype(jnp.float32) + 0.5) * (1.0 / owned)).astype(jnp.int32) for x in slot]
     inner = [x - y * owned for x, y in zip(slot, owner)]
-    row = [y * owned_rows + (x >> 7) for x, y in zip(inner, owner)]
+    by_wide = [jnp.floor((y.astype(jnp.float32) + 0.5) * (1.0 / narrow_count)).astype(jnp.int32) for y in owner]
+    back_w = [wide - y for y in by_wide]
+    back_n = [narrow - (x - y * narrow_count) for x, y in zip(owner, by_wide)]
+    back_w = [jnp.where(x < 0, x + wide_count, x) for x in back_w]
+    back_n = [jnp.where(x < 0, x + narrow_count, x) for x in back_n]
+    row = [(a * narrow_count + b) * owned_rows + (x >> 7) for a, b, x in zip(back_w, back_n, inner)]
     place = [x & 127 for x in inner]
 
     def body(r, found):
@@ -213,7 +232,7 @@
 
 def each_tile(layers, windows, body):
     start, count, most = windows
-    group = 4 // count if count < 3 else 1
+    group = 12 // (2 * count) * 2 if layers % 12 == 0 else 1
 
     def some(step, carry):
         stores = []
@@ -221,8 +240,10 @@
             z = step * group + j
             for i in range(count):
                 stores += body(z, i, jnp.minimum(start + 8 * i + ((z + 16) >> 5), most))
-        for store in stores:
-            store()
+            if len(stores) >= 64 or j == group - 1:
+                for store in stores:
+                    store()
+                stores = []
         return carry
 
     lax.fori_loop(0, layers // group, some, 0)
@@ -304,7 +325,7 @@
 
 
 def forward(
-    order_ref, map_ref, above_ref, below_ref, far_ref, strips_ref, table_ref,
+    order_ref, map_ref, row_a_ref, row_b_ref, far_a_ref, far_b_ref, strip_a_ref, strip_b_ref, table_ref,
     final_ref, e_refs, rate_refs, se_refs, m_ref, ms_ref,
     first_strip_ref, outer_ref, ends_ref, g_ref, gs_ref,
 ):
@@ -315,36 +336,40 @@
     strip_refs = [first_strip_ref, *se_refs]
     every = range(params)
 
+    odd = is_odd("wide")
+    from_before = (jnp.where(odd, 1, 0), jnp.where(odd, 0, 1))
+
     def place(z, carry):
-        k = maps + z * MAP_EDGE
-        g_ref[z, 0:8, :] = above_ref[pl.ds(k + MAP_EDGE - 8, 8), :]
-        g_ref[z, 16:24, :] = below_ref[pl.ds(k, 8), :]
+        for ref, before in zip((row_a_ref, row_b_ref), from_before):
+            k, target = maps + z * MAP_EDGE + before * (MAP_EDGE - 8), pl.ds(16 - 16 * before, 8)
+            g_ref[z, target, :] = ref[pl.ds(k, 8), :]
+            for p in every:
+                k = LEAD + (p * layers + z) * EDGE + before * (EDGE - 8)
+                e_refs[0][p, z, target, :] = ref[pl.ds(k, 8), :]
         for p in every:
-            k = LEAD + (p * layers + z) * EDGE
-            e_refs[0][p, z, 0:8, :] = above_ref[pl.ds(k + EDGE - 8, 8), :]
             e_refs[0][p, z, 8:16, :] = order_ref[p, z]
-            e_refs[0][p, z, 16:24, :] = below_ref[pl.ds(k, 8), :]
         return carry
 
     lax.fori_loop(0, layers, place, 0)
 
-    far_above, far_below = around("wide", far_ref.shape[0])
-    sides = side_strips(params, strips_ref)
-    order, _, cells = merged_strips(params, strips_ref)
+    sides = side_strips(params, strip_a_ref, strip_b_ref)
+    order, _, cells = merged_strips(params, strip_a_ref, strip_b_ref)
     n = CORNER[0]
     for p in every:
         ref = first_strip_ref.at[p]
         ref[0:8, :] = jnp.zeros(tile, jnp.float32)
         ref[16:24, :] = jnp.zeros(tile, jnp.float32)
-        ref[8 - n : 8, :] = far_ref[far_above, n * p : n * p + n, :]
+        a, b = far_a_ref[n * p : n * p + n, :], far_b_ref[n * p : n * p + n, :]
+        ref[8 - n : 8, :] = jnp.where(odd, a, b)
         ref[8:16, :] = order[p]
-        ref[16 : 16 + n, :] = far_ref[far_below, n * p : n * p + n, :]
+        ref[16 : 16 + n, :] = jnp.where(odd, b, a)
         outer_ref[p, 8:16, :] = jnp.where(col == 0, roll(sides[p][0], 1), roll(sides[p][1], 127))
     at, n = params * (CORNER[0] + CORNER[1]), CORNER[2]
     gs_ref[...] = jnp.zeros_like(gs_ref)
-    gs_ref[8 - n : 8, :] = far_ref[far_above, at : at + n, :]
+    a, b = far_a_ref[at : at + n, :], far_b_ref[at : at + n, :]
+    gs_ref[8 - n : 8, :] = jnp.where(odd, a, b)
     gs_ref[8:16, :] = cells
-    gs_ref[16 : 16 + n, :] = far_ref[far_below, at : at + n, :]
+    gs_ref[16 : 16 + n, :] = jnp.where(odd, b, a)
     for r in (0, 8, 16):
         rows = slice(r, r + 8)
         spread_ends(ends_ref, [first_strip_ref[p, rows, :] for p in every], rows)
@@ -407,7 +432,7 @@
 
 
 def backward(
-    cot_ref, map_ref, above_ref, below_ref, far_ref, strips_ref,
+    cot_ref, map_ref, row_a_ref, row_b_ref, far_a_ref, far_b_ref, strip_a_ref, strip_b_ref,
     e_refs, rate_refs, se_refs, m_ref, ms_ref,
     adjoint_ref, sums_ref,
     lam_refs, slam_refs, u_refs, su_refs, ends_ref, work_ref, binned_ref,
@@ -416,28 +441,36 @@
     tile = (8, 128)
     every = range(params)
 
+    odd = is_odd("wide")
+    from_before = (jnp.where(odd, 1, 0), jnp.where(odd, 0, 1))
+
     def place(z, carry):
-        m = [m_ref[z, 8 * i : 8 * i + 8, :] for i in range(3)]
+        for ref, before in zip((row_a_ref, row_b_ref), from_before):
+            rows = pl.ds(16 - 16 * before, 8)
+            m = m_ref[z, rows, :]
+            for p in every:
+                k = LEAD + (p * layers + z) * ADJ_EDGE + before * (ADJ_EDGE - 8)
+                value = ref[pl.ds(k, 8), :]
+                lam_refs[0][p, z, rows, :] = value
+                u_refs[0][p, z, rows, :] = m * value
+        m = m_ref[z, 8:16, :]
         for p in every:
-            k = LEAD + (p * layers + z) * ADJ_EDGE
-            blocks = (above_ref[pl.ds(k + ADJ_EDGE - 8, 8), :], cot_ref[p, z], below_ref[pl.ds(k, 8), :])
-            for i in range(3):
-                lam_refs[0][p, z, 8 * i : 8 * i + 8, :] = blocks[i]
-                u_refs[0][p, z, 8 * i : 8 * i + 8, :] = m[i] * blocks[i]
+            lam_refs[0][p, z, 8:16, :] = cot_ref[p, z]
+            u_refs[0][p, z, 8:16, :] = m * cot_ref[p, z]
         return carry
 
     lax.fori_loop(0, layers, place, 0)
-    far_above, far_below = around("wide", far_ref.shape[0])
-    _, cot, _ = merged_strips(params, strips_ref)
+    _, cot, _ = merged_strips(params, strip_a_ref, strip_b_ref)
     n = CORNER[1]
     for p in every:
         at = params * CORNER[0] + n * p
         ref = slam_refs[0].at[p]
         ref[0:8, :] = jnp.zeros(tile, jnp.float32)
         ref[16:24, :] = jnp.zeros(tile, jnp.float32)
-        ref[8 - n : 8, :] = far_ref[far_above, at : at + n, :]
+        a, b = far_a_ref[at : at + n, :], far_b_ref[at : at + n, :]
+        ref[8 - n : 8, :] = jnp.where(odd, a, b)
         ref[8:16, :] = cot[p]
-        ref[16 : 16 + n, :] = far_ref[far_below, at : at + n, :]
+        ref[16 : 16 + n, :] = jnp.where(odd, b, a)
         for r in (0, 8, 16):
             su_refs[0][p, r : r + 8, :] = ms_ref[r : r + 8, :] * ref[r : r + 8, :]
 
@@ -565,6 +598,11 @@
     return lax.ppermute(value, axis, [(i, (i + by) % count) for i in range(count)])
 
 
+def swapped(value, axis, count, partner):
+    step = [1 if (i + partner) % 2 == 0 else -1 for i in range(count)]
+    return lax.ppermute(value, axis, [(i, (i + by) % count) for i, by in enumerate(step)])
+
+
 def per_device(counts, order_init, cotangent, grain_map, brick_grains, grain_slot, mobility):
     wide_count, narrow_count = counts
     params, layers = order_init.shape[:2]
@@ -578,7 +616,6 @@
 
     owned_rows = -(-owned // 128)
     strip_rows = 8 * (params + 1) + owned_rows
-    strip_rows += -strip_rows % 8
     edge_rows = row_places(params, layers)[1]
     cot_rows = params * layers * ADJ_EDGE + 2 * LEAD
     anywhere, here = pl.BlockSpec(memory_space=pl.ANY), pl.BlockSpec(memory_space=pltpu.VMEM)
@@ -587,40 +624,42 @@
     arguments = (
         order_init, grain_map, cotangent, mobility.reshape(1, owned), brick_grains, grain_slot.reshape(-1, 128)
     )
-    *fetched, down, up = kernel(
-        pack_rows,
-        tuple(jax.ShapeDtypeStruct(x.shape, x.dtype) for x in arguments) + (f32(edge_rows, 128),) * 2,
-        (pltpu.SemaphoreType.DMA((len(arguments),)),), name="pack_rows",
+    *fetched, row_a, row_b, strip_a, strip_b, own = kernel(
+        pack,
+        tuple(jax.ShapeDtypeStruct(x.shape, x.dtype) for x in arguments)
+        + (f32(edge_rows, 128),) * 2 + (f32(strip_rows, 128),) * 2 + (f32(owned_rows, 128),),
+        (pltpu.SemaphoreType.DMA((len(arguments),)),), name="pack",
         in_specs=[pl.BlockSpec(memory_space=pltpu.HBM)] * len(arguments),
     )(*(pltpu.with_memory_space_constraint(x, pltpu.HBM) for x in arguments))
-    order_init, grain_map, cotangent, mobility, brick_grains, grain_slot = fetched
-    above = shifted(down, "wide", wide_count, 1)
-    below = shifted(up, "wide", wide_count, -1)
+    order_init, grain_map, cotangent, _, brick_grains, grain_slot = fetched
+    strip_a = swapped(strip_a, "narrow", narrow_count, 0)
+    strip_b = swapped(strip_b, "narrow", narrow_count, 1)
+    row_a = swapped(row_a, "wide", wide_count, 0)
+    row_b = swapped(row_b, "wide", wide_count, 1)
+    others = [shifted(own, "narrow", narrow_count, d) for d in range(2, narrow_count - 1)]
     slots = kernel(
         find_slots, jax.ShapeDtypeStruct((bricks, 128), jnp.int32), name="find_slots"
     )(brick_grains, grain_slot)
-    strips = kernel(
-        pack_strips, f32(narrow_count, strip_rows, 128),
-        name="pack_strips", in_specs=[here] * 4 + [anywhere],
-    )(order_init, cotangent, grain_map, mobility, down)
-    strips = lax.all_to_all(strips, "narrow", 0, 0, tiled=True)
-
-    far_rows = corner_rows(params) + narrow_count * owned_rows
-    far_rows += -far_rows % 8
-    far = kernel(
-        functools.partial(pack_far, params, owned_rows), f32(wide_count, far_rows, 128),
-        name="pack_far", in_specs=[here, anywhere],
-    )(strips, slots)
-    far = lax.all_to_all(far, "wide", 0, 0, tiled=True)
-
-    table, cot_down, cot_up = kernel(
-        functools.partial(find_mobility, counts, owned, owned_rows),
+
+    block_rows = narrow_count * owned_rows
+    far_rows = corner_rows(params) + block_rows
+    far_a, far_b, block = kernel(
+        functools.partial(pack_far, params),
+        (f32(far_rows, 128),) * 2 + (f32(block_rows, 128),),
+        name="pack_far", in_specs=[here] * 3 + [anywhere] + [here] * len(others),
+    )(strip_a, strip_b, own, slots, *others)
+    far_a = swapped(far_a, "wide", wide_count, 0)
+    far_b = swapped(far_b, "wide", wide_count, 1)
+    others = [shifted(block, "wide", wide_count, d) for d in range(2, wide_count - 1)]
+
+    table, cot_a, cot_b = kernel(
+        functools.partial(find_mobility, counts, owned),
         (f32(16, 128),) + (f32(cot_rows, 128),) * 2,
-        (pltpu.VMEM((16, 128), jnp.int32), vmem(count * owned_rows, 128)),
+        (pltpu.VMEM((16, 128), jnp.int32), vmem(wide_count * block_rows, 128)),
         name="find_mobility",
-    )(slots, far, cotangent)
-    cot_above = shifted(cot_down, "wide", wide_count, 1)
-    cot_below = shifted(cot_up, "wide", wide_count, -1)
+    )(slots, block, far_a, far_b, cotangent, *others)
+    cot_a = swapped(cot_a, "wide", wide_count, 0)
+    cot_b = swapped(cot_b, "wide", wide_count, 1)
 
     padded, strip = (params, layers, ROWS, 128), (params, ROWS, 128)
     final, states, rate, halos, m, ms = kernel(
@@ -631,7 +670,7 @@
         ),
         (vmem(*strip), vmem(*strip), vmem(*padded), vmem(layers, ROWS, 128), vmem(ROWS, 128)),
         name="forward",
-    )(order_init, grain_map, above, below, far, strips, table)
+    )(order_init, grain_map, row_a, row_b, far_a, far_b, strip_a, strip_b, table)
     adjoint, sums = kernel(
         backward,
         (f32(*order_init.shape), f32(count, listed)),
@@ -641,7 +680,7 @@
         ),
         name="backward",
     )(
-        cotangent, grain_map, cot_above, cot_below, far, strips,
+        cotangent, grain_map, cot_a, cot_b, far_a, far_b, strip_a, strip_b,
         states, rate, halos, m, ms,
     )
 

time: 55.9 us -> 45.9 us (0.82)
  waiting for transfers between devices: 10.7 us -> 5.45 us
  Pallas kernels: 22.3 us -> 19.4 us
  starting transfers between devices: 12.6 us -> 11.2 us
    all_to_all x2 -> x0, waiting for transfers between devices: 9.8 us -> none  [the longest x1 5.13 us: per_device(): far = lax.all_to_all(far, 'wide', 0, 0, tiled=True)]
    all_to_all x2 -> x0, starting transfers between devices: 9.67 us -> none  [the longest x1 6.32 us: per_device(): strips = lax.all_to_all(strips, 'narrow', 0, 0, tiled=True)]
    ppermute x0 -> x8, starting transfers between devices: none -> 9.58 us  [swapped(): lax.ppermute(value, axis, [(i, (i + by) % count) for i, by in enumerate(s...]
    ppermute x4 -> x2, waiting for transfers between devices: 0.85 us -> 5.43 us  [shifted(): lax.ppermute(value, axis, [(i, (i + by) % count) for i in range(count)])]
    pallas_call x1, Pallas kernels: 8.02 us -> 6.68 us  [per_device(): kernel(forward, (f32(*order_init.shape), [f32(*padded)] * ITERS, [f32(*pa...]
    ppermute x4 -> x2, starting transfers between devices: 2.91 us -> 1.61 us  [shifted(): lax.ppermute(value, axis, [(i, (i + by) % count) for i in range(count)])]
    pallas_call x4 -> x3, Pallas kernels: 3.55 us -> 2.42 us  [the longest x1 1.79 us: per_device(): kernel(pack, tuple((jax.ShapeDtypeStruct(x.shape, x.dtype) for x in argum...]
  transfers between devices with their start and end apart: 6 -> 10, of which waited for: 3 -> 2; matrix products, arithmetic and copies ran while one was open for 0% -> 0% of each run, Pallas kernels for 19% -> 18%
where the time goes in v6:
time: 45.9 us; the launch traced here: 45.7 us
  Pallas kernels  19.4 us (42%)
  starting transfers between devices  11.2 us (24%)
  blocking collectives  8.91 us (19%)
  waiting for transfers between devices  5.45 us (12%)
  between operations  0.68 us (1%)
    ppermute x8, starting transfers between devices, swapped(): lax.ppermute(value, axis, [(i, (i + by) % count) for i, by in enumerate(s...  9.58 us
    all_to_all x1, blocking collectives, per_device(): every_sum = lax.all_to_all(sums, both, 0, 0, tiled=True)  8.91 us
    pallas_call x1, Pallas kernels, per_device(): kernel(backward, (f32(*order_init.shape), f32(count, listed)), ([vmem(*pa...  7.92 us
    pallas_call x1, Pallas kernels, per_device(): kernel(forward, (f32(*order_init.shape), [f32(*padded)] * ITERS, [f32(*pa...  6.68 us
    ppermute x2, waiting for transfers between devices, shifted(): lax.ppermute(value, axis, [(i, (i + by) % count) for i in range(count)])  5.43 us
    pallas_call x1, Pallas kernels, per_device(): kernel(pack, tuple((jax.ShapeDtypeStruct(x.shape, x.dtype) for x in argum...  1.79 us
    ppermute x2, starting transfers between devices, shifted(): lax.ppermute(value, axis, [(i, (i + by) % count) for i in range(count)])  1.61 us
    pallas_call x1, Pallas kernels, per_device(): kernel(functools.partial(pick_owned, counts, owned), f32(1, owned), (pltp...  1.34 us
  transfers between devices with their start and end apart: 10, of which 2 were waited for; matrix products, arithmetic and copies ran while one was open for 0% of the time, Pallas kernels for 18%

profile of v6, /device:TPU:0, one launch (start us, length us, event | category | flops | bytes accessed | tf_op | source)
XLA Modules:
  0.0 45.7 jit_solution(4901527685186591879)
XLA Ops:
  0.6 1.8 %pack.1 = (f32[8,12,8,128]{3,2,1,0:T(8,128)S(1)}, s32[12,8,128]{2,1,0:T(8,128)S(1)}, f32[8,12,8,128]{3,2,1,0:T(8,128)S(1)}, f32[1,392]{1,0:T(1,128)}, s32[16,64]...) custom-call(f32[8,12,8,128]{3,2,1,0:T(8,128)} %refs_0_.1, ...), custom_call_target="tpu_custom_call" | custom-call | tf_op jit(solution)/shard_map/pack/pallas_call | solution.py:627
  2.4 0.5 %collective-permute-start = (f32[664,128]{1,0:T(8,128)S(1)}, f32[664,128]{1,0:T(8,128)S(1)}, u32[]{:S(2)}, u32[]{:S(2)}) collective-permute-start(f32[664,128]{1,0:T(8,128)S(1)} %get-tuple-element.37), channel_id=1, source_target_pairs={{0,4},{4,0},{8,12},{12,8},{1,5},{5,1},{9,13},{13,9},{2,6},{6,2},{1... | collective-permute-start | bytes 1019912 | tf_op jit(solution)/shard_map/ppermute | solution.py:603
  2.9 2.6 %collective-permute-start.1 = (f32[664,128]{1,0:T(8,128)S(1)}, f32[664,128]{1,0:T(8,128)S(1)}, u32[]{:S(2)}, u32[]{:S(2)}) collective-permute-start(f32[664,128]{1,0:T(8,128)S(1)} %get-tuple-element.38), channel_id=1, source_target_pairs={{0,12},{4,8},{8,4},{12,0},{1,13},{5,9},{9,5},{13,1},{2,14},{6,10},... | collective-permute-start | bytes 1019912 | tf_op jit(solution)/shard_map/ppermute | solution.py:603
  5.6 1.6 %collective-permute-start.2 = (f32[76,128]{1,0:T(8,128)S(1)}, f32[76,128]{1,0:T(8,128)S(1)}, u32[]{:S(2)}, u32[]{:S(2)}) collective-permute-start(f32[76,128]{1,0:T(8,128)S(1)} %get-tuple-element.39), channel_id=1, source_target_pairs={{0,1},{1,0},{2,3},{3,2},{4,5},{5,4},{6,7},{7,6},{8,9},{9,8},{10,11... | collective-permute-start | bytes 116744 | tf_op jit(solution)/shard_map/ppermute | solution.py:603
  7.1 2.5 %collective-permute-start.3 = (f32[76,128]{1,0:T(8,128)S(1)}, f32[76,128]{1,0:T(8,128)S(1)}, u32[]{:S(2)}, u32[]{:S(2)}) collective-permute-start(f32[76,128]{1,0:T(8,128)S(1)} %get-tuple-element.40), channel_id=1, source_target_pairs={{0,3},{1,2},{2,1},{3,0},{4,7},{5,6},{6,5},{7,4},{8,11},{9,10},{10,... | collective-permute-start | bytes 116744 | tf_op jit(solution)/shard_map/ppermute | solution.py:603
  9.6 0.1 collective-permute-start.4
  9.7 1.1 %find_slots.1.slots_ref = s32[16,128]{1,0:T(8,128)S(1)} custom-call(s32[16,64]{1,0:T(8,128)S(1)} %get-tuple-element.42.bricks_ref, s32[49,128]{1,0:T(8,128)S(1)} %get-tuple-element.43.slot_ref), custom_call_target="tpu_custom_call" | custom-call | tf_op jit(solution)/shard_map/find_slots/pallas_call | solution.py:640
  10.8 3.3 %collective-permute-done.4.refs_0_ = f32[4,128]{1,0:T(4,128)S(1)} collective-permute-done((f32[4,128]{1,0:T(4,128)S(1)}, f32[4,128]{1,0:T(4,128)S(1)}, u32[]{:S(2)}, u32[]{:S(2)}) %collective-permute-start.4) | collective-permute-done | bytes 2080 | tf_op jit(solution)/shard_map/ppermute | solution.py:598
  14.1 0.0 collective-permute-done.2.strip_a_ref
  14.1 0.0 collective-permute-done.3.strip_b_ref
  14.1 0.1 pack_far.1
  14.2 0.1 collective-permute-start.5
  14.3 0.7 %collective-permute-start.6 = (f32[88,128]{1,0:T(8,128)S(1)}, f32[88,128]{1,0:T(8,128)S(1)}, u32[]{:S(2)}, u32[]{:S(2)}) collective-permute-start(f32[88,128]{1,0:T(8,128)S(1)} %get-tuple-element.45), channel_id=1, source_target_pairs={{0,12},{4,8},{8,4},{12,0},{1,13},{5,9},{9,5},{13,1},{2,14},{6,10},... | collective-permute-start | bytes 135176 | tf_op jit(solution)/shard_map/ppermute | solution.py:603
  14.9 1.5 %collective-permute-start.7 = (f32[16,128]{1,0:T(8,128)S(1)}, f32[16,128]{1,0:T(8,128)S(1)}, u32[]{:S(2)}, u32[]{:S(2)}) collective-permute-start(f32[16,128]{1,0:T(8,128)S(1)} %get-tuple-element.46.block_ref), channel_id=1, source_target_pairs={{0,8},{4,12},{8,0},{12,4},{1,9},{5,13},{9,1},{13,5},{2,10},{6,14},... | collective-permute-start | bytes 24584 | tf_op jit(solution)/shard_map/ppermute | solution.py:598
  16.4 2.2 %collective-permute-done.7.refs_0_ = f32[16,128]{1,0:T(8,128)S(1)} collective-permute-done((f32[16,128]{1,0:T(8,128)S(1)}, f32[16,128]{1,0:T(8,128)S(1)}, u32[]{:S(2)}, u32[]{:S(2)}) %collective-permute-start.7) | collective-permute-done | bytes 8224 | tf_op jit(solution)/shard_map/ppermute | solution.py:598
  18.6 0.0 collective-permute-done.5.far_a_ref
  18.6 0.0 collective-permute-done.6.far_b_ref
  18.6 0.5 %find_mobility.1 = (f32[16,128]{1,0:T(8,128)S(1)}, f32[400,128]{1,0:T(8,128)S(1)}, f32[400,128]{1,0:T(8,128)S(1)}) custom-call(s32[16,128]{1,0:T(8,128)S(1)} %find_slots.1.slots_ref, f32[16,128]{1,0:T(8,128)S(1)} %get-tuple-element.46.block_ref, f32[88,128]{1,0:T(8,128)S(1)} %collective-permute-done.5.far_a_ref, ...), custom_call_target="tpu_custom_call" | custom-call | tf_op jit(solution)/shard_map/find_mobility/pallas_call | solution.py:655
  19.1 0.1 collective-permute-start.8
  19.2 1.6 %collective-permute-start.9 = (f32[400,128]{1,0:T(8,128)S(1)}, f32[400,128]{1,0:T(8,128)S(1)}, u32[]{:S(2)}, u32[]{:S(2)}) collective-permute-start(f32[400,128]{1,0:T(8,128)S(1)} %get-tuple-element.51), channel_id=1, source_target_pairs={{0,12},{4,8},{8,4},{12,0},{1,13},{5,9},{9,5},{13,1},{2,14},{6,10},... | collective-permute-start | bytes 614408 | tf_op jit(solution)/shard_map/ppermute | solution.py:603
  20.8 6.7 %forward.1 = (f32[8,12,8,128]{3,2,1,0:T(8,128)}, f32[8,12,24,128]{3,2,1,0:T(8,128)S(1)}, f32[8,12,24,128]{3,2,1,0:T(8,128)S(1)}, f32[8,12,24,128]{3,2,1,0:T(8,12...) custom-call(f32[8,12,8,128]{3,2,1,0:T(8,128)S(1)} %get-tuple-element, ...), custom_call_target="tpu_custom_call" | custom-call | tf_op jit(solution)/shard_map/forward/pallas_call | solution.py:665
  27.5 7.9 %backward.1 = (f32[8,12,8,128]{3,2,1,0:T(8,128)}, f32[16,64]{1,0:T(8,128)S(1)}) custom-call(f32[8,12,8,128]{3,2,1,0:T(8,128)S(1)} %get-tuple-element.47.cot_ref, s32[12,8,128]{2,1,0:T(8,128)S(1)} %get-tuple-element.36.map_ref, f32[400,128]{1,0:T(8,128)S(1)} %collective-permute-done.8.row_a_ref, f32[400,128]{1,0:T(8,128)S(1)} %collective-permute-done.9.row_b_ref, ...), custom_call_target="tpu_custom_call" | custom-call | tf_op jit(solution)/shard_map/backward/pallas_call | solution.py:674
  35.4 8.9 %all_to_all.11 = f32[16,1,64]{2,1,0:T(1,128)S(1)} all-to-all(f32[16,1,64]{2,1,0:T(1,128)S(1)} %bitcast.8), channel_id=1, replica_groups=mesh['groups'=2,'wide'=4,'narrow'=4] {'wide','narrow'}, dimensions={0} | all-to-all | bytes 8192 | tf_op jit(solution)/shard_map/all_to_all | solution.py:687
  44.3 1.3 %pick_owned.1 = f32[1,392]{1,0:T(1,128)} custom-call(s32[16,128]{1,0:T(8,128)S(1)} %find_slots.1.slots_ref, f32[16,64]{1,0:T(8,128)S(1)} %bitcast.7), custom_call_target="tpu_custom_call" | custom-call | tf_op jit(solution)/shard_map/pick_owned/pallas_call | solution.py:688
  (4 shorter events, 0.0 us)
Async XLA Ops:
  2.4 18.4 %collective-permute-start = (f32[664,128]{1,0:T(8,128)S(1)}, f32[664,128]{1,0:T(8,128)S(1)}, u32[]{:S(2)}, u32[]{:S(2)}) collective-permute-start(f32[664,128]{1,0:T(8,128)S(1)} %get-tuple-element.37), channel_id=1, source_target_pairs={{0,4},{4,0},{8,12},{12,8},{1,5},{5,1},{9,13},{13,9},{2,6},{6,2},{1... | collective-permute-start | bytes 1019912 | tf_op jit(solution)/shard_map/ppermute | solution.py:603
  2.9 17.9 %collective-permute-start.1 = (f32[664,128]{1,0:T(8,128)S(1)}, f32[664,128]{1,0:T(8,128)S(1)}, u32[]{:S(2)}, u32[]{:S(2)}) collective-permute-start(f32[664,128]{1,0:T(8,128)S(1)} %get-tuple-element.38), channel_id=1, source_target_pairs={{0,12},{4,8},{8,4},{12,0},{1,13},{5,9},{9,5},{13,1},{2,14},{6,10},... | collective-permute-start | bytes 1019912 | tf_op jit(solution)/shard_map/ppermute | solution.py:603
  5.6 8.5 %collective-permute-start.2 = (f32[76,128]{1,0:T(8,128)S(1)}, f32[76,128]{1,0:T(8,128)S(1)}, u32[]{:S(2)}, u32[]{:S(2)}) collective-permute-start(f32[76,128]{1,0:T(8,128)S(1)} %get-tuple-element.39), channel_id=1, source_target_pairs={{0,1},{1,0},{2,3},{3,2},{4,5},{5,4},{6,7},{7,6},{8,9},{9,8},{10,11... | collective-permute-start | bytes 116744 | tf_op jit(solution)/shard_map/ppermute | solution.py:603
  7.1 7.0 %collective-permute-start.3 = (f32[76,128]{1,0:T(8,128)S(1)}, f32[76,128]{1,0:T(8,128)S(1)}, u32[]{:S(2)}, u32[]{:S(2)}) collective-permute-start(f32[76,128]{1,0:T(8,128)S(1)} %get-tuple-element.40), channel_id=1, source_target_pairs={{0,3},{1,2},{2,1},{3,0},{4,7},{5,6},{6,5},{7,4},{8,11},{9,10},{10,... | collective-permute-start | bytes 116744 | tf_op jit(solution)/shard_map/ppermute | solution.py:603
  9.6 4.5 %collective-permute-start.4 = (f32[4,128]{1,0:T(4,128)S(1)}, f32[4,128]{1,0:T(4,128)S(1)}, u32[]{:S(2)}, u32[]{:S(2)}) collective-permute-start(f32[4,128]{1,0:T(4,128)S(1)} %get-tuple-element.41.own_ref), channel_id=1, source_target_pairs={{0,2},{1,3},{2,0},{3,1},{4,6},{5,7},{6,4},{7,5},{8,10},{9,11},{10,... | collective-permute-start | bytes 6152 | tf_op jit(solution)/shard_map/ppermute | solution.py:598
  14.2 4.4 %collective-permute-start.5 = (f32[88,128]{1,0:T(8,128)S(1)}, f32[88,128]{1,0:T(8,128)S(1)}, u32[]{:S(2)}, u32[]{:S(2)}) collective-permute-start(f32[88,128]{1,0:T(8,128)S(1)} %get-tuple-element.44), channel_id=1, source_target_pairs={{0,4},{4,0},{8,12},{12,8},{1,5},{5,1},{9,13},{13,9},{2,6},{6,2},{1... | collective-permute-start | bytes 135176 | tf_op jit(solution)/shard_map/ppermute | solution.py:603
  14.3 4.3 %collective-permute-start.6 = (f32[88,128]{1,0:T(8,128)S(1)}, f32[88,128]{1,0:T(8,128)S(1)}, u32[]{:S(2)}, u32[]{:S(2)}) collective-permute-start(f32[88,128]{1,0:T(8,128)S(1)} %get-tuple-element.45), channel_id=1, source_target_pairs={{0,12},{4,8},{8,4},{12,0},{1,13},{5,9},{9,5},{13,1},{2,14},{6,10},... | collective-permute-start | bytes 135176 | tf_op jit(solution)/shard_map/ppermute | solution.py:603
  14.9 3.7 %collective-permute-start.7 = (f32[16,128]{1,0:T(8,128)S(1)}, f32[16,128]{1,0:T(8,128)S(1)}, u32[]{:S(2)}, u32[]{:S(2)}) collective-permute-start(f32[16,128]{1,0:T(8,128)S(1)} %get-tuple-element.46.block_ref), channel_id=1, source_target_pairs={{0,8},{4,12},{8,0},{12,4},{1,9},{5,13},{9,1},{13,5},{2,10},{6,14},... | collective-permute-start | bytes 24584 | tf_op jit(solution)/shard_map/ppermute | solution.py:598
  19.1 8.4 %collective-permute-start.8 = (f32[400,128]{1,0:T(8,128)S(1)}, f32[400,128]{1,0:T(8,128)S(1)}, u32[]{:S(2)}, u32[]{:S(2)}) collective-permute-start(f32[400,128]{1,0:T(8,128)S(1)} %get-tuple-element.50), channel_id=1, source_target_pairs={{0,4},{4,0},{8,12},{12,8},{1,5},{5,1},{9,13},{13,9},{2,6},{6,2},{1... | collective-permute-start | bytes 614408 | tf_op jit(solution)/shard_map/ppermute | solution.py:603
  19.2 8.3 %collective-permute-start.9 = (f32[400,128]{1,0:T(8,128)S(1)}, f32[400,128]{1,0:T(8,128)S(1)}, u32[]{:S(2)}, u32[]{:S(2)}) collective-permute-start(f32[400,128]{1,0:T(8,128)S(1)} %get-tuple-element.51), channel_id=1, source_target_pairs={{0,12},{4,8},{8,4},{12,0},{1,13},{5,9},{9,5},{13,1},{2,14},{6,10},... | collective-permute-start | bytes 614408 | tf_op jit(solution)/shard_map/ppermute | solution.py:603

commit v7 on v6

--- a/solution.py
+++ b/solution.py
@@ -36,13 +36,13 @@
 def pack(*refs):
     count = (len(refs) - 6) // 2
     sources, targets = refs[:count], refs[count : 2 * count]
-    *row_refs, strip_a_ref, strip_b_ref, own_ref, sems = refs[2 * count :]
+    *row_refs, strip_a_ref, strip_b_ref, block_ref, sems = refs[2 * count :]
     copies = [pltpu.make_async_copy(a, b, sems.at[i]) for i, (a, b) in enumerate(zip(sources, targets))]
     for copy in copies:
         copy.start()
     order_ref, map_ref, cot_ref, mob_ref = targets[:4]
     params, layers = order_ref.shape[:2]
-    maps = row_places(params, layers)[0]
+    maps, cots = row_places(params, layers)
     gap = jnp.zeros((LEAD, 128), jnp.float32)
     odd = is_odd("wide")
     odd_y = is_odd("narrow")
@@ -50,8 +50,10 @@
     for ref in row_refs:
         ref[0:LEAD, :] = gap
         ref[maps - LEAD : maps, :] = gap
-        ref[ref.shape[0] - 2 * LEAD : ref.shape[0] - LEAD, :] = gap
-        ref[ref.shape[0] - LEAD :, :] = gap
+        ref[cots - 2 * LEAD : cots - LEAD, :] = gap
+        ref[cots - LEAD : cots, :] = gap
+    row_refs[0][cots : cots + LEAD, :] = gap
+    row_refs[0][row_refs[0].shape[0] - LEAD :, :] = gap
     copies[0].wait()
     for p in range(params):
         for z in range(layers):
@@ -65,6 +67,11 @@
             ref[k : k + MAP_EDGE, :] = map_ref[z, pl.ds((8 - MAP_EDGE) * is_last, MAP_EDGE), :].astype(jnp.float32)
     for copy in copies[2:]:
         copy.wait()
+    rows = pl.ds((8 - ADJ_EDGE) * last[0], ADJ_EDGE)
+    for p in range(params):
+        for z in range(layers):
+            k = cots + LEAD + (p * layers + z) * ADJ_EDGE
+            row_refs[0][k : k + ADJ_EDGE, :] = cot_ref[p, z, rows, :]
 
     lane = lanes((8, 128))
     zero = jnp.zeros((8, 128), jnp.float32)
@@ -86,14 +93,33 @@
         strip_a_ref[rows, :] = jnp.where(odd_y, left, right)
         strip_b_ref[rows, :] = jnp.where(odd_y, right, left)
     owned = mob_ref.shape[1]
-    at = 8 * (params + 1)
-    for i in range(own_ref.shape[0]):
+    owned_rows = -(-owned // 128)
+    block_ref[...] = jnp.zeros_like(block_ref)
+    first = lax.axis_index("narrow") * owned_rows
+    for i in range(owned_rows):
         size = min(128, owned - 128 * i)
         row = mob_ref[0:1, 128 * i : 128 * i + size]
         if size < 128:
             row = jnp.concatenate([row, jnp.zeros((1, 128 - size), jnp.float32)], axis=1)
-        for ref, k in ((own_ref, i), (strip_a_ref, at + i), (strip_b_ref, at + i)):
-            ref[k : k + 1, :] = row
+        block_ref[pl.ds(first + i, 1), :] = row
+    strip_a_ref[8 * (params + 1) :, :] = block_ref[...]
+
+
+def pack_cot(cot_ref, after_ref, out_ref):
+    params, layers = cot_ref.shape[:2]
+    out_ref[0:LEAD, :] = jnp.zeros((LEAD, 128), jnp.float32)
+    out_ref[out_ref.shape[0] - LEAD :, :] = jnp.zeros((LEAD, 128), jnp.float32)
+    rows = pl.ds(jnp.where(is_odd("wide"), 8 - ADJ_EDGE, 0), ADJ_EDGE)
+    for p in range(params):
+        for z in range(layers):
+            k = LEAD + (p * layers + z) * ADJ_EDGE
+            out_ref[k : k + ADJ_EDGE, :] = cot_ref[p, z, rows, :]
+
+
+def pack_second(strip_ref, block_ref, strip_a_ref, slots_ref, out_ref):
+    at = strip_ref.shape[0]
+    out_ref[0:at, :] = strip_ref[...]
+    out_ref[at:, :] = block_ref[...] + strip_a_ref[at:, :]
 
 
 def row_places(params, layers):
@@ -124,22 +150,10 @@
     return order, cot, jnp.where(first, *fields[params])
 
 
-def pieces_back(odd, own, a, b, others):
-    return [own, jnp.where(odd, a, b), *others, jnp.where(odd, b, a)]
-
-
-def pack_far(params, strip_a_ref, strip_b_ref, own_ref, slots_ref, *refs):
-    *other_refs, far_a_ref, far_b_ref, block_ref = refs
-    rows = own_ref.shape[0]
+def pack_far(params, strip_a_ref, strip_b_ref, block_ref, far_a_ref, far_b_ref):
     at = 8 * (params + 1)
-    pieces = pieces_back(
-        is_odd("narrow"), own_ref[...], strip_a_ref[at : at + rows, :], strip_b_ref[at : at + rows, :],
-        [ref[...] for ref in other_refs],
-    )
     mobs = corner_rows(params)
-    for i, piece in enumerate(pieces):
-        for ref, k in ((block_ref, 0), (far_a_ref, mobs), (far_b_ref, mobs)):
-            ref[k + i * rows : k + (i + 1) * rows, :] = piece
+    far_a_ref[mobs:, :] = block_ref[...] + strip_a_ref[at:, :] + strip_b_ref[at:, :]
     at = 0
     odd = is_odd("wide")
     order, cot, cells = merged_strips(params, strip_a_ref, strip_b_ref)
@@ -152,12 +166,25 @@
         ref[at:mobs, :] = jnp.zeros((mobs - at, 128), jnp.float32)
 
 
+def pack_far_second(corner_ref, sent_ref, far_a_ref, out_ref):
+    at = corner_ref.shape[0]
+    size = sent_ref.shape[0] - at
+    out_ref[0:at, :] = corner_ref[...]
+    odd = is_odd("wide")
+    own, other = sent_ref[at:, :], far_a_ref[at:, :]
+    out_ref[at : at + size, :] = jnp.where(odd, other, own)
+    out_ref[at + size :, :] = jnp.where(odd, own, other)
+
+
 def find_slots(bricks_ref, slot_ref, out_ref):
     count, listed = bricks_ref.shape
     rows = slot_ref.shape[0]
-    pad = jnp.zeros((8, 128 - listed), jnp.int32)
-    for k in range(0, count, 8):
-        grain = jnp.concatenate([bricks_ref[k : k + 8, :], pad], axis=1)
+    for k in range(0, out_ref.shape[0], 8):
+        pairs = [
+            jnp.concatenate([bricks_ref[2 * j : 2 * j + 1, :], bricks_ref[2 * j + 1 : 2 * j + 2, :]], axis=1)
+            for j in range(k, k + 8)
+        ]
+        grain = jnp.concatenate(pairs, axis=0)
         row, col = grain >> 7, grain & 127
 
         def body(r, found, row=row, col=col):
@@ -165,63 +192,46 @@
             taken = jnp.take_along_axis(table, col, axis=1, mode="promise_in_bounds")
             return jnp.where(row == r, taken, found)
 
-        found = lax.fori_loop(0, rows, body, jnp.zeros((8, 128), jnp.int32), unroll=7)
-        out_ref[k : k + 8, :] = jnp.where(lanes((8, 128)) < listed, found, -1)
-
-
-def find_mobility(counts, owned, slots_ref, block_ref, far_a_ref, far_b_ref, cot_ref, *refs):
-    *other_refs, table_ref, cot_a_ref, cot_b_ref, near_ref, mob_ref = refs
-    params, layers = cot_ref.shape[:2]
-    odd = is_odd("wide")
-    last = (jnp.where(odd, 0, 1), jnp.where(odd, 1, 0))
-    for ref in (cot_a_ref, cot_b_ref):
-        ref[0:LEAD, :] = jnp.zeros((LEAD, 128), jnp.float32)
-        ref[ref.shape[0] - LEAD :, :] = jnp.zeros((LEAD, 128), jnp.float32)
-    for p in range(params):
-        for z in range(layers):
-            k = LEAD + (p * layers + z) * ADJ_EDGE
-            for ref, is_last in zip((cot_a_ref, cot_b_ref), last):
-                ref[k : k + ADJ_EDGE, :] = cot_ref[p, z, pl.ds((8 - ADJ_EDGE) * is_last, ADJ_EDGE), :]
-
+        out_ref[k : k + 8, :] = lax.fori_loop(0, rows, body, jnp.zeros((8, 128), jnp.int32), unroll=7)
+
+
+def find_mobility(counts, owned, slots_ref, *refs):
+    *mob_refs, table_ref, near_ref, all_ref = refs
     wide_count, narrow_count = counts
     tile = (8, 128)
     wide, narrow = lax.axis_index("wide"), lax.axis_index("narrow")
-    size, at = block_ref.shape[0], corner_rows(params)
-    owned_rows = size // narrow_count
-    pieces = pieces_back(
-        odd, block_ref[...], far_a_ref[at : at + size, :], far_b_ref[at : at + size, :],
-        [ref[...] for ref in other_refs],
-    )
-    for i, piece in enumerate(pieces):
-        mob_ref[i * size : (i + 1) * size, :] = piece
-    for i in range(3):
-        for j in range(3):
-            w = lax.rem(wide + i - 1 + wide_count, wide_count)
-            n = lax.rem(narrow + j - 1 + narrow_count, narrow_count)
-            near_ref[3 * i + j : 3 * i + j + 1, :] = slots_ref[pl.ds(w * narrow_count + n, 1), :]
-    near_ref[9:16, :] = jnp.zeros((7, 128), jnp.int32)
-    slot = [jnp.maximum(near_ref[k : k + 8, :], 0) for k in (0, 8)]
-    owner = [jnp.floor((x.astype(jnp.float32) + 0.5) * (1.0 / owned)).astype(jnp.int32) for x in slot]
-    inner = [x - y * owned for x, y in zip(slot, owner)]
-    by_wide = [jnp.floor((y.astype(jnp.float32) + 0.5) * (1.0 / narrow_count)).astype(jnp.int32) for y in owner]
-    back_w = [wide - y for y in by_wide]
-    back_n = [narrow - (x - y * narrow_count) for x, y in zip(owner, by_wide)]
-    back_w = [jnp.where(x < 0, x + wide_count, x) for x in back_w]
-    back_n = [jnp.where(x < 0, x + narrow_count, x) for x in back_n]
-    row = [(a * narrow_count + b) * owned_rows + (x >> 7) for a, b, x in zip(back_w, back_n, inner)]
-    place = [x & 127 for x in inner]
+    if len(mob_refs) == 1:
+        mob_ref = mob_refs[0]
+    else:
+        sent_ref, got_ref = mob_refs
+        mob_ref = all_ref
+        size = mob_ref.shape[0] // 2
+        upper = wide >= 2
+        own, other = sent_ref[sent_ref.shape[0] - size :, :], got_ref[got_ref.shape[0] - size :, :]
+        mob_ref[0:size, :] = jnp.where(upper, other, own)
+        mob_ref[size:, :] = jnp.where(upper, own, other)
+    near_ref[...] = jnp.zeros_like(near_ref)
+    for k in range(9):
+        w = lax.rem(wide + k // 3 - 1 + wide_count, wide_count)
+        n = lax.rem(narrow + k % 3 - 1 + narrow_count, narrow_count)
+        brick = w * narrow_count + n
+        row = slots_ref[pl.ds(brick >> 1, 1), :]
+        half = jnp.where((brick & 1) == 0, row[:, 0:64], row[:, 64:128])
+        near_ref[k // 2 : k // 2 + 1, 64 * (k % 2) : 64 * (k % 2) + 64] = half
+    slot = near_ref[...]
+    owned_rows = -(-owned // 128)
+    owner = jnp.floor((slot.astype(jnp.float32) + 0.5) * (1.0 / owned)).astype(jnp.int32)
+    inner = slot - owner * owned
+    row = owner * owned_rows + (inner >> 7)
+    place = inner & 127
 
     def body(r, found):
         values = jnp.broadcast_to(mob_ref[pl.ds(r, 1), :], tile)
-        return tuple(
-            jnp.where(row[k] == r, jnp.take_along_axis(values, place[k], axis=1, mode="promise_in_bounds"), found[k])
-            for k in range(2)
-        )
-
-    zero = jnp.zeros(tile, jnp.float32)
-    found = lax.fori_loop(0, mob_ref.shape[0], body, (zero, zero), unroll=16)
-    for k in range(2):
-        table_ref[8 * k : 8 * k + 8, :] = TIME_STEP * found[k]
+        taken = jnp.take_along_axis(values, place, axis=1, mode="promise_in_bounds")
+        return jnp.where(row == r, taken, found)
+
+    found = lax.fori_loop(0, mob_ref.shape[0], body, jnp.zeros(tile, jnp.float32), unroll=16)
+    table_ref[...] = TIME_STEP * found
 
 
 def total_of(values):
@@ -375,15 +385,15 @@
         spread_ends(ends_ref, [first_strip_ref[p, rows, :] for p in every], rows)
 
     def lookup(index, which):
-        values = jnp.broadcast_to(table_ref[which : which + 1, :], tile)
-        return jnp.take_along_axis(values, index, axis=1, mode="promise_in_bounds")
+        values = jnp.broadcast_to(table_ref[which // 2 : which // 2 + 1, :], tile)
+        return jnp.take_along_axis(values, index + 64 * (which % 2), axis=1, mode="promise_in_bounds")
 
     for i in range(3):
         r = 8 * i
         for z in range(layers):
-            index = map_ref[z] if i == 1 else g_ref[z, r : r + 8, :].astype(jnp.int32) & 127
+            index = map_ref[z] if i == 1 else g_ref[z, r : r + 8, :].astype(jnp.int32) & 63
             m_ref[z, r : r + 8, :] = lookup(index, 3 * i + 1)
-        index = gs_ref[r : r + 8, :].astype(jnp.int32) & 127
+        index = gs_ref[r : r + 8, :].astype(jnp.int32) & 63
         ms_ref[r : r + 8, :] = jnp.where(col < 5, lookup(index, 3 * i), lookup(index, 3 * i + 2))
 
     def step(t, windows, strip_windows, end_windows):
@@ -434,10 +444,12 @@
 def backward(
     cot_ref, map_ref, row_a_ref, row_b_ref, far_a_ref, far_b_ref, strip_a_ref, strip_b_ref,
     e_refs, rate_refs, se_refs, m_ref, ms_ref,
-    adjoint_ref, sums_ref,
-    lam_refs, slam_refs, u_refs, su_refs, ends_ref, work_ref, binned_ref,
+    lam_out_ref, u_out_ref, ends_ref, sums_ref,
+    first_lam_ref, slam_refs, first_u_ref, su_refs, work_ref, binned_ref,
 ):
     params, layers = cot_ref.shape[:2]
+    lam_refs, u_refs = (first_lam_ref, lam_out_ref), (first_u_ref, u_out_ref)
+    cots = row_places(params, layers)[1]
     tile = (8, 128)
     every = range(params)
 
@@ -445,11 +457,11 @@
     from_before = (jnp.where(odd, 1, 0), jnp.where(odd, 0, 1))
 
     def place(z, carry):
-        for ref, before in zip((row_a_ref, row_b_ref), from_before):
+        for ref, base, before in zip((row_a_ref, row_b_ref), (cots, 0), from_before):
             rows = pl.ds(16 - 16 * before, 8)
             m = m_ref[z, rows, :]
             for p in every:
-                k = LEAD + (p * layers + z) * ADJ_EDGE + before * (ADJ_EDGE - 8)
+                k = base + LEAD + (p * layers + z) * ADJ_EDGE + before * (ADJ_EDGE - 8)
                 value = ref[pl.ds(k, 8), :]
                 lam_refs[0][p, z, rows, :] = value
                 u_refs[0][p, z, rows, :] = m * value
@@ -483,7 +495,6 @@
 
     def step(t, slot, windows, strip_windows, end_windows):
         old, old_strip = u_refs[slot], su_refs[slot]
-        last = t == 0
 
         def core(z, i, r):
             rows = pl.ds(r, 8)
@@ -493,19 +504,14 @@
             change = changes(e, u, neighbours(old, ends_ref, u, z, r))
             lam = [lam_refs[slot][p, z, rows, :] for p in every]
             work = total_of([lam[p] * rate_refs[t][p, z, rows, :] for p in every])
-            stores = [put(work_ref, (t, z, i), work)]
+            stores = [put(work_ref, (t - 1, z, i), work)]
             for p in every:
                 new = lam[p] - change[p]
-                if last:
-                    stores.append(put(adjoint_ref, (p, z), new))
-                else:
-                    stores.append(put(lam_refs[1 - slot], (p, z, rows, slice(None)), new))
-                    stores.append(put(u_refs[1 - slot], (p, z, rows, slice(None)), m * new))
+                stores.append(put(lam_refs[1 - slot], (p, z, rows, slice(None)), new))
+                stores.append(put(u_refs[1 - slot], (p, z, rows, slice(None)), m * new))
             return stores
 
         each_tile(layers, windows, core)
-        if last:
-            return
 
         def strip(r):
             rows = pl.ds(r, 8)
@@ -525,14 +531,14 @@
     step(3, 0, (4, 2, 12), (4, 2), (4, 2))
     step(2, 1, (4, 2, 12), (4, 2), (4, 2))
     step(1, 0, (4, 2, 12), (8, 1), (8, 1))
-    step(0, 1, (8, 1, 8), None, None)
 
     grains = [map_ref[z] for z in range(layers)]
     cells = []
     for z in range(layers):
-        upper = work_ref[1, z, 0] + work_ref[2, z, 0] + work_ref[3, z, 0]
-        lower = work_ref[1, z, 1] + work_ref[2, z, 1] + work_ref[3, z, 1]
-        cells.append(jnp.concatenate([upper[4:8], lower[0:4]], axis=0) + work_ref[0, z, 0])
+        upper = work_ref[0, z, 0] + work_ref[1, z, 0] + work_ref[2, z, 0]
+        lower = work_ref[0, z, 1] + work_ref[1, z, 1] + work_ref[2, z, 1]
+        first = total_of([lam_out_ref[p, z, 8:16, :] * rate_refs[0][p, z, 8:16, :] for p in every])
+        cells.append(jnp.concatenate([upper[4:8], lower[0:4]], axis=0) + first)
 
     def bin_one(g, carry):
         kept = [jnp.where(grains[z] == g, cells[z], 0.0) for z in range(layers)]
@@ -546,34 +552,45 @@
         ones, binned_ref[...], (((1,), (1,)), ((), ())),
         precision=lax.Precision.HIGHEST, preferred_element_type=jnp.float32,
     )
-    for k in range(0, sums_ref.shape[0], 8):
-        sums_ref[k : k + 8, :] = sums
-
-
-def pick_owned(counts, owned, slots_ref, sums_ref, out_ref, slot_rows, value_rows, total_ref):
-    wide_count, narrow_count = counts
-    count = wide_count * narrow_count
-    wide, narrow = lax.axis_index("wide"), lax.axis_index("narrow")
-    base = (wide * narrow_count + narrow) * owned
-    listed = sums_ref.shape[1]
+    brick = lax.axis_index("wide") * lax.axis_size("narrow") + lax.axis_index("narrow")
+    sub = lax.broadcasted_iota(jnp.int32, tile, 0)
+    here = (sub == ((brick >> 1) & 7)) & ((lanes(tile) >= 64) == ((brick & 1) == 1))
+    sums_ref[...] = jnp.zeros_like(sums_ref)
+    sums_ref[pl.ds(pl.multiple_of(8 * (brick >> 4), 8), 8), :] = jnp.where(
+        here, jnp.concatenate([sums, sums], axis=1), 0.0
+    )
+
+
+def backward_last(first_e_ref, lam_ref, u_ref, ends_ref, adjoint_ref):
+    params, layers = adjoint_ref.shape[:2]
+    every = range(params)
+
+    def core(z, i, r):
+        rows = pl.ds(r, 8)
+        e = [first_e_ref[p, z, rows, :] for p in every]
+        u = [u_ref[p, z, rows, :] for p in every]
+        change = changes(e, u, neighbours(u_ref, ends_ref, u, z, r))
+        return [put(adjoint_ref, (p, z), lam_ref[p, z, rows, :] - change[p]) for p in every]
+
+    each_tile(layers, (8, 1, 8), core)
+
+
+def pick_owned(owned, slots_ref, sums_ref, out_ref, total_ref):
+    base = (lax.axis_index("wide") * lax.axis_size("narrow") + lax.axis_index("narrow")) * owned
     tile = (8, 128)
-    for k in range(count):
-        slot = slots_ref[k : k + 1, :] - base
-        slot_rows[k] = jnp.broadcast_to(slot, tile)
-        value = jnp.concatenate([sums_ref[k : k + 1, :], jnp.zeros((1, 128 - listed), jnp.float32)], axis=1)
-        value_rows[k] = jnp.broadcast_to(value, tile)
     sub = lax.broadcasted_iota(jnp.int32, tile, 0)
     blocks = total_ref.shape[0] // 8
-    step = 16
+    step = 25
     for first in range(0, blocks, step):
         some = range(first, min(first + step, blocks))
 
         def body(k, acc, some=some):
-            slot, value = slot_rows[k], value_rows[k]
-            shifted = slot - sub
+            shifted = jnp.broadcast_to(slots_ref[pl.ds(k, 1), :], tile) - (sub + base)
+            value = jnp.broadcast_to(sums_ref[pl.ds(k, 1), :], tile)
             return tuple(a + jnp.where(shifted == 8 * j, value, 0.0) for a, j in zip(acc, some))
 
-        acc = lax.fori_loop(0, count, body, tuple(jnp.zeros(tile, jnp.float32) for _ in some), unroll=4)
+        zero = tuple(jnp.zeros(tile, jnp.float32) for _ in some)
+        acc = lax.fori_loop(0, slots_ref.shape[0], body, zero, unroll=8)
         for a, j in zip(acc, some):
             total_ref[8 * j : 8 * j + 8, :] = a
     whole = lax.dot_general(
@@ -594,10 +611,6 @@
     )
 
 
-def shifted(value, axis, count, by):
-    return lax.ppermute(value, axis, [(i, (i + by) % count) for i in range(count)])
-
-
 def swapped(value, axis, count, partner):
     step = [1 if (i + partner) % 2 == 0 else -1 for i in range(count)]
     return lax.ppermute(value, axis, [(i, (i + by) % count) for i, by in enumerate(step)])
@@ -613,53 +626,64 @@
 
     both = ("wide", "narrow")
     count = wide_count * narrow_count
+    small = counts == (4, 4)
+    assert listed == 64 and bricks == count and count % 16 == 0
 
     owned_rows = -(-owned // 128)
-    strip_rows = 8 * (params + 1) + owned_rows
+    block_rows = narrow_count * owned_rows
+    strip_rows = 8 * (params + 1)
     edge_rows = row_places(params, layers)[1]
     cot_rows = params * layers * ADJ_EDGE + 2 * LEAD
-    anywhere, here = pl.BlockSpec(memory_space=pl.ANY), pl.BlockSpec(memory_space=pltpu.VMEM)
     vmem = lambda *shape: pltpu.VMEM(shape, jnp.float32)
 
     arguments = (
         order_init, grain_map, cotangent, mobility.reshape(1, owned), brick_grains, grain_slot.reshape(-1, 128)
     )
-    *fetched, row_a, row_b, strip_a, strip_b, own = kernel(
+    *fetched, near_a, row_b, strip_a, strip_b, block = kernel(
         pack,
         tuple(jax.ShapeDtypeStruct(x.shape, x.dtype) for x in arguments)
-        + (f32(edge_rows, 128),) * 2 + (f32(strip_rows, 128),) * 2 + (f32(owned_rows, 128),),
+        + (
+            f32(edge_rows + cot_rows, 128), f32(edge_rows, 128),
+            f32(strip_rows + block_rows, 128), f32(strip_rows, 128), f32(block_rows, 128),
+        ),
         (pltpu.SemaphoreType.DMA((len(arguments),)),), name="pack",
         in_specs=[pl.BlockSpec(memory_space=pltpu.HBM)] * len(arguments),
     )(*(pltpu.with_memory_space_constraint(x, pltpu.HBM) for x in arguments))
     order_init, grain_map, cotangent, _, brick_grains, grain_slot = fetched
     strip_a = swapped(strip_a, "narrow", narrow_count, 0)
+    near_a = swapped(near_a, "wide", wide_count, 0)
+    row_b = swapped(row_b, "wide", wide_count, 1)
+    slots = kernel(
+        find_slots, jax.ShapeDtypeStruct((bricks // 2, 128), jnp.int32), name="find_slots"
+    )(brick_grains, grain_slot)
+
+    here, anywhere = pl.BlockSpec(memory_space=pltpu.VMEM), pl.BlockSpec(memory_space=pl.ANY)
+    strip_b = kernel(
+        pack_second, f32(strip_rows + block_rows, 128), name="pack_second",
+        in_specs=[here, here, here, anywhere],
+    )(strip_b, block, strip_a, slots)
     strip_b = swapped(strip_b, "narrow", narrow_count, 1)
-    row_a = swapped(row_a, "wide", wide_count, 0)
-    row_b = swapped(row_b, "wide", wide_count, 1)
-    others = [shifted(own, "narrow", narrow_count, d) for d in range(2, narrow_count - 1)]
-    slots = kernel(
-        find_slots, jax.ShapeDtypeStruct((bricks, 128), jnp.int32), name="find_slots"
-    )(brick_grains, grain_slot)
-
-    block_rows = narrow_count * owned_rows
-    far_rows = corner_rows(params) + block_rows
-    far_a, far_b, block = kernel(
+    corners = corner_rows(params)
+    sent, corner_b = kernel(
         functools.partial(pack_far, params),
-        (f32(far_rows, 128),) * 2 + (f32(block_rows, 128),),
-        name="pack_far", in_specs=[here] * 3 + [anywhere] + [here] * len(others),
-    )(strip_a, strip_b, own, slots, *others)
-    far_a = swapped(far_a, "wide", wide_count, 0)
-    far_b = swapped(far_b, "wide", wide_count, 1)
-    others = [shifted(block, "wide", wide_count, d) for d in range(2, wide_count - 1)]
-
-    table, cot_a, cot_b = kernel(
-        functools.partial(find_mobility, counts, owned),
-        (f32(16, 128),) + (f32(cot_rows, 128),) * 2,
-        (pltpu.VMEM((16, 128), jnp.int32), vmem(wide_count * block_rows, 128)),
+        (f32(corners + block_rows, 128), f32(corners, 128)), name="pack_far",
+    )(strip_a, strip_b, block)
+    far_a = swapped(sent, "wide", wide_count, 0)
+    sent = kernel(pack_far_second, f32(corners + 2 * block_rows, 128), name="pack_far_second")(corner_b, sent, far_a)
+    far_b = swapped(sent, "wide", wide_count, 1)
+    cot_b = kernel(pack_cot, f32(cot_rows, 128), name="pack_cot", in_specs=[here, anywhere])(cotangent, sent)
+    cot_b = swapped(cot_b, "wide", wide_count, 1)
+
+    if small:
+        mobs = (sent, far_b)
+    else:
+        own = jnp.pad(mobility, (0, -owned % 128)).reshape(owned_rows, 128)
+        mobs = (lax.all_gather(own, both, axis=0, tiled=True),)
+    table = kernel(
+        functools.partial(find_mobility, counts, owned), f32(8, 128),
+        (pltpu.VMEM((8, 128), jnp.int32), vmem(wide_count * block_rows, 128)),
         name="find_mobility",
-    )(slots, block, far_a, far_b, cotangent, *others)
-    cot_a = swapped(cot_a, "wide", wide_count, 0)
-    cot_b = swapped(cot_b, "wide", wide_count, 1)
+    )(slots, *mobs)
 
     padded, strip = (params, layers, ROWS, 128), (params, ROWS, 128)
     final, states, rate, halos, m, ms = kernel(
@@ -670,27 +694,31 @@
         ),
         (vmem(*strip), vmem(*strip), vmem(*padded), vmem(layers, ROWS, 128), vmem(ROWS, 128)),
         name="forward",
-    )(order_init, grain_map, row_a, row_b, far_a, far_b, strip_a, strip_b, table)
-    adjoint, sums = kernel(
+    )(order_init, grain_map, near_a, row_b, far_a, far_b, strip_a, strip_b, table)
+    lam, u, ends, sums = kernel(
         backward,
-        (f32(*order_init.shape), f32(count, listed)),
+        (f32(*padded), f32(*padded), f32(*padded), f32(bricks // 2, 128)),
         (
-            [vmem(*padded)] * 2, [vmem(*strip)] * 2, [vmem(*padded)] * 2, [vmem(*strip)] * 2,
-            vmem(*padded), vmem(ITERS, layers, 2, 8, 128), vmem(listed, 128),
+            vmem(*padded), [vmem(*strip)] * 2, vmem(*padded), [vmem(*strip)] * 2,
+            vmem(ITERS - 1, layers, 2, 8, 128), vmem(listed, 128),
         ),
         name="backward",
     )(
-        cotangent, grain_map, cot_a, cot_b, far_a, far_b, strip_a, strip_b,
+        cotangent, grain_map, near_a, cot_b, far_a, far_b, strip_a, strip_b,
         states, rate, halos, m, ms,
     )
-
-    every_sum = lax.all_to_all(sums, both, 0, 0, tiled=True)
+    adjoint = kernel(backward_last, f32(*order_init.shape), name="backward_last")(states[0], lam, u, ends)
+
+    if small:
+        for axis in both:
+            for partner in range(2):
+                sums = sums + swapped(sums, axis, 4, partner)
+    else:
+        sums = lax.psum(sums, both)
     grads = kernel(
-        functools.partial(pick_owned, counts, owned),
-        f32(1, owned),
-        (pltpu.VMEM((count, 8, 128), jnp.int32), vmem(count, 8, 128), vmem(owned + -owned % 8, 128)),
-        name="pick_owned",
-    )(slots, every_sum)
+        functools.partial(pick_owned, owned), f32(1, owned),
+        (vmem(owned + -owned % 8, 128),), name="pick_owned",
+    )(slots, sums)
     return final, adjoint, grads.reshape(owned)
 
 

time: 45.9 us -> 51.9 us (1.13)
  waiting for transfers between devices: 5.45 us -> 16.3 us
  blocking collectives: 8.91 us -> 0 us
  starting transfers between devices: 11.2 us -> 16.1 us
  Pallas kernels: 19.4 us -> 18.7 us
    ppermute x8 -> x11, waiting for transfers between devices: 0.02 us -> 16.3 us  [swapped(): lax.ppermute(value, axis, [(i, (i + by) % count) for i, by in enumerate(s...]
    all_to_all x1 -> x0, blocking collectives: 8.91 us -> none  [per_device(): every_sum = lax.all_to_all(sums, both, 0, 0, tiled=True)]
    ppermute x8 -> x11, starting transfers between devices: 9.58 us -> 16.1 us  [swapped(): lax.ppermute(value, axis, [(i, (i + by) % count) for i, by in enumerate(s...]
    ppermute x2 -> x0, waiting for transfers between devices: 5.43 us -> none  [shifted(): lax.ppermute(value, axis, [(i, (i + by) % count) for i in range(count)])]
    ppermute x2 -> x0, starting transfers between devices: 1.61 us -> none  [shifted(): lax.ppermute(value, axis, [(i, (i + by) % count) for i in range(count)])]
    pallas_call x5 -> x9, Pallas kernels: 11 us -> 10.2 us  [the longest x1 6.8 us: per_device(): kernel(backward, (f32(*padded), f32(*padded), f32(*padded), f32(bricks //...]
  transfers between devices with their start and end apart: 10 -> 11, of which waited for: 2 -> 8; matrix products, arithmetic and copies ran while one was open for 0% -> 0% of each run, Pallas kernels for 18% -> 17%
where the time goes in v7:
time: 51.9 us; the launch traced here: 51.8 us
  Pallas kernels  18.7 us (36%)
  waiting for transfers between devices  16.3 us (31%)
  starting transfers between devices  16.1 us (31%)
  between operations  0.7 us (1%)
    ppermute x11, waiting for transfers between devices, swapped(): lax.ppermute(value, axis, [(i, (i + by) % count) for i, by in enumerate(s...  16.3 us
    ppermute x11, starting transfers between devices, swapped(): lax.ppermute(value, axis, [(i, (i + by) % count) for i, by in enumerate(s...  16.1 us
    pallas_call x1, Pallas kernels, per_device(): kernel(backward, (f32(*padded), f32(*padded), f32(*padded), f32(bricks //...  6.8 us
    pallas_call x1, Pallas kernels, per_device(): kernel(forward, (f32(*order_init.shape), [f32(*padded)] * ITERS, [f32(*pa...  6.64 us
    pallas_call x1, Pallas kernels, per_device(): kernel(pack, tuple((jax.ShapeDtypeStruct(x.shape, x.dtype) for x in argum...  1.82 us
    pallas_call x1, Pallas kernels, per_device(): kernel(backward_last, f32(*order_init.shape), name='backward_last')  1.08 us
    pallas_call x1, Pallas kernels, per_device(): kernel(functools.partial(pick_owned, owned), f32(1, owned), (vmem(owned +...  1.05 us
  transfers between devices with their start and end apart: 11, of which 8 were waited for; matrix products, arithmetic and copies ran while one was open for 0% of the time, Pallas kernels for 17%

profile of v7, /device:TPU:0, one launch (start us, length us, event | category | flops | bytes accessed | tf_op | source)
XLA Modules:
  0.0 51.8 jit_solution(5931767055660189903)
XLA Ops:
  0.6 1.8 %pack.1 = (f32[8,12,8,128]{3,2,1,0:T(8,128)S(1)}, s32[12,8,128]{2,1,0:T(8,128)S(1)}, f32[8,12,8,128]{3,2,1,0:T(8,128)S(1)}, f32[1,392]{1,0:T(1,128)}, s32[16,64]...) custom-call(f32[8,12,8,128]{3,2,1,0:T(8,128)} %refs_0_.1, ...), custom_call_target="tpu_custom_call" | custom-call | tf_op jit(solution)/shard_map/pack/pallas_call | solution.py:642
  2.5 0.5 %collective-permute-start = (f32[1064,128]{1,0:T(8,128)S(1)}, f32[1064,128]{1,0:T(8,128)S(1)}, u32[]{:S(2)}, u32[]{:S(2)}) collective-permute-start(f32[1064,128]{1,0:T(8,128)S(1)} %get-tuple-element.35), channel_id=1, source_target_pairs={{0,4},{4,0},{8,12},{12,8},{1,5},{5,1},{9,13},{13,9},{2,6},{6,2},{1... | collective-permute-start | bytes 1634312 | tf_op jit(solution)/shard_map/ppermute | solution.py:616
  3.0 2.6 %collective-permute-start.2 = (f32[88,128]{1,0:T(8,128)S(1)}, f32[88,128]{1,0:T(8,128)S(1)}, u32[]{:S(2)}, u32[]{:S(2)}) collective-permute-start(f32[88,128]{1,0:T(8,128)S(1)} %get-tuple-element.37), channel_id=1, source_target_pairs={{0,1},{1,0},{2,3},{3,2},{4,5},{5,4},{6,7},{7,6},{8,9},{9,8},{10,11... | collective-permute-start | bytes 135176 | tf_op jit(solution)/shard_map/ppermute | solution.py:616
  5.6 1.3 %collective-permute-start.1 = (f32[664,128]{1,0:T(8,128)S(1)}, f32[664,128]{1,0:T(8,128)S(1)}, u32[]{:S(2)}, u32[]{:S(2)}) collective-permute-start(f32[664,128]{1,0:T(8,128)S(1)} %get-tuple-element.36), channel_id=1, source_target_pairs={{0,12},{4,8},{8,4},{12,0},{1,13},{5,9},{9,5},{13,1},{2,14},{6,10},... | collective-permute-start | bytes 1019912 | tf_op jit(solution)/shard_map/ppermute | solution.py:616
  6.9 0.6 %find_slots.1.slots_ref = s32[8,128]{1,0:T(8,128)S(1)} custom-call(s32[16,64]{1,0:T(8,128)S(1)} %get-tuple-element.40.bricks_ref, s32[49,128]{1,0:T(8,128)S(1)} %get-tuple-element.41.slot_ref), custom_call_target="tpu_custom_call" | custom-call | tf_op jit(solution)/shard_map/find_slots/pallas_call | solution.py:656
  7.5 0.4 collective-permute-done.2.strip_a_ref
  7.9 3.8 %collective-permute-start.3 = (f32[88,128]{1,0:T(8,128)S(1)}, f32[88,128]{1,0:T(8,128)S(1)}, u32[]{:S(2)}, u32[]{:S(2)}) collective-permute-start(f32[88,128]{1,0:T(8,128)S(1)} %pack_second.1), channel_id=1, source_target_pairs={{0,3},{1,2},{2,1},{3,0},{4,7},{5,6},{6,5},{7,4},{8,11},{9,10},{10,... | collective-permute-start | bytes 135176 | tf_op jit(solution)/shard_map/ppermute | solution.py:616
  11.7 2.1 %collective-permute-done.3.strip_b_ref = f32[88,128]{1,0:T(8,128)S(1)} collective-permute-done((f32[88,128]{1,0:T(8,128)S(1)}, f32[88,128]{1,0:T(8,128)S(1)}, u32[]{:S(2)}, u32[]{:S(2)}) %collective-permute-start.3) | collective-permute-done | bytes 45088 | tf_op jit(solution)/shard_map/ppermute | solution.py:616
  14.0 1.2 %collective-permute-done.4.far_a_ref = f32[88,128]{1,0:T(8,128)S(1)} collective-permute-done((f32[88,128]{1,0:T(8,128)S(1)}, f32[88,128]{1,0:T(8,128)S(1)}, u32[]{:S(2)}, u32[]{:S(2)}) %collective-permute-start.4) | collective-permute-done | bytes 45088 | tf_op jit(solution)/shard_map/ppermute | solution.py:616
  15.2 1.5 %collective-permute-start.6 = (f32[400,128]{1,0:T(8,128)S(1)}, f32[400,128]{1,0:T(8,128)S(1)}, u32[]{:S(2)}, u32[]{:S(2)}) collective-permute-start(f32[400,128]{1,0:T(8,128)S(1)} %pack_cot.1), channel_id=1, source_target_pairs={{0,12},{4,8},{8,4},{12,0},{1,13},{5,9},{9,5},{13,1},{2,14},{6,10},... | collective-permute-start | bytes 614408 | tf_op jit(solution)/shard_map/ppermute | solution.py:616
  16.7 0.3 collective-permute-start.5
  17.0 6.4 %collective-permute-done.5.refs_1_.far_b_ref = f32[104,128]{1,0:T(8,128)S(1)} collective-permute-done((f32[104,128]{1,0:T(8,128)S(1)}, f32[104,128]{1,0:T(8,128)S(1)}, u32[]{:S(2)}, u32[]{:S(2)}) %collective-permute-start.5) | collective-permute-done | bytes 53280 | tf_op jit(solution)/shard_map/ppermute | solution.py:616
  23.5 0.5 find_mobility.1.table_ref
  24.0 6.6 %forward.1 = (f32[8,12,8,128]{3,2,1,0:T(8,128)}, f32[8,12,24,128]{3,2,1,0:T(8,128)S(1)}, f32[8,12,24,128]{3,2,1,0:T(8,128)S(1)}, f32[8,12,24,128]{3,2,1,0:T(8,12...) custom-call(f32[8,12,8,128]{3,2,1,0:T(8,128)S(1)} %get-tuple-element, ...), custom_call_target="tpu_custom_call" | custom-call | tf_op jit(solution)/shard_map/forward/pallas_call | solution.py:689
  30.7 6.8 %backward.1 = (f32[8,12,24,128]{3,2,1,0:T(8,128)S(1)}, f32[8,12,24,128]{3,2,1,0:T(8,128)S(1)}, f32[8,12,24,128]{3,2,1,0:T(8,128)S(1)}, f32[8,128]{1,0:T(8,128)S(1)}) custom-call(f32[8,12,8,128]{3,2,1,0:T(8,128)S(1)} %get-tuple-element.46.cot_ref, s32[12,8,128]{2,1,0:T(8,128)S(1)} %get-tuple-element.34.map_ref, ...), custom_call_target="tpu_custom_call" | custom-call | tf_op jit(solution)/shard_map/backward/pallas_call | solution.py:698
  37.6 1.0 %collective-permute-done.7 = f32[8,128]{1,0:T(8,128)S(1)} collective-permute-done((f32[8,128]{1,0:T(8,128)S(1)}, f32[8,128]{1,0:T(8,128)S(1)}, u32[]{:S(2)}, u32[]{:S(2)}) %collective-permute-start.7) | collective-permute-done | bytes 4128 | tf_op jit(solution)/shard_map/ppermute | solution.py:616
  38.7 1.4 %collective-permute-start.8 = (f32[8,128]{1,0:T(8,128)S(1)}, f32[8,128]{1,0:T(8,128)S(1)}, u32[]{:S(2)}, u32[]{:S(2)}) collective-permute-start(f32[8,128]{1,0:T(8,128)S(1)} %add.12), channel_id=1, source_target_pairs={{0,12},{4,8},{8,4},{12,0},{1,13},{5,9},{9,5},{13,1},{2,14},{6,10},... | collective-permute-start | bytes 12296 | tf_op jit(solution)/shard_map/ppermute | solution.py:616
  40.1 1.6 %collective-permute-done.8 = f32[8,128]{1,0:T(8,128)S(1)} collective-permute-done((f32[8,128]{1,0:T(8,128)S(1)}, f32[8,128]{1,0:T(8,128)S(1)}, u32[]{:S(2)}, u32[]{:S(2)}) %collective-permute-start.8) | collective-permute-done | bytes 4128 | tf_op jit(solution)/shard_map/ppermute | solution.py:616
  41.7 0.6 %collective-permute-start.9 = (f32[8,128]{1,0:T(8,128)S(1)}, f32[8,128]{1,0:T(8,128)S(1)}, u32[]{:S(2)}, u32[]{:S(2)}) collective-permute-start(f32[8,128]{1,0:T(8,128)S(1)} %add.13), channel_id=1, source_target_pairs={{0,1},{1,0},{2,3},{3,2},{4,5},{5,4},{6,7},{7,6},{8,9},{9,8},{10,11... | collective-permute-start | bytes 12296 | tf_op jit(solution)/shard_map/ppermute | solution.py:616
  42.3 3.0 %collective-permute-done.9 = f32[8,128]{1,0:T(8,128)S(1)} collective-permute-done((f32[8,128]{1,0:T(8,128)S(1)}, f32[8,128]{1,0:T(8,128)S(1)}, u32[]{:S(2)}, u32[]{:S(2)}) %collective-permute-start.9) | collective-permute-done | bytes 4128 | tf_op jit(solution)/shard_map/ppermute | solution.py:616
  45.3 3.8 %collective-permute-start.10 = (f32[8,128]{1,0:T(8,128)S(1)}, f32[8,128]{1,0:T(8,128)S(1)}, u32[]{:S(2)}, u32[]{:S(2)}) collective-permute-start(f32[8,128]{1,0:T(8,128)S(1)} %add.14), channel_id=1, source_target_pairs={{0,3},{1,2},{2,1},{3,0},{4,7},{5,6},{6,5},{7,4},{8,11},{9,10},{10,... | collective-permute-start | bytes 12296 | tf_op jit(solution)/shard_map/ppermute | solution.py:616
  49.1 1.1 %backward_last.1 = f32[8,12,8,128]{3,2,1,0:T(8,128)} custom-call(f32[8,12,24,128]{3,2,1,0:T(8,128)S(1)} %get-tuple-element.45.e_refs_0_.first_e_ref, f32[8,12,24,128]{3,2,1,0:T(8,128)S(1)} %get-tuple-element.59.lam_ref, f32[8,12,24,128]{3,2,1,0:T(8,128)S(1)} %get-tuple-element.60.u_ref, f32[8,12,24,128]{3,2,1,0:T(8,128)S(1)} %get-tuple-element.61.ends_ref), custom_call_target="tpu_custom_call" | custom-call | tf_op jit(solution)/shard_map/backward_last/pallas_call | solution.py:710
  50.2 0.6 %collective-permute-done.10 = f32[8,128]{1,0:T(8,128)S(1)} collective-permute-done((f32[8,128]{1,0:T(8,128)S(1)}, f32[8,128]{1,0:T(8,128)S(1)}, u32[]{:S(2)}, u32[]{:S(2)}) %collective-permute-start.10) | collective-permute-done | bytes 4128 | tf_op jit(solution)/shard_map/ppermute | solution.py:616
  50.7 1.1 %pick_owned.1 = f32[1,392]{1,0:T(1,128)} custom-call(s32[8,128]{1,0:T(8,128)S(1)} %find_slots.1.slots_ref, f32[8,128]{1,0:T(8,128)S(1)} %add.15.sums_ref), custom_call_target="tpu_custom_call" | custom-call | tf_op jit(solution)/shard_map/pick_owned/pallas_call | solution.py:718
  (13 shorter events, 0.4 us)
Async XLA Ops:
  2.5 21.6 %collective-permute-start = (f32[1064,128]{1,0:T(8,128)S(1)}, f32[1064,128]{1,0:T(8,128)S(1)}, u32[]{:S(2)}, u32[]{:S(2)}) collective-permute-start(f32[1064,128]{1,0:T(8,128)S(1)} %get-tuple-element.35), channel_id=1, source_target_pairs={{0,4},{4,0},{8,12},{12,8},{1,5},{5,1},{9,13},{13,9},{2,6},{6,2},{1... | collective-permute-start | bytes 1634312 | tf_op jit(solution)/shard_map/ppermute | solution.py:616
  3.0 4.9 %collective-permute-start.2 = (f32[88,128]{1,0:T(8,128)S(1)}, f32[88,128]{1,0:T(8,128)S(1)}, u32[]{:S(2)}, u32[]{:S(2)}) collective-permute-start(f32[88,128]{1,0:T(8,128)S(1)} %get-tuple-element.37), channel_id=1, source_target_pairs={{0,1},{1,0},{2,3},{3,2},{4,5},{5,4},{6,7},{7,6},{8,9},{9,8},{10,11... | collective-permute-start | bytes 135176 | tf_op jit(solution)/shard_map/ppermute | solution.py:616
  5.6 18.4 %collective-permute-start.1 = (f32[664,128]{1,0:T(8,128)S(1)}, f32[664,128]{1,0:T(8,128)S(1)}, u32[]{:S(2)}, u32[]{:S(2)}) collective-permute-start(f32[664,128]{1,0:T(8,128)S(1)} %get-tuple-element.36), channel_id=1, source_target_pairs={{0,12},{4,8},{8,4},{12,0},{1,13},{5,9},{9,5},{13,1},{2,14},{6,10},... | collective-permute-start | bytes 1019912 | tf_op jit(solution)/shard_map/ppermute | solution.py:616
  7.9 5.9 %collective-permute-start.3 = (f32[88,128]{1,0:T(8,128)S(1)}, f32[88,128]{1,0:T(8,128)S(1)}, u32[]{:S(2)}, u32[]{:S(2)}) collective-permute-start(f32[88,128]{1,0:T(8,128)S(1)} %pack_second.1), channel_id=1, source_target_pairs={{0,3},{1,2},{2,1},{3,0},{4,7},{5,6},{6,5},{7,4},{8,11},{9,10},{10,... | collective-permute-start | bytes 135176 | tf_op jit(solution)/shard_map/ppermute | solution.py:616
  13.9 1.3 %collective-permute-start.4 = (f32[88,128]{1,0:T(8,128)S(1)}, f32[88,128]{1,0:T(8,128)S(1)}, u32[]{:S(2)}, u32[]{:S(2)}) collective-permute-start(f32[88,128]{1,0:T(8,128)S(1)} %get-tuple-element.42.sent_ref), channel_id=1, source_target_pairs={{0,4},{4,0},{8,12},{12,8},{1,5},{5,1},{9,13},{13,9},{2,6},{6,2},{1... | collective-permute-start | bytes 135176 | tf_op jit(solution)/shard_map/ppermute | solution.py:616
  15.2 15.4 %collective-permute-start.6 = (f32[400,128]{1,0:T(8,128)S(1)}, f32[400,128]{1,0:T(8,128)S(1)}, u32[]{:S(2)}, u32[]{:S(2)}) collective-permute-start(f32[400,128]{1,0:T(8,128)S(1)} %pack_cot.1), channel_id=1, source_target_pairs={{0,12},{4,8},{8,4},{12,0},{1,13},{5,9},{9,5},{13,1},{2,14},{6,10},... | collective-permute-start | bytes 614408 | tf_op jit(solution)/shard_map/ppermute | solution.py:616
  16.7 6.8 %collective-permute-start.5 = (f32[104,128]{1,0:T(8,128)S(1)}, f32[104,128]{1,0:T(8,128)S(1)}, u32[]{:S(2)}, u32[]{:S(2)}) collective-permute-start(f32[104,128]{1,0:T(8,128)S(1)} %pack_far_second.1.refs_0_.after_ref), channel_id=1, source_target_pairs={{0,12},{4,8},{8,4},{12,0},{1,13},{5,9},{9,5},{13,1},{2,14},{6,10},... | collective-permute-start | bytes 159752 | tf_op jit(solution)/shard_map/ppermute | solution.py:616
  37.5 1.2 %collective-permute-start.7 = (f32[8,128]{1,0:T(8,128)S(1)}, f32[8,128]{1,0:T(8,128)S(1)}, u32[]{:S(2)}, u32[]{:S(2)}) collective-permute-start(f32[8,128]{1,0:T(8,128)S(1)} %get-tuple-element.62), channel_id=1, source_target_pairs={{0,4},{4,0},{8,12},{12,8},{1,5},{5,1},{9,13},{13,9},{2,6},{6,2},{1... | collective-permute-start | bytes 12296 | tf_op jit(solution)/shard_map/ppermute | solution.py:616
  38.7 3.0 %collective-permute-start.8 = (f32[8,128]{1,0:T(8,128)S(1)}, f32[8,128]{1,0:T(8,128)S(1)}, u32[]{:S(2)}, u32[]{:S(2)}) collective-permute-start(f32[8,128]{1,0:T(8,128)S(1)} %add.12), channel_id=1, source_target_pairs={{0,12},{4,8},{8,4},{12,0},{1,13},{5,9},{9,5},{13,1},{2,14},{6,10},... | collective-permute-start | bytes 12296 | tf_op jit(solution)/shard_map/ppermute | solution.py:616
  41.7 3.6 %collective-permute-start.9 = (f32[8,128]{1,0:T(8,128)S(1)}, f32[8,128]{1,0:T(8,128)S(1)}, u32[]{:S(2)}, u32[]{:S(2)}) collective-permute-start(f32[8,128]{1,0:T(8,128)S(1)} %add.13), channel_id=1, source_target_pairs={{0,1},{1,0},{2,3},{3,2},{4,5},{5,4},{6,7},{7,6},{8,9},{9,8},{10,11... | collective-permute-start | bytes 12296 | tf_op jit(solution)/shard_map/ppermute | solution.py:616
  45.3 5.4 %collective-permute-start.10 = (f32[8,128]{1,0:T(8,128)S(1)}, f32[8,128]{1,0:T(8,128)S(1)}, u32[]{:S(2)}, u32[]{:S(2)}) collective-permute-start(f32[8,128]{1,0:T(8,128)S(1)} %add.14), channel_id=1, source_target_pairs={{0,3},{1,2},{2,1},{3,0},{4,7},{5,6},{6,5},{7,4},{8,11},{9,10},{10,... | collective-permute-start | bytes 12296 | tf_op jit(solution)/shard_map/ppermute | solution.py:616

commit v8 on v7

--- a/solution.py
+++ b/solution.py
@@ -33,45 +33,18 @@
     return lax.rem(lax.axis_index(axis), 2) == 1
 
 
-def pack(*refs):
-    count = (len(refs) - 6) // 2
+def pack_strips(*refs):
+    count = (len(refs) - 4) // 2
     sources, targets = refs[:count], refs[count : 2 * count]
-    *row_refs, strip_a_ref, strip_b_ref, block_ref, sems = refs[2 * count :]
+    strip_a_ref, strip_b_ref, block_ref, sems = refs[2 * count :]
     copies = [pltpu.make_async_copy(a, b, sems.at[i]) for i, (a, b) in enumerate(zip(sources, targets))]
     for copy in copies:
         copy.start()
     order_ref, map_ref, cot_ref, mob_ref = targets[:4]
     params, layers = order_ref.shape[:2]
-    maps, cots = row_places(params, layers)
-    gap = jnp.zeros((LEAD, 128), jnp.float32)
-    odd = is_odd("wide")
-    odd_y = is_odd("narrow")
-    last = (jnp.where(odd, 0, 1), jnp.where(odd, 1, 0))
-    for ref in row_refs:
-        ref[0:LEAD, :] = gap
-        ref[maps - LEAD : maps, :] = gap
-        ref[cots - 2 * LEAD : cots - LEAD, :] = gap
-        ref[cots - LEAD : cots, :] = gap
-    row_refs[0][cots : cots + LEAD, :] = gap
-    row_refs[0][row_refs[0].shape[0] - LEAD :, :] = gap
-    copies[0].wait()
-    for p in range(params):
-        for z in range(layers):
-            k = LEAD + (p * layers + z) * EDGE
-            for ref, is_last in zip(row_refs, last):
-                ref[k : k + EDGE, :] = order_ref[p, z, pl.ds((8 - EDGE) * is_last, EDGE), :]
-    copies[1].wait()
-    for z in range(layers):
-        k = maps + z * MAP_EDGE
-        for ref, is_last in zip(row_refs, last):
-            ref[k : k + MAP_EDGE, :] = map_ref[z, pl.ds((8 - MAP_EDGE) * is_last, MAP_EDGE), :].astype(jnp.float32)
-    for copy in copies[2:]:
+    odd = is_odd("narrow")
+    for copy in copies:
         copy.wait()
-    rows = pl.ds((8 - ADJ_EDGE) * last[0], ADJ_EDGE)
-    for p in range(params):
-        for z in range(layers):
-            k = cots + LEAD + (p * layers + z) * ADJ_EDGE
-            row_refs[0][k : k + ADJ_EDGE, :] = cot_ref[p, z, rows, :]
 
     lane = lanes((8, 128))
     zero = jnp.zeros((8, 128), jnp.float32)
@@ -90,8 +63,8 @@
                 right = jnp.where(span(10 * z + 5, 4), roll(cot_ref[field, z], 10 * z + 9), right)
                 left = jnp.where(span(10 * z + 1, 4), roll(cot_ref[field, z], 10 * z + 1), left)
         rows = slice(8 * field, 8 * field + 8)
-        strip_a_ref[rows, :] = jnp.where(odd_y, left, right)
-        strip_b_ref[rows, :] = jnp.where(odd_y, right, left)
+        strip_a_ref[rows, :] = jnp.where(odd, left, right)
+        strip_b_ref[rows, :] = jnp.where(odd, right, left)
     owned = mob_ref.shape[1]
     owned_rows = -(-owned // 128)
     block_ref[...] = jnp.zeros_like(block_ref)
@@ -102,7 +75,38 @@
         if size < 128:
             row = jnp.concatenate([row, jnp.zeros((1, 128 - size), jnp.float32)], axis=1)
         block_ref[pl.ds(first + i, 1), :] = row
-    strip_a_ref[8 * (params + 1) :, :] = block_ref[...]
+    for ref in (strip_a_ref, strip_b_ref):
+        ref[8 * (params + 1) :, :] = block_ref[...]
+
+
+def pack_rows(order_ref, map_ref, cot_ref, after_ref, near_a_ref, row_b_ref):
+    params, layers = order_ref.shape[:2]
+    maps, cots = row_places(params, layers)
+    gap = jnp.zeros((LEAD, 128), jnp.float32)
+    odd = is_odd("wide")
+    last = (jnp.where(odd, 0, 1), jnp.where(odd, 1, 0))
+    row_refs = (near_a_ref, row_b_ref)
+    for ref in row_refs:
+        ref[0:LEAD, :] = gap
+        ref[maps - LEAD : maps, :] = gap
+        ref[cots - 2 * LEAD : cots - LEAD, :] = gap
+        ref[cots - LEAD : cots, :] = gap
+    near_a_ref[cots : cots + LEAD, :] = gap
+    near_a_ref[near_a_ref.shape[0] - LEAD :, :] = gap
+    for p in range(params):
+        for z in range(layers):
+            k = LEAD + (p * layers + z) * EDGE
+            for ref, is_last in zip(row_refs, last):
+                ref[k : k + EDGE, :] = order_ref[p, z, pl.ds((8 - EDGE) * is_last, EDGE), :]
+    for z in range(layers):
+        k = maps + z * MAP_EDGE
+        for ref, is_last in zip(row_refs, last):
+            ref[k : k + MAP_EDGE, :] = map_ref[z, pl.ds((8 - MAP_EDGE) * is_last, MAP_EDGE), :].astype(jnp.float32)
+    rows = pl.ds((8 - ADJ_EDGE) * last[0], ADJ_EDGE)
+    for p in range(params):
+        for z in range(layers):
+            k = cots + LEAD + (p * layers + z) * ADJ_EDGE
+            near_a_ref[k : k + ADJ_EDGE, :] = cot_ref[p, z, rows, :]
 
 
 def pack_cot(cot_ref, after_ref, out_ref):
@@ -116,12 +120,6 @@
             out_ref[k : k + ADJ_EDGE, :] = cot_ref[p, z, rows, :]
 
 
-def pack_second(strip_ref, block_ref, strip_a_ref, slots_ref, out_ref):
-    at = strip_ref.shape[0]
-    out_ref[0:at, :] = strip_ref[...]
-    out_ref[at:, :] = block_ref[...] + strip_a_ref[at:, :]
-
-
 def row_places(params, layers):
     maps = LEAD + params * layers * EDGE + LEAD
     length = maps + layers * MAP_EDGE
@@ -150,10 +148,14 @@
     return order, cot, jnp.where(first, *fields[params])
 
 
-def pack_far(params, strip_a_ref, strip_b_ref, block_ref, far_a_ref, far_b_ref):
+def pack_far(params, strip_a_ref, strip_b_ref, block_ref, *refs):
+    *other_refs, far_a_ref, far_b_ref, out_block_ref = refs
     at = 8 * (params + 1)
     mobs = corner_rows(params)
-    far_a_ref[mobs:, :] = block_ref[...] + strip_a_ref[at:, :] + strip_b_ref[at:, :]
+    block = block_ref[...] + strip_a_ref[at:, :] + strip_b_ref[at:, :]
+    for ref in other_refs:
+        block = block + ref[...]
+    out_block_ref[...] = block
     at = 0
     odd = is_odd("wide")
     order, cot, cells = merged_strips(params, strip_a_ref, strip_b_ref)
@@ -164,19 +166,10 @@
             at += n
     for ref in (far_a_ref, far_b_ref):
         ref[at:mobs, :] = jnp.zeros((mobs - at, 128), jnp.float32)
-
-
-def pack_far_second(corner_ref, sent_ref, far_a_ref, out_ref):
-    at = corner_ref.shape[0]
-    size = sent_ref.shape[0] - at
-    out_ref[0:at, :] = corner_ref[...]
-    odd = is_odd("wide")
-    own, other = sent_ref[at:, :], far_a_ref[at:, :]
-    out_ref[at : at + size, :] = jnp.where(odd, other, own)
-    out_ref[at + size :, :] = jnp.where(odd, own, other)
-
-
-def find_slots(bricks_ref, slot_ref, out_ref):
+        ref[mobs:, :] = block
+
+
+def find_slots(bricks_ref, slot_ref, after_ref, out_ref):
     count, listed = bricks_ref.shape
     rows = slot_ref.shape[0]
     for k in range(0, out_ref.shape[0], 8):
@@ -203,13 +196,16 @@
     if len(mob_refs) == 1:
         mob_ref = mob_refs[0]
     else:
-        sent_ref, got_ref = mob_refs
+        block_ref, far_a_ref, far_b_ref, other_ref = mob_refs
         mob_ref = all_ref
-        size = mob_ref.shape[0] // 2
-        upper = wide >= 2
-        own, other = sent_ref[sent_ref.shape[0] - size :, :], got_ref[got_ref.shape[0] - size :, :]
-        mob_ref[0:size, :] = jnp.where(upper, other, own)
-        mob_ref[size:, :] = jnp.where(upper, own, other)
+        size = block_ref.shape[0]
+        odd = is_odd("wide")
+        step = jnp.where(odd, 1, 3)
+        for place, ref in (
+            (wide, block_ref), (wide + 4 - step, far_a_ref), (wide + step, far_b_ref), (wide + 2, other_ref)
+        ):
+            at = pl.multiple_of(size * (place & 3), size)
+            mob_ref[pl.ds(at, size), :] = ref[ref.shape[0] - size :, :]
     near_ref[...] = jnp.zeros_like(near_ref)
     for k in range(9):
         w = lax.rem(wide + k // 3 - 1 + wide_count, wide_count)
@@ -552,13 +548,8 @@
         ones, binned_ref[...], (((1,), (1,)), ((), ())),
         precision=lax.Precision.HIGHEST, preferred_element_type=jnp.float32,
     )
-    brick = lax.axis_index("wide") * lax.axis_size("narrow") + lax.axis_index("narrow")
-    sub = lax.broadcasted_iota(jnp.int32, tile, 0)
-    here = (sub == ((brick >> 1) & 7)) & ((lanes(tile) >= 64) == ((brick & 1) == 1))
-    sums_ref[...] = jnp.zeros_like(sums_ref)
-    sums_ref[pl.ds(pl.multiple_of(8 * (brick >> 4), 8), 8), :] = jnp.where(
-        here, jnp.concatenate([sums, sums], axis=1), 0.0
-    )
+    for k in range(0, sums_ref.shape[0], 8):
+        sums_ref[k : k + 8, :] = sums
 
 
 def backward_last(first_e_ref, lam_ref, u_ref, ends_ref, adjoint_ref):
@@ -575,9 +566,12 @@
     each_tile(layers, (8, 1, 8), core)
 
 
-def pick_owned(owned, slots_ref, sums_ref, out_ref, total_ref):
+def pick_owned(owned, slots_ref, sums_ref, out_ref, total_ref, dense_ref):
     base = (lax.axis_index("wide") * lax.axis_size("narrow") + lax.axis_index("narrow")) * owned
     tile = (8, 128)
+    for k in range(dense_ref.shape[0]):
+        dense_ref[k : k + 1, 0:64] = sums_ref[2 * k : 2 * k + 1, :]
+        dense_ref[k : k + 1, 64:128] = sums_ref[2 * k + 1 : 2 * k + 2, :]
     sub = lax.broadcasted_iota(jnp.int32, tile, 0)
     blocks = total_ref.shape[0] // 8
     step = 25
@@ -586,7 +580,7 @@
 
         def body(k, acc, some=some):
             shifted = jnp.broadcast_to(slots_ref[pl.ds(k, 1), :], tile) - (sub + base)
-            value = jnp.broadcast_to(sums_ref[pl.ds(k, 1), :], tile)
+            value = jnp.broadcast_to(dense_ref[pl.ds(k, 1), :], tile)
             return tuple(a + jnp.where(shifted == 8 * j, value, 0.0) for a, j in zip(acc, some))
 
         zero = tuple(jnp.zeros(tile, jnp.float32) for _ in some)
@@ -604,11 +598,17 @@
     return jax.ShapeDtypeStruct(shape, jnp.float32)
 
 
-def kernel(body, out_shape, scratch=(), name=None, **specs):
+def kernel(body, out_shape, scratch=(), name=None, cost=0, **specs):
+    if cost:
+        specs["cost_estimate"] = pl.CostEstimate(flops=cost, bytes_accessed=cost // 1000, transcendentals=0)
     return pl.pallas_call(
         body, out_shape=out_shape, scratch_shapes=list(scratch), name=name, **specs,
         compiler_params=pltpu.CompilerParams(vmem_limit_bytes=VMEM_LIMIT),
     )
+
+
+def opposite(value, axis):
+    return lax.ppermute(value, axis, [(i, (i + 2) % 4) for i in range(4)])
 
 
 def swapped(value, axis, count, partner):
@@ -639,50 +639,48 @@
     arguments = (
         order_init, grain_map, cotangent, mobility.reshape(1, owned), brick_grains, grain_slot.reshape(-1, 128)
     )
-    *fetched, near_a, row_b, strip_a, strip_b, block = kernel(
-        pack,
+    here, anywhere = pl.BlockSpec(memory_space=pltpu.VMEM), pl.BlockSpec(memory_space=pl.ANY)
+    *fetched, strip_a, strip_b, block = kernel(
+        pack_strips,
         tuple(jax.ShapeDtypeStruct(x.shape, x.dtype) for x in arguments)
-        + (
-            f32(edge_rows + cot_rows, 128), f32(edge_rows, 128),
-            f32(strip_rows + block_rows, 128), f32(strip_rows, 128), f32(block_rows, 128),
-        ),
-        (pltpu.SemaphoreType.DMA((len(arguments),)),), name="pack",
+        + (f32(strip_rows + block_rows, 128),) * 2 + (f32(block_rows, 128),),
+        (pltpu.SemaphoreType.DMA((len(arguments),)),), name="pack_strips",
         in_specs=[pl.BlockSpec(memory_space=pltpu.HBM)] * len(arguments),
     )(*(pltpu.with_memory_space_constraint(x, pltpu.HBM) for x in arguments))
     order_init, grain_map, cotangent, _, brick_grains, grain_slot = fetched
+    near_a, row_b = kernel(
+        pack_rows, (f32(edge_rows + cot_rows, 128), f32(edge_rows, 128)), name="pack_rows",
+        in_specs=[here] * 3 + [anywhere],
+    )(order_init, grain_map, cotangent, strip_b)
+    strip_b = swapped(strip_b, "narrow", narrow_count, 1)
     strip_a = swapped(strip_a, "narrow", narrow_count, 0)
+    others = [opposite(block, "narrow")] if small else []
     near_a = swapped(near_a, "wide", wide_count, 0)
     row_b = swapped(row_b, "wide", wide_count, 1)
+
+    corners = corner_rows(params)
+    far_a, far_b, block = kernel(
+        functools.partial(pack_far, params),
+        (f32(corners + block_rows, 128),) * 2 + (f32(block_rows, 128),), name="pack_far", cost=100_000_000_000,
+    )(strip_a, strip_b, block, *others)
+    far_b = swapped(far_b, "wide", wide_count, 1)
+    far_a = swapped(far_a, "wide", wide_count, 0)
     slots = kernel(
-        find_slots, jax.ShapeDtypeStruct((bricks // 2, 128), jnp.int32), name="find_slots"
-    )(brick_grains, grain_slot)
-
-    here, anywhere = pl.BlockSpec(memory_space=pltpu.VMEM), pl.BlockSpec(memory_space=pl.ANY)
-    strip_b = kernel(
-        pack_second, f32(strip_rows + block_rows, 128), name="pack_second",
-        in_specs=[here, here, here, anywhere],
-    )(strip_b, block, strip_a, slots)
-    strip_b = swapped(strip_b, "narrow", narrow_count, 1)
-    corners = corner_rows(params)
-    sent, corner_b = kernel(
-        functools.partial(pack_far, params),
-        (f32(corners + block_rows, 128), f32(corners, 128)), name="pack_far",
-    )(strip_a, strip_b, block)
-    far_a = swapped(sent, "wide", wide_count, 0)
-    sent = kernel(pack_far_second, f32(corners + 2 * block_rows, 128), name="pack_far_second")(corner_b, sent, far_a)
-    far_b = swapped(sent, "wide", wide_count, 1)
-    cot_b = kernel(pack_cot, f32(cot_rows, 128), name="pack_cot", in_specs=[here, anywhere])(cotangent, sent)
+        find_slots, jax.ShapeDtypeStruct((bricks // 2, 128), jnp.int32), name="find_slots",
+        in_specs=[here, here, anywhere],
+    )(brick_grains, grain_slot, block)
+    cot_b = kernel(pack_cot, f32(cot_rows, 128), name="pack_cot", in_specs=[here, anywhere])(cotangent, far_a)
     cot_b = swapped(cot_b, "wide", wide_count, 1)
 
     if small:
-        mobs = (sent, far_b)
+        mobs = (block, far_a, far_b, opposite(block, "wide"))
     else:
         own = jnp.pad(mobility, (0, -owned % 128)).reshape(owned_rows, 128)
         mobs = (lax.all_gather(own, both, axis=0, tiled=True),)
     table = kernel(
         functools.partial(find_mobility, counts, owned), f32(8, 128),
         (pltpu.VMEM((8, 128), jnp.int32), vmem(wide_count * block_rows, 128)),
-        name="find_mobility",
+        name="find_mobility", cost=3_000_000_000,
     )(slots, *mobs)
 
     padded, strip = (params, layers, ROWS, 128), (params, ROWS, 128)
@@ -693,11 +691,11 @@
             [f32(*strip)] * (ITERS - 1), f32(layers, ROWS, 128), f32(ROWS, 128),
         ),
         (vmem(*strip), vmem(*strip), vmem(*padded), vmem(layers, ROWS, 128), vmem(ROWS, 128)),
-        name="forward",
+        name="forward", cost=0,
     )(order_init, grain_map, near_a, row_b, far_a, far_b, strip_a, strip_b, table)
     lam, u, ends, sums = kernel(
         backward,
-        (f32(*padded), f32(*padded), f32(*padded), f32(bricks // 2, 128)),
+        (f32(*padded), f32(*padded), f32(*padded), f32(bricks, listed)),
         (
             vmem(*padded), [vmem(*strip)] * 2, vmem(*padded), [vmem(*strip)] * 2,
             vmem(ITERS - 1, layers, 2, 8, 128), vmem(listed, 128),
@@ -709,15 +707,10 @@
     )
     adjoint = kernel(backward_last, f32(*order_init.shape), name="backward_last")(states[0], lam, u, ends)
 
-    if small:
-        for axis in both:
-            for partner in range(2):
-                sums = sums + swapped(sums, axis, 4, partner)
-    else:
-        sums = lax.psum(sums, both)
+    sums = lax.all_to_all(sums, both, 0, 0, tiled=True)
     grads = kernel(
         functools.partial(pick_owned, owned), f32(1, owned),
-        (vmem(owned + -owned % 8, 128),), name="pick_owned",
+        (vmem(owned + -owned % 8, 128), vmem(bricks // 2, 128)), name="pick_owned",
     )(slots, sums)
     return final, adjoint, grads.reshape(owned)
 

time: 51.9 us -> 48.3 us (0.931)
  waiting for transfers between devices: 16.3 us -> 9.95 us
  local copies, waits for them, and re-layouts: 0 us -> 2.94 us
  starting transfers between devices: 16.1 us -> 15.5 us
    ppermute x11 -> x7, waiting for transfers between devices: 16.3 us -> 0.02 us  [swapped(): lax.ppermute(value, axis, [(i, (i + by) % count) for i, by in enumerate(s...]
    ppermute x11 -> x7, starting transfers between devices: 16.1 us -> 9.86 us  [swapped(): lax.ppermute(value, axis, [(i, (i + by) % count) for i, by in enumerate(s...]
    ppermute x0 -> x2, waiting for transfers between devices: none -> 5.89 us  [opposite(): return lax.ppermute(value, axis, [(i, (i + 2) % 4) for i in range(4)])]
    all_to_all x0 -> x1, starting transfers between devices: none -> 4.98 us  [per_device(): sums = lax.all_to_all(sums, both, 0, 0, tiled=True)]
    all_to_all x0 -> x1, waiting for transfers between devices: none -> 4.05 us  [per_device(): sums = lax.all_to_all(sums, both, 0, 0, tiled=True)]
    unnamed x0 -> x6, local copies, waits for them, and re-layouts: none -> 2.94 us
    ppermute x0 -> x2, starting transfers between devices: none -> 0.65 us  [opposite(): return lax.ppermute(value, axis, [(i, (i + 2) % 4) for i in range(4)])]
    pallas_call x4 -> x3, Pallas kernels: 8.63 us -> 8.8 us  [the longest x1 6.91 us: per_device(): kernel(backward, (f32(*padded), f32(*padded), f32(*padded), f32(bricks, l...]
  transfers between devices with their start and end apart: 11 -> 10, of which waited for: 8 -> 3; matrix products, arithmetic and copies ran while one was open for 0% -> 0% of each run, Pallas kernels for 17% -> 19%
where the time goes in v8:
time: 48.3 us; the launch traced here: 48 us
  Pallas kernels  18.9 us (39%)
  starting transfers between devices  15.5 us (32%)
  waiting for transfers between devices  9.95 us (21%)
  local copies, waits for them, and re-layouts  2.94 us (6%)
  between operations  0.72 us (1%)
    ppermute x7, starting transfers between devices, swapped(): lax.ppermute(value, axis, [(i, (i + by) % count) for i, by in enumerate(s...  9.86 us
    pallas_call x1, Pallas kernels, per_device(): kernel(backward, (f32(*padded), f32(*padded), f32(*padded), f32(bricks, l...  6.91 us
    pallas_call x1, Pallas kernels, per_device(): kernel(forward, (f32(*order_init.shape), [f32(*padded)] * ITERS, [f32(*pa...  6.68 us
    ppermute x2, waiting for transfers between devices, opposite(): return lax.ppermute(value, axis, [(i, (i + 2) % 4) for i in range(4)])  5.89 us
    all_to_all x1, starting transfers between devices, per_device(): sums = lax.all_to_all(sums, both, 0, 0, tiled=True)  4.98 us
    all_to_all x1, waiting for transfers between devices, per_device(): sums = lax.all_to_all(sums, both, 0, 0, tiled=True)  4.05 us
    unnamed x6, local copies, waits for them, and re-layouts  2.94 us
    pallas_call x1, Pallas kernels, per_device(): kernel(pack_strips, tuple((jax.ShapeDtypeStruct(x.shape, x.dtype) for x i...  1.78 us
  transfers between devices with their start and end apart: 10, of which 3 were waited for; matrix products, arithmetic and copies ran while one was open for 0% of the time, Pallas kernels for 19%

profile of v8, /device:TPU:0, one launch (start us, length us, event | category | flops | bytes accessed | tf_op | source)
XLA Modules:
  0.0 48.0 jit_solution(4219008433807384071)
XLA Ops:
  0.6 1.8 %pack_strips.1 = (f32[8,12,8,128]{3,2,1,0:T(8,128)S(1)}, s32[12,8,128]{2,1,0:T(8,128)S(1)}, f32[8,12,8,128]{3,2,1,0:T(8,128)S(1)}, f32[1,392]{1,0:T(1,128)}, s32...) custom-call(f32[8,12,8,128]{3,2,1,0:T(8,128)} %refs_0_.1, ...), custom_call_target="tpu_custom_call" | custom-call | tf_op jit(solution)/shard_map/pack_strips/pallas_call | solution.py:643
  2.4 3.1 %collective-permute-start.2 = (f32[88,128]{1,0:T(8,128)S(1)}, f32[88,128]{1,0:T(8,128)S(1)}, u32[]{:S(2)}, u32[]{:S(2)}) collective-permute-start(f32[88,128]{1,0:T(8,128)S(1)} %get-tuple-element.40), channel_id=1, source_target_pairs={{0,1},{1,0},{2,3},{3,2},{4,5},{5,4},{6,7},{7,6},{8,9},{9,8},{10,11... | collective-permute-start | bytes 135176 | tf_op jit(solution)/shard_map/ppermute | solution.py:616
  5.5 2.5 %collective-permute-start.3 = (f32[88,128]{1,0:T(8,128)S(1)}, f32[88,128]{1,0:T(8,128)S(1)}, u32[]{:S(2)}, u32[]{:S(2)}) collective-permute-start(f32[88,128]{1,0:T(8,128)S(1)} %get-tuple-element.37.after_ref), channel_id=1, source_target_pairs={{0,3},{1,2},{2,1},{3,0},{4,7},{5,6},{6,5},{7,4},{8,11},{9,10},{10,... | collective-permute-start | bytes 135176 | tf_op jit(solution)/shard_map/ppermute | solution.py:616
  8.0 0.1 collective-permute-start.4
  8.1 0.1 pack_rows.1
  8.2 0.4 collective-permute-start.1
  8.7 1.2 %collective-permute-start = (f32[1064,128]{1,0:T(8,128)S(1)}, f32[1064,128]{1,0:T(8,128)S(1)}, u32[]{:S(2)}, u32[]{:S(2)}) collective-permute-start(f32[1064,128]{1,0:T(8,128)S(1)} %get-tuple-element.38), channel_id=1, source_target_pairs={{0,4},{4,0},{8,12},{12,8},{1,5},{5,1},{9,13},{13,9},{2,6},{6,2},{1... | collective-permute-start | bytes 1634312 | tf_op jit(solution)/shard_map/ppermute | solution.py:616
  9.9 2.6 %collective-permute-done.4.refs_0_ = f32[16,128]{1,0:T(8,128)S(1)} collective-permute-done((f32[16,128]{1,0:T(8,128)S(1)}, f32[16,128]{1,0:T(8,128)S(1)}, u32[]{:S(2)}, u32[]{:S(2)}) %collective-permute-start.4) | collective-permute-done | bytes 8224 | tf_op jit(solution)/shard_map/ppermute | solution.py:611
  12.5 0.1 pack_far.1
  12.7 1.6 %collective-permute-start.6 = (f32[88,128]{1,0:T(8,128)S(1)}, f32[88,128]{1,0:T(8,128)S(1)}, u32[]{:S(2)}, u32[]{:S(2)}) collective-permute-start(f32[88,128]{1,0:T(8,128)S(1)} %get-tuple-element.43), channel_id=1, source_target_pairs={{0,12},{4,8},{8,4},{12,0},{1,13},{5,9},{9,5},{13,1},{2,14},{6,10},... | collective-permute-start | bytes 135176 | tf_op jit(solution)/shard_map/ppermute | solution.py:616
  14.3 0.5 %collective-permute-start.7 = (f32[16,128]{1,0:T(8,128)S(1)}, f32[16,128]{1,0:T(8,128)S(1)}, u32[]{:S(2)}, u32[]{:S(2)}) collective-permute-start(f32[16,128]{1,0:T(8,128)S(1)} %get-tuple-element.46.after_ref.refs_0_), channel_id=1, source_target_pairs={{0,8},{4,12},{8,0},{12,4},{1,9},{5,13},{9,1},{13,5},{2,10},{6,14},... | collective-permute-start | bytes 24584 | tf_op jit(solution)/shard_map/ppermute | solution.py:611
  14.9 0.6 %find_slots.1.slots_ref = s32[8,128]{1,0:T(8,128)S(1)} custom-call(s32[16,64]{1,0:T(8,128)S(1)} %get-tuple-element.44.bricks_ref, s32[49,128]{1,0:T(8,128)S(1)} %get-tuple-element.45.slot_ref, f32[16,128]{1,0:T(8,128)S(1)} %get-tuple-element.46.after_ref.refs_0_), custom_call_target="tpu_custom_call" | custom-call | tf_op jit(solution)/shard_map/find_slots/pallas_call | solution.py:668
  15.6 0.9 %collective-permute-start.8 = (f32[400,128]{1,0:T(8,128)S(1)}, f32[400,128]{1,0:T(8,128)S(1)}, u32[]{:S(2)}, u32[]{:S(2)}) collective-permute-start(f32[400,128]{1,0:T(8,128)S(1)} %pack_cot.1), channel_id=1, source_target_pairs={{0,12},{4,8},{8,4},{12,0},{1,13},{5,9},{9,5},{13,1},{2,14},{6,10},... | collective-permute-start | bytes 614408 | tf_op jit(solution)/shard_map/ppermute | solution.py:616
  16.5 3.2 %collective-permute-done.7.refs_3_ = f32[16,128]{1,0:T(8,128)S(1)} collective-permute-done((f32[16,128]{1,0:T(8,128)S(1)}, f32[16,128]{1,0:T(8,128)S(1)}, u32[]{:S(2)}, u32[]{:S(2)}) %collective-permute-start.7) | collective-permute-done | bytes 8224 | tf_op jit(solution)/shard_map/ppermute | solution.py:611
  19.7 0.5 %find_mobility.1.table_ref = f32[8,128]{1,0:T(8,128)S(1)} custom-call(s32[8,128]{1,0:T(8,128)S(1)} %find_slots.1.slots_ref, f32[16,128]{1,0:T(8,128)S(1)} %get-tuple-element.46.after_ref.refs_0_, f32[88,128]{1,0:T(8,128)S(1)} %collective-permute-done.5.refs_1_.far_a_ref.after_ref, f32[88,128]{1,0:T(8,128)S(1)} %collective-permute-done.6.refs_2_.far_b_ref, ...), custom_call_target="tpu_custom_call" | custom-call | flops 3000000000 | bytes 3000000 | tf_op jit(solution)/shard_map/find_mobility/pallas_call | solution.py:680
  20.3 6.7 %forward.1 = (f32[8,12,8,128]{3,2,1,0:T(8,128)}, f32[8,12,24,128]{3,2,1,0:T(8,128)S(1)}, f32[8,12,24,128]{3,2,1,0:T(8,128)S(1)}, f32[8,12,24,128]{3,2,1,0:T(8,12...) custom-call(f32[8,12,8,128]{3,2,1,0:T(8,128)S(1)} %get-tuple-element, ...), custom_call_target="tpu_custom_call" | custom-call | tf_op jit(solution)/shard_map/forward/pallas_call | solution.py:687
  27.0 6.9 %backward.1 = (f32[8,12,24,128]{3,2,1,0:T(8,128)S(1)}, f32[8,12,24,128]{3,2,1,0:T(8,128)S(1)}, f32[8,12,24,128]{3,2,1,0:T(8,128)S(1)}, f32[16,64]{1,0:T(8,128)S(1)}) custom-call(f32[8,12,8,128]{3,2,1,0:T(8,128)S(1)} %get-tuple-element.36.cot_ref, s32[12,8,128]{2,1,0:T(8,128)S(1)} %get-tuple-element.35.map_ref, ...), custom_call_target="tpu_custom_call" | custom-call | tf_op jit(solution)/shard_map/backward/pallas_call | solution.py:696
  33.9 1.1 %copy-done = f32[8,12,24,128]{3,2,1,0:T(8,128)} copy-done((f32[8,12,24,128]{3,2,1,0:T(8,128)}, f32[8,12,24,128]{3,2,1,0:T(8,128)S(1)}, u32[]{:S(2)}) %copy-start) | copy-done | bytes 1179672
  35.0 0.6 %copy-done.2 = f32[16,64]{1,0:T(8,128)} copy-done((f32[16,64]{1,0:T(8,128)}, f32[16,64]{1,0:T(8,128)S(1)}, u32[]{:S(2)}) %copy-start.2) | copy-done | bytes 4120
  35.6 5.0 %all-to-all-start = ((f32[16,1,64]{2,1,0:T(1,128)}), f32[16,1,64]{2,1,0:T(1,128)S(1)}, u32[]{:S(2)}, u32[]{:S(2)}) async-start(f32[16,1,64]{2,1,0:T(1,128)} %bitcast.8), calls=%async_computation | async-start | bytes 16384 | tf_op jit(solution)/shard_map/all_to_all | solution.py:710
  40.5 1.3 %copy-done.1 = f32[8,12,24,128]{3,2,1,0:T(8,128)S(1)} copy-done((f32[8,12,24,128]{3,2,1,0:T(8,128)S(1)}, f32[8,12,24,128]{3,2,1,0:T(8,128)}, u32[]{:S(2)}) %copy-start.1) | copy-done | bytes 1179672
  41.8 1.1 %backward_last.1 = f32[8,12,8,128]{3,2,1,0:T(8,128)} custom-call(f32[8,12,24,128]{3,2,1,0:T(8,128)S(1)} %get-tuple-element.48.e_refs_0_.first_e_ref, f32[8,12,24,128]{3,2,1,0:T(8,128)S(1)} %get-tuple-element.61.lam_ref, f32[8,12,24,128]{3,2,1,0:T(8,128)S(1)} %get-tuple-element.62.u_ref, f32[8,12,24,128]{3,2,1,0:T(8,128)S(1)} %copy-done.1), custom_call_target="tpu_custom_call" | custom-call | tf_op jit(solution)/shard_map/backward_last/pallas_call | solution.py:708
  42.9 4.0 %all-to-all-done = f32[16,1,64]{2,1,0:T(1,128)S(1)} async-done(((f32[16,1,64]{2,1,0:T(1,128)}), f32[16,1,64]{2,1,0:T(1,128)S(1)}, u32[]{:S(2)}, u32[]{:S(2)}) %all-to-all-start) | async-done | bytes 4128 | tf_op jit(solution)/shard_map/all_to_all | solution.py:710
  46.9 1.1 %pick_owned.1 = f32[1,392]{1,0:T(1,128)} custom-call(s32[8,128]{1,0:T(8,128)S(1)} %find_slots.1.slots_ref, f32[16,64]{1,0:T(8,128)S(1)} %bitcast.7), custom_call_target="tpu_custom_call" | custom-call | tf_op jit(solution)/shard_map/pick_owned/pallas_call | solution.py:711
  (12 shorter events, 0.1 us)
Async XLA Ops:
  2.4 10.1 %collective-permute-start.2 = (f32[88,128]{1,0:T(8,128)S(1)}, f32[88,128]{1,0:T(8,128)S(1)}, u32[]{:S(2)}, u32[]{:S(2)}) collective-permute-start(f32[88,128]{1,0:T(8,128)S(1)} %get-tuple-element.40), channel_id=1, source_target_pairs={{0,1},{1,0},{2,3},{3,2},{4,5},{5,4},{6,7},{7,6},{8,9},{9,8},{10,11... | collective-permute-start | bytes 135176 | tf_op jit(solution)/shard_map/ppermute | solution.py:616
  5.5 7.0 %collective-permute-start.3 = (f32[88,128]{1,0:T(8,128)S(1)}, f32[88,128]{1,0:T(8,128)S(1)}, u32[]{:S(2)}, u32[]{:S(2)}) collective-permute-start(f32[88,128]{1,0:T(8,128)S(1)} %get-tuple-element.37.after_ref), channel_id=1, source_target_pairs={{0,3},{1,2},{2,1},{3,0},{4,7},{5,6},{6,5},{7,4},{8,11},{9,10},{10,... | collective-permute-start | bytes 135176 | tf_op jit(solution)/shard_map/ppermute | solution.py:616
  8.0 4.5 %collective-permute-start.4 = (f32[16,128]{1,0:T(8,128)S(1)}, f32[16,128]{1,0:T(8,128)S(1)}, u32[]{:S(2)}, u32[]{:S(2)}) collective-permute-start(f32[16,128]{1,0:T(8,128)S(1)} %get-tuple-element.41.block_ref), channel_id=1, source_target_pairs={{0,2},{1,3},{2,0},{3,1},{4,6},{5,7},{6,4},{7,5},{8,10},{9,11},{10,... | collective-permute-start | bytes 24584 | tf_op jit(solution)/shard_map/ppermute | solution.py:611
  8.2 12.0 %collective-permute-start.1 = (f32[664,128]{1,0:T(8,128)S(1)}, f32[664,128]{1,0:T(8,128)S(1)}, u32[]{:S(2)}, u32[]{:S(2)}) collective-permute-start(f32[664,128]{1,0:T(8,128)S(1)} %get-tuple-element.39), channel_id=1, source_target_pairs={{0,12},{4,8},{8,4},{12,0},{1,13},{5,9},{9,5},{13,1},{2,14},{6,10},... | collective-permute-start | bytes 1019912 | tf_op jit(solution)/shard_map/ppermute | solution.py:616
  8.7 11.6 %collective-permute-start = (f32[1064,128]{1,0:T(8,128)S(1)}, f32[1064,128]{1,0:T(8,128)S(1)}, u32[]{:S(2)}, u32[]{:S(2)}) collective-permute-start(f32[1064,128]{1,0:T(8,128)S(1)} %get-tuple-element.38), channel_id=1, source_target_pairs={{0,4},{4,0},{8,12},{12,8},{1,5},{5,1},{9,13},{13,9},{2,6},{6,2},{1... | collective-permute-start | bytes 1634312 | tf_op jit(solution)/shard_map/ppermute | solution.py:616
  12.6 2.8 %collective-permute-start.5 = (f32[88,128]{1,0:T(8,128)S(1)}, f32[88,128]{1,0:T(8,128)S(1)}, u32[]{:S(2)}, u32[]{:S(2)}) collective-permute-start(f32[88,128]{1,0:T(8,128)S(1)} %get-tuple-element.42), channel_id=1, source_target_pairs={{0,4},{4,0},{8,12},{12,8},{1,5},{5,1},{9,13},{13,9},{2,6},{6,2},{1... | collective-permute-start | bytes 135176 | tf_op jit(solution)/shard_map/ppermute | solution.py:616
  12.7 7.0 %collective-permute-start.6 = (f32[88,128]{1,0:T(8,128)S(1)}, f32[88,128]{1,0:T(8,128)S(1)}, u32[]{:S(2)}, u32[]{:S(2)}) collective-permute-start(f32[88,128]{1,0:T(8,128)S(1)} %get-tuple-element.43), channel_id=1, source_target_pairs={{0,12},{4,8},{8,4},{12,0},{1,13},{5,9},{9,5},{13,1},{2,14},{6,10},... | collective-permute-start | bytes 135176 | tf_op jit(solution)/shard_map/ppermute | solution.py:616
  14.3 5.4 %collective-permute-start.7 = (f32[16,128]{1,0:T(8,128)S(1)}, f32[16,128]{1,0:T(8,128)S(1)}, u32[]{:S(2)}, u32[]{:S(2)}) collective-permute-start(f32[16,128]{1,0:T(8,128)S(1)} %get-tuple-element.46.after_ref.refs_0_), channel_id=1, source_target_pairs={{0,8},{4,12},{8,0},{12,4},{1,9},{5,13},{9,1},{13,5},{2,10},{6,14},... | collective-permute-start | bytes 24584 | tf_op jit(solution)/shard_map/ppermute | solution.py:611
  15.6 11.4 %collective-permute-start.8 = (f32[400,128]{1,0:T(8,128)S(1)}, f32[400,128]{1,0:T(8,128)S(1)}, u32[]{:S(2)}, u32[]{:S(2)}) collective-permute-start(f32[400,128]{1,0:T(8,128)S(1)} %pack_cot.1), channel_id=1, source_target_pairs={{0,12},{4,8},{8,4},{12,0},{1,13},{5,9},{9,5},{13,1},{2,14},{6,10},... | collective-permute-start | bytes 614408 | tf_op jit(solution)/shard_map/ppermute | solution.py:616
  33.9 1.1 %copy-start = (f32[8,12,24,128]{3,2,1,0:T(8,128)}, f32[8,12,24,128]{3,2,1,0:T(8,128)S(1)}, u32[]{:S(2)}) copy-start(f32[8,12,24,128]{3,2,1,0:T(8,128)S(1)} %get-tuple-element.63.ends_ref) | copy-start | bytes 3538948
  35.0 0.6 %copy-start.2 = (f32[16,64]{1,0:T(8,128)}, f32[16,64]{1,0:T(8,128)S(1)}, u32[]{:S(2)}) copy-start(f32[16,64]{1,0:T(8,128)S(1)} %get-tuple-element.64) | copy-start | bytes 12292
  35.6 11.4 %all-to-all-start = ((f32[16,1,64]{2,1,0:T(1,128)}), f32[16,1,64]{2,1,0:T(1,128)S(1)}, u32[]{:S(2)}, u32[]{:S(2)}) async-start(f32[16,1,64]{2,1,0:T(1,128)} %bitcast.8), calls=%async_computation | async-start | bytes 16384 | tf_op jit(solution)/shard_map/all_to_all | solution.py:710
  40.5 1.3 %copy-start.1 = (f32[8,12,24,128]{3,2,1,0:T(8,128)S(1)}, f32[8,12,24,128]{3,2,1,0:T(8,128)}, u32[]{:S(2)}) copy-start(f32[8,12,24,128]{3,2,1,0:T(8,128)} %copy-done) | copy-start | bytes 3538948

commit v9 on v8

--- a/solution.py
+++ b/solution.py
@@ -75,8 +75,7 @@
         if size < 128:
             row = jnp.concatenate([row, jnp.zeros((1, 128 - size), jnp.float32)], axis=1)
         block_ref[pl.ds(first + i, 1), :] = row
-    for ref in (strip_a_ref, strip_b_ref):
-        ref[8 * (params + 1) :, :] = block_ref[...]
+    strip_b_ref[8 * (params + 1) :, :] = block_ref[...]
 
 
 def pack_rows(order_ref, map_ref, cot_ref, after_ref, near_a_ref, row_b_ref):
@@ -109,6 +108,12 @@
             near_a_ref[k : k + ADJ_EDGE, :] = cot_ref[p, z, rows, :]
 
 
+def pack_second(strip_ref, block_ref, strip_b_ref, out_ref):
+    at = strip_ref.shape[0]
+    out_ref[0:at, :] = strip_ref[...]
+    out_ref[at:, :] = block_ref[...] + strip_b_ref[at:, :]
+
+
 def pack_cot(cot_ref, after_ref, out_ref):
     params, layers = cot_ref.shape[:2]
     out_ref[0:LEAD, :] = jnp.zeros((LEAD, 128), jnp.float32)
@@ -149,12 +154,10 @@
 
 
 def pack_far(params, strip_a_ref, strip_b_ref, block_ref, *refs):
-    *other_refs, far_a_ref, far_b_ref, out_block_ref = refs
+    far_a_ref, far_b_ref, out_block_ref = refs
     at = 8 * (params + 1)
     mobs = corner_rows(params)
     block = block_ref[...] + strip_a_ref[at:, :] + strip_b_ref[at:, :]
-    for ref in other_refs:
-        block = block + ref[...]
     out_block_ref[...] = block
     at = 0
     odd = is_odd("wide")
@@ -440,11 +443,10 @@
 def backward(
     cot_ref, map_ref, row_a_ref, row_b_ref, far_a_ref, far_b_ref, strip_a_ref, strip_b_ref,
     e_refs, rate_refs, se_refs, m_ref, ms_ref,
-    lam_out_ref, u_out_ref, ends_ref, sums_ref,
-    first_lam_ref, slam_refs, first_u_ref, su_refs, work_ref, binned_ref,
+    adjoint_ref, sums_ref,
+    lam_refs, slam_refs, u_refs, su_refs, ends_ref, work_ref, binned_ref,
 ):
     params, layers = cot_ref.shape[:2]
-    lam_refs, u_refs = (first_lam_ref, lam_out_ref), (first_u_ref, u_out_ref)
     cots = row_places(params, layers)[1]
     tile = (8, 128)
     every = range(params)
@@ -528,12 +530,21 @@
     step(2, 1, (4, 2, 12), (4, 2), (4, 2))
     step(1, 0, (4, 2, 12), (8, 1), (8, 1))
 
+    def last(z, i, r):
+        rows = pl.ds(r, 8)
+        e = [e_refs[0][p, z, rows, :] for p in every]
+        u = [u_refs[1][p, z, rows, :] for p in every]
+        change = changes(e, u, neighbours(u_refs[1], ends_ref, u, z, r))
+        return [put(adjoint_ref, (p, z), lam_refs[1][p, z, rows, :] - change[p]) for p in every]
+
+    each_tile(layers, (8, 1, 8), last)
+
     grains = [map_ref[z] for z in range(layers)]
     cells = []
     for z in range(layers):
         upper = work_ref[0, z, 0] + work_ref[1, z, 0] + work_ref[2, z, 0]
         lower = work_ref[0, z, 1] + work_ref[1, z, 1] + work_ref[2, z, 1]
-        first = total_of([lam_out_ref[p, z, 8:16, :] * rate_refs[0][p, z, 8:16, :] for p in every])
+        first = total_of([lam_refs[1][p, z, 8:16, :] * rate_refs[0][p, z, 8:16, :] for p in every])
         cells.append(jnp.concatenate([upper[4:8], lower[0:4]], axis=0) + first)
 
     def bin_one(g, carry):
@@ -550,20 +561,6 @@
     )
     for k in range(0, sums_ref.shape[0], 8):
         sums_ref[k : k + 8, :] = sums
-
-
-def backward_last(first_e_ref, lam_ref, u_ref, ends_ref, adjoint_ref):
-    params, layers = adjoint_ref.shape[:2]
-    every = range(params)
-
-    def core(z, i, r):
-        rows = pl.ds(r, 8)
-        e = [first_e_ref[p, z, rows, :] for p in every]
-        u = [u_ref[p, z, rows, :] for p in every]
-        change = changes(e, u, neighbours(u_ref, ends_ref, u, z, r))
-        return [put(adjoint_ref, (p, z), lam_ref[p, z, rows, :] - change[p]) for p in every]
-
-    each_tile(layers, (8, 1, 8), core)
 
 
 def pick_owned(owned, slots_ref, sums_ref, out_ref, total_ref, dense_ref):
@@ -643,7 +640,7 @@
     *fetched, strip_a, strip_b, block = kernel(
         pack_strips,
         tuple(jax.ShapeDtypeStruct(x.shape, x.dtype) for x in arguments)
-        + (f32(strip_rows + block_rows, 128),) * 2 + (f32(block_rows, 128),),
+        + (f32(strip_rows, 128), f32(strip_rows + block_rows, 128), f32(block_rows, 128)),
         (pltpu.SemaphoreType.DMA((len(arguments),)),), name="pack_strips",
         in_specs=[pl.BlockSpec(memory_space=pltpu.HBM)] * len(arguments),
     )(*(pltpu.with_memory_space_constraint(x, pltpu.HBM) for x in arguments))
@@ -653,16 +650,18 @@
         in_specs=[here] * 3 + [anywhere],
     )(order_init, grain_map, cotangent, strip_b)
     strip_b = swapped(strip_b, "narrow", narrow_count, 1)
-    strip_a = swapped(strip_a, "narrow", narrow_count, 0)
-    others = [opposite(block, "narrow")] if small else []
     near_a = swapped(near_a, "wide", wide_count, 0)
     row_b = swapped(row_b, "wide", wide_count, 1)
+    strip_a = kernel(pack_second, f32(strip_rows + block_rows, 128), name="pack_second", cost=100_000_000_000)(
+        strip_a, block, strip_b
+    )
+    strip_a = swapped(strip_a, "narrow", narrow_count, 0)
 
     corners = corner_rows(params)
     far_a, far_b, block = kernel(
         functools.partial(pack_far, params),
-        (f32(corners + block_rows, 128),) * 2 + (f32(block_rows, 128),), name="pack_far", cost=100_000_000_000,
-    )(strip_a, strip_b, block, *others)
+        (f32(corners + block_rows, 128),) * 2 + (f32(block_rows, 128),), name="pack_far", cost=0,
+    )(strip_a, strip_b, block)
     far_b = swapped(far_b, "wide", wide_count, 1)
     far_a = swapped(far_a, "wide", wide_count, 0)
     slots = kernel(
@@ -680,7 +679,7 @@
     table = kernel(
         functools.partial(find_mobility, counts, owned), f32(8, 128),
         (pltpu.VMEM((8, 128), jnp.int32), vmem(wide_count * block_rows, 128)),
-        name="find_mobility", cost=3_000_000_000,
+        name="find_mobility", cost=2_500_000_000,
     )(slots, *mobs)
 
     padded, strip = (params, layers, ROWS, 128), (params, ROWS, 128)
@@ -693,11 +692,11 @@
         (vmem(*strip), vmem(*strip), vmem(*padded), vmem(layers, ROWS, 128), vmem(ROWS, 128)),
         name="forward", cost=0,
     )(order_init, grain_map, near_a, row_b, far_a, far_b, strip_a, strip_b, table)
-    lam, u, ends, sums = kernel(
+    adjoint, sums = kernel(
         backward,
-        (f32(*padded), f32(*padded), f32(*padded), f32(bricks, listed)),
+        (f32(*order_init.shape), f32(bricks, listed)),
         (
-            vmem(*padded), [vmem(*strip)] * 2, vmem(*padded), [vmem(*strip)] * 2,
+            [vmem(*padded)] * 2, [vmem(*strip)] * 2, [vmem(*padded)] * 2, [vmem(*strip)] * 2, vmem(*padded),
             vmem(ITERS - 1, layers, 2, 8, 128), vmem(listed, 128),
         ),
         name="backward",
@@ -705,7 +704,6 @@
         cotangent, grain_map, near_a, cot_b, far_a, far_b, strip_a, strip_b,
         states, rate, halos, m, ms,
     )
-    adjoint = kernel(backward_last, f32(*order_init.shape), name="backward_last")(states[0], lam, u, ends)
 
     sums = lax.all_to_all(sums, both, 0, 0, tiled=True)
     grads = kernel(

time: 48.3 us -> 46.9 us (0.971)
  blocking collectives: 0 us -> 11.3 us
  starting transfers between devices: 15.5 us -> 10.7 us
  waiting for transfers between devices: 9.95 us -> 5.19 us
  local copies, waits for them, and re-layouts: 2.94 us -> 0 us
    all_to_all x0 -> x1, blocking collectives: none -> 11.3 us  [per_device(): sums = lax.all_to_all(sums, both, 0, 0, tiled=True)]
    all_to_all x1 -> x0, starting transfers between devices: 4.98 us -> none  [per_device(): sums = lax.all_to_all(sums, both, 0, 0, tiled=True)]
    ppermute x2 -> x1, waiting for transfers between devices: 5.89 us -> 1.48 us  [opposite(): return lax.ppermute(value, axis, [(i, (i + 2) % 4) for i in range(4)])]
    all_to_all x1 -> x0, waiting for transfers between devices: 4.05 us -> none  [per_device(): sums = lax.all_to_all(sums, both, 0, 0, tiled=True)]
    ppermute x7, waiting for transfers between devices: 0.02 us -> 3.71 us  [swapped(): lax.ppermute(value, axis, [(i, (i + by) % count) for i, by in enumerate(s...]
    unnamed x6 -> x0, local copies, waits for them, and re-layouts: 2.94 us -> none
    ppermute x7, starting transfers between devices: 9.86 us -> 10.4 us  [swapped(): lax.ppermute(value, axis, [(i, (i + by) % count) for i, by in enumerate(s...]
  transfers between devices with their start and end apart: 10 -> 8, of which waited for: 3 -> 3; matrix products, arithmetic and copies ran while one was open for 0% -> 0% of each run, Pallas kernels for 19% -> 17%
where the time goes in v9:
time: 46.9 us; the launch traced here: 46.7 us
  Pallas kernels  18.8 us (40%)
  blocking collectives  11.3 us (24%)
  starting transfers between devices  10.7 us (23%)
  waiting for transfers between devices  5.19 us (11%)
  between operations  0.71 us (2%)
    all_to_all x1, blocking collectives, per_device(): sums = lax.all_to_all(sums, both, 0, 0, tiled=True)  11.3 us
    ppermute x7, starting transfers between devices, swapped(): lax.ppermute(value, axis, [(i, (i + by) % count) for i, by in enumerate(s...  10.4 us
    pallas_call x1, Pallas kernels, per_device(): kernel(backward, (f32(*order_init.shape), f32(bricks, listed)), ([vmem(*p...  7.77 us
    pallas_call x1, Pallas kernels, per_device(): kernel(forward, (f32(*order_init.shape), [f32(*padded)] * ITERS, [f32(*pa...  6.69 us
    ppermute x7, waiting for transfers between devices, swapped(): lax.ppermute(value, axis, [(i, (i + by) % count) for i, by in enumerate(s...  3.71 us
    pallas_call x1, Pallas kernels, per_device(): kernel(pack_strips, tuple((jax.ShapeDtypeStruct(x.shape, x.dtype) for x i...  1.78 us
    ppermute x1, waiting for transfers between devices, opposite(): return lax.ppermute(value, axis, [(i, (i + 2) % 4) for i in range(4)])  1.48 us
    pallas_call x1, Pallas kernels, per_device(): kernel(functools.partial(pick_owned, owned), f32(1, owned), (vmem(owned +...  1.13 us
  transfers between devices with their start and end apart: 8, of which 3 were waited for; matrix products, arithmetic and copies ran while one was open for 0% of the time, Pallas kernels for 17%

profile of v9, /device:TPU:0, one launch (start us, length us, event | category | flops | bytes accessed | tf_op | source)
XLA Modules:
  0.0 46.7 jit_solution(14716722858916623781)
XLA Ops:
  0.6 1.8 %pack_strips.1 = (f32[8,12,8,128]{3,2,1,0:T(8,128)S(1)}, s32[12,8,128]{2,1,0:T(8,128)S(1)}, f32[8,12,8,128]{3,2,1,0:T(8,128)S(1)}, f32[1,392]{1,0:T(1,128)}, s32...) custom-call(f32[8,12,8,128]{3,2,1,0:T(8,128)} %refs_0_.1, ...), custom_call_target="tpu_custom_call" | custom-call | tf_op jit(solution)/shard_map/pack_strips/pallas_call | solution.py:640
  2.4 5.1 %collective-permute-start.2 = (f32[88,128]{1,0:T(8,128)S(1)}, f32[88,128]{1,0:T(8,128)S(1)}, u32[]{:S(2)}, u32[]{:S(2)}) collective-permute-start(f32[88,128]{1,0:T(8,128)S(1)} %get-tuple-element.35.after_ref), channel_id=1, source_target_pairs={{0,3},{1,2},{2,1},{3,0},{4,7},{5,6},{6,5},{7,4},{8,11},{9,10},{10,... | collective-permute-start | bytes 135176 | tf_op jit(solution)/shard_map/ppermute | solution.py:613
  7.5 0.1 pack_rows.1
  7.7 0.1 collective-permute-start
  7.7 1.6 %collective-permute-start.1 = (f32[664,128]{1,0:T(8,128)S(1)}, f32[664,128]{1,0:T(8,128)S(1)}, u32[]{:S(2)}, u32[]{:S(2)}) collective-permute-start(f32[664,128]{1,0:T(8,128)S(1)} %get-tuple-element.37), channel_id=1, source_target_pairs={{0,12},{4,8},{8,4},{12,0},{1,13},{5,9},{9,5},{13,1},{2,14},{6,10},... | collective-permute-start | bytes 1019912 | tf_op jit(solution)/shard_map/ppermute | solution.py:613
  9.3 0.3 collective-permute-done.2.strip_b_ref
  9.6 0.6 %collective-permute-start.3 = (f32[88,128]{1,0:T(8,128)S(1)}, f32[88,128]{1,0:T(8,128)S(1)}, u32[]{:S(2)}, u32[]{:S(2)}) collective-permute-start(f32[88,128]{1,0:T(8,128)S(1)} %pack_second.1), channel_id=1, source_target_pairs={{0,1},{1,0},{2,3},{3,2},{4,5},{5,4},{6,7},{7,6},{8,9},{9,8},{10,11... | collective-permute-start | bytes 135176 | tf_op jit(solution)/shard_map/ppermute | solution.py:613
  10.2 3.4 %collective-permute-done.3.strip_a_ref = f32[88,128]{1,0:T(8,128)S(1)} collective-permute-done((f32[88,128]{1,0:T(8,128)S(1)}, f32[88,128]{1,0:T(8,128)S(1)}, u32[]{:S(2)}, u32[]{:S(2)}) %collective-permute-start.3) | collective-permute-done | bytes 45088 | tf_op jit(solution)/shard_map/ppermute | solution.py:613
  13.7 0.1 pack_far.1
  13.8 0.1 collective-permute-start.4
  13.8 1.8 %collective-permute-start.5 = (f32[88,128]{1,0:T(8,128)S(1)}, f32[88,128]{1,0:T(8,128)S(1)}, u32[]{:S(2)}, u32[]{:S(2)}) collective-permute-start(f32[88,128]{1,0:T(8,128)S(1)} %get-tuple-element.41), channel_id=1, source_target_pairs={{0,12},{4,8},{8,4},{12,0},{1,13},{5,9},{9,5},{13,1},{2,14},{6,10},... | collective-permute-start | bytes 135176 | tf_op jit(solution)/shard_map/ppermute | solution.py:613
  15.6 0.4 collective-permute-start.6
  16.0 0.6 %find_slots.1.slots_ref = s32[8,128]{1,0:T(8,128)S(1)} custom-call(s32[16,64]{1,0:T(8,128)S(1)} %get-tuple-element.42.bricks_ref, s32[49,128]{1,0:T(8,128)S(1)} %get-tuple-element.43.slot_ref, f32[16,128]{1,0:T(8,128)S(1)} %get-tuple-element.44.after_ref.refs_0_), custom_call_target="tpu_custom_call" | custom-call | tf_op jit(solution)/shard_map/find_slots/pallas_call | solution.py:667
  16.6 0.1 pack_cot.1
  16.7 1.1 %collective-permute-start.7 = (f32[400,128]{1,0:T(8,128)S(1)}, f32[400,128]{1,0:T(8,128)S(1)}, u32[]{:S(2)}, u32[]{:S(2)}) collective-permute-start(f32[400,128]{1,0:T(8,128)S(1)} %pack_cot.1), channel_id=1, source_target_pairs={{0,12},{4,8},{8,4},{12,0},{1,13},{5,9},{9,5},{13,1},{2,14},{6,10},... | collective-permute-start | bytes 614408 | tf_op jit(solution)/shard_map/ppermute | solution.py:613
  17.8 1.5 %collective-permute-done.6.refs_3_ = f32[16,128]{1,0:T(8,128)S(1)} collective-permute-done((f32[16,128]{1,0:T(8,128)S(1)}, f32[16,128]{1,0:T(8,128)S(1)}, u32[]{:S(2)}, u32[]{:S(2)}) %collective-permute-start.6) | collective-permute-done | bytes 8224 | tf_op jit(solution)/shard_map/ppermute | solution.py:608
  19.3 0.0 collective-permute-done.5.refs_2_.far_b_ref
  19.3 0.5 %find_mobility.1.table_ref = f32[8,128]{1,0:T(8,128)S(1)} custom-call(s32[8,128]{1,0:T(8,128)S(1)} %find_slots.1.slots_ref, f32[16,128]{1,0:T(8,128)S(1)} %get-tuple-element.44.after_ref.refs_0_, f32[88,128]{1,0:T(8,128)S(1)} %collective-permute-done.4.refs_1_.far_a_ref.after_ref, f32[88,128]{1,0:T(8,128)S(1)} %collective-permute-done.5.refs_2_.far_b_ref, ...), custom_call_target="tpu_custom_call" | custom-call | flops 2500000000 | bytes 2500000 | tf_op jit(solution)/shard_map/find_mobility/pallas_call | solution.py:679
  19.8 0.0 collective-permute-done.row_a_ref
  19.8 6.7 %forward.1 = (f32[8,12,8,128]{3,2,1,0:T(8,128)}, f32[8,12,24,128]{3,2,1,0:T(8,128)S(1)}, f32[8,12,24,128]{3,2,1,0:T(8,128)S(1)}, f32[8,12,24,128]{3,2,1,0:T(8,12...) custom-call(f32[8,12,8,128]{3,2,1,0:T(8,128)S(1)} %get-tuple-element, ...), custom_call_target="tpu_custom_call" | custom-call | tf_op jit(solution)/shard_map/forward/pallas_call | solution.py:686
  26.5 0.0 collective-permute-done.7.row_b_ref
  26.5 7.8 %backward.1 = (f32[8,12,8,128]{3,2,1,0:T(8,128)}, f32[16,64]{1,0:T(8,128)S(1)}) custom-call(f32[8,12,8,128]{3,2,1,0:T(8,128)S(1)} %get-tuple-element.34.cot_ref, s32[12,8,128]{2,1,0:T(8,128)S(1)} %get-tuple-element.33.map_ref, f32[1064,128]{1,0:T(8,128)S(1)} %collective-permute-done.row_a_ref, f32[400,128]{1,0:T(8,128)S(1)} %collective-permute-done.7.row_b_ref, ...), custom_call_target="tpu_custom_call" | custom-call | tf_op jit(solution)/shard_map/backward/pallas_call | solution.py:695
  34.3 11.3 %all_to_all.11 = f32[16,1,64]{2,1,0:T(1,128)S(1)} all-to-all(f32[16,1,64]{2,1,0:T(1,128)S(1)} %bitcast.8), channel_id=1, replica_groups=mesh['groups'=2,'wide'=4,'narrow'=4] {'wide','narrow'}, dimensions={0} | all-to-all | bytes 8192 | tf_op jit(solution)/shard_map/all_to_all | solution.py:708
  45.6 1.1 %pick_owned.1 = f32[1,392]{1,0:T(1,128)} custom-call(s32[8,128]{1,0:T(8,128)S(1)} %find_slots.1.slots_ref, f32[16,64]{1,0:T(8,128)S(1)} %bitcast.7), custom_call_target="tpu_custom_call" | custom-call | tf_op jit(solution)/shard_map/pick_owned/pallas_call | solution.py:709
  (3 shorter events, 0.0 us)
Async XLA Ops:
  2.4 7.2 %collective-permute-start.2 = (f32[88,128]{1,0:T(8,128)S(1)}, f32[88,128]{1,0:T(8,128)S(1)}, u32[]{:S(2)}, u32[]{:S(2)}) collective-permute-start(f32[88,128]{1,0:T(8,128)S(1)} %get-tuple-element.35.after_ref), channel_id=1, source_target_pairs={{0,3},{1,2},{2,1},{3,0},{4,7},{5,6},{6,5},{7,4},{8,11},{9,10},{10,... | collective-permute-start | bytes 135176 | tf_op jit(solution)/shard_map/ppermute | solution.py:613
  7.7 12.1 %collective-permute-start = (f32[1064,128]{1,0:T(8,128)S(1)}, f32[1064,128]{1,0:T(8,128)S(1)}, u32[]{:S(2)}, u32[]{:S(2)}) collective-permute-start(f32[1064,128]{1,0:T(8,128)S(1)} %get-tuple-element.36), channel_id=1, source_target_pairs={{0,4},{4,0},{8,12},{12,8},{1,5},{5,1},{9,13},{13,9},{2,6},{6,2},{1... | collective-permute-start | bytes 1634312 | tf_op jit(solution)/shard_map/ppermute | solution.py:613
  7.7 12.1 %collective-permute-start.1 = (f32[664,128]{1,0:T(8,128)S(1)}, f32[664,128]{1,0:T(8,128)S(1)}, u32[]{:S(2)}, u32[]{:S(2)}) collective-permute-start(f32[664,128]{1,0:T(8,128)S(1)} %get-tuple-element.37), channel_id=1, source_target_pairs={{0,12},{4,8},{8,4},{12,0},{1,13},{5,9},{9,5},{13,1},{2,14},{6,10},... | collective-permute-start | bytes 1019912 | tf_op jit(solution)/shard_map/ppermute | solution.py:613
  9.6 4.0 %collective-permute-start.3 = (f32[88,128]{1,0:T(8,128)S(1)}, f32[88,128]{1,0:T(8,128)S(1)}, u32[]{:S(2)}, u32[]{:S(2)}) collective-permute-start(f32[88,128]{1,0:T(8,128)S(1)} %pack_second.1), channel_id=1, source_target_pairs={{0,1},{1,0},{2,3},{3,2},{4,5},{5,4},{6,7},{7,6},{8,9},{9,8},{10,11... | collective-permute-start | bytes 135176 | tf_op jit(solution)/shard_map/ppermute | solution.py:613
  13.8 2.8 %collective-permute-start.4 = (f32[88,128]{1,0:T(8,128)S(1)}, f32[88,128]{1,0:T(8,128)S(1)}, u32[]{:S(2)}, u32[]{:S(2)}) collective-permute-start(f32[88,128]{1,0:T(8,128)S(1)} %get-tuple-element.40), channel_id=1, source_target_pairs={{0,4},{4,0},{8,12},{12,8},{1,5},{5,1},{9,13},{13,9},{2,6},{6,2},{1... | collective-permute-start | bytes 135176 | tf_op jit(solution)/shard_map/ppermute | solution.py:613
  13.8 5.4 %collective-permute-start.5 = (f32[88,128]{1,0:T(8,128)S(1)}, f32[88,128]{1,0:T(8,128)S(1)}, u32[]{:S(2)}, u32[]{:S(2)}) collective-permute-start(f32[88,128]{1,0:T(8,128)S(1)} %get-tuple-element.41), channel_id=1, source_target_pairs={{0,12},{4,8},{8,4},{12,0},{1,13},{5,9},{9,5},{13,1},{2,14},{6,10},... | collective-permute-start | bytes 135176 | tf_op jit(solution)/shard_map/ppermute | solution.py:613
  15.6 3.7 %collective-permute-start.6 = (f32[16,128]{1,0:T(8,128)S(1)}, f32[16,128]{1,0:T(8,128)S(1)}, u32[]{:S(2)}, u32[]{:S(2)}) collective-permute-start(f32[16,128]{1,0:T(8,128)S(1)} %get-tuple-element.44.after_ref.refs_0_), channel_id=1, source_target_pairs={{0,8},{4,12},{8,0},{12,4},{1,9},{5,13},{9,1},{13,5},{2,10},{6,14},... | collective-permute-start | bytes 24584 | tf_op jit(solution)/shard_map/ppermute | solution.py:608
  16.7 9.8 %collective-permute-start.7 = (f32[400,128]{1,0:T(8,128)S(1)}, f32[400,128]{1,0:T(8,128)S(1)}, u32[]{:S(2)}, u32[]{:S(2)}) collective-permute-start(f32[400,128]{1,0:T(8,128)S(1)} %pack_cot.1), channel_id=1, source_target_pairs={{0,12},{4,8},{8,4},{12,0},{1,13},{5,9},{9,5},{13,1},{2,14},{6,10},... | collective-permute-start | bytes 614408 | tf_op jit(solution)/shard_map/ppermute | solution.py:613

commit v10 on v9

--- a/solution.py
+++ b/solution.py
@@ -33,19 +33,9 @@
     return lax.rem(lax.axis_index(axis), 2) == 1
 
 
-def pack_strips(*refs):
-    count = (len(refs) - 4) // 2
-    sources, targets = refs[:count], refs[count : 2 * count]
-    strip_a_ref, strip_b_ref, block_ref, sems = refs[2 * count :]
-    copies = [pltpu.make_async_copy(a, b, sems.at[i]) for i, (a, b) in enumerate(zip(sources, targets))]
-    for copy in copies:
-        copy.start()
-    order_ref, map_ref, cot_ref, mob_ref = targets[:4]
+def pack_strips(order_ref, map_ref, cot_ref, mob_ref, after_ref, strip_a_ref, strip_b_ref, block_ref):
     params, layers = order_ref.shape[:2]
     odd = is_odd("narrow")
-    for copy in copies:
-        copy.wait()
-
     lane = lanes((8, 128))
     zero = jnp.zeros((8, 128), jnp.float32)
 
@@ -75,10 +65,18 @@
         if size < 128:
             row = jnp.concatenate([row, jnp.zeros((1, 128 - size), jnp.float32)], axis=1)
         block_ref[pl.ds(first + i, 1), :] = row
-    strip_b_ref[8 * (params + 1) :, :] = block_ref[...]
-
-
-def pack_rows(order_ref, map_ref, cot_ref, after_ref, near_a_ref, row_b_ref):
+    for ref in (strip_a_ref, strip_b_ref):
+        ref[8 * (params + 1) :, :] = block_ref[...]
+
+
+def pack_rows(*refs):
+    count = (len(refs) - 3) // 2
+    sources, targets = refs[:count], refs[count : 2 * count]
+    near_a_ref, row_b_ref, sems = refs[2 * count :]
+    copies = [pltpu.make_async_copy(a, b, sems.at[i]) for i, (a, b) in enumerate(zip(sources, targets))]
+    for copy in copies:
+        copy.start()
+    order_ref, map_ref, cot_ref = targets[:3]
     params, layers = order_ref.shape[:2]
     maps, cots = row_places(params, layers)
     gap = jnp.zeros((LEAD, 128), jnp.float32)
@@ -92,11 +90,14 @@
         ref[cots - LEAD : cots, :] = gap
     near_a_ref[cots : cots + LEAD, :] = gap
     near_a_ref[near_a_ref.shape[0] - LEAD :, :] = gap
+    copies[0].wait()
     for p in range(params):
         for z in range(layers):
             k = LEAD + (p * layers + z) * EDGE
             for ref, is_last in zip(row_refs, last):
                 ref[k : k + EDGE, :] = order_ref[p, z, pl.ds((8 - EDGE) * is_last, EDGE), :]
+    for copy in copies[1:]:
+        copy.wait()
     for z in range(layers):
         k = maps + z * MAP_EDGE
         for ref, is_last in zip(row_refs, last):
@@ -108,12 +109,6 @@
             near_a_ref[k : k + ADJ_EDGE, :] = cot_ref[p, z, rows, :]
 
 
-def pack_second(strip_ref, block_ref, strip_b_ref, out_ref):
-    at = strip_ref.shape[0]
-    out_ref[0:at, :] = strip_ref[...]
-    out_ref[at:, :] = block_ref[...] + strip_b_ref[at:, :]
-
-
 def pack_cot(cot_ref, after_ref, out_ref):
     params, layers = cot_ref.shape[:2]
     out_ref[0:LEAD, :] = jnp.zeros((LEAD, 128), jnp.float32)
@@ -154,10 +149,12 @@
 
 
 def pack_far(params, strip_a_ref, strip_b_ref, block_ref, *refs):
-    far_a_ref, far_b_ref, out_block_ref = refs
+    *other_refs, far_a_ref, far_b_ref, out_block_ref = refs
     at = 8 * (params + 1)
     mobs = corner_rows(params)
     block = block_ref[...] + strip_a_ref[at:, :] + strip_b_ref[at:, :]
+    for ref in other_refs:
+        block = block + ref[...]
     out_block_ref[...] = block
     at = 0
     odd = is_odd("wide")
@@ -273,19 +270,16 @@
     return store
 
 
-def neighbours(ref, ends_ref, values, z, r):
-    params, layers = ref.shape[:2]
+def neighbours(ref, ends_ref, value, p, z, r):
+    layers = ref.shape[1]
     lane = lanes((8, 128))
     rows, before, after = pl.ds(r, 8), pl.ds(r - 1, 8), pl.ds(r + 1, 8)
     below, above = jnp.maximum(z - 1, 0), jnp.minimum(z + 1, layers - 1)
-    near = []
-    for p in range(params):
-        ends = ends_ref[p, z, rows, :]
-        left = roll(jnp.where(lane == 127, ends, values[p]), 1)
-        right = roll(jnp.where(lane == 0, ends, values[p]), 127)
-        total = (left + right) + (ref[p, z, before, :] + ref[p, z, after, :])
-        near.append(total + (ref[p, below, rows, :] + ref[p, above, rows, :]))
-    return near
+    ends = ends_ref[p, z, rows, :]
+    left = roll(jnp.where(lane == 127, ends, value), 1)
+    right = roll(jnp.where(lane == 0, ends, value), 127)
+    total = (left + right) + (ref[p, z, before, :] + ref[p, z, after, :])
+    return total + (ref[p, below, rows, :] + ref[p, above, rows, :])
 
 
 def strip_neighbours(ref, core_ref, values, r, outer_ref=None):
@@ -320,17 +314,12 @@
             ends_ref[p, z, rows, :] = roll(values[p], 123 - 10 * z)
 
 
-def rates(e, near):
-    squares = [x * x for x in e]
-    base = 1.5 * total_of(squares) + 5.0
-    return [x * (base - 0.5 * y) - n for x, y, n in zip(e, squares, near)]
-
-
-def changes(e, u, near):
-    squares = [x * x for x in e]
-    base = 1.5 * total_of(squares) + 5.0
-    inner = 3.0 * total_of([x * y for x, y in zip(e, u)])
-    return [y * (base - 1.5 * s) + x * inner - n for x, y, s, n in zip(e, u, squares, near)]
+def base_of(e):
+    return 1.5 * total_of([x * x for x in e]) + 5.0
+
+
+def inner_of(e, u):
+    return 3.0 * total_of([x * y for x, y in zip(e, u)])
 
 
 def forward(
@@ -401,13 +390,14 @@
 
         def core(z, i, r):
             rows = pl.ds(r, 8)
-            e = [old[p, z, rows, :] for p in every]
+            base = base_of([old[p, z, rows, :] for p in every])
             m = m_ref[z, rows, :]
-            rate = rates(e, neighbours(old, ends_ref, e, z, r))
             stores = []
             for p in every:
-                new = e[p] - m * rate[p]
-                stores.append(put(rate_refs[t], (p, z, rows, slice(None)), rate[p]))
+                e = old[p, z, rows, :]
+                rate = e * (base - 0.5 * (e * e)) - neighbours(old, ends_ref, e, p, z, r)
+                new = e - m * rate
+                stores.append(put(rate_refs[t], (p, z, rows, slice(None)), rate))
                 if last:
                     stores.append(put(final_ref, (p, z), new))
                 else:
@@ -422,9 +412,11 @@
             rows = pl.ds(r, 8)
             e = [old_strip[p, rows, :] for p in every]
             m = ms_ref[rows, :]
-            rate = rates(e, strip_neighbours(old_strip, old, e, r, outer_ref if t == 0 else None))
+            base = base_of(e)
+            near = strip_neighbours(old_strip, old, e, r, outer_ref if t == 0 else None)
             for p in every:
-                strip_refs[t + 1][p, rows, :] = e[p] - m * rate[p]
+                rate = e[p] * (base - 0.5 * (e[p] * e[p])) - near[p]
+                strip_refs[t + 1][p, rows, :] = e[p] - m * rate
 
         each_window(strip_windows, strip)
 
@@ -498,13 +490,14 @@
             rows = pl.ds(r, 8)
             e = [e_refs[t][p, z, rows, :] for p in every]
             u = [old[p, z, rows, :] for p in every]
+            base, inner = base_of(e), inner_of(e, u)
             m = m_ref[z, rows, :]
-            change = changes(e, u, neighbours(old, ends_ref, u, z, r))
-            lam = [lam_refs[slot][p, z, rows, :] for p in every]
-            work = total_of([lam[p] * rate_refs[t][p, z, rows, :] for p in every])
+            work = total_of([lam_refs[slot][p, z, rows, :] * rate_refs[t][p, z, rows, :] for p in every])
             stores = [put(work_ref, (t - 1, z, i), work)]
             for p in every:
-                new = lam[p] - change[p]
+                e, u = e_refs[t][p, z, rows, :], old[p, z, rows, :]
+                change = u * (base - 1.5 * (e * e)) + e * inner - neighbours(old, ends_ref, u, p, z, r)
+                new = lam_refs[slot][p, z, rows, :] - change
                 stores.append(put(lam_refs[1 - slot], (p, z, rows, slice(None)), new))
                 stores.append(put(u_refs[1 - slot], (p, z, rows, slice(None)), m * new))
             return stores
@@ -516,9 +509,11 @@
             e = [se_refs[t - 1][p, rows, :] for p in every]
             u = [old_strip[p, rows, :] for p in every]
             m = ms_ref[rows, :]
-            change = changes(e, u, strip_neighbours(old_strip, old, u, r))
+            base, inner = base_of(e), inner_of(e, u)
+            near = strip_neighbours(old_strip, old, u, r)
             for p in every:
-                new = slam_refs[slot][p, rows, :] - change[p]
+                change = u[p] * (base - 1.5 * (e[p] * e[p])) + e[p] * inner - near[p]
+                new = slam_refs[slot][p, rows, :] - change
                 slam_refs[1 - slot][p, rows, :] = new
                 su_refs[1 - slot][p, rows, :] = m * new
 
@@ -534,8 +529,13 @@
         rows = pl.ds(r, 8)
         e = [e_refs[0][p, z, rows, :] for p in every]
         u = [u_refs[1][p, z, rows, :] for p in every]
-        change = changes(e, u, neighbours(u_refs[1], ends_ref, u, z, r))
-        return [put(adjoint_ref, (p, z), lam_refs[1][p, z, rows, :] - change[p]) for p in every]
+        base, inner = base_of(e), inner_of(e, u)
+        stores = []
+        for p in every:
+            e, u = e_refs[0][p, z, rows, :], u_refs[1][p, z, rows, :]
+            change = u * (base - 1.5 * (e * e)) + e * inner - neighbours(u_refs[1], ends_ref, u, p, z, r)
+            stores.append(put(adjoint_ref, (p, z), lam_refs[1][p, z, rows, :] - change))
+        return stores
 
     each_tile(layers, (8, 1, 8), last)
 
@@ -637,31 +637,29 @@
         order_init, grain_map, cotangent, mobility.reshape(1, owned), brick_grains, grain_slot.reshape(-1, 128)
     )
     here, anywhere = pl.BlockSpec(memory_space=pltpu.VMEM), pl.BlockSpec(memory_space=pl.ANY)
-    *fetched, strip_a, strip_b, block = kernel(
-        pack_strips,
+    *fetched, near_a, row_b = kernel(
+        pack_rows,
         tuple(jax.ShapeDtypeStruct(x.shape, x.dtype) for x in arguments)
-        + (f32(strip_rows, 128), f32(strip_rows + block_rows, 128), f32(block_rows, 128)),
-        (pltpu.SemaphoreType.DMA((len(arguments),)),), name="pack_strips",
+        + (f32(edge_rows + cot_rows, 128), f32(edge_rows, 128)),
+        (pltpu.SemaphoreType.DMA((len(arguments),)),), name="pack_rows",
         in_specs=[pl.BlockSpec(memory_space=pltpu.HBM)] * len(arguments),
     )(*(pltpu.with_memory_space_constraint(x, pltpu.HBM) for x in arguments))
-    order_init, grain_map, cotangent, _, brick_grains, grain_slot = fetched
-    near_a, row_b = kernel(
-        pack_rows, (f32(edge_rows + cot_rows, 128), f32(edge_rows, 128)), name="pack_rows",
-        in_specs=[here] * 3 + [anywhere],
-    )(order_init, grain_map, cotangent, strip_b)
+    order_init, grain_map, cotangent, mobility_row, brick_grains, grain_slot = fetched
+    strip_a, strip_b, block = kernel(
+        pack_strips, (f32(strip_rows + block_rows, 128),) * 2 + (f32(block_rows, 128),),
+        name="pack_strips", in_specs=[here] * 4 + [anywhere],
+    )(order_init, grain_map, cotangent, mobility_row, row_b)
+    row_b = swapped(row_b, "wide", wide_count, 1)
+    near_a = swapped(near_a, "wide", wide_count, 0)
     strip_b = swapped(strip_b, "narrow", narrow_count, 1)
-    near_a = swapped(near_a, "wide", wide_count, 0)
-    row_b = swapped(row_b, "wide", wide_count, 1)
-    strip_a = kernel(pack_second, f32(strip_rows + block_rows, 128), name="pack_second", cost=100_000_000_000)(
-        strip_a, block, strip_b
-    )
     strip_a = swapped(strip_a, "narrow", narrow_count, 0)
+    others = [opposite(block, "narrow")] if small else []
 
     corners = corner_rows(params)
     far_a, far_b, block = kernel(
         functools.partial(pack_far, params),
         (f32(corners + block_rows, 128),) * 2 + (f32(block_rows, 128),), name="pack_far", cost=0,
-    )(strip_a, strip_b, block)
+    )(strip_a, strip_b, block, *others)
     far_b = swapped(far_b, "wide", wide_count, 1)
     far_a = swapped(far_a, "wide", wide_count, 0)
     slots = kernel(

time: 46.9 us -> 44.9 us (0.957)
  blocking collectives: 11.3 us -> 9.94 us
  starting transfers between devices: 10.7 us -> 9.65 us
  waiting for transfers between devices: 5.19 us -> 5.84 us
    ppermute x1 -> x2, waiting for transfers between devices: 1.48 us -> 5.83 us  [opposite(): return lax.ppermute(value, axis, [(i, (i + 2) % 4) for i in range(4)])]
    ppermute x7, waiting for transfers between devices: 3.71 us -> 0.02 us  [swapped(): lax.ppermute(value, axis, [(i, (i + by) % count) for i, by in enumerate(s...]
    ppermute x7, starting transfers between devices: 10.4 us -> 8.04 us  [swapped(): lax.ppermute(value, axis, [(i, (i + by) % count) for i, by in enumerate(s...]
    all_to_all x1, blocking collectives: 11.3 us -> 9.94 us  [per_device(): sums = lax.all_to_all(sums, both, 0, 0, tiled=True)]
    ppermute x1 -> x2, starting transfers between devices: 0.37 us -> 1.61 us  [opposite(): return lax.ppermute(value, axis, [(i, (i + 2) % 4) for i in range(4)])]
    pallas_call x3 -> x2, Pallas kernels: 1.9 us -> 1.63 us  [the longest x1 1.24 us: per_device(): kernel(pack_rows, tuple((jax.ShapeDtypeStruct(x.shape, x.dtype) for x in...]
  transfers between devices with their start and end apart: 8 -> 9, of which waited for: 3 -> 2; matrix products, arithmetic and copies ran while one was open for 0% -> 0% of each run, Pallas kernels for 17% -> 19%
where the time goes in v10:
time: 44.9 us; the launch traced here: 44.7 us
  Pallas kernels  18.6 us (41%)
  blocking collectives  9.94 us (22%)
  starting transfers between devices  9.65 us (21%)
  waiting for transfers between devices  5.84 us (13%)
  between operations  0.71 us (2%)
    all_to_all x1, blocking collectives, per_device(): sums = lax.all_to_all(sums, both, 0, 0, tiled=True)  9.94 us
    ppermute x7, starting transfers between devices, swapped(): lax.ppermute(value, axis, [(i, (i + by) % count) for i, by in enumerate(s...  8.04 us
    pallas_call x1, Pallas kernels, per_device(): kernel(backward, (f32(*order_init.shape), f32(bricks, listed)), ([vmem(*p...  7.86 us
    pallas_call x1, Pallas kernels, per_device(): kernel(forward, (f32(*order_init.shape), [f32(*padded)] * ITERS, [f32(*pa...  6.69 us
    ppermute x2, waiting for transfers between devices, opposite(): return lax.ppermute(value, axis, [(i, (i + 2) % 4) for i in range(4)])  5.83 us
    ppermute x2, starting transfers between devices, opposite(): return lax.ppermute(value, axis, [(i, (i + 2) % 4) for i in range(4)])  1.61 us
    pallas_call x1, Pallas kernels, per_device(): kernel(pack_rows, tuple((jax.ShapeDtypeStruct(x.shape, x.dtype) for x in...  1.24 us
    pallas_call x1, Pallas kernels, per_device(): kernel(functools.partial(pick_owned, owned), f32(1, owned), (vmem(owned +...  1.13 us
  transfers between devices with their start and end apart: 9, of which 2 were waited for; matrix products, arithmetic and copies ran while one was open for 0% of the time, Pallas kernels for 19%

profile of v10, /device:TPU:0, one launch (start us, length us, event | category | flops | bytes accessed | tf_op | source)
XLA Modules:
  0.0 44.7 jit_solution(11881834288711647836)
XLA Ops:
  0.6 1.2 %pack_rows.1 = (f32[8,12,8,128]{3,2,1,0:T(8,128)S(1)}, s32[12,8,128]{2,1,0:T(8,128)S(1)}, f32[8,12,8,128]{3,2,1,0:T(8,128)S(1)}, f32[1,392]{1,0:T(1,128)S(1)}, s...) custom-call(f32[8,12,8,128]{3,2,1,0:T(8,128)} %refs_0_.1, ...), custom_call_target="tpu_custom_call" | custom-call | tf_op jit(solution)/shard_map/pack_rows/pallas_call | solution.py:640
  1.9 0.5 %collective-permute-start = (f32[1064,128]{1,0:T(8,128)S(1)}, f32[1064,128]{1,0:T(8,128)S(1)}, u32[]{:S(2)}, u32[]{:S(2)}) collective-permute-start(f32[1064,128]{1,0:T(8,128)S(1)} %get-tuple-element.35), channel_id=1, source_target_pairs={{0,4},{4,0},{8,12},{12,8},{1,5},{5,1},{9,13},{13,9},{2,6},{6,2},{1... | collective-permute-start | bytes 1634312 | tf_op jit(solution)/shard_map/ppermute | solution.py:613
  2.4 2.6 %collective-permute-start.1 = (f32[664,128]{1,0:T(8,128)S(1)}, f32[664,128]{1,0:T(8,128)S(1)}, u32[]{:S(2)}, u32[]{:S(2)}) collective-permute-start(f32[664,128]{1,0:T(8,128)S(1)} %get-tuple-element.36.after_ref), channel_id=1, source_target_pairs={{0,12},{4,8},{8,4},{12,0},{1,13},{5,9},{9,5},{13,1},{2,14},{6,10},... | collective-permute-start | bytes 1019912 | tf_op jit(solution)/shard_map/ppermute | solution.py:613
  5.0 0.4 pack_strips.1
  5.4 1.6 %collective-permute-start.2 = (f32[88,128]{1,0:T(8,128)S(1)}, f32[88,128]{1,0:T(8,128)S(1)}, u32[]{:S(2)}, u32[]{:S(2)}) collective-permute-start(f32[88,128]{1,0:T(8,128)S(1)} %get-tuple-element.39), channel_id=1, source_target_pairs={{0,1},{1,0},{2,3},{3,2},{4,5},{5,4},{6,7},{7,6},{8,9},{9,8},{10,11... | collective-permute-start | bytes 135176 | tf_op jit(solution)/shard_map/ppermute | solution.py:613
  7.1 2.5 %collective-permute-start.3 = (f32[88,128]{1,0:T(8,128)S(1)}, f32[88,128]{1,0:T(8,128)S(1)}, u32[]{:S(2)}, u32[]{:S(2)}) collective-permute-start(f32[88,128]{1,0:T(8,128)S(1)} %get-tuple-element.40), channel_id=1, source_target_pairs={{0,3},{1,2},{2,1},{3,0},{4,7},{5,6},{6,5},{7,4},{8,11},{9,10},{10,... | collective-permute-start | bytes 135176 | tf_op jit(solution)/shard_map/ppermute | solution.py:613
  9.5 0.1 collective-permute-start.4
  9.6 4.4 %collective-permute-done.4.refs_0_ = f32[16,128]{1,0:T(8,128)S(1)} collective-permute-done((f32[16,128]{1,0:T(8,128)S(1)}, f32[16,128]{1,0:T(8,128)S(1)}, u32[]{:S(2)}, u32[]{:S(2)}) %collective-permute-start.4) | collective-permute-done | bytes 8224 | tf_op jit(solution)/shard_map/ppermute | solution.py:608
  14.1 0.0 collective-permute-done.2.strip_a_ref
  14.1 0.0 collective-permute-done.3.strip_b_ref
  14.1 0.1 pack_far.1
  14.2 0.1 collective-permute-start.5
  14.3 0.7 %collective-permute-start.6 = (f32[88,128]{1,0:T(8,128)S(1)}, f32[88,128]{1,0:T(8,128)S(1)}, u32[]{:S(2)}, u32[]{:S(2)}) collective-permute-start(f32[88,128]{1,0:T(8,128)S(1)} %get-tuple-element.43), channel_id=1, source_target_pairs={{0,12},{4,8},{8,4},{12,0},{1,13},{5,9},{9,5},{13,1},{2,14},{6,10},... | collective-permute-start | bytes 135176 | tf_op jit(solution)/shard_map/ppermute | solution.py:613
  14.9 1.5 %collective-permute-start.7 = (f32[16,128]{1,0:T(8,128)S(1)}, f32[16,128]{1,0:T(8,128)S(1)}, u32[]{:S(2)}, u32[]{:S(2)}) collective-permute-start(f32[16,128]{1,0:T(8,128)S(1)} %get-tuple-element.46.after_ref.refs_0_), channel_id=1, source_target_pairs={{0,8},{4,12},{8,0},{12,4},{1,9},{5,13},{9,1},{13,5},{2,10},{6,14},... | collective-permute-start | bytes 24584 | tf_op jit(solution)/shard_map/ppermute | solution.py:608
  16.4 0.6 %find_slots.1.slots_ref = s32[8,128]{1,0:T(8,128)S(1)} custom-call(s32[16,64]{1,0:T(8,128)S(1)} %get-tuple-element.44.bricks_ref, s32[49,128]{1,0:T(8,128)S(1)} %get-tuple-element.45.slot_ref, f32[16,128]{1,0:T(8,128)S(1)} %get-tuple-element.46.after_ref.refs_0_), custom_call_target="tpu_custom_call" | custom-call | tf_op jit(solution)/shard_map/find_slots/pallas_call | solution.py:665
  17.0 0.0 collective-permute-done.5.refs_1_.far_a_ref.after_ref
  17.0 0.1 pack_cot.1
  17.1 0.1 collective-permute-start.8
  17.2 1.4 %collective-permute-done.7.refs_3_ = f32[16,128]{1,0:T(8,128)S(1)} collective-permute-done((f32[16,128]{1,0:T(8,128)S(1)}, f32[16,128]{1,0:T(8,128)S(1)}, u32[]{:S(2)}, u32[]{:S(2)}) %collective-permute-start.7) | collective-permute-done | bytes 8224 | tf_op jit(solution)/shard_map/ppermute | solution.py:608
  18.6 0.5 %find_mobility.1.table_ref = f32[8,128]{1,0:T(8,128)S(1)} custom-call(s32[8,128]{1,0:T(8,128)S(1)} %find_slots.1.slots_ref, f32[16,128]{1,0:T(8,128)S(1)} %get-tuple-element.46.after_ref.refs_0_, f32[88,128]{1,0:T(8,128)S(1)} %collective-permute-done.5.refs_1_.far_a_ref.after_ref, f32[88,128]{1,0:T(8,128)S(1)} %collective-permute-done.6.refs_2_.far_b_ref, ...), custom_call_target="tpu_custom_call" | custom-call | flops 2500000000 | bytes 2500000 | tf_op jit(solution)/shard_map/find_mobility/pallas_call | solution.py:677
  19.1 6.7 %forward.1 = (f32[8,12,8,128]{3,2,1,0:T(8,128)}, f32[8,12,24,128]{3,2,1,0:T(8,128)S(1)}, f32[8,12,24,128]{3,2,1,0:T(8,128)S(1)}, f32[8,12,24,128]{3,2,1,0:T(8,12...) custom-call(f32[8,12,8,128]{3,2,1,0:T(8,128)S(1)} %get-tuple-element, ...), custom_call_target="tpu_custom_call" | custom-call | tf_op jit(solution)/shard_map/forward/pallas_call | solution.py:684
  25.8 7.9 %backward.1 = (f32[8,12,8,128]{3,2,1,0:T(8,128)}, f32[16,64]{1,0:T(8,128)S(1)}) custom-call(f32[8,12,8,128]{3,2,1,0:T(8,128)S(1)} %get-tuple-element.37.cot_ref, s32[12,8,128]{2,1,0:T(8,128)S(1)} %get-tuple-element.34.map_ref, f32[1064,128]{1,0:T(8,128)S(1)} %collective-permute-done.row_a_ref, f32[400,128]{1,0:T(8,128)S(1)} %collective-permute-done.8.row_b_ref, ...), custom_call_target="tpu_custom_call" | custom-call | tf_op jit(solution)/shard_map/backward/pallas_call | solution.py:693
  33.7 9.9 %all_to_all.11 = f32[16,1,64]{2,1,0:T(1,128)S(1)} all-to-all(f32[16,1,64]{2,1,0:T(1,128)S(1)} %bitcast.8), channel_id=1, replica_groups=mesh['groups'=2,'wide'=4,'narrow'=4] {'wide','narrow'}, dimensions={0} | all-to-all | bytes 8192 | tf_op jit(solution)/shard_map/all_to_all | solution.py:706
  43.6 1.1 %pick_owned.1 = f32[1,392]{1,0:T(1,128)} custom-call(s32[8,128]{1,0:T(8,128)S(1)} %find_slots.1.slots_ref, f32[16,64]{1,0:T(8,128)S(1)} %bitcast.7), custom_call_target="tpu_custom_call" | custom-call | tf_op jit(solution)/shard_map/pick_owned/pallas_call | solution.py:707
  (4 shorter events, 0.0 us)
Async XLA Ops:
  1.9 17.2 %collective-permute-start = (f32[1064,128]{1,0:T(8,128)S(1)}, f32[1064,128]{1,0:T(8,128)S(1)}, u32[]{:S(2)}, u32[]{:S(2)}) collective-permute-start(f32[1064,128]{1,0:T(8,128)S(1)} %get-tuple-element.35), channel_id=1, source_target_pairs={{0,4},{4,0},{8,12},{12,8},{1,5},{5,1},{9,13},{13,9},{2,6},{6,2},{1... | collective-permute-start | bytes 1634312 | tf_op jit(solution)/shard_map/ppermute | solution.py:613
  2.4 16.7 %collective-permute-start.1 = (f32[664,128]{1,0:T(8,128)S(1)}, f32[664,128]{1,0:T(8,128)S(1)}, u32[]{:S(2)}, u32[]{:S(2)}) collective-permute-start(f32[664,128]{1,0:T(8,128)S(1)} %get-tuple-element.36.after_ref), channel_id=1, source_target_pairs={{0,12},{4,8},{8,4},{12,0},{1,13},{5,9},{9,5},{13,1},{2,14},{6,10},... | collective-permute-start | bytes 1019912 | tf_op jit(solution)/shard_map/ppermute | solution.py:613
  5.4 8.7 %collective-permute-start.2 = (f32[88,128]{1,0:T(8,128)S(1)}, f32[88,128]{1,0:T(8,128)S(1)}, u32[]{:S(2)}, u32[]{:S(2)}) collective-permute-start(f32[88,128]{1,0:T(8,128)S(1)} %get-tuple-element.39), channel_id=1, source_target_pairs={{0,1},{1,0},{2,3},{3,2},{4,5},{5,4},{6,7},{7,6},{8,9},{9,8},{10,11... | collective-permute-start | bytes 135176 | tf_op jit(solution)/shard_map/ppermute | solution.py:613
  7.1 7.0 %collective-permute-start.3 = (f32[88,128]{1,0:T(8,128)S(1)}, f32[88,128]{1,0:T(8,128)S(1)}, u32[]{:S(2)}, u32[]{:S(2)}) collective-permute-start(f32[88,128]{1,0:T(8,128)S(1)} %get-tuple-element.40), channel_id=1, source_target_pairs={{0,3},{1,2},{2,1},{3,0},{4,7},{5,6},{6,5},{7,4},{8,11},{9,10},{10,... | collective-permute-start | bytes 135176 | tf_op jit(solution)/shard_map/ppermute | solution.py:613
  9.5 4.5 %collective-permute-start.4 = (f32[16,128]{1,0:T(8,128)S(1)}, f32[16,128]{1,0:T(8,128)S(1)}, u32[]{:S(2)}, u32[]{:S(2)}) collective-permute-start(f32[16,128]{1,0:T(8,128)S(1)} %get-tuple-element.41.block_ref), channel_id=1, source_target_pairs={{0,2},{1,3},{2,0},{3,1},{4,6},{5,7},{6,4},{7,5},{8,10},{9,11},{10,... | collective-permute-start | bytes 24584 | tf_op jit(solution)/shard_map/ppermute | solution.py:608
  14.2 2.8 %collective-permute-start.5 = (f32[88,128]{1,0:T(8,128)S(1)}, f32[88,128]{1,0:T(8,128)S(1)}, u32[]{:S(2)}, u32[]{:S(2)}) collective-permute-start(f32[88,128]{1,0:T(8,128)S(1)} %get-tuple-element.42), channel_id=1, source_target_pairs={{0,4},{4,0},{8,12},{12,8},{1,5},{5,1},{9,13},{13,9},{2,6},{6,2},{1... | collective-permute-start | bytes 135176 | tf_op jit(solution)/shard_map/ppermute | solution.py:613
  14.3 4.3 %collective-permute-start.6 = (f32[88,128]{1,0:T(8,128)S(1)}, f32[88,128]{1,0:T(8,128)S(1)}, u32[]{:S(2)}, u32[]{:S(2)}) collective-permute-start(f32[88,128]{1,0:T(8,128)S(1)} %get-tuple-element.43), channel_id=1, source_target_pairs={{0,12},{4,8},{8,4},{12,0},{1,13},{5,9},{9,5},{13,1},{2,14},{6,10},... | collective-permute-start | bytes 135176 | tf_op jit(solution)/shard_map/ppermute | solution.py:613
  14.9 3.7 %collective-permute-start.7 = (f32[16,128]{1,0:T(8,128)S(1)}, f32[16,128]{1,0:T(8,128)S(1)}, u32[]{:S(2)}, u32[]{:S(2)}) collective-permute-start(f32[16,128]{1,0:T(8,128)S(1)} %get-tuple-element.46.after_ref.refs_0_), channel_id=1, source_target_pairs={{0,8},{4,12},{8,0},{12,4},{1,9},{5,13},{9,1},{13,5},{2,10},{6,14},... | collective-permute-start | bytes 24584 | tf_op jit(solution)/shard_map/ppermute | solution.py:608
  17.1 8.7 %collective-permute-start.8 = (f32[400,128]{1,0:T(8,128)S(1)}, f32[400,128]{1,0:T(8,128)S(1)}, u32[]{:S(2)}, u32[]{:S(2)}) collective-permute-start(f32[400,128]{1,0:T(8,128)S(1)} %pack_cot.1), channel_id=1, source_target_pairs={{0,12},{4,8},{8,4},{12,0},{1,13},{5,9},{9,5},{13,1},{2,14},{6,10},... | collective-permute-start | bytes 614408 | tf_op jit(solution)/shard_map/ppermute | solution.py:613

commit v11 on v10

--- a/solution.py
+++ b/solution.py
@@ -33,9 +33,19 @@
     return lax.rem(lax.axis_index(axis), 2) == 1
 
 
-def pack_strips(order_ref, map_ref, cot_ref, mob_ref, after_ref, strip_a_ref, strip_b_ref, block_ref):
+def pack_strips(*refs):
+    count = (len(refs) - 4) // 2
+    sources, targets = refs[:count], refs[count : 2 * count]
+    strip_a_ref, strip_b_ref, block_ref, sems = refs[2 * count :]
+    copies = [pltpu.make_async_copy(a, b, sems.at[i]) for i, (a, b) in enumerate(zip(sources, targets))]
+    for copy in copies:
+        copy.start()
+    order_ref, map_ref, cot_ref, mob_ref = targets[:4]
     params, layers = order_ref.shape[:2]
     odd = is_odd("narrow")
+    for copy in copies:
+        copy.wait()
+
     lane = lanes((8, 128))
     zero = jnp.zeros((8, 128), jnp.float32)
 
@@ -69,14 +79,11 @@
         ref[8 * (params + 1) :, :] = block_ref[...]
 
 
-def pack_rows(*refs):
-    count = (len(refs) - 3) // 2
-    sources, targets = refs[:count], refs[count : 2 * count]
-    near_a_ref, row_b_ref, sems = refs[2 * count :]
-    copies = [pltpu.make_async_copy(a, b, sems.at[i]) for i, (a, b) in enumerate(zip(sources, targets))]
-    for copy in copies:
-        copy.start()
-    order_ref, map_ref, cot_ref = targets[:3]
+def pack_rows(
+    order_ref, map_ref, cot_ref, strip_ref, block_ref, after_ref, near_a_ref, row_b_ref, strip_a_ref, out_block_ref
+):
+    strip_a_ref[...] = strip_ref[...]
+    out_block_ref[...] = block_ref[...]
     params, layers = order_ref.shape[:2]
     maps, cots = row_places(params, layers)
     gap = jnp.zeros((LEAD, 128), jnp.float32)
@@ -90,14 +97,11 @@
         ref[cots - LEAD : cots, :] = gap
     near_a_ref[cots : cots + LEAD, :] = gap
     near_a_ref[near_a_ref.shape[0] - LEAD :, :] = gap
-    copies[0].wait()
     for p in range(params):
         for z in range(layers):
             k = LEAD + (p * layers + z) * EDGE
             for ref, is_last in zip(row_refs, last):
                 ref[k : k + EDGE, :] = order_ref[p, z, pl.ds((8 - EDGE) * is_last, EDGE), :]
-    for copy in copies[1:]:
-        copy.wait()
     for z in range(layers):
         k = maps + z * MAP_EDGE
         for ref, is_last in zip(row_refs, last):
@@ -107,6 +111,10 @@
         for z in range(layers):
             k = cots + LEAD + (p * layers + z) * ADJ_EDGE
             near_a_ref[k : k + ADJ_EDGE, :] = cot_ref[p, z, rows, :]
+
+
+def relay(strip_ref, out_ref):
+    out_ref[...] = strip_ref[...]
 
 
 def pack_cot(cot_ref, after_ref, out_ref):
@@ -637,21 +645,23 @@
         order_init, grain_map, cotangent, mobility.reshape(1, owned), brick_grains, grain_slot.reshape(-1, 128)
     )
     here, anywhere = pl.BlockSpec(memory_space=pltpu.VMEM), pl.BlockSpec(memory_space=pl.ANY)
-    *fetched, near_a, row_b = kernel(
-        pack_rows,
+    *fetched, strip_a, strip_b, block = kernel(
+        pack_strips,
         tuple(jax.ShapeDtypeStruct(x.shape, x.dtype) for x in arguments)
-        + (f32(edge_rows + cot_rows, 128), f32(edge_rows, 128)),
-        (pltpu.SemaphoreType.DMA((len(arguments),)),), name="pack_rows",
+        + (f32(strip_rows + block_rows, 128),) * 2 + (f32(block_rows, 128),),
+        (pltpu.SemaphoreType.DMA((len(arguments),)),), name="pack_strips",
         in_specs=[pl.BlockSpec(memory_space=pltpu.HBM)] * len(arguments),
     )(*(pltpu.with_memory_space_constraint(x, pltpu.HBM) for x in arguments))
-    order_init, grain_map, cotangent, mobility_row, brick_grains, grain_slot = fetched
-    strip_a, strip_b, block = kernel(
-        pack_strips, (f32(strip_rows + block_rows, 128),) * 2 + (f32(block_rows, 128),),
-        name="pack_strips", in_specs=[here] * 4 + [anywhere],
-    )(order_init, grain_map, cotangent, mobility_row, row_b)
+    order_init, grain_map, cotangent, _, brick_grains, grain_slot = fetched
+    near_a, row_b, strip_a, block = kernel(
+        pack_rows,
+        (f32(edge_rows + cot_rows, 128), f32(edge_rows, 128), f32(strip_rows + block_rows, 128), f32(block_rows, 128)),
+        name="pack_rows", in_specs=[here] * 5 + [anywhere],
+    )(order_init, grain_map, cotangent, strip_a, block, strip_b)
     row_b = swapped(row_b, "wide", wide_count, 1)
     near_a = swapped(near_a, "wide", wide_count, 0)
     strip_b = swapped(strip_b, "narrow", narrow_count, 1)
+    strip_b = kernel(relay, f32(*strip_b.shape), name="relay", cost=600_000_000)(strip_b)
     strip_a = swapped(strip_a, "narrow", narrow_count, 0)
     others = [opposite(block, "narrow")] if small else []
 

time: 44.9 us -> 44.9 us (level)
  blocking collectives: 9.94 us -> 9.38 us
    ppermute x7, starting transfers between devices: 8.04 us -> 7.25 us  [swapped(): lax.ppermute(value, axis, [(i, (i + by) % count) for i, by in enumerate(s...]
    ppermute x2, starting transfers between devices: 1.61 us -> 2.32 us  [opposite(): return lax.ppermute(value, axis, [(i, (i + 2) % 4) for i in range(4)])]
    all_to_all x1, blocking collectives: 9.94 us -> 9.38 us  [per_device(): sums = lax.all_to_all(sums, both, 0, 0, tiled=True)]
    pallas_call x2 -> x3, Pallas kernels: 1.63 us -> 1.91 us  [the longest x1 1.78 us: per_device(): kernel(pack_strips, tuple((jax.ShapeDtypeStruct(x.shape, x.dtype) for x i...]
  transfers between devices with their start and end apart: 9 -> 9, of which waited for: 2 -> 3; matrix products, arithmetic and copies ran while one was open for 0% -> 0% of each run, Pallas kernels for 19% -> 18%
where the time goes in v11:
time: 44.9 us; the launch traced here: 44.8 us
  Pallas kernels  18.9 us (42%)
  starting transfers between devices  9.57 us (21%)
  blocking collectives  9.38 us (21%)
  waiting for transfers between devices  6.24 us (14%)
  between operations  0.72 us (2%)
    all_to_all x1, blocking collectives, per_device(): sums = lax.all_to_all(sums, both, 0, 0, tiled=True)  9.38 us
    pallas_call x1, Pallas kernels, per_device(): kernel(backward, (f32(*order_init.shape), f32(bricks, listed)), ([vmem(*p...  7.86 us
    ppermute x7, starting transfers between devices, swapped(): lax.ppermute(value, axis, [(i, (i + by) % count) for i, by in enumerate(s...  7.25 us
    pallas_call x1, Pallas kernels, per_device(): kernel(forward, (f32(*order_init.shape), [f32(*padded)] * ITERS, [f32(*pa...  6.69 us
    ppermute x2, waiting for transfers between devices, opposite(): return lax.ppermute(value, axis, [(i, (i + 2) % 4) for i in range(4)])  5.96 us
    ppermute x2, starting transfers between devices, opposite(): return lax.ppermute(value, axis, [(i, (i + 2) % 4) for i in range(4)])  2.32 us
    pallas_call x1, Pallas kernels, per_device(): kernel(pack_strips, tuple((jax.ShapeDtypeStruct(x.shape, x.dtype) for x i...  1.78 us
    pallas_call x1, Pallas kernels, per_device(): kernel(functools.partial(pick_owned, owned), f32(1, owned), (vmem(owned +...  1.13 us
  transfers between devices with their start and end apart: 9, of which 3 were waited for; matrix products, arithmetic and copies ran while one was open for 0% of the time, Pallas kernels for 18%

profile of v11, /device:TPU:0, one launch (start us, length us, event | category | flops | bytes accessed | tf_op | source)
XLA Modules:
  0.0 44.8 jit_solution(785277881785898115)
XLA Ops:
  0.6 1.8 %pack_strips.1 = (f32[8,12,8,128]{3,2,1,0:T(8,128)S(1)}, s32[12,8,128]{2,1,0:T(8,128)S(1)}, f32[8,12,8,128]{3,2,1,0:T(8,128)S(1)}, f32[1,392]{1,0:T(1,128)}, s32...) custom-call(f32[8,12,8,128]{3,2,1,0:T(8,128)} %refs_0_.1, ...), custom_call_target="tpu_custom_call" | custom-call | tf_op jit(solution)/shard_map/pack_strips/pallas_call | solution.py:648
  2.4 0.1 pack_rows.1
  2.6 0.5 %collective-permute-start = (f32[1064,128]{1,0:T(8,128)S(1)}, f32[1064,128]{1,0:T(8,128)S(1)}, u32[]{:S(2)}, u32[]{:S(2)}) collective-permute-start(f32[1064,128]{1,0:T(8,128)S(1)} %get-tuple-element.40), channel_id=1, source_target_pairs={{0,4},{4,0},{8,12},{12,8},{1,5},{5,1},{9,13},{13,9},{2,6},{6,2},{1... | collective-permute-start | bytes 1634312 | tf_op jit(solution)/shard_map/ppermute | solution.py:621
  3.1 4.7 %collective-permute-start.3 = (f32[88,128]{1,0:T(8,128)S(1)}, f32[88,128]{1,0:T(8,128)S(1)}, u32[]{:S(2)}, u32[]{:S(2)}) collective-permute-start(f32[88,128]{1,0:T(8,128)S(1)} %get-tuple-element.39.after_ref), channel_id=1, source_target_pairs={{0,3},{1,2},{2,1},{3,0},{4,7},{5,6},{6,5},{7,4},{8,11},{9,10},{10,... | collective-permute-start | bytes 135176 | tf_op jit(solution)/shard_map/ppermute | solution.py:621
  7.7 1.3 %collective-permute-start.1 = (f32[664,128]{1,0:T(8,128)S(1)}, f32[664,128]{1,0:T(8,128)S(1)}, u32[]{:S(2)}, u32[]{:S(2)}) collective-permute-start(f32[664,128]{1,0:T(8,128)S(1)} %get-tuple-element.41), channel_id=1, source_target_pairs={{0,12},{4,8},{8,4},{12,0},{1,13},{5,9},{9,5},{13,1},{2,14},{6,10},... | collective-permute-start | bytes 1019912 | tf_op jit(solution)/shard_map/ppermute | solution.py:621
  9.0 0.0 collective-permute-start.2
  9.0 0.8 %collective-permute-start.4 = (f32[16,128]{1,0:T(8,128)S(1)}, f32[16,128]{1,0:T(8,128)S(1)}, u32[]{:S(2)}, u32[]{:S(2)}) collective-permute-start(f32[16,128]{1,0:T(8,128)S(1)} %get-tuple-element.43.block_ref), channel_id=1, source_target_pairs={{0,2},{1,3},{2,0},{3,1},{4,6},{5,7},{6,4},{7,5},{8,10},{9,11},{10,... | collective-permute-start | bytes 24584 | tf_op jit(solution)/shard_map/ppermute | solution.py:616
  9.8 0.3 collective-permute-done.3.strip_ref
  10.1 3.5 %collective-permute-done.4.refs_0_ = f32[16,128]{1,0:T(8,128)S(1)} collective-permute-done((f32[16,128]{1,0:T(8,128)S(1)}, f32[16,128]{1,0:T(8,128)S(1)}, u32[]{:S(2)}, u32[]{:S(2)}) %collective-permute-start.4) | collective-permute-done | bytes 8224 | tf_op jit(solution)/shard_map/ppermute | solution.py:616
  13.6 0.0 collective-permute-done.2.strip_a_ref
  13.6 0.1 pack_far.1
  13.7 0.1 collective-permute-start.5
  13.7 0.7 %collective-permute-start.6 = (f32[88,128]{1,0:T(8,128)S(1)}, f32[88,128]{1,0:T(8,128)S(1)}, u32[]{:S(2)}, u32[]{:S(2)}) collective-permute-start(f32[88,128]{1,0:T(8,128)S(1)} %get-tuple-element.45), channel_id=1, source_target_pairs={{0,12},{4,8},{8,4},{12,0},{1,13},{5,9},{9,5},{13,1},{2,14},{6,10},... | collective-permute-start | bytes 135176 | tf_op jit(solution)/shard_map/ppermute | solution.py:621
  14.4 1.5 %collective-permute-start.7 = (f32[16,128]{1,0:T(8,128)S(1)}, f32[16,128]{1,0:T(8,128)S(1)}, u32[]{:S(2)}, u32[]{:S(2)}) collective-permute-start(f32[16,128]{1,0:T(8,128)S(1)} %get-tuple-element.48.after_ref.refs_0_), channel_id=1, source_target_pairs={{0,8},{4,12},{8,0},{12,4},{1,9},{5,13},{9,1},{13,5},{2,10},{6,14},... | collective-permute-start | bytes 24584 | tf_op jit(solution)/shard_map/ppermute | solution.py:616
  15.9 0.6 %find_slots.1.slots_ref = s32[8,128]{1,0:T(8,128)S(1)} custom-call(s32[16,64]{1,0:T(8,128)S(1)} %get-tuple-element.46.bricks_ref, s32[49,128]{1,0:T(8,128)S(1)} %get-tuple-element.47.slot_ref, f32[16,128]{1,0:T(8,128)S(1)} %get-tuple-element.48.after_ref.refs_0_), custom_call_target="tpu_custom_call" | custom-call | tf_op jit(solution)/shard_map/find_slots/pallas_call | solution.py:675
  16.5 0.0 collective-permute-done.5.refs_1_.far_a_ref.after_ref
  16.5 0.1 pack_cot.1
  16.6 0.1 collective-permute-start.8
  16.7 2.5 %collective-permute-done.7.refs_3_ = f32[16,128]{1,0:T(8,128)S(1)} collective-permute-done((f32[16,128]{1,0:T(8,128)S(1)}, f32[16,128]{1,0:T(8,128)S(1)}, u32[]{:S(2)}, u32[]{:S(2)}) %collective-permute-start.7) | collective-permute-done | bytes 8224 | tf_op jit(solution)/shard_map/ppermute | solution.py:616
  19.2 0.5 %find_mobility.1.table_ref = f32[8,128]{1,0:T(8,128)S(1)} custom-call(s32[8,128]{1,0:T(8,128)S(1)} %find_slots.1.slots_ref, f32[16,128]{1,0:T(8,128)S(1)} %get-tuple-element.48.after_ref.refs_0_, f32[88,128]{1,0:T(8,128)S(1)} %collective-permute-done.5.refs_1_.far_a_ref.after_ref, f32[88,128]{1,0:T(8,128)S(1)} %collective-permute-done.6.refs_2_.far_b_ref, ...), custom_call_target="tpu_custom_call" | custom-call | flops 2500000000 | bytes 2500000 | tf_op jit(solution)/shard_map/find_mobility/pallas_call | solution.py:687
  19.7 6.7 %forward.1 = (f32[8,12,8,128]{3,2,1,0:T(8,128)}, f32[8,12,24,128]{3,2,1,0:T(8,128)S(1)}, f32[8,12,24,128]{3,2,1,0:T(8,128)S(1)}, f32[8,12,24,128]{3,2,1,0:T(8,12...) custom-call(f32[8,12,8,128]{3,2,1,0:T(8,128)S(1)} %get-tuple-element, ...), custom_call_target="tpu_custom_call" | custom-call | tf_op jit(solution)/shard_map/forward/pallas_call | solution.py:694
  26.4 7.9 %backward.1 = (f32[8,12,8,128]{3,2,1,0:T(8,128)}, f32[16,64]{1,0:T(8,128)S(1)}) custom-call(f32[8,12,8,128]{3,2,1,0:T(8,128)S(1)} %get-tuple-element.36.cot_ref, s32[12,8,128]{2,1,0:T(8,128)S(1)} %get-tuple-element.35.map_ref, f32[1064,128]{1,0:T(8,128)S(1)} %collective-permute-done.row_a_ref, f32[400,128]{1,0:T(8,128)S(1)} %collective-permute-done.8.row_b_ref, ...), custom_call_target="tpu_custom_call" | custom-call | tf_op jit(solution)/shard_map/backward/pallas_call | solution.py:703
  34.3 9.4 %all_to_all.11 = f32[16,1,64]{2,1,0:T(1,128)S(1)} all-to-all(f32[16,1,64]{2,1,0:T(1,128)S(1)} %bitcast.8), channel_id=1, replica_groups=mesh['groups'=2,'wide'=4,'narrow'=4] {'wide','narrow'}, dimensions={0} | all-to-all | bytes 8192 | tf_op jit(solution)/shard_map/all_to_all | solution.py:716
  43.6 1.1 %pick_owned.1 = f32[1,392]{1,0:T(1,128)} custom-call(s32[8,128]{1,0:T(8,128)S(1)} %find_slots.1.slots_ref, f32[16,64]{1,0:T(8,128)S(1)} %bitcast.7), custom_call_target="tpu_custom_call" | custom-call | tf_op jit(solution)/shard_map/pick_owned/pallas_call | solution.py:717
  (5 shorter events, 0.0 us)
Async XLA Ops:
  2.6 17.1 %collective-permute-start = (f32[1064,128]{1,0:T(8,128)S(1)}, f32[1064,128]{1,0:T(8,128)S(1)}, u32[]{:S(2)}, u32[]{:S(2)}) collective-permute-start(f32[1064,128]{1,0:T(8,128)S(1)} %get-tuple-element.40), channel_id=1, source_target_pairs={{0,4},{4,0},{8,12},{12,8},{1,5},{5,1},{9,13},{13,9},{2,6},{6,2},{1... | collective-permute-start | bytes 1634312 | tf_op jit(solution)/shard_map/ppermute | solution.py:621
  3.1 7.0 %collective-permute-start.3 = (f32[88,128]{1,0:T(8,128)S(1)}, f32[88,128]{1,0:T(8,128)S(1)}, u32[]{:S(2)}, u32[]{:S(2)}) collective-permute-start(f32[88,128]{1,0:T(8,128)S(1)} %get-tuple-element.39.after_ref), channel_id=1, source_target_pairs={{0,3},{1,2},{2,1},{3,0},{4,7},{5,6},{6,5},{7,4},{8,11},{9,10},{10,... | collective-permute-start | bytes 135176 | tf_op jit(solution)/shard_map/ppermute | solution.py:621
  7.7 11.9 %collective-permute-start.1 = (f32[664,128]{1,0:T(8,128)S(1)}, f32[664,128]{1,0:T(8,128)S(1)}, u32[]{:S(2)}, u32[]{:S(2)}) collective-permute-start(f32[664,128]{1,0:T(8,128)S(1)} %get-tuple-element.41), channel_id=1, source_target_pairs={{0,12},{4,8},{8,4},{12,0},{1,13},{5,9},{9,5},{13,1},{2,14},{6,10},... | collective-permute-start | bytes 1019912 | tf_op jit(solution)/shard_map/ppermute | solution.py:621
  9.0 4.6 %collective-permute-start.2 = (f32[88,128]{1,0:T(8,128)S(1)}, f32[88,128]{1,0:T(8,128)S(1)}, u32[]{:S(2)}, u32[]{:S(2)}) collective-permute-start(f32[88,128]{1,0:T(8,128)S(1)} %get-tuple-element.42), channel_id=1, source_target_pairs={{0,1},{1,0},{2,3},{3,2},{4,5},{5,4},{6,7},{7,6},{8,9},{9,8},{10,11... | collective-permute-start | bytes 135176 | tf_op jit(solution)/shard_map/ppermute | solution.py:621
  9.0 4.5 %collective-permute-start.4 = (f32[16,128]{1,0:T(8,128)S(1)}, f32[16,128]{1,0:T(8,128)S(1)}, u32[]{:S(2)}, u32[]{:S(2)}) collective-permute-start(f32[16,128]{1,0:T(8,128)S(1)} %get-tuple-element.43.block_ref), channel_id=1, source_target_pairs={{0,2},{1,3},{2,0},{3,1},{4,6},{5,7},{6,4},{7,5},{8,10},{9,11},{10,... | collective-permute-start | bytes 24584 | tf_op jit(solution)/shard_map/ppermute | solution.py:616
  13.7 2.8 %collective-permute-start.5 = (f32[88,128]{1,0:T(8,128)S(1)}, f32[88,128]{1,0:T(8,128)S(1)}, u32[]{:S(2)}, u32[]{:S(2)}) collective-permute-start(f32[88,128]{1,0:T(8,128)S(1)} %get-tuple-element.44), channel_id=1, source_target_pairs={{0,4},{4,0},{8,12},{12,8},{1,5},{5,1},{9,13},{13,9},{2,6},{6,2},{1... | collective-permute-start | bytes 135176 | tf_op jit(solution)/shard_map/ppermute | solution.py:621
  13.7 5.4 %collective-permute-start.6 = (f32[88,128]{1,0:T(8,128)S(1)}, f32[88,128]{1,0:T(8,128)S(1)}, u32[]{:S(2)}, u32[]{:S(2)}) collective-permute-start(f32[88,128]{1,0:T(8,128)S(1)} %get-tuple-element.45), channel_id=1, source_target_pairs={{0,12},{4,8},{8,4},{12,0},{1,13},{5,9},{9,5},{13,1},{2,14},{6,10},... | collective-permute-start | bytes 135176 | tf_op jit(solution)/shard_map/ppermute | solution.py:621
  14.4 4.8 %collective-permute-start.7 = (f32[16,128]{1,0:T(8,128)S(1)}, f32[16,128]{1,0:T(8,128)S(1)}, u32[]{:S(2)}, u32[]{:S(2)}) collective-permute-start(f32[16,128]{1,0:T(8,128)S(1)} %get-tuple-element.48.after_ref.refs_0_), channel_id=1, source_target_pairs={{0,8},{4,12},{8,0},{12,4},{1,9},{5,13},{9,1},{13,5},{2,10},{6,14},... | collective-permute-start | bytes 24584 | tf_op jit(solution)/shard_map/ppermute | solution.py:616
  16.6 9.8 %collective-permute-start.8 = (f32[400,128]{1,0:T(8,128)S(1)}, f32[400,128]{1,0:T(8,128)S(1)}, u32[]{:S(2)}, u32[]{:S(2)}) collective-permute-start(f32[400,128]{1,0:T(8,128)S(1)} %pack_cot.1), channel_id=1, source_target_pairs={{0,12},{4,8},{8,4},{12,0},{1,13},{5,9},{9,5},{13,1},{2,14},{6,10},... | collective-permute-start | bytes 614408 | tf_op jit(solution)/shard_map/ppermute | solution.py:621

commit v12 on v10

--- a/solution.py
+++ b/solution.py
@@ -13,7 +13,7 @@
 EDGE = 6
 MAP_EDGE = 5
 ADJ_EDGE = 4
-ROWS = 24
+ROWS = 32
 COLS = 10
 LEAD = 8
 CORNER = (5, 3, 4)
@@ -245,7 +245,9 @@
         for j in range(group):
             z = step * group + j
             for i in range(count):
-                stores += body(z, i, jnp.minimum(start + 8 * i + ((z + 16) >> 5), most))
+                r = jnp.minimum(start + 8 * i + ((z + 16) >> 5), most)
+                rows = pl.ds(start + 8 * i, 8) if start % 8 == 0 else pl.ds(r, 8)
+                stores += body(z, i, rows, r)
             if len(stores) >= 64 or j == group - 1:
                 for store in stores:
                     store()
@@ -256,11 +258,14 @@
 
 
 def each_window(windows, body):
+    start, count, most = windows
+
     def one(i, carry):
-        body(windows[0] + 8 * i)
+        r = jnp.minimum(start + 8 * i, most)
+        body(pl.ds(pl.multiple_of(r, 8) if start % 8 == 0 else r, 8), r)
         return carry
 
-    lax.fori_loop(0, windows[1], one, 0)
+    lax.fori_loop(0, count, one, 0)
 
 
 def put(ref, index, value):
@@ -270,10 +275,10 @@
     return store
 
 
-def neighbours(ref, ends_ref, value, p, z, r):
+def neighbours(ref, ends_ref, value, p, z, rows, r):
     layers = ref.shape[1]
     lane = lanes((8, 128))
-    rows, before, after = pl.ds(r, 8), pl.ds(r - 1, 8), pl.ds(r + 1, 8)
+    before, after = pl.ds(r - 1, 8), pl.ds(r + 1, 8)
     below, above = jnp.maximum(z - 1, 0), jnp.minimum(z + 1, layers - 1)
     ends = ends_ref[p, z, rows, :]
     left = roll(jnp.where(lane == 127, ends, value), 1)
@@ -282,11 +287,11 @@
     return total + (ref[p, below, rows, :] + ref[p, above, rows, :])
 
 
-def strip_neighbours(ref, core_ref, values, r, outer_ref=None):
+def strip_neighbours(ref, core_ref, values, rows, r, outer_ref=None):
     params, layers = core_ref.shape[:2]
     lane = lanes((8, 128))
     col = lane % COLS
-    rows, before, after = pl.ds(r, 8), pl.ds(r - 1, 8), pl.ds(r + 1, 8)
+    before, after = pl.ds(r - 1, 8), pl.ds(r + 1, 8)
     near = []
     for p in range(params):
         value = values[p]
@@ -339,13 +344,13 @@
 
     def place(z, carry):
         for ref, before in zip((row_a_ref, row_b_ref), from_before):
-            k, target = maps + z * MAP_EDGE + before * (MAP_EDGE - 8), pl.ds(16 - 16 * before, 8)
+            k, target = maps + z * MAP_EDGE + before * (MAP_EDGE - 8), pl.ds(20 - 16 * before, 8)
             g_ref[z, target, :] = ref[pl.ds(k, 8), :]
             for p in every:
                 k = LEAD + (p * layers + z) * EDGE + before * (EDGE - 8)
                 e_refs[0][p, z, target, :] = ref[pl.ds(k, 8), :]
         for p in every:
-            e_refs[0][p, z, 8:16, :] = order_ref[p, z]
+            e_refs[0][p, z, 12:20, :] = order_ref[p, z]
         return carry
 
     lax.fori_loop(0, layers, place, 0)
@@ -355,29 +360,31 @@
     n = CORNER[0]
     for p in every:
         ref = first_strip_ref.at[p]
-        ref[0:8, :] = jnp.zeros(tile, jnp.float32)
-        ref[16:24, :] = jnp.zeros(tile, jnp.float32)
+        ref[4:12, :] = jnp.zeros(tile, jnp.float32)
+        ref[20:28, :] = jnp.zeros(tile, jnp.float32)
         a, b = far_a_ref[n * p : n * p + n, :], far_b_ref[n * p : n * p + n, :]
-        ref[8 - n : 8, :] = jnp.where(odd, a, b)
-        ref[8:16, :] = order[p]
-        ref[16 : 16 + n, :] = jnp.where(odd, b, a)
-        outer_ref[p, 8:16, :] = jnp.where(col == 0, roll(sides[p][0], 1), roll(sides[p][1], 127))
+        ref[12 - n : 12, :] = jnp.where(odd, a, b)
+        ref[12:20, :] = order[p]
+        ref[20 : 20 + n, :] = jnp.where(odd, b, a)
+        outer_ref[p, 12:20, :] = jnp.where(col == 0, roll(sides[p][0], 1), roll(sides[p][1], 127))
     at, n = params * (CORNER[0] + CORNER[1]), CORNER[2]
     gs_ref[...] = jnp.zeros_like(gs_ref)
     a, b = far_a_ref[at : at + n, :], far_b_ref[at : at + n, :]
-    gs_ref[8 - n : 8, :] = jnp.where(odd, a, b)
-    gs_ref[8:16, :] = cells
-    gs_ref[16 : 16 + n, :] = jnp.where(odd, b, a)
-    for r in (0, 8, 16):
-        rows = slice(r, r + 8)
+    gs_ref[12 - n : 12, :] = jnp.where(odd, a, b)
+    gs_ref[12:20, :] = cells
+    gs_ref[20 : 20 + n, :] = jnp.where(odd, b, a)
+
+    def first_ends(rows, r):
         spread_ends(ends_ref, [first_strip_ref[p, rows, :] for p in every], rows)
+
+    each_window((7, 3, 17), first_ends)
 
     def lookup(index, which):
         values = jnp.broadcast_to(table_ref[which // 2 : which // 2 + 1, :], tile)
         return jnp.take_along_axis(values, index + 64 * (which % 2), axis=1, mode="promise_in_bounds")
 
     for i in range(3):
-        r = 8 * i
+        r = 4 + 8 * i
         for z in range(layers):
             index = map_ref[z] if i == 1 else g_ref[z, r : r + 8, :].astype(jnp.int32) & 63
             m_ref[z, r : r + 8, :] = lookup(index, 3 * i + 1)
@@ -388,14 +395,13 @@
         old, old_strip = e_refs[t], strip_refs[t]
         last = t == ITERS - 1
 
-        def core(z, i, r):
-            rows = pl.ds(r, 8)
+        def core(z, i, rows, r):
             base = base_of([old[p, z, rows, :] for p in every])
             m = m_ref[z, rows, :]
             stores = []
             for p in every:
                 e = old[p, z, rows, :]
-                rate = e * (base - 0.5 * (e * e)) - neighbours(old, ends_ref, e, p, z, r)
+                rate = e * (base - 0.5 * (e * e)) - neighbours(old, ends_ref, e, p, z, rows, r)
                 new = e - m * rate
                 stores.append(put(rate_refs[t], (p, z, rows, slice(None)), rate))
                 if last:
@@ -408,28 +414,26 @@
         if last:
             return
 
-        def strip(r):
-            rows = pl.ds(r, 8)
+        def strip(rows, r):
             e = [old_strip[p, rows, :] for p in every]
             m = ms_ref[rows, :]
             base = base_of(e)
-            near = strip_neighbours(old_strip, old, e, r, outer_ref if t == 0 else None)
+            near = strip_neighbours(old_strip, old, e, rows, r, outer_ref if t == 0 else None)
             for p in every:
                 rate = e[p] * (base - 0.5 * (e[p] * e[p])) - near[p]
                 strip_refs[t + 1][p, rows, :] = e[p] - m * rate
 
         each_window(strip_windows, strip)
 
-        def ends(r):
-            rows = pl.ds(r, 8)
+        def ends(rows, r):
             spread_ends(ends_ref, [strip_refs[t + 1][p, rows, :] for p in every], rows)
 
         each_window(end_windows, ends)
 
-    step(0, (3, 3, 13), (4, 2), (4, 2))
-    step(1, (4, 2, 12), (4, 2), (4, 2))
-    step(2, (4, 2, 12), (4, 2), (8, 1))
-    step(3, (8, 1, 8), None, None)
+    step(0, (7, 3, 17), (8, 2, 16), (8, 2, 16))
+    step(1, (8, 2, 16), (8, 2, 16), (8, 2, 16))
+    step(2, (8, 2, 16), (8, 2, 16), (12, 1, 12))
+    step(3, (12, 1, 12), None, None)
 
 
 def backward(
@@ -448,17 +452,17 @@
 
     def place(z, carry):
         for ref, base, before in zip((row_a_ref, row_b_ref), (cots, 0), from_before):
-            rows = pl.ds(16 - 16 * before, 8)
+            rows = pl.ds(20 - 16 * before, 8)
             m = m_ref[z, rows, :]
             for p in every:
                 k = base + LEAD + (p * layers + z) * ADJ_EDGE + before * (ADJ_EDGE - 8)
                 value = ref[pl.ds(k, 8), :]
                 lam_refs[0][p, z, rows, :] = value
                 u_refs[0][p, z, rows, :] = m * value
-        m = m_ref[z, 8:16, :]
+        m = m_ref[z, 12:20, :]
         for p in every:
-            lam_refs[0][p, z, 8:16, :] = cot_ref[p, z]
-            u_refs[0][p, z, 8:16, :] = m * cot_ref[p, z]
+            lam_refs[0][p, z, 12:20, :] = cot_ref[p, z]
+            u_refs[0][p, z, 12:20, :] = m * cot_ref[p, z]
         return carry
 
     lax.fori_loop(0, layers, place, 0)
@@ -467,18 +471,17 @@
     for p in every:
         at = params * CORNER[0] + n * p
         ref = slam_refs[0].at[p]
-        ref[0:8, :] = jnp.zeros(tile, jnp.float32)
-        ref[16:24, :] = jnp.zeros(tile, jnp.float32)
+        ref[4:12, :] = jnp.zeros(tile, jnp.float32)
+        ref[20:28, :] = jnp.zeros(tile, jnp.float32)
         a, b = far_a_ref[at : at + n, :], far_b_ref[at : at + n, :]
-        ref[8 - n : 8, :] = jnp.where(odd, a, b)
-        ref[8:16, :] = cot[p]
-        ref[16 : 16 + n, :] = jnp.where(odd, b, a)
-        for r in (0, 8, 16):
+        ref[12 - n : 12, :] = jnp.where(odd, a, b)
+        ref[12:20, :] = cot[p]
+        ref[20 : 20 + n, :] = jnp.where(odd, b, a)
+        for r in (4, 12, 20):
             su_refs[0][p, r : r + 8, :] = ms_ref[r : r + 8, :] * ref[r : r + 8, :]
 
     def spread(slot, windows):
-        def ends(r):
-            rows = pl.ds(r, 8)
+        def ends(rows, r):
             spread_ends(ends_ref, [su_refs[slot][p, rows, :] for p in every], rows)
 
         each_window(windows, ends)
@@ -486,8 +489,7 @@
     def step(t, slot, windows, strip_windows, end_windows):
         old, old_strip = u_refs[slot], su_refs[slot]
 
-        def core(z, i, r):
-            rows = pl.ds(r, 8)
+        def core(z, i, rows, r):
             e = [e_refs[t][p, z, rows, :] for p in every]
             u = [old[p, z, rows, :] for p in every]
             base, inner = base_of(e), inner_of(e, u)
@@ -496,7 +498,7 @@
             stores = [put(work_ref, (t - 1, z, i), work)]
             for p in every:
                 e, u = e_refs[t][p, z, rows, :], old[p, z, rows, :]
-                change = u * (base - 1.5 * (e * e)) + e * inner - neighbours(old, ends_ref, u, p, z, r)
+                change = u * (base - 1.5 * (e * e)) + e * inner - neighbours(old, ends_ref, u, p, z, rows, r)
                 new = lam_refs[slot][p, z, rows, :] - change
                 stores.append(put(lam_refs[1 - slot], (p, z, rows, slice(None)), new))
                 stores.append(put(u_refs[1 - slot], (p, z, rows, slice(None)), m * new))
@@ -504,13 +506,12 @@
 
         each_tile(layers, windows, core)
 
-        def strip(r):
-            rows = pl.ds(r, 8)
+        def strip(rows, r):
             e = [se_refs[t - 1][p, rows, :] for p in every]
             u = [old_strip[p, rows, :] for p in every]
             m = ms_ref[rows, :]
             base, inner = base_of(e), inner_of(e, u)
-            near = strip_neighbours(old_strip, old, u, r)
+            near = strip_neighbours(old_strip, old, u, rows, r)
             for p in every:
                 change = u[p] * (base - 1.5 * (e[p] * e[p])) + e[p] * inner - near[p]
                 new = slam_refs[slot][p, rows, :] - change
@@ -520,31 +521,30 @@
         each_window(strip_windows, strip)
         spread(1 - slot, end_windows)
 
-    spread(0, (4, 2))
-    step(3, 0, (4, 2, 12), (4, 2), (4, 2))
-    step(2, 1, (4, 2, 12), (4, 2), (4, 2))
-    step(1, 0, (4, 2, 12), (8, 1), (8, 1))
-
-    def last(z, i, r):
-        rows = pl.ds(r, 8)
+    spread(0, (8, 2, 16))
+    step(3, 0, (8, 2, 16), (8, 2, 16), (8, 2, 16))
+    step(2, 1, (8, 2, 16), (8, 2, 16), (8, 2, 16))
+    step(1, 0, (8, 2, 16), (12, 1, 12), (12, 1, 12))
+
+    def last(z, i, rows, r):
         e = [e_refs[0][p, z, rows, :] for p in every]
         u = [u_refs[1][p, z, rows, :] for p in every]
         base, inner = base_of(e), inner_of(e, u)
         stores = []
         for p in every:
             e, u = e_refs[0][p, z, rows, :], u_refs[1][p, z, rows, :]
-            change = u * (base - 1.5 * (e * e)) + e * inner - neighbours(u_refs[1], ends_ref, u, p, z, r)
+            change = u * (base - 1.5 * (e * e)) + e * inner - neighbours(u_refs[1], ends_ref, u, p, z, rows, r)
             stores.append(put(adjoint_ref, (p, z), lam_refs[1][p, z, rows, :] - change))
         return stores
 
-    each_tile(layers, (8, 1, 8), last)
+    each_tile(layers, (12, 1, 12), last)
 
     grains = [map_ref[z] for z in range(layers)]
     cells = []
     for z in range(layers):
         upper = work_ref[0, z, 0] + work_ref[1, z, 0] + work_ref[2, z, 0]
         lower = work_ref[0, z, 1] + work_ref[1, z, 1] + work_ref[2, z, 1]
-        first = total_of([lam_refs[1][p, z, 8:16, :] * rate_refs[0][p, z, 8:16, :] for p in every])
+        first = total_of([lam_refs[1][p, z, 12:20, :] * rate_refs[0][p, z, 12:20, :] for p in every])
         cells.append(jnp.concatenate([upper[4:8], lower[0:4]], axis=0) + first)
 
     def bin_one(g, carry):

time: 44.9 us -> 45.9 us (1.022)
  Pallas kernels: 18.6 us -> 19.5 us
    pallas_call x1, Pallas kernels: 6.69 us -> 7.26 us  [per_device(): kernel(forward, (f32(*order_init.shape), [f32(*padded)] * ITERS, [f32(*pa...]
  transfers between devices with their start and end apart: 9 -> 9, of which waited for: 2 -> 2; matrix products, arithmetic and copies ran while one was open for 0% -> 0% of each run, Pallas kernels for 19% -> 20%
where the time goes in v12:
time: 45.9 us; the launch traced here: 45.7 us
  Pallas kernels  19.5 us (42%)
  blocking collectives  9.94 us (22%)
  starting transfers between devices  9.65 us (21%)
  waiting for transfers between devices  5.84 us (13%)
  between operations  0.71 us (2%)
    all_to_all x1, blocking collectives, per_device(): sums = lax.all_to_all(sums, both, 0, 0, tiled=True)  9.94 us
    pallas_call x1, Pallas kernels, per_device(): kernel(backward, (f32(*order_init.shape), f32(bricks, listed)), ([vmem(*p...  8.24 us
    ppermute x7, starting transfers between devices, swapped(): lax.ppermute(value, axis, [(i, (i + by) % count) for i, by in enumerate(s...  8.04 us
    pallas_call x1, Pallas kernels, per_device(): kernel(forward, (f32(*order_init.shape), [f32(*padded)] * ITERS, [f32(*pa...  7.26 us
    ppermute x2, waiting for transfers between devices, opposite(): return lax.ppermute(value, axis, [(i, (i + 2) % 4) for i in range(4)])  5.83 us
    ppermute x2, starting transfers between devices, opposite(): return lax.ppermute(value, axis, [(i, (i + 2) % 4) for i in range(4)])  1.61 us
    pallas_call x1, Pallas kernels, per_device(): kernel(pack_rows, tuple((jax.ShapeDtypeStruct(x.shape, x.dtype) for x in...  1.24 us
    pallas_call x1, Pallas kernels, per_device(): kernel(functools.partial(pick_owned, owned), f32(1, owned), (vmem(owned +...  1.13 us
  transfers between devices with their start and end apart: 9, of which 2 were waited for; matrix products, arithmetic and copies ran while one was open for 0% of the time, Pallas kernels for 20%

profile of v12, /device:TPU:0, one launch (start us, length us, event | category | flops | bytes accessed | tf_op | source)
XLA Modules:
  0.0 45.7 jit_solution(7142215041386444687)
XLA Ops:
  0.6 1.2 %pack_rows.1 = (f32[8,12,8,128]{3,2,1,0:T(8,128)S(1)}, s32[12,8,128]{2,1,0:T(8,128)S(1)}, f32[8,12,8,128]{3,2,1,0:T(8,128)S(1)}, f32[1,392]{1,0:T(1,128)S(1)}, s...) custom-call(f32[8,12,8,128]{3,2,1,0:T(8,128)} %refs_0_.1, ...), custom_call_target="tpu_custom_call" | custom-call | tf_op jit(solution)/shard_map/pack_rows/pallas_call | solution.py:640
  1.9 0.5 %collective-permute-start = (f32[1064,128]{1,0:T(8,128)S(1)}, f32[1064,128]{1,0:T(8,128)S(1)}, u32[]{:S(2)}, u32[]{:S(2)}) collective-permute-start(f32[1064,128]{1,0:T(8,128)S(1)} %get-tuple-element.35), channel_id=1, source_target_pairs={{0,4},{4,0},{8,12},{12,8},{1,5},{5,1},{9,13},{13,9},{2,6},{6,2},{1... | collective-permute-start | bytes 1634312 | tf_op jit(solution)/shard_map/ppermute | solution.py:613
  2.4 2.6 %collective-permute-start.1 = (f32[664,128]{1,0:T(8,128)S(1)}, f32[664,128]{1,0:T(8,128)S(1)}, u32[]{:S(2)}, u32[]{:S(2)}) collective-permute-start(f32[664,128]{1,0:T(8,128)S(1)} %get-tuple-element.36.after_ref), channel_id=1, source_target_pairs={{0,12},{4,8},{8,4},{12,0},{1,13},{5,9},{9,5},{13,1},{2,14},{6,10},... | collective-permute-start | bytes 1019912 | tf_op jit(solution)/shard_map/ppermute | solution.py:613
  5.0 0.4 pack_strips.1
  5.4 1.6 %collective-permute-start.2 = (f32[88,128]{1,0:T(8,128)S(1)}, f32[88,128]{1,0:T(8,128)S(1)}, u32[]{:S(2)}, u32[]{:S(2)}) collective-permute-start(f32[88,128]{1,0:T(8,128)S(1)} %get-tuple-element.39), channel_id=1, source_target_pairs={{0,1},{1,0},{2,3},{3,2},{4,5},{5,4},{6,7},{7,6},{8,9},{9,8},{10,11... | collective-permute-start | bytes 135176 | tf_op jit(solution)/shard_map/ppermute | solution.py:613
  7.1 2.5 %collective-permute-start.3 = (f32[88,128]{1,0:T(8,128)S(1)}, f32[88,128]{1,0:T(8,128)S(1)}, u32[]{:S(2)}, u32[]{:S(2)}) collective-permute-start(f32[88,128]{1,0:T(8,128)S(1)} %get-tuple-element.40), channel_id=1, source_target_pairs={{0,3},{1,2},{2,1},{3,0},{4,7},{5,6},{6,5},{7,4},{8,11},{9,10},{10,... | collective-permute-start | bytes 135176 | tf_op jit(solution)/shard_map/ppermute | solution.py:613
  9.5 0.1 collective-permute-start.4
  9.6 4.4 %collective-permute-done.4.refs_0_ = f32[16,128]{1,0:T(8,128)S(1)} collective-permute-done((f32[16,128]{1,0:T(8,128)S(1)}, f32[16,128]{1,0:T(8,128)S(1)}, u32[]{:S(2)}, u32[]{:S(2)}) %collective-permute-start.4) | collective-permute-done | bytes 8224 | tf_op jit(solution)/shard_map/ppermute | solution.py:608
  14.1 0.1 pack_far.1
  14.2 0.1 collective-permute-start.5
  14.3 0.7 %collective-permute-start.6 = (f32[88,128]{1,0:T(8,128)S(1)}, f32[88,128]{1,0:T(8,128)S(1)}, u32[]{:S(2)}, u32[]{:S(2)}) collective-permute-start(f32[88,128]{1,0:T(8,128)S(1)} %get-tuple-element.43), channel_id=1, source_target_pairs={{0,12},{4,8},{8,4},{12,0},{1,13},{5,9},{9,5},{13,1},{2,14},{6,10},... | collective-permute-start | bytes 135176 | tf_op jit(solution)/shard_map/ppermute | solution.py:613
  14.9 1.5 %collective-permute-start.7 = (f32[16,128]{1,0:T(8,128)S(1)}, f32[16,128]{1,0:T(8,128)S(1)}, u32[]{:S(2)}, u32[]{:S(2)}) collective-permute-start(f32[16,128]{1,0:T(8,128)S(1)} %get-tuple-element.46.after_ref.refs_0_), channel_id=1, source_target_pairs={{0,8},{4,12},{8,0},{12,4},{1,9},{5,13},{9,1},{13,5},{2,10},{6,14},... | collective-permute-start | bytes 24584 | tf_op jit(solution)/shard_map/ppermute | solution.py:608
  16.4 0.6 %find_slots.1.slots_ref = s32[8,128]{1,0:T(8,128)S(1)} custom-call(s32[16,64]{1,0:T(8,128)S(1)} %get-tuple-element.44.bricks_ref, s32[49,128]{1,0:T(8,128)S(1)} %get-tuple-element.45.slot_ref, f32[16,128]{1,0:T(8,128)S(1)} %get-tuple-element.46.after_ref.refs_0_), custom_call_target="tpu_custom_call" | custom-call | tf_op jit(solution)/shard_map/find_slots/pallas_call | solution.py:665
  17.0 0.0 collective-permute-done.5.refs_1_.far_a_ref.after_ref
  17.0 0.1 pack_cot.1
  17.1 0.1 collective-permute-start.8
  17.2 1.4 %collective-permute-done.7.refs_3_ = f32[16,128]{1,0:T(8,128)S(1)} collective-permute-done((f32[16,128]{1,0:T(8,128)S(1)}, f32[16,128]{1,0:T(8,128)S(1)}, u32[]{:S(2)}, u32[]{:S(2)}) %collective-permute-start.7) | collective-permute-done | bytes 8224 | tf_op jit(solution)/shard_map/ppermute | solution.py:608
  18.6 0.0 collective-permute-done.6.refs_2_.far_b_ref
  18.6 0.5 %find_mobility.1.table_ref = f32[8,128]{1,0:T(8,128)S(1)} custom-call(s32[8,128]{1,0:T(8,128)S(1)} %find_slots.1.slots_ref, f32[16,128]{1,0:T(8,128)S(1)} %get-tuple-element.46.after_ref.refs_0_, f32[88,128]{1,0:T(8,128)S(1)} %collective-permute-done.5.refs_1_.far_a_ref.after_ref, f32[88,128]{1,0:T(8,128)S(1)} %collective-permute-done.6.refs_2_.far_b_ref, ...), custom_call_target="tpu_custom_call" | custom-call | flops 2500000000 | bytes 2500000 | tf_op jit(solution)/shard_map/find_mobility/pallas_call | solution.py:677
  19.1 0.0 collective-permute-done.1.row_b_ref
  19.1 7.3 %forward.1 = (f32[8,12,8,128]{3,2,1,0:T(8,128)}, f32[8,12,32,128]{3,2,1,0:T(8,128)S(1)}, f32[8,12,32,128]{3,2,1,0:T(8,128)S(1)}, f32[8,12,32,128]{3,2,1,0:T(8,12...) custom-call(f32[8,12,8,128]{3,2,1,0:T(8,128)S(1)} %get-tuple-element, ...), custom_call_target="tpu_custom_call" | custom-call | tf_op jit(solution)/shard_map/forward/pallas_call | solution.py:684
  26.4 8.2 %backward.1 = (f32[8,12,8,128]{3,2,1,0:T(8,128)}, f32[16,64]{1,0:T(8,128)S(1)}) custom-call(f32[8,12,8,128]{3,2,1,0:T(8,128)S(1)} %get-tuple-element.37.cot_ref, s32[12,8,128]{2,1,0:T(8,128)S(1)} %get-tuple-element.34.map_ref, f32[1064,128]{1,0:T(8,128)S(1)} %collective-permute-done.row_a_ref, f32[400,128]{1,0:T(8,128)S(1)} %collective-permute-done.8.row_b_ref, ...), custom_call_target="tpu_custom_call" | custom-call | tf_op jit(solution)/shard_map/backward/pallas_call | solution.py:693
  34.6 9.9 %all_to_all.11 = f32[16,1,64]{2,1,0:T(1,128)S(1)} all-to-all(f32[16,1,64]{2,1,0:T(1,128)S(1)} %bitcast.8), channel_id=1, replica_groups=mesh['groups'=2,'wide'=4,'narrow'=4] {'wide','narrow'}, dimensions={0} | all-to-all | bytes 8192 | tf_op jit(solution)/shard_map/all_to_all | solution.py:706
  44.6 1.1 %pick_owned.1 = f32[1,392]{1,0:T(1,128)} custom-call(s32[8,128]{1,0:T(8,128)S(1)} %find_slots.1.slots_ref, f32[16,64]{1,0:T(8,128)S(1)} %bitcast.7), custom_call_target="tpu_custom_call" | custom-call | tf_op jit(solution)/shard_map/pick_owned/pallas_call | solution.py:707
  (4 shorter events, 0.0 us)
Async XLA Ops:
  1.9 17.2 %collective-permute-start = (f32[1064,128]{1,0:T(8,128)S(1)}, f32[1064,128]{1,0:T(8,128)S(1)}, u32[]{:S(2)}, u32[]{:S(2)}) collective-permute-start(f32[1064,128]{1,0:T(8,128)S(1)} %get-tuple-element.35), channel_id=1, source_target_pairs={{0,4},{4,0},{8,12},{12,8},{1,5},{5,1},{9,13},{13,9},{2,6},{6,2},{1... | collective-permute-start | bytes 1634312 | tf_op jit(solution)/shard_map/ppermute | solution.py:613
  2.4 16.7 %collective-permute-start.1 = (f32[664,128]{1,0:T(8,128)S(1)}, f32[664,128]{1,0:T(8,128)S(1)}, u32[]{:S(2)}, u32[]{:S(2)}) collective-permute-start(f32[664,128]{1,0:T(8,128)S(1)} %get-tuple-element.36.after_ref), channel_id=1, source_target_pairs={{0,12},{4,8},{8,4},{12,0},{1,13},{5,9},{9,5},{13,1},{2,14},{6,10},... | collective-permute-start | bytes 1019912 | tf_op jit(solution)/shard_map/ppermute | solution.py:613
  5.4 8.7 %collective-permute-start.2 = (f32[88,128]{1,0:T(8,128)S(1)}, f32[88,128]{1,0:T(8,128)S(1)}, u32[]{:S(2)}, u32[]{:S(2)}) collective-permute-start(f32[88,128]{1,0:T(8,128)S(1)} %get-tuple-element.39), channel_id=1, source_target_pairs={{0,1},{1,0},{2,3},{3,2},{4,5},{5,4},{6,7},{7,6},{8,9},{9,8},{10,11... | collective-permute-start | bytes 135176 | tf_op jit(solution)/shard_map/ppermute | solution.py:613
  7.1 7.0 %collective-permute-start.3 = (f32[88,128]{1,0:T(8,128)S(1)}, f32[88,128]{1,0:T(8,128)S(1)}, u32[]{:S(2)}, u32[]{:S(2)}) collective-permute-start(f32[88,128]{1,0:T(8,128)S(1)} %get-tuple-element.40), channel_id=1, source_target_pairs={{0,3},{1,2},{2,1},{3,0},{4,7},{5,6},{6,5},{7,4},{8,11},{9,10},{10,... | collective-permute-start | bytes 135176 | tf_op jit(solution)/shard_map/ppermute | solution.py:613
  9.5 4.5 %collective-permute-start.4 = (f32[16,128]{1,0:T(8,128)S(1)}, f32[16,128]{1,0:T(8,128)S(1)}, u32[]{:S(2)}, u32[]{:S(2)}) collective-permute-start(f32[16,128]{1,0:T(8,128)S(1)} %get-tuple-element.41.block_ref), channel_id=1, source_target_pairs={{0,2},{1,3},{2,0},{3,1},{4,6},{5,7},{6,4},{7,5},{8,10},{9,11},{10,... | collective-permute-start | bytes 24584 | tf_op jit(solution)/shard_map/ppermute | solution.py:608
  14.2 2.8 %collective-permute-start.5 = (f32[88,128]{1,0:T(8,128)S(1)}, f32[88,128]{1,0:T(8,128)S(1)}, u32[]{:S(2)}, u32[]{:S(2)}) collective-permute-start(f32[88,128]{1,0:T(8,128)S(1)} %get-tuple-element.42), channel_id=1, source_target_pairs={{0,4},{4,0},{8,12},{12,8},{1,5},{5,1},{9,13},{13,9},{2,6},{6,2},{1... | collective-permute-start | bytes 135176 | tf_op jit(solution)/shard_map/ppermute | solution.py:613
  14.3 4.3 %collective-permute-start.6 = (f32[88,128]{1,0:T(8,128)S(1)}, f32[88,128]{1,0:T(8,128)S(1)}, u32[]{:S(2)}, u32[]{:S(2)}) collective-permute-start(f32[88,128]{1,0:T(8,128)S(1)} %get-tuple-element.43), channel_id=1, source_target_pairs={{0,12},{4,8},{8,4},{12,0},{1,13},{5,9},{9,5},{13,1},{2,14},{6,10},... | collective-permute-start | bytes 135176 | tf_op jit(solution)/shard_map/ppermute | solution.py:613
  14.9 3.7 %collective-permute-start.7 = (f32[16,128]{1,0:T(8,128)S(1)}, f32[16,128]{1,0:T(8,128)S(1)}, u32[]{:S(2)}, u32[]{:S(2)}) collective-permute-start(f32[16,128]{1,0:T(8,128)S(1)} %get-tuple-element.46.after_ref.refs_0_), channel_id=1, source_target_pairs={{0,8},{4,12},{8,0},{12,4},{1,9},{5,13},{9,1},{13,5},{2,10},{6,14},... | collective-permute-start | bytes 24584 | tf_op jit(solution)/shard_map/ppermute | solution.py:608
  17.1 9.3 %collective-permute-start.8 = (f32[400,128]{1,0:T(8,128)S(1)}, f32[400,128]{1,0:T(8,128)S(1)}, u32[]{:S(2)}, u32[]{:S(2)}) collective-permute-start(f32[400,128]{1,0:T(8,128)S(1)} %pack_cot.1), channel_id=1, source_target_pairs={{0,12},{4,8},{8,4},{12,0},{1,13},{5,9},{9,5},{13,1},{2,14},{6,10},... | collective-permute-start | bytes 614408 | tf_op jit(solution)/shard_map/ppermute | solution.py:613

commit v13 on v10

--- a/solution.py
+++ b/solution.py
@@ -238,21 +238,15 @@
 
 def each_tile(layers, windows, body):
     start, count, most = windows
-    group = 12 // (2 * count) * 2 if layers % 12 == 0 else 1
-
-    def some(step, carry):
-        stores = []
-        for j in range(group):
-            z = step * group + j
-            for i in range(count):
-                stores += body(z, i, jnp.minimum(start + 8 * i + ((z + 16) >> 5), most))
-            if len(stores) >= 64 or j == group - 1:
-                for store in stores:
-                    store()
-                stores = []
-        return carry
-
-    lax.fori_loop(0, layers // group, some, 0)
+    nothing = lax.axis_index("wide") >> 20
+    stores = []
+    for z in range(layers):
+        for i in range(count):
+            stores += body(z, i, jnp.minimum(start + 8 * i, most) + nothing)
+        if len(stores) >= 32 or z == layers - 1:
+            for store in stores:
+                store()
+            stores = []
 
 
 def each_window(windows, body):
@@ -274,7 +268,7 @@
     layers = ref.shape[1]
     lane = lanes((8, 128))
     rows, before, after = pl.ds(r, 8), pl.ds(r - 1, 8), pl.ds(r + 1, 8)
-    below, above = jnp.maximum(z - 1, 0), jnp.minimum(z + 1, layers - 1)
+    below, above = max(z - 1, 0), min(z + 1, layers - 1)
     ends = ends_ref[p, z, rows, :]
     left = roll(jnp.where(lane == 127, ends, value), 1)
     right = roll(jnp.where(lane == 0, ends, value), 127)

time: 44.9 us -> 43.9 us (0.978)
  Pallas kernels: 18.6 us -> 17.6 us
    pallas_call x1, Pallas kernels: 7.86 us -> 7.19 us  [per_device(): kernel(backward, (f32(*order_init.shape), f32(bricks, listed)), ([vmem(*p...]
  transfers between devices with their start and end apart: 9 -> 9, of which waited for: 2 -> 2; matrix products, arithmetic and copies ran while one was open for 0% -> 0% of each run, Pallas kernels for 19% -> 18%
where the time goes in v13:
time: 43.9 us; the launch traced here: 43.7 us
  Pallas kernels  17.6 us (40%)
  blocking collectives  9.94 us (23%)
  starting transfers between devices  9.65 us (22%)
  waiting for transfers between devices  5.84 us (13%)
  between operations  0.71 us (2%)
    all_to_all x1, blocking collectives, per_device(): sums = lax.all_to_all(sums, both, 0, 0, tiled=True)  9.94 us
    ppermute x7, starting transfers between devices, swapped(): lax.ppermute(value, axis, [(i, (i + by) % count) for i, by in enumerate(s...  8.04 us
    pallas_call x1, Pallas kernels, per_device(): kernel(backward, (f32(*order_init.shape), f32(bricks, listed)), ([vmem(*p...  7.19 us
    pallas_call x1, Pallas kernels, per_device(): kernel(forward, (f32(*order_init.shape), [f32(*padded)] * ITERS, [f32(*pa...  6.33 us
    ppermute x2, waiting for transfers between devices, opposite(): return lax.ppermute(value, axis, [(i, (i + 2) % 4) for i in range(4)])  5.83 us
    ppermute x2, starting transfers between devices, opposite(): return lax.ppermute(value, axis, [(i, (i + 2) % 4) for i in range(4)])  1.61 us
    pallas_call x1, Pallas kernels, per_device(): kernel(pack_rows, tuple((jax.ShapeDtypeStruct(x.shape, x.dtype) for x in...  1.24 us
    pallas_call x1, Pallas kernels, per_device(): kernel(functools.partial(pick_owned, owned), f32(1, owned), (vmem(owned +...  1.13 us
  transfers between devices with their start and end apart: 9, of which 2 were waited for; matrix products, arithmetic and copies ran while one was open for 0% of the time, Pallas kernels for 18%

profile of v13, /device:TPU:0, one launch (start us, length us, event | category | flops | bytes accessed | tf_op | source)
XLA Modules:
  0.0 43.7 jit_solution(17102976713310827759)
XLA Ops:
  0.6 1.2 %pack_rows.1 = (f32[8,12,8,128]{3,2,1,0:T(8,128)S(1)}, s32[12,8,128]{2,1,0:T(8,128)S(1)}, f32[8,12,8,128]{3,2,1,0:T(8,128)S(1)}, f32[1,392]{1,0:T(1,128)S(1)}, s...) custom-call(f32[8,12,8,128]{3,2,1,0:T(8,128)} %refs_0_.1, ...), custom_call_target="tpu_custom_call" | custom-call | tf_op jit(solution)/shard_map/pack_rows/pallas_call | solution.py:634
  1.9 0.5 %collective-permute-start = (f32[1064,128]{1,0:T(8,128)S(1)}, f32[1064,128]{1,0:T(8,128)S(1)}, u32[]{:S(2)}, u32[]{:S(2)}) collective-permute-start(f32[1064,128]{1,0:T(8,128)S(1)} %get-tuple-element.35), channel_id=1, source_target_pairs={{0,4},{4,0},{8,12},{12,8},{1,5},{5,1},{9,13},{13,9},{2,6},{6,2},{1... | collective-permute-start | bytes 1634312 | tf_op jit(solution)/shard_map/ppermute | solution.py:607
  2.4 2.6 %collective-permute-start.1 = (f32[664,128]{1,0:T(8,128)S(1)}, f32[664,128]{1,0:T(8,128)S(1)}, u32[]{:S(2)}, u32[]{:S(2)}) collective-permute-start(f32[664,128]{1,0:T(8,128)S(1)} %get-tuple-element.36.after_ref), channel_id=1, source_target_pairs={{0,12},{4,8},{8,4},{12,0},{1,13},{5,9},{9,5},{13,1},{2,14},{6,10},... | collective-permute-start | bytes 1019912 | tf_op jit(solution)/shard_map/ppermute | solution.py:607
  5.0 0.4 pack_strips.1
  5.4 1.6 %collective-permute-start.2 = (f32[88,128]{1,0:T(8,128)S(1)}, f32[88,128]{1,0:T(8,128)S(1)}, u32[]{:S(2)}, u32[]{:S(2)}) collective-permute-start(f32[88,128]{1,0:T(8,128)S(1)} %get-tuple-element.39), channel_id=1, source_target_pairs={{0,1},{1,0},{2,3},{3,2},{4,5},{5,4},{6,7},{7,6},{8,9},{9,8},{10,11... | collective-permute-start | bytes 135176 | tf_op jit(solution)/shard_map/ppermute | solution.py:607
  7.1 2.5 %collective-permute-start.3 = (f32[88,128]{1,0:T(8,128)S(1)}, f32[88,128]{1,0:T(8,128)S(1)}, u32[]{:S(2)}, u32[]{:S(2)}) collective-permute-start(f32[88,128]{1,0:T(8,128)S(1)} %get-tuple-element.40), channel_id=1, source_target_pairs={{0,3},{1,2},{2,1},{3,0},{4,7},{5,6},{6,5},{7,4},{8,11},{9,10},{10,... | collective-permute-start | bytes 135176 | tf_op jit(solution)/shard_map/ppermute | solution.py:607
  9.5 0.1 collective-permute-start.4
  9.6 4.4 %collective-permute-done.4.refs_0_ = f32[16,128]{1,0:T(8,128)S(1)} collective-permute-done((f32[16,128]{1,0:T(8,128)S(1)}, f32[16,128]{1,0:T(8,128)S(1)}, u32[]{:S(2)}, u32[]{:S(2)}) %collective-permute-start.4) | collective-permute-done | bytes 8224 | tf_op jit(solution)/shard_map/ppermute | solution.py:602
  14.1 0.0 collective-permute-done.2.strip_a_ref
  14.1 0.0 collective-permute-done.3.strip_b_ref
  14.1 0.1 pack_far.1
  14.2 0.1 collective-permute-start.5
  14.3 0.7 %collective-permute-start.6 = (f32[88,128]{1,0:T(8,128)S(1)}, f32[88,128]{1,0:T(8,128)S(1)}, u32[]{:S(2)}, u32[]{:S(2)}) collective-permute-start(f32[88,128]{1,0:T(8,128)S(1)} %get-tuple-element.43), channel_id=1, source_target_pairs={{0,12},{4,8},{8,4},{12,0},{1,13},{5,9},{9,5},{13,1},{2,14},{6,10},... | collective-permute-start | bytes 135176 | tf_op jit(solution)/shard_map/ppermute | solution.py:607
  14.9 1.5 %collective-permute-start.7 = (f32[16,128]{1,0:T(8,128)S(1)}, f32[16,128]{1,0:T(8,128)S(1)}, u32[]{:S(2)}, u32[]{:S(2)}) collective-permute-start(f32[16,128]{1,0:T(8,128)S(1)} %get-tuple-element.46.after_ref.refs_0_), channel_id=1, source_target_pairs={{0,8},{4,12},{8,0},{12,4},{1,9},{5,13},{9,1},{13,5},{2,10},{6,14},... | collective-permute-start | bytes 24584 | tf_op jit(solution)/shard_map/ppermute | solution.py:602
  16.4 0.6 %find_slots.1.slots_ref = s32[8,128]{1,0:T(8,128)S(1)} custom-call(s32[16,64]{1,0:T(8,128)S(1)} %get-tuple-element.44.bricks_ref, s32[49,128]{1,0:T(8,128)S(1)} %get-tuple-element.45.slot_ref, f32[16,128]{1,0:T(8,128)S(1)} %get-tuple-element.46.after_ref.refs_0_), custom_call_target="tpu_custom_call" | custom-call | tf_op jit(solution)/shard_map/find_slots/pallas_call | solution.py:659
  17.0 0.0 collective-permute-done.5.refs_1_.far_a_ref.after_ref
  17.0 0.1 pack_cot.1
  17.1 0.1 collective-permute-start.8
  17.2 1.4 %collective-permute-done.7.refs_3_ = f32[16,128]{1,0:T(8,128)S(1)} collective-permute-done((f32[16,128]{1,0:T(8,128)S(1)}, f32[16,128]{1,0:T(8,128)S(1)}, u32[]{:S(2)}, u32[]{:S(2)}) %collective-permute-start.7) | collective-permute-done | bytes 8224 | tf_op jit(solution)/shard_map/ppermute | solution.py:602
  18.6 0.5 %find_mobility.1.table_ref = f32[8,128]{1,0:T(8,128)S(1)} custom-call(s32[8,128]{1,0:T(8,128)S(1)} %find_slots.1.slots_ref, f32[16,128]{1,0:T(8,128)S(1)} %get-tuple-element.46.after_ref.refs_0_, f32[88,128]{1,0:T(8,128)S(1)} %collective-permute-done.5.refs_1_.far_a_ref.after_ref, f32[88,128]{1,0:T(8,128)S(1)} %collective-permute-done.6.refs_2_.far_b_ref, ...), custom_call_target="tpu_custom_call" | custom-call | flops 2500000000 | bytes 2500000 | tf_op jit(solution)/shard_map/find_mobility/pallas_call | solution.py:671
  19.1 6.3 %forward.1 = (f32[8,12,8,128]{3,2,1,0:T(8,128)}, f32[8,12,24,128]{3,2,1,0:T(8,128)S(1)}, f32[8,12,24,128]{3,2,1,0:T(8,128)S(1)}, f32[8,12,24,128]{3,2,1,0:T(8,12...) custom-call(f32[8,12,8,128]{3,2,1,0:T(8,128)S(1)} %get-tuple-element, ...), custom_call_target="tpu_custom_call" | custom-call | tf_op jit(solution)/shard_map/forward/pallas_call | solution.py:678
  25.4 7.2 %backward.1 = (f32[8,12,8,128]{3,2,1,0:T(8,128)}, f32[16,64]{1,0:T(8,128)S(1)}) custom-call(f32[8,12,8,128]{3,2,1,0:T(8,128)S(1)} %get-tuple-element.37.cot_ref, s32[12,8,128]{2,1,0:T(8,128)S(1)} %get-tuple-element.34.map_ref, f32[1064,128]{1,0:T(8,128)S(1)} %collective-permute-done.row_a_ref, f32[400,128]{1,0:T(8,128)S(1)} %collective-permute-done.8.row_b_ref, ...), custom_call_target="tpu_custom_call" | custom-call | tf_op jit(solution)/shard_map/backward/pallas_call | solution.py:687
  32.6 9.9 %all_to_all.11 = f32[16,1,64]{2,1,0:T(1,128)S(1)} all-to-all(f32[16,1,64]{2,1,0:T(1,128)S(1)} %bitcast.8), channel_id=1, replica_groups=mesh['groups'=2,'wide'=4,'narrow'=4] {'wide','narrow'}, dimensions={0} | all-to-all | bytes 8192 | tf_op jit(solution)/shard_map/all_to_all | solution.py:700
  42.6 1.1 %pick_owned.1 = f32[1,392]{1,0:T(1,128)} custom-call(s32[8,128]{1,0:T(8,128)S(1)} %find_slots.1.slots_ref, f32[16,64]{1,0:T(8,128)S(1)} %bitcast.7), custom_call_target="tpu_custom_call" | custom-call | tf_op jit(solution)/shard_map/pick_owned/pallas_call | solution.py:701
  (4 shorter events, 0.0 us)
Async XLA Ops:
  1.9 17.2 %collective-permute-start = (f32[1064,128]{1,0:T(8,128)S(1)}, f32[1064,128]{1,0:T(8,128)S(1)}, u32[]{:S(2)}, u32[]{:S(2)}) collective-permute-start(f32[1064,128]{1,0:T(8,128)S(1)} %get-tuple-element.35), channel_id=1, source_target_pairs={{0,4},{4,0},{8,12},{12,8},{1,5},{5,1},{9,13},{13,9},{2,6},{6,2},{1... | collective-permute-start | bytes 1634312 | tf_op jit(solution)/shard_map/ppermute | solution.py:607
  2.4 16.7 %collective-permute-start.1 = (f32[664,128]{1,0:T(8,128)S(1)}, f32[664,128]{1,0:T(8,128)S(1)}, u32[]{:S(2)}, u32[]{:S(2)}) collective-permute-start(f32[664,128]{1,0:T(8,128)S(1)} %get-tuple-element.36.after_ref), channel_id=1, source_target_pairs={{0,12},{4,8},{8,4},{12,0},{1,13},{5,9},{9,5},{13,1},{2,14},{6,10},... | collective-permute-start | bytes 1019912 | tf_op jit(solution)/shard_map/ppermute | solution.py:607
  5.4 8.7 %collective-permute-start.2 = (f32[88,128]{1,0:T(8,128)S(1)}, f32[88,128]{1,0:T(8,128)S(1)}, u32[]{:S(2)}, u32[]{:S(2)}) collective-permute-start(f32[88,128]{1,0:T(8,128)S(1)} %get-tuple-element.39), channel_id=1, source_target_pairs={{0,1},{1,0},{2,3},{3,2},{4,5},{5,4},{6,7},{7,6},{8,9},{9,8},{10,11... | collective-permute-start | bytes 135176 | tf_op jit(solution)/shard_map/ppermute | solution.py:607
  7.1 7.0 %collective-permute-start.3 = (f32[88,128]{1,0:T(8,128)S(1)}, f32[88,128]{1,0:T(8,128)S(1)}, u32[]{:S(2)}, u32[]{:S(2)}) collective-permute-start(f32[88,128]{1,0:T(8,128)S(1)} %get-tuple-element.40), channel_id=1, source_target_pairs={{0,3},{1,2},{2,1},{3,0},{4,7},{5,6},{6,5},{7,4},{8,11},{9,10},{10,... | collective-permute-start | bytes 135176 | tf_op jit(solution)/shard_map/ppermute | solution.py:607
  9.5 4.5 %collective-permute-start.4 = (f32[16,128]{1,0:T(8,128)S(1)}, f32[16,128]{1,0:T(8,128)S(1)}, u32[]{:S(2)}, u32[]{:S(2)}) collective-permute-start(f32[16,128]{1,0:T(8,128)S(1)} %get-tuple-element.41.block_ref), channel_id=1, source_target_pairs={{0,2},{1,3},{2,0},{3,1},{4,6},{5,7},{6,4},{7,5},{8,10},{9,11},{10,... | collective-permute-start | bytes 24584 | tf_op jit(solution)/shard_map/ppermute | solution.py:602
  14.2 2.8 %collective-permute-start.5 = (f32[88,128]{1,0:T(8,128)S(1)}, f32[88,128]{1,0:T(8,128)S(1)}, u32[]{:S(2)}, u32[]{:S(2)}) collective-permute-start(f32[88,128]{1,0:T(8,128)S(1)} %get-tuple-element.42), channel_id=1, source_target_pairs={{0,4},{4,0},{8,12},{12,8},{1,5},{5,1},{9,13},{13,9},{2,6},{6,2},{1... | collective-permute-start | bytes 135176 | tf_op jit(solution)/shard_map/ppermute | solution.py:607
  14.3 4.3 %collective-permute-start.6 = (f32[88,128]{1,0:T(8,128)S(1)}, f32[88,128]{1,0:T(8,128)S(1)}, u32[]{:S(2)}, u32[]{:S(2)}) collective-permute-start(f32[88,128]{1,0:T(8,128)S(1)} %get-tuple-element.43), channel_id=1, source_target_pairs={{0,12},{4,8},{8,4},{12,0},{1,13},{5,9},{9,5},{13,1},{2,14},{6,10},... | collective-permute-start | bytes 135176 | tf_op jit(solution)/shard_map/ppermute | solution.py:607
  14.9 3.7 %collective-permute-start.7 = (f32[16,128]{1,0:T(8,128)S(1)}, f32[16,128]{1,0:T(8,128)S(1)}, u32[]{:S(2)}, u32[]{:S(2)}) collective-permute-start(f32[16,128]{1,0:T(8,128)S(1)} %get-tuple-element.46.after_ref.refs_0_), channel_id=1, source_target_pairs={{0,8},{4,12},{8,0},{12,4},{1,9},{5,13},{9,1},{13,5},{2,10},{6,14},... | collective-permute-start | bytes 24584 | tf_op jit(solution)/shard_map/ppermute | solution.py:602
  17.1 8.3 %collective-permute-start.8 = (f32[400,128]{1,0:T(8,128)S(1)}, f32[400,128]{1,0:T(8,128)S(1)}, u32[]{:S(2)}, u32[]{:S(2)}) collective-permute-start(f32[400,128]{1,0:T(8,128)S(1)} %pack_cot.1), channel_id=1, source_target_pairs={{0,12},{4,8},{8,4},{12,0},{1,13},{5,9},{9,5},{13,1},{2,14},{6,10},... | collective-permute-start | bytes 614408 | tf_op jit(solution)/shard_map/ppermute | solution.py:607

commit v14 on v13

--- a/solution.py
+++ b/solution.py
@@ -185,7 +185,7 @@
             taken = jnp.take_along_axis(table, col, axis=1, mode="promise_in_bounds")
             return jnp.where(row == r, taken, found)
 
-        out_ref[k : k + 8, :] = lax.fori_loop(0, rows, body, jnp.zeros((8, 128), jnp.int32), unroll=7)
+        out_ref[k : k + 8, :] = lax.fori_loop(0, rows, body, jnp.zeros((8, 128), jnp.int32), unroll=49)
 
 
 def find_mobility(counts, owned, slots_ref, *refs):
@@ -226,7 +226,7 @@
         taken = jnp.take_along_axis(values, place, axis=1, mode="promise_in_bounds")
         return jnp.where(row == r, taken, found)
 
-    found = lax.fori_loop(0, mob_ref.shape[0], body, jnp.zeros(tile, jnp.float32), unroll=16)
+    found = lax.fori_loop(0, mob_ref.shape[0], body, jnp.zeros(tile, jnp.float32), unroll=32)
     table_ref[...] = TIME_STEP * found
 
 
@@ -250,11 +250,9 @@
 
 
 def each_window(windows, body):
-    def one(i, carry):
-        body(windows[0] + 8 * i)
-        return carry
-
-    lax.fori_loop(0, windows[1], one, 0)
+    nothing = lax.axis_index("wide") >> 20
+    for i in range(windows[1]):
+        body(windows[0] + 8 * i + nothing)
 
 
 def put(ref, index, value):
@@ -342,7 +340,8 @@
             e_refs[0][p, z, 8:16, :] = order_ref[p, z]
         return carry
 
-    lax.fori_loop(0, layers, place, 0)
+    for z in range(layers):
+        place(z, 0)
 
     sides = side_strips(params, strip_a_ref, strip_b_ref)
     order, _, cells = merged_strips(params, strip_a_ref, strip_b_ref)
@@ -455,7 +454,8 @@
             u_refs[0][p, z, 8:16, :] = m * cot_ref[p, z]
         return carry
 
-    lax.fori_loop(0, layers, place, 0)
+    for z in range(layers):
+        place(z, 0)
     _, cot, _ = merged_strips(params, strip_a_ref, strip_b_ref)
     n = CORNER[1]
     for p in every:
@@ -547,7 +547,7 @@
         binned_ref[pl.ds(g, 1), :] = jnp.sum(total, axis=0, keepdims=True)
         return carry
 
-    lax.fori_loop(0, binned_ref.shape[0], bin_one, 0, unroll=4)
+    lax.fori_loop(0, binned_ref.shape[0], bin_one, 0, unroll=16)
     ones = jnp.full((8, 128), -TIME_STEP, jnp.float32)
     sums = lax.dot_general(
         ones, binned_ref[...], (((1,), (1,)), ((), ())),

time: 43.9 us -> 46 us (1.048)
  Pallas kernels: 17.6 us -> 19.2 us
    pallas_call x1, Pallas kernels: 6.33 us -> 7.97 us  [per_device(): kernel(forward, (f32(*order_init.shape), [f32(*padded)] * ITERS, [f32(*pa...]
    pallas_call x1, Pallas kernels: 7.19 us -> 7.8 us  [per_device(): kernel(backward, (f32(*order_init.shape), f32(bricks, listed)), ([vmem(*p...]
  transfers between devices with their start and end apart: 9 -> 9, of which waited for: 2 -> 2; matrix products, arithmetic and copies ran while one was open for 0% -> 0% of each run, Pallas kernels for 18% -> 20%
where the time goes in v14:
time: 46 us; the launch traced here: 45.8 us
  Pallas kernels  19.2 us (42%)
  blocking collectives  9.94 us (22%)
  starting transfers between devices  9.65 us (21%)
  waiting for transfers between devices  6.26 us (14%)
  between operations  0.72 us (2%)
    all_to_all x1, blocking collectives, per_device(): sums = lax.all_to_all(sums, both, 0, 0, tiled=True)  9.94 us
    ppermute x7, starting transfers between devices, swapped(): lax.ppermute(value, axis, [(i, (i + by) % count) for i, by in enumerate(s...  8.04 us
    pallas_call x1, Pallas kernels, per_device(): kernel(forward, (f32(*order_init.shape), [f32(*padded)] * ITERS, [f32(*pa...  7.97 us
    pallas_call x1, Pallas kernels, per_device(): kernel(backward, (f32(*order_init.shape), f32(bricks, listed)), ([vmem(*p...  7.8 us
    ppermute x2, waiting for transfers between devices, opposite(): return lax.ppermute(value, axis, [(i, (i + 2) % 4) for i in range(4)])  6.24 us
    ppermute x2, starting transfers between devices, opposite(): return lax.ppermute(value, axis, [(i, (i + 2) % 4) for i in range(4)])  1.61 us
    pallas_call x1, Pallas kernels, per_device(): kernel(pack_rows, tuple((jax.ShapeDtypeStruct(x.shape, x.dtype) for x in...  1.24 us
    pallas_call x1, Pallas kernels, per_device(): kernel(functools.partial(pick_owned, owned), f32(1, owned), (vmem(owned +...  1.13 us
  transfers between devices with their start and end apart: 9, of which 2 were waited for; matrix products, arithmetic and copies ran while one was open for 0% of the time, Pallas kernels for 20%

profile of v14, /device:TPU:0, one launch (start us, length us, event | category | flops | bytes accessed | tf_op | source)
XLA Modules:
  0.0 45.8 jit_solution(6168889131496651875)
XLA Ops:
  0.6 1.2 %pack_rows.1 = (f32[8,12,8,128]{3,2,1,0:T(8,128)S(1)}, s32[12,8,128]{2,1,0:T(8,128)S(1)}, f32[8,12,8,128]{3,2,1,0:T(8,128)S(1)}, f32[1,392]{1,0:T(1,128)S(1)}, s...) custom-call(f32[8,12,8,128]{3,2,1,0:T(8,128)} %refs_0_.1, ...), custom_call_target="tpu_custom_call" | custom-call | tf_op jit(solution)/shard_map/pack_rows/pallas_call | solution.py:634
  1.9 0.5 %collective-permute-start = (f32[1064,128]{1,0:T(8,128)S(1)}, f32[1064,128]{1,0:T(8,128)S(1)}, u32[]{:S(2)}, u32[]{:S(2)}) collective-permute-start(f32[1064,128]{1,0:T(8,128)S(1)} %get-tuple-element.35), channel_id=1, source_target_pairs={{0,4},{4,0},{8,12},{12,8},{1,5},{5,1},{9,13},{13,9},{2,6},{6,2},{1... | collective-permute-start | bytes 1634312 | tf_op jit(solution)/shard_map/ppermute | solution.py:607
  2.4 2.6 %collective-permute-start.1 = (f32[664,128]{1,0:T(8,128)S(1)}, f32[664,128]{1,0:T(8,128)S(1)}, u32[]{:S(2)}, u32[]{:S(2)}) collective-permute-start(f32[664,128]{1,0:T(8,128)S(1)} %get-tuple-element.36.after_ref), channel_id=1, source_target_pairs={{0,12},{4,8},{8,4},{12,0},{1,13},{5,9},{9,5},{13,1},{2,14},{6,10},... | collective-permute-start | bytes 1019912 | tf_op jit(solution)/shard_map/ppermute | solution.py:607
  5.0 0.4 pack_strips.1
  5.4 1.6 %collective-permute-start.2 = (f32[88,128]{1,0:T(8,128)S(1)}, f32[88,128]{1,0:T(8,128)S(1)}, u32[]{:S(2)}, u32[]{:S(2)}) collective-permute-start(f32[88,128]{1,0:T(8,128)S(1)} %get-tuple-element.39), channel_id=1, source_target_pairs={{0,1},{1,0},{2,3},{3,2},{4,5},{5,4},{6,7},{7,6},{8,9},{9,8},{10,11... | collective-permute-start | bytes 135176 | tf_op jit(solution)/shard_map/ppermute | solution.py:607
  7.1 2.5 %collective-permute-start.3 = (f32[88,128]{1,0:T(8,128)S(1)}, f32[88,128]{1,0:T(8,128)S(1)}, u32[]{:S(2)}, u32[]{:S(2)}) collective-permute-start(f32[88,128]{1,0:T(8,128)S(1)} %get-tuple-element.40), channel_id=1, source_target_pairs={{0,3},{1,2},{2,1},{3,0},{4,7},{5,6},{6,5},{7,4},{8,11},{9,10},{10,... | collective-permute-start | bytes 135176 | tf_op jit(solution)/shard_map/ppermute | solution.py:607
  9.5 0.1 collective-permute-start.4
  9.6 4.4 %collective-permute-done.4.refs_0_ = f32[16,128]{1,0:T(8,128)S(1)} collective-permute-done((f32[16,128]{1,0:T(8,128)S(1)}, f32[16,128]{1,0:T(8,128)S(1)}, u32[]{:S(2)}, u32[]{:S(2)}) %collective-permute-start.4) | collective-permute-done | bytes 8224 | tf_op jit(solution)/shard_map/ppermute | solution.py:602
  14.1 0.0 collective-permute-done.2.strip_a_ref
  14.1 0.0 collective-permute-done.3.strip_b_ref
  14.1 0.1 pack_far.1
  14.2 0.1 collective-permute-start.5
  14.3 0.7 %collective-permute-start.6 = (f32[88,128]{1,0:T(8,128)S(1)}, f32[88,128]{1,0:T(8,128)S(1)}, u32[]{:S(2)}, u32[]{:S(2)}) collective-permute-start(f32[88,128]{1,0:T(8,128)S(1)} %get-tuple-element.43), channel_id=1, source_target_pairs={{0,12},{4,8},{8,4},{12,0},{1,13},{5,9},{9,5},{13,1},{2,14},{6,10},... | collective-permute-start | bytes 135176 | tf_op jit(solution)/shard_map/ppermute | solution.py:607
  14.9 1.5 %collective-permute-start.7 = (f32[16,128]{1,0:T(8,128)S(1)}, f32[16,128]{1,0:T(8,128)S(1)}, u32[]{:S(2)}, u32[]{:S(2)}) collective-permute-start(f32[16,128]{1,0:T(8,128)S(1)} %get-tuple-element.46.after_ref.refs_0_), channel_id=1, source_target_pairs={{0,8},{4,12},{8,0},{12,4},{1,9},{5,13},{9,1},{13,5},{2,10},{6,14},... | collective-permute-start | bytes 24584 | tf_op jit(solution)/shard_map/ppermute | solution.py:602
  16.4 0.2 find_slots.1.slots_ref
  16.6 0.0 collective-permute-done.5.refs_1_.far_a_ref.after_ref
  16.6 0.1 pack_cot.1
  16.7 0.1 collective-permute-start.8
  16.8 1.8 %collective-permute-done.7.refs_3_ = f32[16,128]{1,0:T(8,128)S(1)} collective-permute-done((f32[16,128]{1,0:T(8,128)S(1)}, f32[16,128]{1,0:T(8,128)S(1)}, u32[]{:S(2)}, u32[]{:S(2)}) %collective-permute-start.7) | collective-permute-done | bytes 8224 | tf_op jit(solution)/shard_map/ppermute | solution.py:602
  18.6 0.4 find_mobility.1.table_ref
  19.0 8.0 %forward.1 = (f32[8,12,8,128]{3,2,1,0:T(8,128)}, f32[8,12,24,128]{3,2,1,0:T(8,128)S(1)}, f32[8,12,24,128]{3,2,1,0:T(8,128)S(1)}, f32[8,12,24,128]{3,2,1,0:T(8,12...) custom-call(f32[8,12,8,128]{3,2,1,0:T(8,128)S(1)} %get-tuple-element, ...), custom_call_target="tpu_custom_call" | custom-call | tf_op jit(solution)/shard_map/forward/pallas_call | solution.py:678
  26.9 7.8 %backward.1 = (f32[8,12,8,128]{3,2,1,0:T(8,128)}, f32[16,64]{1,0:T(8,128)S(1)}) custom-call(f32[8,12,8,128]{3,2,1,0:T(8,128)S(1)} %get-tuple-element.37.cot_ref, s32[12,8,128]{2,1,0:T(8,128)S(1)} %get-tuple-element.34.map_ref, f32[1064,128]{1,0:T(8,128)S(1)} %collective-permute-done.row_a_ref, f32[400,128]{1,0:T(8,128)S(1)} %collective-permute-done.8.row_b_ref, ...), custom_call_target="tpu_custom_call" | custom-call | tf_op jit(solution)/shard_map/backward/pallas_call | solution.py:687
  34.7 9.9 %all_to_all.11 = f32[16,1,64]{2,1,0:T(1,128)S(1)} all-to-all(f32[16,1,64]{2,1,0:T(1,128)S(1)} %bitcast.8), channel_id=1, replica_groups=mesh['groups'=2,'wide'=4,'narrow'=4] {'wide','narrow'}, dimensions={0} | all-to-all | bytes 8192 | tf_op jit(solution)/shard_map/all_to_all | solution.py:700
  44.7 1.1 %pick_owned.1 = f32[1,392]{1,0:T(1,128)} custom-call(s32[8,128]{1,0:T(8,128)S(1)} %find_slots.1.slots_ref, f32[16,64]{1,0:T(8,128)S(1)} %bitcast.7), custom_call_target="tpu_custom_call" | custom-call | tf_op jit(solution)/shard_map/pick_owned/pallas_call | solution.py:701
  (4 shorter events, 0.0 us)
Async XLA Ops:
  1.9 17.1 %collective-permute-start = (f32[1064,128]{1,0:T(8,128)S(1)}, f32[1064,128]{1,0:T(8,128)S(1)}, u32[]{:S(2)}, u32[]{:S(2)}) collective-permute-start(f32[1064,128]{1,0:T(8,128)S(1)} %get-tuple-element.35), channel_id=1, source_target_pairs={{0,4},{4,0},{8,12},{12,8},{1,5},{5,1},{9,13},{13,9},{2,6},{6,2},{1... | collective-permute-start | bytes 1634312 | tf_op jit(solution)/shard_map/ppermute | solution.py:607
  2.4 16.6 %collective-permute-start.1 = (f32[664,128]{1,0:T(8,128)S(1)}, f32[664,128]{1,0:T(8,128)S(1)}, u32[]{:S(2)}, u32[]{:S(2)}) collective-permute-start(f32[664,128]{1,0:T(8,128)S(1)} %get-tuple-element.36.after_ref), channel_id=1, source_target_pairs={{0,12},{4,8},{8,4},{12,0},{1,13},{5,9},{9,5},{13,1},{2,14},{6,10},... | collective-permute-start | bytes 1019912 | tf_op jit(solution)/shard_map/ppermute | solution.py:607
  5.4 8.7 %collective-permute-start.2 = (f32[88,128]{1,0:T(8,128)S(1)}, f32[88,128]{1,0:T(8,128)S(1)}, u32[]{:S(2)}, u32[]{:S(2)}) collective-permute-start(f32[88,128]{1,0:T(8,128)S(1)} %get-tuple-element.39), channel_id=1, source_target_pairs={{0,1},{1,0},{2,3},{3,2},{4,5},{5,4},{6,7},{7,6},{8,9},{9,8},{10,11... | collective-permute-start | bytes 135176 | tf_op jit(solution)/shard_map/ppermute | solution.py:607
  7.1 7.0 %collective-permute-start.3 = (f32[88,128]{1,0:T(8,128)S(1)}, f32[88,128]{1,0:T(8,128)S(1)}, u32[]{:S(2)}, u32[]{:S(2)}) collective-permute-start(f32[88,128]{1,0:T(8,128)S(1)} %get-tuple-element.40), channel_id=1, source_target_pairs={{0,3},{1,2},{2,1},{3,0},{4,7},{5,6},{6,5},{7,4},{8,11},{9,10},{10,... | collective-permute-start | bytes 135176 | tf_op jit(solution)/shard_map/ppermute | solution.py:607
  9.5 4.5 %collective-permute-start.4 = (f32[16,128]{1,0:T(8,128)S(1)}, f32[16,128]{1,0:T(8,128)S(1)}, u32[]{:S(2)}, u32[]{:S(2)}) collective-permute-start(f32[16,128]{1,0:T(8,128)S(1)} %get-tuple-element.41.block_ref), channel_id=1, source_target_pairs={{0,2},{1,3},{2,0},{3,1},{4,6},{5,7},{6,4},{7,5},{8,10},{9,11},{10,... | collective-permute-start | bytes 24584 | tf_op jit(solution)/shard_map/ppermute | solution.py:602
  14.2 2.4 %collective-permute-start.5 = (f32[88,128]{1,0:T(8,128)S(1)}, f32[88,128]{1,0:T(8,128)S(1)}, u32[]{:S(2)}, u32[]{:S(2)}) collective-permute-start(f32[88,128]{1,0:T(8,128)S(1)} %get-tuple-element.42), channel_id=1, source_target_pairs={{0,4},{4,0},{8,12},{12,8},{1,5},{5,1},{9,13},{13,9},{2,6},{6,2},{1... | collective-permute-start | bytes 135176 | tf_op jit(solution)/shard_map/ppermute | solution.py:607
  14.3 4.3 %collective-permute-start.6 = (f32[88,128]{1,0:T(8,128)S(1)}, f32[88,128]{1,0:T(8,128)S(1)}, u32[]{:S(2)}, u32[]{:S(2)}) collective-permute-start(f32[88,128]{1,0:T(8,128)S(1)} %get-tuple-element.43), channel_id=1, source_target_pairs={{0,12},{4,8},{8,4},{12,0},{1,13},{5,9},{9,5},{13,1},{2,14},{6,10},... | collective-permute-start | bytes 135176 | tf_op jit(solution)/shard_map/ppermute | solution.py:607
  14.9 3.7 %collective-permute-start.7 = (f32[16,128]{1,0:T(8,128)S(1)}, f32[16,128]{1,0:T(8,128)S(1)}, u32[]{:S(2)}, u32[]{:S(2)}) collective-permute-start(f32[16,128]{1,0:T(8,128)S(1)} %get-tuple-element.46.after_ref.refs_0_), channel_id=1, source_target_pairs={{0,8},{4,12},{8,0},{12,4},{1,9},{5,13},{9,1},{13,5},{2,10},{6,14},... | collective-permute-start | bytes 24584 | tf_op jit(solution)/shard_map/ppermute | solution.py:602
  16.7 10.3 %collective-permute-start.8 = (f32[400,128]{1,0:T(8,128)S(1)}, f32[400,128]{1,0:T(8,128)S(1)}, u32[]{:S(2)}, u32[]{:S(2)}) collective-permute-start(f32[400,128]{1,0:T(8,128)S(1)} %pack_cot.1), channel_id=1, source_target_pairs={{0,12},{4,8},{8,4},{12,0},{1,13},{5,9},{9,5},{13,1},{2,14},{6,10},... | collective-permute-start | bytes 614408 | tf_op jit(solution)/shard_map/ppermute | solution.py:607

commit v15 on v13

--- a/solution.py
+++ b/solution.py
@@ -185,7 +185,7 @@
             taken = jnp.take_along_axis(table, col, axis=1, mode="promise_in_bounds")
             return jnp.where(row == r, taken, found)
 
-        out_ref[k : k + 8, :] = lax.fori_loop(0, rows, body, jnp.zeros((8, 128), jnp.int32), unroll=7)
+        out_ref[k : k + 8, :] = lax.fori_loop(0, rows, body, jnp.zeros((8, 128), jnp.int32), unroll=49)
 
 
 def find_mobility(counts, owned, slots_ref, *refs):
@@ -226,7 +226,7 @@
         taken = jnp.take_along_axis(values, place, axis=1, mode="promise_in_bounds")
         return jnp.where(row == r, taken, found)
 
-    found = lax.fori_loop(0, mob_ref.shape[0], body, jnp.zeros(tile, jnp.float32), unroll=16)
+    found = lax.fori_loop(0, mob_ref.shape[0], body, jnp.zeros(tile, jnp.float32), unroll=32)
     table_ref[...] = TIME_STEP * found
 
 
@@ -243,7 +243,7 @@
     for z in range(layers):
         for i in range(count):
             stores += body(z, i, jnp.minimum(start + 8 * i, most) + nothing)
-        if len(stores) >= 32 or z == layers - 1:
+        if len(stores) >= 64 or z == layers - 1:
             for store in stores:
                 store()
             stores = []

time: 43.9 us -> 43.8 us (level)
  Pallas kernels: 17.6 us -> 17 us
  transfers between devices with their start and end apart: 9 -> 9, of which waited for: 2 -> 2; matrix products, arithmetic and copies ran while one was open for 0% -> 0% of each run, Pallas kernels for 18% -> 17%
where the time goes in v15:
time: 43.8 us; the launch traced here: 43.6 us
  Pallas kernels  17 us (39%)
  blocking collectives  9.94 us (23%)
  starting transfers between devices  9.65 us (22%)
  waiting for transfers between devices  6.26 us (14%)
  between operations  0.72 us (2%)
    all_to_all x1, blocking collectives, per_device(): sums = lax.all_to_all(sums, both, 0, 0, tiled=True)  9.94 us
    ppermute x7, starting transfers between devices, swapped(): lax.ppermute(value, axis, [(i, (i + by) % count) for i, by in enumerate(s...  8.04 us
    pallas_call x1, Pallas kernels, per_device(): kernel(backward, (f32(*order_init.shape), f32(bricks, listed)), ([vmem(*p...  7.26 us
    pallas_call x1, Pallas kernels, per_device(): kernel(forward, (f32(*order_init.shape), [f32(*padded)] * ITERS, [f32(*pa...  6.31 us
    ppermute x2, waiting for transfers between devices, opposite(): return lax.ppermute(value, axis, [(i, (i + 2) % 4) for i in range(4)])  6.24 us
    ppermute x2, starting transfers between devices, opposite(): return lax.ppermute(value, axis, [(i, (i + 2) % 4) for i in range(4)])  1.61 us
    pallas_call x1, Pallas kernels, per_device(): kernel(pack_rows, tuple((jax.ShapeDtypeStruct(x.shape, x.dtype) for x in...  1.24 us
    pallas_call x1, Pallas kernels, per_device(): kernel(functools.partial(pick_owned, owned), f32(1, owned), (vmem(owned +...  1.13 us
  transfers between devices with their start and end apart: 9, of which 2 were waited for; matrix products, arithmetic and copies ran while one was open for 0% of the time, Pallas kernels for 17%

profile of v15, /device:TPU:0, one launch (start us, length us, event | category | flops | bytes accessed | tf_op | source)
XLA Modules:
  0.0 43.6 jit_solution(14821293598571651587)
XLA Ops:
  0.6 1.2 %pack_rows.1 = (f32[8,12,8,128]{3,2,1,0:T(8,128)S(1)}, s32[12,8,128]{2,1,0:T(8,128)S(1)}, f32[8,12,8,128]{3,2,1,0:T(8,128)S(1)}, f32[1,392]{1,0:T(1,128)S(1)}, s...) custom-call(f32[8,12,8,128]{3,2,1,0:T(8,128)} %refs_0_.1, ...), custom_call_target="tpu_custom_call" | custom-call | tf_op jit(solution)/shard_map/pack_rows/pallas_call | solution.py:634
  1.9 0.5 %collective-permute-start = (f32[1064,128]{1,0:T(8,128)S(1)}, f32[1064,128]{1,0:T(8,128)S(1)}, u32[]{:S(2)}, u32[]{:S(2)}) collective-permute-start(f32[1064,128]{1,0:T(8,128)S(1)} %get-tuple-element.35), channel_id=1, source_target_pairs={{0,4},{4,0},{8,12},{12,8},{1,5},{5,1},{9,13},{13,9},{2,6},{6,2},{1... | collective-permute-start | bytes 1634312 | tf_op jit(solution)/shard_map/ppermute | solution.py:607
  2.4 2.6 %collective-permute-start.1 = (f32[664,128]{1,0:T(8,128)S(1)}, f32[664,128]{1,0:T(8,128)S(1)}, u32[]{:S(2)}, u32[]{:S(2)}) collective-permute-start(f32[664,128]{1,0:T(8,128)S(1)} %get-tuple-element.36.after_ref), channel_id=1, source_target_pairs={{0,12},{4,8},{8,4},{12,0},{1,13},{5,9},{9,5},{13,1},{2,14},{6,10},... | collective-permute-start | bytes 1019912 | tf_op jit(solution)/shard_map/ppermute | solution.py:607
  5.0 0.4 pack_strips.1
  5.4 1.6 %collective-permute-start.2 = (f32[88,128]{1,0:T(8,128)S(1)}, f32[88,128]{1,0:T(8,128)S(1)}, u32[]{:S(2)}, u32[]{:S(2)}) collective-permute-start(f32[88,128]{1,0:T(8,128)S(1)} %get-tuple-element.39), channel_id=1, source_target_pairs={{0,1},{1,0},{2,3},{3,2},{4,5},{5,4},{6,7},{7,6},{8,9},{9,8},{10,11... | collective-permute-start | bytes 135176 | tf_op jit(solution)/shard_map/ppermute | solution.py:607
  7.1 2.5 %collective-permute-start.3 = (f32[88,128]{1,0:T(8,128)S(1)}, f32[88,128]{1,0:T(8,128)S(1)}, u32[]{:S(2)}, u32[]{:S(2)}) collective-permute-start(f32[88,128]{1,0:T(8,128)S(1)} %get-tuple-element.40), channel_id=1, source_target_pairs={{0,3},{1,2},{2,1},{3,0},{4,7},{5,6},{6,5},{7,4},{8,11},{9,10},{10,... | collective-permute-start | bytes 135176 | tf_op jit(solution)/shard_map/ppermute | solution.py:607
  9.5 0.1 collective-permute-start.4
  9.6 4.4 %collective-permute-done.4.refs_0_ = f32[16,128]{1,0:T(8,128)S(1)} collective-permute-done((f32[16,128]{1,0:T(8,128)S(1)}, f32[16,128]{1,0:T(8,128)S(1)}, u32[]{:S(2)}, u32[]{:S(2)}) %collective-permute-start.4) | collective-permute-done | bytes 8224 | tf_op jit(solution)/shard_map/ppermute | solution.py:602
  14.1 0.0 collective-permute-done.2.strip_a_ref
  14.1 0.0 collective-permute-done.3.strip_b_ref
  14.1 0.1 pack_far.1
  14.2 0.1 collective-permute-start.5
  14.3 0.7 %collective-permute-start.6 = (f32[88,128]{1,0:T(8,128)S(1)}, f32[88,128]{1,0:T(8,128)S(1)}, u32[]{:S(2)}, u32[]{:S(2)}) collective-permute-start(f32[88,128]{1,0:T(8,128)S(1)} %get-tuple-element.43), channel_id=1, source_target_pairs={{0,12},{4,8},{8,4},{12,0},{1,13},{5,9},{9,5},{13,1},{2,14},{6,10},... | collective-permute-start | bytes 135176 | tf_op jit(solution)/shard_map/ppermute | solution.py:607
  14.9 1.5 %collective-permute-start.7 = (f32[16,128]{1,0:T(8,128)S(1)}, f32[16,128]{1,0:T(8,128)S(1)}, u32[]{:S(2)}, u32[]{:S(2)}) collective-permute-start(f32[16,128]{1,0:T(8,128)S(1)} %get-tuple-element.46.after_ref.refs_0_), channel_id=1, source_target_pairs={{0,8},{4,12},{8,0},{12,4},{1,9},{5,13},{9,1},{13,5},{2,10},{6,14},... | collective-permute-start | bytes 24584 | tf_op jit(solution)/shard_map/ppermute | solution.py:602
  16.4 0.2 find_slots.1.slots_ref
  16.6 0.0 collective-permute-done.5.refs_1_.far_a_ref.after_ref
  16.6 0.1 pack_cot.1
  16.7 0.1 collective-permute-start.8
  16.8 1.8 %collective-permute-done.7.refs_3_ = f32[16,128]{1,0:T(8,128)S(1)} collective-permute-done((f32[16,128]{1,0:T(8,128)S(1)}, f32[16,128]{1,0:T(8,128)S(1)}, u32[]{:S(2)}, u32[]{:S(2)}) %collective-permute-start.7) | collective-permute-done | bytes 8224 | tf_op jit(solution)/shard_map/ppermute | solution.py:602
  18.6 0.4 find_mobility.1.table_ref
  19.0 6.3 %forward.1 = (f32[8,12,8,128]{3,2,1,0:T(8,128)}, f32[8,12,24,128]{3,2,1,0:T(8,128)S(1)}, f32[8,12,24,128]{3,2,1,0:T(8,128)S(1)}, f32[8,12,24,128]{3,2,1,0:T(8,12...) custom-call(f32[8,12,8,128]{3,2,1,0:T(8,128)S(1)} %get-tuple-element, ...), custom_call_target="tpu_custom_call" | custom-call | tf_op jit(solution)/shard_map/forward/pallas_call | solution.py:678
  25.3 7.3 %backward.1 = (f32[8,12,8,128]{3,2,1,0:T(8,128)}, f32[16,64]{1,0:T(8,128)S(1)}) custom-call(f32[8,12,8,128]{3,2,1,0:T(8,128)S(1)} %get-tuple-element.37.cot_ref, s32[12,8,128]{2,1,0:T(8,128)S(1)} %get-tuple-element.34.map_ref, f32[1064,128]{1,0:T(8,128)S(1)} %collective-permute-done.row_a_ref, f32[400,128]{1,0:T(8,128)S(1)} %collective-permute-done.8.row_b_ref, ...), custom_call_target="tpu_custom_call" | custom-call | tf_op jit(solution)/shard_map/backward/pallas_call | solution.py:687
  32.5 9.9 %all_to_all.11 = f32[16,1,64]{2,1,0:T(1,128)S(1)} all-to-all(f32[16,1,64]{2,1,0:T(1,128)S(1)} %bitcast.8), channel_id=1, replica_groups=mesh['groups'=2,'wide'=4,'narrow'=4] {'wide','narrow'}, dimensions={0} | all-to-all | bytes 8192 | tf_op jit(solution)/shard_map/all_to_all | solution.py:700
  42.5 1.1 %pick_owned.1 = f32[1,392]{1,0:T(1,128)} custom-call(s32[8,128]{1,0:T(8,128)S(1)} %find_slots.1.slots_ref, f32[16,64]{1,0:T(8,128)S(1)} %bitcast.7), custom_call_target="tpu_custom_call" | custom-call | tf_op jit(solution)/shard_map/pick_owned/pallas_call | solution.py:701
  (4 shorter events, 0.0 us)
Async XLA Ops:
  1.9 17.1 %collective-permute-start = (f32[1064,128]{1,0:T(8,128)S(1)}, f32[1064,128]{1,0:T(8,128)S(1)}, u32[]{:S(2)}, u32[]{:S(2)}) collective-permute-start(f32[1064,128]{1,0:T(8,128)S(1)} %get-tuple-element.35), channel_id=1, source_target_pairs={{0,4},{4,0},{8,12},{12,8},{1,5},{5,1},{9,13},{13,9},{2,6},{6,2},{1... | collective-permute-start | bytes 1634312 | tf_op jit(solution)/shard_map/ppermute | solution.py:607
  2.4 16.6 %collective-permute-start.1 = (f32[664,128]{1,0:T(8,128)S(1)}, f32[664,128]{1,0:T(8,128)S(1)}, u32[]{:S(2)}, u32[]{:S(2)}) collective-permute-start(f32[664,128]{1,0:T(8,128)S(1)} %get-tuple-element.36.after_ref), channel_id=1, source_target_pairs={{0,12},{4,8},{8,4},{12,0},{1,13},{5,9},{9,5},{13,1},{2,14},{6,10},... | collective-permute-start | bytes 1019912 | tf_op jit(solution)/shard_map/ppermute | solution.py:607
  5.4 8.7 %collective-permute-start.2 = (f32[88,128]{1,0:T(8,128)S(1)}, f32[88,128]{1,0:T(8,128)S(1)}, u32[]{:S(2)}, u32[]{:S(2)}) collective-permute-start(f32[88,128]{1,0:T(8,128)S(1)} %get-tuple-element.39), channel_id=1, source_target_pairs={{0,1},{1,0},{2,3},{3,2},{4,5},{5,4},{6,7},{7,6},{8,9},{9,8},{10,11... | collective-permute-start | bytes 135176 | tf_op jit(solution)/shard_map/ppermute | solution.py:607
  7.1 7.0 %collective-permute-start.3 = (f32[88,128]{1,0:T(8,128)S(1)}, f32[88,128]{1,0:T(8,128)S(1)}, u32[]{:S(2)}, u32[]{:S(2)}) collective-permute-start(f32[88,128]{1,0:T(8,128)S(1)} %get-tuple-element.40), channel_id=1, source_target_pairs={{0,3},{1,2},{2,1},{3,0},{4,7},{5,6},{6,5},{7,4},{8,11},{9,10},{10,... | collective-permute-start | bytes 135176 | tf_op jit(solution)/shard_map/ppermute | solution.py:607
  9.5 4.5 %collective-permute-start.4 = (f32[16,128]{1,0:T(8,128)S(1)}, f32[16,128]{1,0:T(8,128)S(1)}, u32[]{:S(2)}, u32[]{:S(2)}) collective-permute-start(f32[16,128]{1,0:T(8,128)S(1)} %get-tuple-element.41.block_ref), channel_id=1, source_target_pairs={{0,2},{1,3},{2,0},{3,1},{4,6},{5,7},{6,4},{7,5},{8,10},{9,11},{10,... | collective-permute-start | bytes 24584 | tf_op jit(solution)/shard_map/ppermute | solution.py:602
  14.2 2.4 %collective-permute-start.5 = (f32[88,128]{1,0:T(8,128)S(1)}, f32[88,128]{1,0:T(8,128)S(1)}, u32[]{:S(2)}, u32[]{:S(2)}) collective-permute-start(f32[88,128]{1,0:T(8,128)S(1)} %get-tuple-element.42), channel_id=1, source_target_pairs={{0,4},{4,0},{8,12},{12,8},{1,5},{5,1},{9,13},{13,9},{2,6},{6,2},{1... | collective-permute-start | bytes 135176 | tf_op jit(solution)/shard_map/ppermute | solution.py:607
  14.3 4.3 %collective-permute-start.6 = (f32[88,128]{1,0:T(8,128)S(1)}, f32[88,128]{1,0:T(8,128)S(1)}, u32[]{:S(2)}, u32[]{:S(2)}) collective-permute-start(f32[88,128]{1,0:T(8,128)S(1)} %get-tuple-element.43), channel_id=1, source_target_pairs={{0,12},{4,8},{8,4},{12,0},{1,13},{5,9},{9,5},{13,1},{2,14},{6,10},... | collective-permute-start | bytes 135176 | tf_op jit(solution)/shard_map/ppermute | solution.py:607
  14.9 3.7 %collective-permute-start.7 = (f32[16,128]{1,0:T(8,128)S(1)}, f32[16,128]{1,0:T(8,128)S(1)}, u32[]{:S(2)}, u32[]{:S(2)}) collective-permute-start(f32[16,128]{1,0:T(8,128)S(1)} %get-tuple-element.46.after_ref.refs_0_), channel_id=1, source_target_pairs={{0,8},{4,12},{8,0},{12,4},{1,9},{5,13},{9,1},{13,5},{2,10},{6,14},... | collective-permute-start | bytes 24584 | tf_op jit(solution)/shard_map/ppermute | solution.py:602
  16.7 8.6 %collective-permute-start.8 = (f32[400,128]{1,0:T(8,128)S(1)}, f32[400,128]{1,0:T(8,128)S(1)}, u32[]{:S(2)}, u32[]{:S(2)}) collective-permute-start(f32[400,128]{1,0:T(8,128)S(1)} %pack_cot.1), channel_id=1, source_target_pairs={{0,12},{4,8},{8,4},{12,0},{1,13},{5,9},{9,5},{13,1},{2,14},{6,10},... | collective-permute-start | bytes 614408 | tf_op jit(solution)/shard_map/ppermute | solution.py:607

commit v16 on v15

--- a/solution.py
+++ b/solution.py
@@ -243,7 +243,7 @@
     for z in range(layers):
         for i in range(count):
             stores += body(z, i, jnp.minimum(start + 8 * i, most) + nothing)
-        if len(stores) >= 64 or z == layers - 1:
+        if len(stores) >= 16 or z == layers - 1:
             for store in stores:
                 store()
             stores = []

time: 43.8 us -> 43.8 us (level)
  no operation moved by 1% of the time
where the time goes in v16:
time: 43.8 us; the launch traced here: 43.6 us
  Pallas kernels  17 us (39%)
  blocking collectives  9.94 us (23%)
  starting transfers between devices  9.65 us (22%)
  waiting for transfers between devices  6.26 us (14%)
  between operations  0.72 us (2%)
    all_to_all x1, blocking collectives, per_device(): sums = lax.all_to_all(sums, both, 0, 0, tiled=True)  9.94 us
    ppermute x7, starting transfers between devices, swapped(): lax.ppermute(value, axis, [(i, (i + by) % count) for i, by in enumerate(s...  8.04 us
    pallas_call x1, Pallas kernels, per_device(): kernel(backward, (f32(*order_init.shape), f32(bricks, listed)), ([vmem(*p...  7.19 us
    pallas_call x1, Pallas kernels, per_device(): kernel(forward, (f32(*order_init.shape), [f32(*padded)] * ITERS, [f32(*pa...  6.34 us
    ppermute x2, waiting for transfers between devices, opposite(): return lax.ppermute(value, axis, [(i, (i + 2) % 4) for i in range(4)])  6.24 us
    ppermute x2, starting transfers between devices, opposite(): return lax.ppermute(value, axis, [(i, (i + 2) % 4) for i in range(4)])  1.61 us
    pallas_call x1, Pallas kernels, per_device(): kernel(pack_rows, tuple((jax.ShapeDtypeStruct(x.shape, x.dtype) for x in...  1.24 us
    pallas_call x1, Pallas kernels, per_device(): kernel(functools.partial(pick_owned, owned), f32(1, owned), (vmem(owned +...  1.13 us
  transfers between devices with their start and end apart: 9, of which 2 were waited for; matrix products, arithmetic and copies ran while one was open for 0% of the time, Pallas kernels for 17%

profile of v16, /device:TPU:0, one launch (start us, length us, event | category | flops | bytes accessed | tf_op | source)
XLA Modules:
  0.0 43.6 jit_solution(10062281611872604028)
XLA Ops:
  0.6 1.2 %pack_rows.1 = (f32[8,12,8,128]{3,2,1,0:T(8,128)S(1)}, s32[12,8,128]{2,1,0:T(8,128)S(1)}, f32[8,12,8,128]{3,2,1,0:T(8,128)S(1)}, f32[1,392]{1,0:T(1,128)S(1)}, s...) custom-call(f32[8,12,8,128]{3,2,1,0:T(8,128)} %refs_0_.1, ...), custom_call_target="tpu_custom_call" | custom-call | tf_op jit(solution)/shard_map/pack_rows/pallas_call | solution.py:634
  1.9 0.5 %collective-permute-start = (f32[1064,128]{1,0:T(8,128)S(1)}, f32[1064,128]{1,0:T(8,128)S(1)}, u32[]{:S(2)}, u32[]{:S(2)}) collective-permute-start(f32[1064,128]{1,0:T(8,128)S(1)} %get-tuple-element.35), channel_id=1, source_target_pairs={{0,4},{4,0},{8,12},{12,8},{1,5},{5,1},{9,13},{13,9},{2,6},{6,2},{1... | collective-permute-start | bytes 1634312 | tf_op jit(solution)/shard_map/ppermute | solution.py:607
  2.4 2.6 %collective-permute-start.1 = (f32[664,128]{1,0:T(8,128)S(1)}, f32[664,128]{1,0:T(8,128)S(1)}, u32[]{:S(2)}, u32[]{:S(2)}) collective-permute-start(f32[664,128]{1,0:T(8,128)S(1)} %get-tuple-element.36.after_ref), channel_id=1, source_target_pairs={{0,12},{4,8},{8,4},{12,0},{1,13},{5,9},{9,5},{13,1},{2,14},{6,10},... | collective-permute-start | bytes 1019912 | tf_op jit(solution)/shard_map/ppermute | solution.py:607
  5.0 0.4 pack_strips.1
  5.4 1.6 %collective-permute-start.2 = (f32[88,128]{1,0:T(8,128)S(1)}, f32[88,128]{1,0:T(8,128)S(1)}, u32[]{:S(2)}, u32[]{:S(2)}) collective-permute-start(f32[88,128]{1,0:T(8,128)S(1)} %get-tuple-element.39), channel_id=1, source_target_pairs={{0,1},{1,0},{2,3},{3,2},{4,5},{5,4},{6,7},{7,6},{8,9},{9,8},{10,11... | collective-permute-start | bytes 135176 | tf_op jit(solution)/shard_map/ppermute | solution.py:607
  7.1 2.5 %collective-permute-start.3 = (f32[88,128]{1,0:T(8,128)S(1)}, f32[88,128]{1,0:T(8,128)S(1)}, u32[]{:S(2)}, u32[]{:S(2)}) collective-permute-start(f32[88,128]{1,0:T(8,128)S(1)} %get-tuple-element.40), channel_id=1, source_target_pairs={{0,3},{1,2},{2,1},{3,0},{4,7},{5,6},{6,5},{7,4},{8,11},{9,10},{10,... | collective-permute-start | bytes 135176 | tf_op jit(solution)/shard_map/ppermute | solution.py:607
  9.5 0.1 collective-permute-start.4
  9.6 4.4 %collective-permute-done.4.refs_0_ = f32[16,128]{1,0:T(8,128)S(1)} collective-permute-done((f32[16,128]{1,0:T(8,128)S(1)}, f32[16,128]{1,0:T(8,128)S(1)}, u32[]{:S(2)}, u32[]{:S(2)}) %collective-permute-start.4) | collective-permute-done | bytes 8224 | tf_op jit(solution)/shard_map/ppermute | solution.py:602
  14.1 0.0 collective-permute-done.2.strip_a_ref
  14.1 0.0 collective-permute-done.3.strip_b_ref
  14.1 0.1 pack_far.1
  14.2 0.1 collective-permute-start.5
  14.3 0.7 %collective-permute-start.6 = (f32[88,128]{1,0:T(8,128)S(1)}, f32[88,128]{1,0:T(8,128)S(1)}, u32[]{:S(2)}, u32[]{:S(2)}) collective-permute-start(f32[88,128]{1,0:T(8,128)S(1)} %get-tuple-element.43), channel_id=1, source_target_pairs={{0,12},{4,8},{8,4},{12,0},{1,13},{5,9},{9,5},{13,1},{2,14},{6,10},... | collective-permute-start | bytes 135176 | tf_op jit(solution)/shard_map/ppermute | solution.py:607
  14.9 1.5 %collective-permute-start.7 = (f32[16,128]{1,0:T(8,128)S(1)}, f32[16,128]{1,0:T(8,128)S(1)}, u32[]{:S(2)}, u32[]{:S(2)}) collective-permute-start(f32[16,128]{1,0:T(8,128)S(1)} %get-tuple-element.46.after_ref.refs_0_), channel_id=1, source_target_pairs={{0,8},{4,12},{8,0},{12,4},{1,9},{5,13},{9,1},{13,5},{2,10},{6,14},... | collective-permute-start | bytes 24584 | tf_op jit(solution)/shard_map/ppermute | solution.py:602
  16.4 0.2 find_slots.1.slots_ref
  16.6 0.0 collective-permute-done.5.refs_1_.far_a_ref.after_ref
  16.6 0.1 pack_cot.1
  16.7 0.1 collective-permute-start.8
  16.8 1.8 %collective-permute-done.7.refs_3_ = f32[16,128]{1,0:T(8,128)S(1)} collective-permute-done((f32[16,128]{1,0:T(8,128)S(1)}, f32[16,128]{1,0:T(8,128)S(1)}, u32[]{:S(2)}, u32[]{:S(2)}) %collective-permute-start.7) | collective-permute-done | bytes 8224 | tf_op jit(solution)/shard_map/ppermute | solution.py:602
  18.6 0.4 find_mobility.1.table_ref
  19.0 6.3 %forward.1 = (f32[8,12,8,128]{3,2,1,0:T(8,128)}, f32[8,12,24,128]{3,2,1,0:T(8,128)S(1)}, f32[8,12,24,128]{3,2,1,0:T(8,128)S(1)}, f32[8,12,24,128]{3,2,1,0:T(8,12...) custom-call(f32[8,12,8,128]{3,2,1,0:T(8,128)S(1)} %get-tuple-element, ...), custom_call_target="tpu_custom_call" | custom-call | tf_op jit(solution)/shard_map/forward/pallas_call | solution.py:678
  25.3 7.2 %backward.1 = (f32[8,12,8,128]{3,2,1,0:T(8,128)}, f32[16,64]{1,0:T(8,128)S(1)}) custom-call(f32[8,12,8,128]{3,2,1,0:T(8,128)S(1)} %get-tuple-element.37.cot_ref, s32[12,8,128]{2,1,0:T(8,128)S(1)} %get-tuple-element.34.map_ref, f32[1064,128]{1,0:T(8,128)S(1)} %collective-permute-done.row_a_ref, f32[400,128]{1,0:T(8,128)S(1)} %collective-permute-done.8.row_b_ref, ...), custom_call_target="tpu_custom_call" | custom-call | tf_op jit(solution)/shard_map/backward/pallas_call | solution.py:687
  32.5 9.9 %all_to_all.11 = f32[16,1,64]{2,1,0:T(1,128)S(1)} all-to-all(f32[16,1,64]{2,1,0:T(1,128)S(1)} %bitcast.8), channel_id=1, replica_groups=mesh['groups'=2,'wide'=4,'narrow'=4] {'wide','narrow'}, dimensions={0} | all-to-all | bytes 8192 | tf_op jit(solution)/shard_map/all_to_all | solution.py:700
  42.4 1.1 %pick_owned.1 = f32[1,392]{1,0:T(1,128)} custom-call(s32[8,128]{1,0:T(8,128)S(1)} %find_slots.1.slots_ref, f32[16,64]{1,0:T(8,128)S(1)} %bitcast.7), custom_call_target="tpu_custom_call" | custom-call | tf_op jit(solution)/shard_map/pick_owned/pallas_call | solution.py:701
  (4 shorter events, 0.0 us)
Async XLA Ops:
  1.9 17.1 %collective-permute-start = (f32[1064,128]{1,0:T(8,128)S(1)}, f32[1064,128]{1,0:T(8,128)S(1)}, u32[]{:S(2)}, u32[]{:S(2)}) collective-permute-start(f32[1064,128]{1,0:T(8,128)S(1)} %get-tuple-element.35), channel_id=1, source_target_pairs={{0,4},{4,0},{8,12},{12,8},{1,5},{5,1},{9,13},{13,9},{2,6},{6,2},{1... | collective-permute-start | bytes 1634312 | tf_op jit(solution)/shard_map/ppermute | solution.py:607
  2.4 16.6 %collective-permute-start.1 = (f32[664,128]{1,0:T(8,128)S(1)}, f32[664,128]{1,0:T(8,128)S(1)}, u32[]{:S(2)}, u32[]{:S(2)}) collective-permute-start(f32[664,128]{1,0:T(8,128)S(1)} %get-tuple-element.36.after_ref), channel_id=1, source_target_pairs={{0,12},{4,8},{8,4},{12,0},{1,13},{5,9},{9,5},{13,1},{2,14},{6,10},... | collective-permute-start | bytes 1019912 | tf_op jit(solution)/shard_map/ppermute | solution.py:607
  5.4 8.7 %collective-permute-start.2 = (f32[88,128]{1,0:T(8,128)S(1)}, f32[88,128]{1,0:T(8,128)S(1)}, u32[]{:S(2)}, u32[]{:S(2)}) collective-permute-start(f32[88,128]{1,0:T(8,128)S(1)} %get-tuple-element.39), channel_id=1, source_target_pairs={{0,1},{1,0},{2,3},{3,2},{4,5},{5,4},{6,7},{7,6},{8,9},{9,8},{10,11... | collective-permute-start | bytes 135176 | tf_op jit(solution)/shard_map/ppermute | solution.py:607
  7.1 7.0 %collective-permute-start.3 = (f32[88,128]{1,0:T(8,128)S(1)}, f32[88,128]{1,0:T(8,128)S(1)}, u32[]{:S(2)}, u32[]{:S(2)}) collective-permute-start(f32[88,128]{1,0:T(8,128)S(1)} %get-tuple-element.40), channel_id=1, source_target_pairs={{0,3},{1,2},{2,1},{3,0},{4,7},{5,6},{6,5},{7,4},{8,11},{9,10},{10,... | collective-permute-start | bytes 135176 | tf_op jit(solution)/shard_map/ppermute | solution.py:607
  9.5 4.5 %collective-permute-start.4 = (f32[16,128]{1,0:T(8,128)S(1)}, f32[16,128]{1,0:T(8,128)S(1)}, u32[]{:S(2)}, u32[]{:S(2)}) collective-permute-start(f32[16,128]{1,0:T(8,128)S(1)} %get-tuple-element.41.block_ref), channel_id=1, source_target_pairs={{0,2},{1,3},{2,0},{3,1},{4,6},{5,7},{6,4},{7,5},{8,10},{9,11},{10,... | collective-permute-start | bytes 24584 | tf_op jit(solution)/shard_map/ppermute | solution.py:602
  14.2 2.4 %collective-permute-start.5 = (f32[88,128]{1,0:T(8,128)S(1)}, f32[88,128]{1,0:T(8,128)S(1)}, u32[]{:S(2)}, u32[]{:S(2)}) collective-permute-start(f32[88,128]{1,0:T(8,128)S(1)} %get-tuple-element.42), channel_id=1, source_target_pairs={{0,4},{4,0},{8,12},{12,8},{1,5},{5,1},{9,13},{13,9},{2,6},{6,2},{1... | collective-permute-start | bytes 135176 | tf_op jit(solution)/shard_map/ppermute | solution.py:607
  14.3 4.3 %collective-permute-start.6 = (f32[88,128]{1,0:T(8,128)S(1)}, f32[88,128]{1,0:T(8,128)S(1)}, u32[]{:S(2)}, u32[]{:S(2)}) collective-permute-start(f32[88,128]{1,0:T(8,128)S(1)} %get-tuple-element.43), channel_id=1, source_target_pairs={{0,12},{4,8},{8,4},{12,0},{1,13},{5,9},{9,5},{13,1},{2,14},{6,10},... | collective-permute-start | bytes 135176 | tf_op jit(solution)/shard_map/ppermute | solution.py:607
  14.9 3.7 %collective-permute-start.7 = (f32[16,128]{1,0:T(8,128)S(1)}, f32[16,128]{1,0:T(8,128)S(1)}, u32[]{:S(2)}, u32[]{:S(2)}) collective-permute-start(f32[16,128]{1,0:T(8,128)S(1)} %get-tuple-element.46.after_ref.refs_0_), channel_id=1, source_target_pairs={{0,8},{4,12},{8,0},{12,4},{1,9},{5,13},{9,1},{13,5},{2,10},{6,14},... | collective-permute-start | bytes 24584 | tf_op jit(solution)/shard_map/ppermute | solution.py:602
  16.7 8.6 %collective-permute-start.8 = (f32[400,128]{1,0:T(8,128)S(1)}, f32[400,128]{1,0:T(8,128)S(1)}, u32[]{:S(2)}, u32[]{:S(2)}) collective-permute-start(f32[400,128]{1,0:T(8,128)S(1)} %pack_cot.1), channel_id=1, source_target_pairs={{0,12},{4,8},{8,4},{12,0},{1,13},{5,9},{9,5},{13,1},{2,14},{6,10},... | collective-permute-start | bytes 614408 | tf_op jit(solution)/shard_map/ppermute | solution.py:607
